TPU v7x, 32 devices: a whole 2x2x4 slice. The times are simulated.
32 devices in a mesh: lat: 4 (over y, core), lon: 8 (over z, x).
Axes of the slice: x: 2, y: 2, z: 4, core: 2. Of those that a mesh axis runs over, the one named last changes fastest.
Arguments:
- latent: bfloat16 [8, 96, 640], P('lat', 'lon'), may hold values from -6 to 6
- lon_filter: bfloat16 [9, 96], replicated, may hold values from -0.625 to 0.625
- mix_weight: bfloat16 [9, 640, 20], P(None, 'lon'), may hold values from -1.25 to 1.25
- band_weight: bfloat16 [9, 8, 3], P(None, 'lat'), may hold values from -1.25 to 1.25
- offsets: int32 [8], P('lat'), may hold values from -2 to 7, as said below
- w_up: bfloat16 [640, 1280], replicated, may hold values from -0.25 to 0.25
- w_down: bfloat16 [1280, 640], replicated, may hold values from -0.15625 to 0.15625
Outputs:
- result: bfloat16 [8, 96, 640], P('lat', 'lon')
Inputs may be any that keep to these rules, and one draw needn't show every extreme that they name: offsets[i] - i lies between -2 and 0, so a band's rows lie within 2 rows of its output row; in every aligned block of 2 rows the first row's band starts 2 rows below it and the last row's band ends 2 rows above it.
All inputs are finite; a program needn't handle non-finite values.
Results may differ from a plain program's by a relative error of at most 0.0095.
Values may be sent and summed in bfloat16 or wider, within the bound.
No kernel may reach another device: no remote copies, remote signals or barrier semaphores. Data moves between devices by JAX's collectives and lax.ppermute only.
A program may use at most 128 MiB of HBM per device.

v0:
```python
import functools

import jax
import jax.numpy as jnp
from jax import lax
from jax.experimental import pallas as pl
from jax.experimental.pallas import tpu as pltpu
from jax.sharding import PartitionSpec as P

F32 = jnp.float32
BF16 = jnp.bfloat16
LANES = 128
SUBLANES = 8


def up_to(size, step):
    return -(-size // step) * step


def column_and_side():
    place = lax.axis_index("lon")
    return place // 2, place % 2


def message_rows(block):
    tiles = block // LANES
    return up_to(3 * SUBLANES * tiles + (SUBLANES if block % LANES else 0), 2 * SUBLANES)


def lanes_of(block):
    return up_to(block, LANES)


def fold(points, block):
    whole, rest = divmod(block, LANES)
    parts = [points[:, tile * LANES : (tile + 1) * LANES] for tile in range(whole)]
    if rest:
        odd = points[:, whole * LANES : (whole + 1) * LANES]
        kept = lax.broadcasted_iota(jnp.int32, (SUBLANES, LANES), 1) < rest
        shared = None
        for third in range(3):
            piece = jnp.where(kept, odd[third * SUBLANES : (third + 1) * SUBLANES], 0.0)
            piece = pltpu.roll(piece, third * rest, 1) if third else piece
            shared = piece if shared is None else shared + piece
        parts.append(shared)
    filled = sum(part.shape[0] for part in parts)
    if message_rows(block) > filled:
        parts.append(jnp.zeros((message_rows(block) - filled, LANES), F32))
    return jnp.concatenate(parts, axis=0).astype(BF16)


def unfold(message, block):
    whole, rest = divmod(block, LANES)
    groups = []
    for third in range(3):
        first = third * SUBLANES
        parts = [
            message[tile * 3 * SUBLANES + first : tile * 3 * SUBLANES + first + SUBLANES]
            for tile in range(whole)
        ]
        if rest:
            odd = message[whole * 3 * SUBLANES : whole * 3 * SUBLANES + SUBLANES]
            parts.append(pltpu.roll(odd, LANES - third * rest, 1) if third else odd)
        groups.append(jnp.concatenate(parts, axis=1) if len(parts) > 1 else parts[0])
    return groups


def group_points(latent_ref, points):
    width, rows, _ = latent_ref.shape
    rest = width - SUBLANES
    for row in range(rows):
        points[row * SUBLANES : (row + 1) * SUBLANES] = latent_ref[:SUBLANES, row, :].astype(F32)
        at = rows * SUBLANES + row * rest
        points[at : at + rest] = latent_ref[SUBLANES:, row, :].astype(F32)


def pack_kernel(latent_ref, *refs):
    *out_refs, points, stage = refs
    columns = len(out_refs)
    chans = latent_ref.shape[2]
    block = chans // columns
    column, _ = column_and_side()
    group_points(latent_ref, points)
    own = points[...]
    for target in range(columns):
        turned = pltpu.roll(own, chans - target * block, 1) if target else own
        stage[target] = fold(turned[:, : lanes_of(block)], block)
    for apart in range(columns):
        out_refs[apart][...] = stage[column ^ apart]


def column_kernel(order, *refs):
    *in_refs, out_ref = refs
    column, _ = column_and_side()
    for apart, ref in zip(order, in_refs):
        out_ref[column ^ apart] = ref[...]


def sides_kernel(own_ref, mate_ref, out_ref):
    _, side = column_and_side()
    out_ref[:, side] = own_ref[...]
    out_ref[:, 1 - side] = mate_ref[...]


def tables_kernel(width, filter_ref, band_ref, table_ref, first):
    bases, lons = filter_ref.shape
    taps, rows, _ = band_ref.shape
    step, places = first.shape[1:]
    columns = places // (2 * step)
    _, side = column_and_side()
    lat = lax.axis_index("lat")
    below = (lat > 0).astype(F32)
    above = (lat < lax.axis_size("lat") - 1).astype(F32)
    inside = [[below, below, 1.0], [1.0, above, above]]
    slots = [[0, 1, 2], [2, 0, 1]]
    profile = filter_ref[...]
    band = band_ref[...].astype(F32)
    source = lax.broadcasted_iota(jnp.int32, (lons, places), 0)
    place = lax.broadcasted_iota(jnp.int32, (lons, places), 1)
    within = place % step
    apart = source + (place // step) * width + within + (lons - side * width)
    for _ in range(3):
        apart = jnp.where(apart >= lons, apart - lons, apart)
    apart = jnp.where(within < width, apart, -1)
    first[...] = jnp.zeros_like(first)
    for lon in range(width):
        pick = (apart == lon).astype(F32).astype(BF16)
        first[:, lon, :] = jnp.dot(profile, pick, preferred_element_type=F32)
    for basis in range(bases):
        circle = first[basis]
        for column in range(columns):
            turned = pltpu.roll(circle, column * 2 * step, 1) if column else circle
            at = (basis * columns + column) * step
            for row in range(rows):
                for tap in range(taps):
                    weight = band[tap, row : row + 1, basis : basis + 1] * inside[row][tap]
                    to = slots[row][tap] * places
                    table_ref[row, at : at + step, to : to + places] = (weight * turned).astype(
                        BF16
                    )


def squares_kernel(own_ref, mate_ref, squares_ref, padded):
    bases, group, half = own_ref.shape
    lanes = squares_ref.shape[1]
    _, side = column_and_side()
    first = side == 0
    own = own_ref[...].astype(F32)
    mate = mate_ref[...].astype(F32)
    padded[...] = jnp.zeros_like(padded)
    padded[0, :, :group, :half] = jnp.where(first, own, mate)
    padded[1, :, :group, :half] = jnp.where(first, mate, own)
    members = padded.shape[2]
    into = lax.broadcasted_iota(jnp.int32, (lanes, members), 0)
    member = lax.broadcasted_iota(jnp.int32, (lanes, members), 1)
    repeat = (into % group == member).astype(F32).astype(BF16)
    row = lax.broadcasted_iota(jnp.int32, (lanes, lanes), 0)
    column = lax.broadcasted_iota(jnp.int32, (lanes, lanes), 1)
    same = (row // group == column // group) & (row < 2 * half) & (column < 2 * half)
    for basis in range(bases):
        weights = padded[0, basis] + pltpu.roll(padded[1, basis], half, 1)
        repeated = jnp.dot(repeat, weights.astype(BF16), preferred_element_type=F32)
        squares_ref[basis * lanes : (basis + 1) * lanes] = jnp.where(same, repeated, 0.0).astype(
            BF16
        )


def rows_of(message, block, rest):
    groups = unfold(message.astype(F32), block)
    last = (groups[2], pltpu.roll(groups[2], SUBLANES - rest, 0))
    return [jnp.concatenate([groups[row], last[row]], axis=0).astype(BF16) for row in range(2)]


def unpack_kernel(block, width, own_ref, out_ref):
    for at in range(own_ref.shape[0]):
        for row, read in enumerate(rows_of(own_ref[at], block, width - SUBLANES)):
            out_ref[row, at] = read


def conv_kernel(block, width, *refs):
    odd_mate, odd_own, even, mate, own, table_ref, squares_ref, *refs = refs
    *out_refs, field, spread, stage = refs
    columns = len(out_refs)
    lanes = squares_ref.shape[1]
    bases = squares_ref.shape[0] // lanes
    rows, _, inner = table_ref.shape
    places = inner // 3
    step = places // (2 * columns)
    half = places // 2
    rest = width - SUBLANES
    column, side = column_and_side()
    odd = lax.axis_index("lat") % 2

    def place(row, slot, at, read):
        first = pl.multiple_of(slot * places + at * step, step)
        field[row, pl.ds(first, step)] = read

    for at in range(columns):
        for row in range(rows):
            place(row, 2, 2 * at + side, own[row, at])
        for row, read in enumerate(rows_of(mate[at], block, rest)):
            place(row, 2, 2 * at + 1 - side, read)
        for half_at in range(2):
            for slot, read in enumerate(rows_of(even[at, half_at], block, rest)):
                place(1 - odd, slot, 2 * at + half_at, read)
        for message_side, ref in ((side, odd_own), (1 - side, odd_mate)):
            for slot, read in enumerate(rows_of(ref[at], block, rest)):
                place(odd, slot, 2 * at + message_side, read)
    for row in range(rows):
        over = jnp.dot(table_ref[row], field[row], preferred_element_type=F32).astype(BF16)
        for basis in range(bases):
            spread[row * half : (row + 1) * half, basis * lanes : (basis + 1) * lanes] = over[
                basis * half : (basis + 1) * half
            ]
    mixed = jnp.dot(spread[...], squares_ref[...], preferred_element_type=F32)
    upper = lax.broadcasted_iota(jnp.int32, (SUBLANES, lanes), 0) < rest
    for target in range(columns):
        top = mixed[target * step : (target + 1) * step]
        bottom = mixed[half + target * step : half + (target + 1) * step]
        last = jnp.where(upper, top[SUBLANES:], pltpu.roll(bottom[SUBLANES:], rest, 0))
        points = jnp.concatenate([top[:SUBLANES], bottom[:SUBLANES], last], axis=0)
        stage[target] = fold(points, block)
    for apart in range(columns):
        out_refs[apart][...] = stage[column ^ apart]


def tail_kernel(order, *refs):
    columns = len(order)
    back_refs = refs[:columns]
    latent_ref, up_ref, down_ref, out_ref, points, stage = refs[columns:]
    width, rows, chans = latent_ref.shape
    rest = width - SUBLANES
    block = chans // columns
    lanes = lanes_of(block)
    column, _ = column_and_side()
    for apart, ref in zip(order, back_refs):
        stage[column ^ apart] = ref[...]
    group_points(latent_ref, points)
    kept = lax.broadcasted_iota(jnp.int32, (3 * SUBLANES, lanes), 1) < block
    convolved = None
    for target in range(columns):
        piece = jnp.concatenate(unfold(stage[target].astype(F32), block), axis=0)
        piece = jnp.where(kept, piece, 0.0)
        if chans > lanes:
            gap = jnp.zeros((3 * SUBLANES, chans - lanes), F32)
            piece = jnp.concatenate([piece, gap], axis=1)
        piece = pltpu.roll(piece, target * block, 1) if target else piece
        convolved = piece if convolved is None else convolved + piece
    summed = (points[...] + convolved).astype(BF16).astype(F32)
    centred = summed - jnp.mean(summed, axis=1, keepdims=True)
    variance = jnp.mean(centred * centred, axis=1, keepdims=True)
    normed = (centred * lax.rsqrt(variance + 1e-05)).astype(BF16)
    hidden = jnp.dot(normed, up_ref[...], preferred_element_type=F32)
    hidden = (0.5 * hidden * (1.0 + lax.erf(hidden * 0.5**0.5))).astype(BF16)
    result = summed + jnp.dot(hidden, down_ref[...], preferred_element_type=F32)
    for row in range(rows):
        out_ref[:SUBLANES, row, :] = result[row * SUBLANES : (row + 1) * SUBLANES].astype(BF16)
        at = rows * SUBLANES + row * rest
        out_ref[SUBLANES:, row, :] = result[at : at + rest].astype(BF16)


VMEM = pl.BlockSpec(memory_space=pltpu.VMEM)


def call(kernel, name, out_shape, scratch, work, *operands):
    several = isinstance(out_shape, tuple)
    return pl.pallas_call(
        kernel,
        out_shape=out_shape,
        in_specs=[VMEM] * len(operands),
        out_specs=(VMEM,) * len(out_shape) if several else VMEM,
        scratch_shapes=scratch,
        compiler_params=pltpu.CompilerParams(vmem_limit_bytes=24 * 2**20),
        cost_estimate=pl.CostEstimate(flops=work, bytes_accessed=10**6, transcendentals=0),
        name=name,
    )(*operands)


def over_columns(messages, count):
    arrived = {0: messages[0]}
    for apart in reversed(range(1, count // 2)):
        pairs = [(i, ((i // 2) ^ apart) * 2 + i % 2) for i in range(count)]
        arrived[apart] = lax.ppermute(messages[apart], "lon", pairs)
    return arrived


def over_sides(block, count):
    return lax.ppermute(block, "lon", [(i, i ^ 1) for i in range(count)])


def swap(block, count, partner):
    pairs = []
    for lat in range(lax.axis_size("lat")):
        for lon in range(count):
            to_lat, to_lon = partner(lat, lon)
            pairs.append((lat * count + lon, to_lat * count + to_lon))
    return lax.ppermute(block, ("lat", "lon"), pairs)


def odd_pair(lat, lon, to_lon, rows):
    to = lat + 1 if lat % 2 else lat - 1
    return (to, to_lon) if 0 <= to < rows else (lat, lon ^ 1)


def local(latent, lon_filter, mix_weight, band_weight, offsets, w_up, w_down):
    rows, width, chans = latent.shape
    bases, lons = lon_filter.shape
    half, group = mix_weight.shape[1:]
    taps = band_weight.shape[2]
    count = lons // width
    columns = count // 2
    block = 2 * half
    step = up_to(width, 2 * SUBLANES)
    places = count * step
    lanes = lanes_of(block)
    height = message_rows(block)
    assert rows == 2 and taps == 3 and columns & (columns - 1) == 0
    assert lax.axis_size("lat") % 2 == 0
    assert SUBLANES < width and rows * (width - SUBLANES) <= SUBLANES
    assert 3 * (block % LANES) <= LANES

    far_first = tuple(reversed(range(columns)))
    last_first = (far_first[1:-1] + far_first[:1] + (0,)) if columns > 2 else far_first
    message = jax.ShapeDtypeStruct((height, LANES), BF16)
    messages = (message,) * columns
    stage = pltpu.VMEM((columns, height, LANES), BF16)
    points = pltpu.VMEM((3 * SUBLANES, chans), F32)
    lon_first = jnp.transpose(latent, (1, 0, 2))
    mix_own = jnp.transpose(mix_weight, (0, 2, 1))

    packed = call(pack_kernel, "pack", messages, [points, stage], 10**9, lon_first)
    arrived = over_columns(packed, count)
    mix_mate = over_sides(mix_own, count)
    table = call(
        functools.partial(tables_kernel, width),
        "tables",
        jax.ShapeDtypeStruct((rows, bases * places // 2, taps * places), BF16),
        [pltpu.VMEM((bases, step, places), F32)],
        10**9,
        lon_filter,
        jnp.transpose(band_weight, (2, 1, 0)),
    )
    squares = call(
        squares_kernel,
        "squares",
        jax.ShapeDtypeStruct((bases * lanes, lanes), BF16),
        [pltpu.VMEM((2, bases, up_to(group, 2 * SUBLANES), lanes), F32)],
        10**9,
        mix_own,
        mix_mate,
    )
    gathered = jax.ShapeDtypeStruct((columns, height, LANES), BF16)
    own_side = call(
        functools.partial(column_kernel, far_first),
        "join_columns",
        gathered,
        [],
        10**8,
        *[arrived[apart] for apart in far_first],
    )
    lats = lax.axis_size("lat")
    mate_side = swap(own_side, count, lambda lat, lon: (lat, lon ^ 1))
    odd_mate = swap(own_side, count, lambda lat, lon: odd_pair(lat, lon, lon ^ 1, lats))
    odd_own = swap(own_side, count, lambda lat, lon: odd_pair(lat, lon, lon, lats))
    own_rows = call(
        functools.partial(unpack_kernel, block, width),
        "unpack",
        jax.ShapeDtypeStruct((rows, columns, step, lanes), BF16),
        [],
        10**9,
        own_side,
    )
    circle = jax.ShapeDtypeStruct((columns, 2, height, LANES), BF16)
    home = call(sides_kernel, "join_sides", circle, [], 10**8, own_side, mate_side)
    even = swap(home, count, lambda lat, lon: (lat ^ 1, lon))
    mixed = call(
        functools.partial(conv_kernel, block, width),
        "conv",
        messages,
        [
            pltpu.VMEM((rows, taps * places, lanes), BF16),
            pltpu.VMEM((rows * places // 2, bases * lanes), BF16),
            stage,
        ],
        10**10,
        odd_mate,
        odd_own,
        even,
        mate_side,
        own_rows,
        table,
        squares,
    )
    back = over_columns(mixed, count)
    result = call(
        functools.partial(tail_kernel, last_first),
        "tail",
        jax.ShapeDtypeStruct(lon_first.shape, BF16),
        [points, stage],
        10**9,
        *[back[apart] for apart in last_first],
        lon_first,
        w_up,
        w_down,
    )
    return jnp.transpose(result, (1, 0, 2))


def solution(mesh):
    return jax.shard_map(
        local,
        mesh=mesh,
        in_specs=(
            P("lat", "lon", None),
            P(),
            P(None, "lon", None),
            P(None, "lat", None),
            P("lat"),
            P(),
            P(),
        ),
        out_specs=P("lat", "lon", None),
        check_vma=False,
    )
```

profile of v0, /device:TPU:0, one launch (start us, length us, event | category | flops | bytes accessed | tf_op | source)
XLA Modules:
  0.0 25.8 jit_solution(2982094426818876801)
XLA Ops:
  0.0 0.0 copy-start.3
  0.0 0.8 %copy-done.3 = bf16[2,12,640]{2,0,1:T(2,128)(2,1)S(1)} copy-done((bf16[2,12,640]{2,0,1:T(2,128)(2,1)S(1)}, bf16[2,12,640]{2,0,1:T(2,128)(2,1)}, u32[]{:S(2)}) %copy-start.3) | copy-done | bytes 30744
  0.8 0.0 copy-start.2
  0.8 0.0 copy-start.5
  0.8 0.0 copy-start.6
  0.8 0.2 pack.1
  0.9 5.1 %collective-permute-start = (bf16[32,128]{1,0:T(8,128)(2,1)S(1)}, bf16[32,128]{1,0:T(8,128)(2,1)S(1)}, u32[]{:S(2)}, u32[]{:S(2)}) collective-permute-start(bf16[32,128]{1,0:T(8,128)(2,1)S(1)} %get-tuple-element.13), channel_id=1, source_target_pairs={{0,6},{1,7},{2,4},{3,5},{4,2},{5,3},{6,0},{7,1},{8,14},{9,15},{10,... | collective-permute-start | bytes 24584 | tf_op jit(solution)/shard_map/ppermute | solution.py:283
  6.1 0.0 collective-permute-start.1
  6.1 0.6 %collective-permute-start.2 = (bf16[32,128]{1,0:T(8,128)(2,1)S(1)}, bf16[32,128]{1,0:T(8,128)(2,1)S(1)}, u32[]{:S(2)}, u32[]{:S(2)}) collective-permute-start(bf16[32,128]{1,0:T(8,128)(2,1)S(1)} %get-tuple-element.15), channel_id=1, source_target_pairs={{0,2},{1,3},{2,0},{3,1},{4,6},{5,7},{6,4},{7,5},{8,10},{9,11},{10,... | collective-permute-start | bytes 24584 | tf_op jit(solution)/shard_map/ppermute | solution.py:283
  6.7 0.0 copy-done.2
  6.7 1.6 %collective-permute-start.7 = (bf16[9,20,80]{2,1,0:T(8,128)(2,1)S(1)}, bf16[9,20,80]{2,1,0:T(8,128)(2,1)S(1)}, u32[]{:S(2)}, u32[]{:S(2)}) collective-permute-start(bf16[9,20,80]{2,1,0:T(8,128)(2,1)S(1)} %bitcast.4), channel_id=1, source_target_pairs={{0,1},{1,0},{2,3},{3,2},{4,5},{5,4},{6,7},{7,6},{8,9},{9,8},{10,11... | collective-permute-start | bytes 86408 | tf_op jit(solution)/shard_map/ppermute | solution.py:288
  8.3 0.0 copy-done.5
  8.3 0.0 copy-done.6
  8.3 0.4 %tables.1.refs_5_ = bf16[2,576,384]{2,1,0:T(8,128)(2,1)S(1)} custom-call(bf16[9,96]{1,0:T(8,128)(2,1)S(1)} %copy-done.5, bf16[3,2,9]{2,1,0:T(2,128)(2,1)S(1)} %bitcast.8), custom_call_target="tpu_custom_call" | custom-call | flops 1000000000 | bytes 1000000 | tf_op jit(solution)/shard_map/tables/pallas_call | solution.py:267
  8.7 0.0 collective-permute-done.refs_0_
  8.8 1.8 %collective-permute-done.1.refs_1_ = bf16[32,128]{1,0:T(8,128)(2,1)S(1)} collective-permute-done((bf16[32,128]{1,0:T(8,128)(2,1)S(1)}, bf16[32,128]{1,0:T(8,128)(2,1)S(1)}, u32[]{:S(2)}, u32[]{:S(2)}) %collective-permute-start.1) | collective-permute-done | bytes 8224 | tf_op jit(solution)/shard_map/ppermute | solution.py:283
  10.6 0.0 collective-permute-done.2.refs_2_
  10.6 1.6 %collective-permute-start.5 = (bf16[4,32,128]{2,1,0:T(8,128)(2,1)S(1)}, bf16[4,32,128]{2,1,0:T(8,128)(2,1)S(1)}, u32[]{:S(2)}, u32[]{:S(2)}) collective-permute-start(bf16[4,32,128]{2,1,0:T(8,128)(2,1)S(1)} %join_columns.1.own_ref), channel_id=1, source_target_pairs={{0,1},{1,0},{2,3},{3,2},{4,5},{5,4},{6,7},{7,6},{8,9},{9,8},{10,11... | collective-permute-start | bytes 98312 | tf_op jit(solution)/shard_map/ppermute | solution.py:297
  12.2 0.1 unpack.1.refs_4_
  12.2 0.5 %collective-permute-start.3 = (bf16[4,32,128]{2,1,0:T(8,128)(2,1)S(1)}, bf16[4,32,128]{2,1,0:T(8,128)(2,1)S(1)}, u32[]{:S(2)}, u32[]{:S(2)}) collective-permute-start(bf16[4,32,128]{2,1,0:T(8,128)(2,1)S(1)} %join_columns.1.own_ref), channel_id=1, source_target_pairs={{0,1},{1,0},{2,3},{3,2},{4,5},{5,4},{6,7},{7,6},{8,17},{9,16},{10,... | collective-permute-start | bytes 98312 | tf_op jit(solution)/shard_map/ppermute | solution.py:297
  12.8 1.5 %collective-permute-start.4 = (bf16[4,32,128]{2,1,0:T(8,128)(2,1)S(1)}, bf16[4,32,128]{2,1,0:T(8,128)(2,1)S(1)}, u32[]{:S(2)}, u32[]{:S(2)}) collective-permute-start(bf16[4,32,128]{2,1,0:T(8,128)(2,1)S(1)} %join_columns.1.own_ref), channel_id=1, source_target_pairs={{0,1},{1,0},{2,3},{3,2},{4,5},{5,4},{6,7},{7,6},{8,16},{9,17},{10,... | collective-permute-start | bytes 98312 | tf_op jit(solution)/shard_map/ppermute | solution.py:297
  14.3 0.3 %collective-permute-done.5.mate_ref.refs_3_ = bf16[4,32,128]{2,1,0:T(8,128)(2,1)S(1)} collective-permute-done((bf16[4,32,128]{2,1,0:T(8,128)(2,1)S(1)}, bf16[4,32,128]{2,1,0:T(8,128)(2,1)S(1)}, u32[]{:S(2)}, u32[]{:S(2)}) %collective-permute-start.5) | collective-permute-done | bytes 32800 | tf_op jit(solution)/shard_map/ppermute | solution.py:297
  14.6 0.1 collective-permute-start.6
  14.7 0.0 collective-permute-done.7.mate_ref
  14.7 0.5 %squares.1.refs_6_ = bf16[2304,256]{1,0:T(8,128)(2,1)S(1)} custom-call(bf16[9,20,80]{2,1,0:T(8,128)(2,1)S(1)} %bitcast.5, bf16[9,20,80]{2,1,0:T(8,128)(2,1)S(1)} %collective-permute-done.7.mate_ref), custom_call_target="tpu_custom_call" | custom-call | flops 1000000000 | bytes 1000000 | tf_op jit(solution)/shard_map/squares/pallas_call | solution.py:267
  15.3 0.0 copy-start
  15.3 0.0 copy-start.1
  15.3 0.0 copy-start.4
  15.3 0.9 %collective-permute-done.3.refs_0_ = bf16[4,32,128]{2,1,0:T(8,128)(2,1)S(1)} collective-permute-done((bf16[4,32,128]{2,1,0:T(8,128)(2,1)S(1)}, bf16[4,32,128]{2,1,0:T(8,128)(2,1)S(1)}, u32[]{:S(2)}, u32[]{:S(2)}) %collective-permute-start.3) | collective-permute-done | bytes 32800 | tf_op jit(solution)/shard_map/ppermute | solution.py:297
  16.2 0.7 %collective-permute-done.4.refs_1_ = bf16[4,32,128]{2,1,0:T(8,128)(2,1)S(1)} collective-permute-done((bf16[4,32,128]{2,1,0:T(8,128)(2,1)S(1)}, bf16[4,32,128]{2,1,0:T(8,128)(2,1)S(1)}, u32[]{:S(2)}, u32[]{:S(2)}) %collective-permute-start.4) | collective-permute-done | bytes 32800 | tf_op jit(solution)/shard_map/ppermute | solution.py:297
  16.9 0.0 collective-permute-done.6.refs_2_
  16.9 1.1 %conv.1 = (bf16[32,128]{1,0:T(8,128)(2,1)S(1)}, bf16[32,128]{1,0:T(8,128)(2,1)S(1)}, bf16[32,128]{1,0:T(8,128)(2,1)S(1)}, bf16[32,128]{1,0:T(8,128)(2,1)S(1)}) custom-call(bf16[4,32,128]{2,1,0:T(8,128)(2,1)S(1)} %collective-permute-done.3.refs_0_, bf16[4,32,128]{2,1,0:T(8,128)(2,1)S(1)} %collective-permute-done.4.refs_1_, ...), custom_call_target="tpu_custom_call" | custom-call | flops 10000000000 | bytes 1000000 | tf_op jit(solution)/shard_map/conv/pallas_call | solution.py:267
  18.0 1.7 %collective-permute-start.10 = (bf16[32,128]{1,0:T(8,128)(2,1)S(1)}, bf16[32,128]{1,0:T(8,128)(2,1)S(1)}, u32[]{:S(2)}, u32[]{:S(2)}) collective-permute-start(bf16[32,128]{1,0:T(8,128)(2,1)S(1)} %get-tuple-element.19), channel_id=1, source_target_pairs={{0,6},{1,7},{2,4},{3,5},{4,2},{5,3},{6,0},{7,1},{8,14},{9,15},{10,... | collective-permute-start | bytes 24584 | tf_op jit(solution)/shard_map/ppermute | solution.py:283
  19.6 0.4 %collective-permute-start.8 = (bf16[32,128]{1,0:T(8,128)(2,1)S(1)}, bf16[32,128]{1,0:T(8,128)(2,1)S(1)}, u32[]{:S(2)}, u32[]{:S(2)}) collective-permute-start(bf16[32,128]{1,0:T(8,128)(2,1)S(1)} %get-tuple-element.17), channel_id=1, source_target_pairs={{0,4},{1,5},{2,6},{3,7},{4,0},{5,1},{6,2},{7,3},{8,12},{9,13},{10,... | collective-permute-start | bytes 24584 | tf_op jit(solution)/shard_map/ppermute | solution.py:283
  20.1 2.4 %collective-permute-start.9 = (bf16[32,128]{1,0:T(8,128)(2,1)S(1)}, bf16[32,128]{1,0:T(8,128)(2,1)S(1)}, u32[]{:S(2)}, u32[]{:S(2)}) collective-permute-start(bf16[32,128]{1,0:T(8,128)(2,1)S(1)} %get-tuple-element.18), channel_id=1, source_target_pairs={{0,2},{1,3},{2,0},{3,1},{4,6},{5,7},{6,4},{7,5},{8,10},{9,11},{10,... | collective-permute-start | bytes 24584 | tf_op jit(solution)/shard_map/ppermute | solution.py:283
  22.4 1.1 %collective-permute-done.10.refs_2_ = bf16[32,128]{1,0:T(8,128)(2,1)S(1)} collective-permute-done((bf16[32,128]{1,0:T(8,128)(2,1)S(1)}, bf16[32,128]{1,0:T(8,128)(2,1)S(1)}, u32[]{:S(2)}, u32[]{:S(2)}) %collective-permute-start.10) | collective-permute-done | bytes 8224 | tf_op jit(solution)/shard_map/ppermute | solution.py:283
  23.5 0.7 %collective-permute-done.8.refs_0_ = bf16[32,128]{1,0:T(8,128)(2,1)S(1)} collective-permute-done((bf16[32,128]{1,0:T(8,128)(2,1)S(1)}, bf16[32,128]{1,0:T(8,128)(2,1)S(1)}, u32[]{:S(2)}, u32[]{:S(2)}) %collective-permute-start.8) | collective-permute-done | bytes 8224 | tf_op jit(solution)/shard_map/ppermute | solution.py:283
  24.2 0.0 collective-permute-done.9.refs_1_
  24.2 0.0 copy-done
  24.2 0.0 copy-done.1
  24.2 0.0 copy-done.4
  24.2 1.6 %tail.1 = bf16[12,2,640]{2,1,0:T(2,128)(2,1)} custom-call(bf16[32,128]{1,0:T(8,128)(2,1)S(1)} %collective-permute-done.8.refs_0_, bf16[32,128]{1,0:T(8,128)(2,1)S(1)} %collective-permute-done.9.refs_1_, bf16[32,128]{1,0:T(8,128)(2,1)S(1)} %collective-permute-done.10.refs_2_, bf16[32,128]{1,0:T(8,128)(2,1)S(1)} %get-tuple-element.20.refs_3_, ...), custom_call_target="tpu_custom_call" | custom-call | flops 1000000000 | bytes 1000000 | tf_op jit(solution)/shard_map/tail/pallas_call | solution.py:267
  (2 shorter events, 0.0 us)
Async XLA Ops:
  0.0 0.8 %copy-start.3 = (bf16[2,12,640]{2,0,1:T(2,128)(2,1)S(1)}, bf16[2,12,640]{2,0,1:T(2,128)(2,1)}, u32[]{:S(2)}) copy-start(bf16[2,12,640]{2,0,1:T(2,128)(2,1)} %param.7) | copy-start | bytes 92164
  0.8 5.9 %copy-start.2 = (bf16[9,80,20]{1,2,0:T(8,128)(2,1)S(1)}, bf16[9,80,20]{1,2,0:T(8,128)(2,1)}, u32[]{:S(2)}) copy-start(bf16[9,80,20]{1,2,0:T(8,128)(2,1)} %param.9) | copy-start | bytes 86404
  0.8 7.6 %copy-start.5 = (bf16[9,96]{1,0:T(8,128)(2,1)S(1)}, bf16[9,96]{1,0:T(8,128)(2,1)}, u32[]{:S(2)}) copy-start(bf16[9,96]{1,0:T(8,128)(2,1)} %filter_ref.1) | copy-start | bytes 5188
  0.8 7.6 %copy-start.6 = (bf16[9,2,3]{0,1,2:T(2,128)(2,1)S(1)}, bf16[9,2,3]{0,1,2:T(2,128)(2,1)}, u32[]{:S(2)}) copy-start(bf16[9,2,3]{0,1,2:T(2,128)(2,1)} %param.10) | copy-start | bytes 328
  0.9 7.8 %collective-permute-start = (bf16[32,128]{1,0:T(8,128)(2,1)S(1)}, bf16[32,128]{1,0:T(8,128)(2,1)S(1)}, u32[]{:S(2)}, u32[]{:S(2)}) collective-permute-start(bf16[32,128]{1,0:T(8,128)(2,1)S(1)} %get-tuple-element.13), channel_id=1, source_target_pairs={{0,6},{1,7},{2,4},{3,5},{4,2},{5,3},{6,0},{7,1},{8,14},{9,15},{10,... | collective-permute-start | bytes 24584 | tf_op jit(solution)/shard_map/ppermute | solution.py:283
  6.1 4.5 %collective-permute-start.1 = (bf16[32,128]{1,0:T(8,128)(2,1)S(1)}, bf16[32,128]{1,0:T(8,128)(2,1)S(1)}, u32[]{:S(2)}, u32[]{:S(2)}) collective-permute-start(bf16[32,128]{1,0:T(8,128)(2,1)S(1)} %get-tuple-element.14), channel_id=1, source_target_pairs={{0,4},{1,5},{2,6},{3,7},{4,0},{5,1},{6,2},{7,3},{8,12},{9,13},{10,... | collective-permute-start | bytes 24584 | tf_op jit(solution)/shard_map/ppermute | solution.py:283
  6.1 4.5 %collective-permute-start.2 = (bf16[32,128]{1,0:T(8,128)(2,1)S(1)}, bf16[32,128]{1,0:T(8,128)(2,1)S(1)}, u32[]{:S(2)}, u32[]{:S(2)}) collective-permute-start(bf16[32,128]{1,0:T(8,128)(2,1)S(1)} %get-tuple-element.15), channel_id=1, source_target_pairs={{0,2},{1,3},{2,0},{3,1},{4,6},{5,7},{6,4},{7,5},{8,10},{9,11},{10,... | collective-permute-start | bytes 24584 | tf_op jit(solution)/shard_map/ppermute | solution.py:283
  6.7 8.0 %collective-permute-start.7 = (bf16[9,20,80]{2,1,0:T(8,128)(2,1)S(1)}, bf16[9,20,80]{2,1,0:T(8,128)(2,1)S(1)}, u32[]{:S(2)}, u32[]{:S(2)}) collective-permute-start(bf16[9,20,80]{2,1,0:T(8,128)(2,1)S(1)} %bitcast.4), channel_id=1, source_target_pairs={{0,1},{1,0},{2,3},{3,2},{4,5},{5,4},{6,7},{7,6},{8,9},{9,8},{10,11... | collective-permute-start | bytes 86408 | tf_op jit(solution)/shard_map/ppermute | solution.py:288
  10.6 4.0 %collective-permute-start.5 = (bf16[4,32,128]{2,1,0:T(8,128)(2,1)S(1)}, bf16[4,32,128]{2,1,0:T(8,128)(2,1)S(1)}, u32[]{:S(2)}, u32[]{:S(2)}) collective-permute-start(bf16[4,32,128]{2,1,0:T(8,128)(2,1)S(1)} %join_columns.1.own_ref), channel_id=1, source_target_pairs={{0,1},{1,0},{2,3},{3,2},{4,5},{5,4},{6,7},{7,6},{8,9},{9,8},{10,11... | collective-permute-start | bytes 98312 | tf_op jit(solution)/shard_map/ppermute | solution.py:297
  12.2 3.9 %collective-permute-start.3 = (bf16[4,32,128]{2,1,0:T(8,128)(2,1)S(1)}, bf16[4,32,128]{2,1,0:T(8,128)(2,1)S(1)}, u32[]{:S(2)}, u32[]{:S(2)}) collective-permute-start(bf16[4,32,128]{2,1,0:T(8,128)(2,1)S(1)} %join_columns.1.own_ref), channel_id=1, source_target_pairs={{0,1},{1,0},{2,3},{3,2},{4,5},{5,4},{6,7},{7,6},{8,17},{9,16},{10,... | collective-permute-start | bytes 98312 | tf_op jit(solution)/shard_map/ppermute | solution.py:297
  12.8 4.1 %collective-permute-start.4 = (bf16[4,32,128]{2,1,0:T(8,128)(2,1)S(1)}, bf16[4,32,128]{2,1,0:T(8,128)(2,1)S(1)}, u32[]{:S(2)}, u32[]{:S(2)}) collective-permute-start(bf16[4,32,128]{2,1,0:T(8,128)(2,1)S(1)} %join_columns.1.own_ref), channel_id=1, source_target_pairs={{0,1},{1,0},{2,3},{3,2},{4,5},{5,4},{6,7},{7,6},{8,16},{9,17},{10,... | collective-permute-start | bytes 98312 | tf_op jit(solution)/shard_map/ppermute | solution.py:297
  14.6 2.3 %collective-permute-start.6 = (bf16[4,2,32,128]{3,2,1,0:T(8,128)(2,1)S(1)}, bf16[4,2,32,128]{3,2,1,0:T(8,128)(2,1)S(1)}, u32[]{:S(2)}, u32[]{:S(2)}) collective-permute-start(bf16[4,2,32,128]{3,2,1,0:T(8,128)(2,1)S(1)} %join_sides.1), channel_id=1, source_target_pairs={{0,8},{1,9},{2,10},{3,11},{4,12},{5,13},{6,14},{7,15},{8,0},{9,1},... | collective-permute-start | bytes 196616 | tf_op jit(solution)/shard_map/ppermute | solution.py:297
  15.3 8.9 %copy-start = (bf16[640,1280]{1,0:T(8,128)(2,1)S(1)}, bf16[640,1280]{1,0:T(8,128)(2,1)}, u32[]{:S(2)}) copy-start(bf16[640,1280]{1,0:T(8,128)(2,1)} %refs_5_.1) | copy-start | bytes 4915204
  15.3 8.9 %copy-start.1 = (bf16[1280,640]{1,0:T(8,128)(2,1)S(1)}, bf16[1280,640]{1,0:T(8,128)(2,1)}, u32[]{:S(2)}) copy-start(bf16[1280,640]{1,0:T(8,128)(2,1)} %refs_6_.1) | copy-start | bytes 4915204
  15.3 8.9 %copy-start.4 = (bf16[2,12,640]{2,0,1:T(2,128)(2,1)S(1)}, bf16[2,12,640]{2,0,1:T(2,128)(2,1)}, u32[]{:S(2)}) copy-start(bf16[2,12,640]{2,0,1:T(2,128)(2,1)} %param.7) | copy-start | bytes 92164
  18.0 5.5 %collective-permute-start.10 = (bf16[32,128]{1,0:T(8,128)(2,1)S(1)}, bf16[32,128]{1,0:T(8,128)(2,1)S(1)}, u32[]{:S(2)}, u32[]{:S(2)}) collective-permute-start(bf16[32,128]{1,0:T(8,128)(2,1)S(1)} %get-tuple-element.19), channel_id=1, source_target_pairs={{0,6},{1,7},{2,4},{3,5},{4,2},{5,3},{6,0},{7,1},{8,14},{9,15},{10,... | collective-permute-start | bytes 24584 | tf_op jit(solution)/shard_map/ppermute | solution.py:283
  19.6 4.5 %collective-permute-start.8 = (bf16[32,128]{1,0:T(8,128)(2,1)S(1)}, bf16[32,128]{1,0:T(8,128)(2,1)S(1)}, u32[]{:S(2)}, u32[]{:S(2)}) collective-permute-start(bf16[32,128]{1,0:T(8,128)(2,1)S(1)} %get-tuple-element.17), channel_id=1, source_target_pairs={{0,4},{1,5},{2,6},{3,7},{4,0},{5,1},{6,2},{7,3},{8,12},{9,13},{10,... | collective-permute-start | bytes 24584 | tf_op jit(solution)/shard_map/ppermute | solution.py:283
  20.1 4.1 %collective-permute-start.9 = (bf16[32,128]{1,0:T(8,128)(2,1)S(1)}, bf16[32,128]{1,0:T(8,128)(2,1)S(1)}, u32[]{:S(2)}, u32[]{:S(2)}) collective-permute-start(bf16[32,128]{1,0:T(8,128)(2,1)S(1)} %get-tuple-element.18), channel_id=1, source_target_pairs={{0,2},{1,3},{2,0},{3,1},{4,6},{5,7},{6,4},{7,5},{8,10},{9,11},{10,... | collective-permute-start | bytes 24584 | tf_op jit(solution)/shard_map/ppermute | solution.py:283
where the time goes:
time: 26 us; the launch traced here: 25.8 us
  starting transfers between devices  15.5 us (60%)
  waiting for transfers between devices  5.54 us (21%)
  Pallas kernels  3.88 us (15%)
  local copies, waits for them, and re-layouts  0.78 us (3%)
    ppermute x6, starting transfers between devices, over_columns(): arrived[apart] = lax.ppermute(messages[apart], 'lon', pairs)  10.2 us
    pallas_call x8, Pallas kernels, call(): pl.pallas_call(kernel, out_shape=out_shape, in_specs=[VMEM] * len(operand...  3.88 us
    ppermute x4, starting transfers between devices, swap(): return lax.ppermute(block, ('lat', 'lon'), pairs)  3.66 us
    ppermute x6, waiting for transfers between devices, over_columns(): arrived[apart] = lax.ppermute(messages[apart], 'lon', pairs)  3.61 us
    ppermute x4, waiting for transfers between devices, swap(): return lax.ppermute(block, ('lat', 'lon'), pairs)  1.93 us
    ppermute x1, starting transfers between devices, over_sides(): return lax.ppermute(block, 'lon', [(i, i ^ 1) for i in range(count)])  1.63 us
    unnamed x14, local copies, waits for them, and re-layouts  0.78 us
  transfers between devices with their start and end apart: 11, of which 6 were waited for; matrix products, arithmetic and copies ran while one was open for 0% of the time, Pallas kernels for 4%

commit v1 on v0

--- a/solution.py
+++ b/solution.py
@@ -177,8 +177,25 @@
             out_ref[row, at] = read
 
 
-def conv_kernel(block, width, *refs):
-    odd_mate, odd_own, even, mate, own, table_ref, squares_ref, *refs = refs
+def own_kernel(block, width, mate, own, table_ref, part_ref, field):
+    rows, columns, step, _ = own.shape
+    places = field.shape[1]
+    side = lax.axis_index("lon") % 2
+    for at in range(columns):
+        first = pl.multiple_of((2 * at + side) * step, step)
+        other = pl.multiple_of((2 * at + 1 - side) * step, step)
+        for row, read in enumerate(rows_of(mate[at], block, width - SUBLANES)):
+            field[row, pl.ds(first, step)] = own[row, at]
+            field[row, pl.ds(other, step)] = read
+    for row in range(rows):
+        part_ref[row] = jnp.dot(
+            table_ref[row, :, 2 * places :], field[row], preferred_element_type=F32
+        )
+
+
+def conv_kernel(
+    block, width, odd_own, odd_mate, even, part_ref, table_ref, squares_ref, *refs
+):
     *out_refs, field, spread, stage = refs
     columns = len(out_refs)
     lanes = squares_ref.shape[1]
@@ -191,23 +208,21 @@
     column, side = column_and_side()
     odd = lax.axis_index("lat") % 2
 
-    def place(row, slot, at, read):
-        first = pl.multiple_of(slot * places + at * step, step)
-        field[row, pl.ds(first, step)] = read
+    def place(row, at, message):
+        for slot, read in enumerate(rows_of(message, block, rest)):
+            first = pl.multiple_of(slot * places + at * step, step)
+            field[row, pl.ds(first, step)] = read
 
     for at in range(columns):
-        for row in range(rows):
-            place(row, 2, 2 * at + side, own[row, at])
-        for row, read in enumerate(rows_of(mate[at], block, rest)):
-            place(row, 2, 2 * at + 1 - side, read)
-        for half_at in range(2):
-            for slot, read in enumerate(rows_of(even[at, half_at], block, rest)):
-                place(1 - odd, slot, 2 * at + half_at, read)
-        for message_side, ref in ((side, odd_own), (1 - side, odd_mate)):
-            for slot, read in enumerate(rows_of(ref[at], block, rest)):
-                place(odd, slot, 2 * at + message_side, read)
+        place(1 - odd, 2 * at, even[at, 0])
+        place(1 - odd, 2 * at + 1, even[at, 1])
+        place(odd, 2 * at + side, odd_own[at])
+        place(odd, 2 * at + 1 - side, odd_mate[at])
     for row in range(rows):
-        over = jnp.dot(table_ref[row], field[row], preferred_element_type=F32).astype(BF16)
+        over = jnp.dot(
+            table_ref[row, :, : 2 * places], field[row], preferred_element_type=F32
+        )
+        over = (over + part_ref[row]).astype(BF16)
         for basis in range(bases):
             spread[row * half : (row + 1) * half, basis * lanes : (basis + 1) * lanes] = over[
                 basis * half : (basis + 1) * half
@@ -320,7 +335,8 @@
     assert 3 * (block % LANES) <= LANES
 
     far_first = tuple(reversed(range(columns)))
-    last_first = (far_first[1:-1] + far_first[:1] + (0,)) if columns > 2 else far_first
+    if columns > 3:
+        far_first = (far_first[1], far_first[0]) + far_first[2:]
     message = jax.ShapeDtypeStruct((height, LANES), BF16)
     messages = (message,) * columns
     stage = pltpu.VMEM((columns, height, LANES), BF16)
@@ -340,15 +356,6 @@
         lon_filter,
         jnp.transpose(band_weight, (2, 1, 0)),
     )
-    squares = call(
-        squares_kernel,
-        "squares",
-        jax.ShapeDtypeStruct((bases * lanes, lanes), BF16),
-        [pltpu.VMEM((2, bases, up_to(group, 2 * SUBLANES), lanes), F32)],
-        10**9,
-        mix_own,
-        mix_mate,
-    )
     gathered = jax.ShapeDtypeStruct((columns, height, LANES), BF16)
     own_side = call(
         functools.partial(column_kernel, far_first),
@@ -373,32 +380,51 @@
     circle = jax.ShapeDtypeStruct((columns, 2, height, LANES), BF16)
     home = call(sides_kernel, "join_sides", circle, [], 10**8, own_side, mate_side)
     even = swap(home, count, lambda lat, lon: (lat ^ 1, lon))
+    mix_mate, _ = lax.optimization_barrier((mix_mate, home))
+    squares = call(
+        squares_kernel,
+        "squares",
+        jax.ShapeDtypeStruct((bases * lanes, lanes), BF16),
+        [pltpu.VMEM((2, bases, up_to(group, 2 * SUBLANES), lanes), F32)],
+        10**9,
+        mix_own,
+        mix_mate,
+    )
+    part = call(
+        functools.partial(own_kernel, block, width),
+        "conv_own",
+        jax.ShapeDtypeStruct((rows, bases * places // 2, lanes), F32),
+        [pltpu.VMEM((rows, places, lanes), BF16)],
+        10**9,
+        mate_side,
+        own_rows,
+        table,
+    )
     mixed = call(
         functools.partial(conv_kernel, block, width),
         "conv",
         messages,
         [
-            pltpu.VMEM((rows, taps * places, lanes), BF16),
+            pltpu.VMEM((rows, 2 * places, lanes), BF16),
             pltpu.VMEM((rows * places // 2, bases * lanes), BF16),
-            stage,
+            pltpu.VMEM((columns, height, LANES), BF16),
         ],
         10**10,
+        odd_own,
         odd_mate,
-        odd_own,
         even,
-        mate_side,
-        own_rows,
+        part,
         table,
         squares,
     )
     back = over_columns(mixed, count)
     result = call(
-        functools.partial(tail_kernel, last_first),
+        functools.partial(tail_kernel, far_first),
         "tail",
         jax.ShapeDtypeStruct(lon_first.shape, BF16),
         [points, stage],
         10**9,
-        *[back[apart] for apart in last_first],
+        *[back[apart] for apart in far_first],
         lon_first,
         w_up,
         w_down,

time: 26 us -> 26.1 us (level)
  starting transfers between devices: 15.5 us -> 14.4 us
  waiting for transfers between devices: 5.54 us -> 6.55 us
    ppermute x6, waiting for transfers between devices: 3.61 us -> 5.09 us  [over_columns(): arrived[apart] = lax.ppermute(messages[apart], 'lon', pairs)]
    ppermute x6, starting transfers between devices: 10.2 us -> 9.23 us  [over_columns(): arrived[apart] = lax.ppermute(messages[apart], 'lon', pairs)]
    ppermute x4, waiting for transfers between devices: 1.93 us -> 1.46 us  [swap(): return lax.ppermute(block, ('lat', 'lon'), pairs)]
    pallas_call x8 -> x9, Pallas kernels: 3.88 us -> 4.11 us  [call(): pl.pallas_call(kernel, out_shape=out_shape, in_specs=[VMEM] * len(operand...]
  transfers between devices with their start and end apart: 11 -> 11, of which waited for: 6 -> 6; matrix products, arithmetic and copies ran while one was open for 0% -> 0% of each run, Pallas kernels for 4% -> 5%
where the time goes in v1:
time: 26.1 us; the launch traced here: 25.9 us
  starting transfers between devices  14.4 us (55%)
  waiting for transfers between devices  6.55 us (25%)
  Pallas kernels  4.11 us (16%)
  local copies, waits for them, and re-layouts  0.78 us (3%)
    ppermute x6, starting transfers between devices, over_columns(): arrived[apart] = lax.ppermute(messages[apart], 'lon', pairs)  9.23 us
    ppermute x6, waiting for transfers between devices, over_columns(): arrived[apart] = lax.ppermute(messages[apart], 'lon', pairs)  5.09 us
    pallas_call x9, Pallas kernels, call(): pl.pallas_call(kernel, out_shape=out_shape, in_specs=[VMEM] * len(operand...  4.11 us
    ppermute x4, starting transfers between devices, swap(): return lax.ppermute(block, ('lat', 'lon'), pairs)  3.65 us
    ppermute x1, starting transfers between devices, over_sides(): return lax.ppermute(block, 'lon', [(i, i ^ 1) for i in range(count)])  1.49 us
    ppermute x4, waiting for transfers between devices, swap(): return lax.ppermute(block, ('lat', 'lon'), pairs)  1.46 us
    unnamed x14, local copies, waits for them, and re-layouts  0.78 us
  transfers between devices with their start and end apart: 11, of which 6 were waited for; matrix products, arithmetic and copies ran while one was open for 0% of the time, Pallas kernels for 5%

profile of v1, /device:TPU:0, one launch (start us, length us, event | category | flops | bytes accessed | tf_op | source)
XLA Modules:
  0.0 25.9 jit_solution(1962474726700592326)
XLA Ops:
  0.0 0.0 copy-start.3
  0.0 0.8 %copy-done.3 = bf16[2,12,640]{2,0,1:T(2,128)(2,1)S(1)} copy-done((bf16[2,12,640]{2,0,1:T(2,128)(2,1)S(1)}, bf16[2,12,640]{2,0,1:T(2,128)(2,1)}, u32[]{:S(2)}) %copy-start.3) | copy-done | bytes 30744
  0.8 0.0 copy-start.2
  0.8 0.0 copy-start.5
  0.8 0.0 copy-start.6
  0.8 0.2 pack.1
  0.9 4.1 %collective-permute-start = (bf16[32,128]{1,0:T(8,128)(2,1)S(1)}, bf16[32,128]{1,0:T(8,128)(2,1)S(1)}, u32[]{:S(2)}, u32[]{:S(2)}) collective-permute-start(bf16[32,128]{1,0:T(8,128)(2,1)S(1)} %get-tuple-element.14), channel_id=1, source_target_pairs={{0,4},{1,5},{2,6},{3,7},{4,0},{5,1},{6,2},{7,3},{8,12},{9,13},{10,... | collective-permute-start | bytes 24584 | tf_op jit(solution)/shard_map/ppermute | solution.py:298
  5.0 1.3 %collective-permute-start.1 = (bf16[32,128]{1,0:T(8,128)(2,1)S(1)}, bf16[32,128]{1,0:T(8,128)(2,1)S(1)}, u32[]{:S(2)}, u32[]{:S(2)}) collective-permute-start(bf16[32,128]{1,0:T(8,128)(2,1)S(1)} %get-tuple-element.15), channel_id=1, source_target_pairs={{0,6},{1,7},{2,4},{3,5},{4,2},{5,3},{6,0},{7,1},{8,14},{9,15},{10,... | collective-permute-start | bytes 24584 | tf_op jit(solution)/shard_map/ppermute | solution.py:298
  6.4 0.2 collective-permute-start.2
  6.6 0.0 copy-done.2
  6.6 1.5 %collective-permute-start.7 = (bf16[9,20,80]{2,1,0:T(8,128)(2,1)S(1)}, bf16[9,20,80]{2,1,0:T(8,128)(2,1)S(1)}, u32[]{:S(2)}, u32[]{:S(2)}) collective-permute-start(bf16[9,20,80]{2,1,0:T(8,128)(2,1)S(1)} %bitcast.4), channel_id=1, source_target_pairs={{0,1},{1,0},{2,3},{3,2},{4,5},{5,4},{6,7},{7,6},{8,9},{9,8},{10,11... | collective-permute-start | bytes 86408 | tf_op jit(solution)/shard_map/ppermute | solution.py:303
  8.1 0.0 copy-done.5
  8.1 0.0 copy-done.6
  8.1 0.4 %tables.1.table_ref = bf16[2,576,384]{2,1,0:T(8,128)(2,1)S(1)} custom-call(bf16[9,96]{1,0:T(8,128)(2,1)S(1)} %copy-done.5, bf16[3,2,9]{2,1,0:T(2,128)(2,1)S(1)} %bitcast.8), custom_call_target="tpu_custom_call" | custom-call | flops 1000000000 | bytes 1000000 | tf_op jit(solution)/shard_map/tables/pallas_call | solution.py:282
  8.5 0.0 collective-permute-done.refs_0_
  8.5 1.9 %collective-permute-done.1.refs_1_ = bf16[32,128]{1,0:T(8,128)(2,1)S(1)} collective-permute-done((bf16[32,128]{1,0:T(8,128)(2,1)S(1)}, bf16[32,128]{1,0:T(8,128)(2,1)S(1)}, u32[]{:S(2)}, u32[]{:S(2)}) %collective-permute-start.1) | collective-permute-done | bytes 8224 | tf_op jit(solution)/shard_map/ppermute | solution.py:298
  10.5 0.0 collective-permute-done.2.refs_2_
  10.5 1.6 %collective-permute-start.5 = (bf16[4,32,128]{2,1,0:T(8,128)(2,1)S(1)}, bf16[4,32,128]{2,1,0:T(8,128)(2,1)S(1)}, u32[]{:S(2)}, u32[]{:S(2)}) collective-permute-start(bf16[4,32,128]{2,1,0:T(8,128)(2,1)S(1)} %join_columns.1.own_ref), channel_id=1, source_target_pairs={{0,1},{1,0},{2,3},{3,2},{4,5},{5,4},{6,7},{7,6},{8,9},{9,8},{10,11... | collective-permute-start | bytes 98312 | tf_op jit(solution)/shard_map/ppermute | solution.py:312
  12.1 0.5 %collective-permute-start.4 = (bf16[4,32,128]{2,1,0:T(8,128)(2,1)S(1)}, bf16[4,32,128]{2,1,0:T(8,128)(2,1)S(1)}, u32[]{:S(2)}, u32[]{:S(2)}) collective-permute-start(bf16[4,32,128]{2,1,0:T(8,128)(2,1)S(1)} %join_columns.1.own_ref), channel_id=1, source_target_pairs={{0,1},{1,0},{2,3},{3,2},{4,5},{5,4},{6,7},{7,6},{8,17},{9,16},{10,... | collective-permute-start | bytes 98312 | tf_op jit(solution)/shard_map/ppermute | solution.py:312
  12.6 1.5 %collective-permute-start.3 = (bf16[4,32,128]{2,1,0:T(8,128)(2,1)S(1)}, bf16[4,32,128]{2,1,0:T(8,128)(2,1)S(1)}, u32[]{:S(2)}, u32[]{:S(2)}) collective-permute-start(bf16[4,32,128]{2,1,0:T(8,128)(2,1)S(1)} %join_columns.1.own_ref), channel_id=1, source_target_pairs={{0,1},{1,0},{2,3},{3,2},{4,5},{5,4},{6,7},{7,6},{8,16},{9,17},{10,... | collective-permute-start | bytes 98312 | tf_op jit(solution)/shard_map/ppermute | solution.py:312
  14.1 0.1 unpack.1.own
  14.2 0.3 %collective-permute-done.5.mate_ref.mate = bf16[4,32,128]{2,1,0:T(8,128)(2,1)S(1)} collective-permute-done((bf16[4,32,128]{2,1,0:T(8,128)(2,1)S(1)}, bf16[4,32,128]{2,1,0:T(8,128)(2,1)S(1)}, u32[]{:S(2)}, u32[]{:S(2)}) %collective-permute-start.5) | collective-permute-done | bytes 32800 | tf_op jit(solution)/shard_map/ppermute | solution.py:312
  14.5 0.1 collective-permute-start.6
  14.6 0.0 collective-permute-done.7.mate_ref
  14.6 0.6 %squares.1.squares_ref = bf16[2304,256]{1,0:T(8,128)(2,1)S(1)} custom-call(bf16[9,20,80]{2,1,0:T(8,128)(2,1)S(1)} %bitcast.5, bf16[9,20,80]{2,1,0:T(8,128)(2,1)S(1)} %collective-permute-done.7.mate_ref), custom_call_target="tpu_custom_call" | custom-call | flops 1000000000 | bytes 1000000 | tf_op jit(solution)/shard_map/squares/pallas_call | solution.py:282
  15.1 0.4 %conv_own.1.part_ref = f32[2,576,256]{2,1,0:T(8,128)S(1)} custom-call(bf16[4,32,128]{2,1,0:T(8,128)(2,1)S(1)} %collective-permute-done.5.mate_ref.mate, bf16[2,4,16,256]{3,2,1,0:T(8,128)(2,1)S(1)} %unpack.1.own, bf16[2,576,384]{2,1,0:T(8,128)(2,1)S(1)} %tables.1.table_ref), custom_call_target="tpu_custom_call" | custom-call | flops 1000000000 | bytes 1000000 | tf_op jit(solution)/shard_map/conv_own/pallas_call | solution.py:282
  15.5 0.0 copy-start
  15.5 0.0 copy-start.1
  15.5 0.0 copy-start.4
  15.6 0.4 %collective-permute-done.4.odd_mate = bf16[4,32,128]{2,1,0:T(8,128)(2,1)S(1)} collective-permute-done((bf16[4,32,128]{2,1,0:T(8,128)(2,1)S(1)}, bf16[4,32,128]{2,1,0:T(8,128)(2,1)S(1)}, u32[]{:S(2)}, u32[]{:S(2)}) %collective-permute-start.4) | collective-permute-done | bytes 32800 | tf_op jit(solution)/shard_map/ppermute | solution.py:312
  16.0 0.7 %collective-permute-done.3.odd_own = bf16[4,32,128]{2,1,0:T(8,128)(2,1)S(1)} collective-permute-done((bf16[4,32,128]{2,1,0:T(8,128)(2,1)S(1)}, bf16[4,32,128]{2,1,0:T(8,128)(2,1)S(1)}, u32[]{:S(2)}, u32[]{:S(2)}) %collective-permute-start.3) | collective-permute-done | bytes 32800 | tf_op jit(solution)/shard_map/ppermute | solution.py:312
  16.7 0.0 collective-permute-done.6.even
  16.7 0.9 %conv.1 = (bf16[32,128]{1,0:T(8,128)(2,1)S(1)}, bf16[32,128]{1,0:T(8,128)(2,1)S(1)}, bf16[32,128]{1,0:T(8,128)(2,1)S(1)}, bf16[32,128]{1,0:T(8,128)(2,1)S(1)}) custom-call(bf16[4,32,128]{2,1,0:T(8,128)(2,1)S(1)} %collective-permute-done.3.odd_own, bf16[4,32,128]{2,1,0:T(8,128)(2,1)S(1)} %collective-permute-done.4.odd_mate, ...), custom_call_target="tpu_custom_call" | custom-call | flops 10000000000 | bytes 1000000 | tf_op jit(solution)/shard_map/conv/pallas_call | solution.py:282
  17.6 1.2 %collective-permute-start.8 = (bf16[32,128]{1,0:T(8,128)(2,1)S(1)}, bf16[32,128]{1,0:T(8,128)(2,1)S(1)}, u32[]{:S(2)}, u32[]{:S(2)}) collective-permute-start(bf16[32,128]{1,0:T(8,128)(2,1)S(1)} %get-tuple-element.19), channel_id=1, source_target_pairs={{0,4},{1,5},{2,6},{3,7},{4,0},{5,1},{6,2},{7,3},{8,12},{9,13},{10,... | collective-permute-start | bytes 24584 | tf_op jit(solution)/shard_map/ppermute | solution.py:298
  18.9 1.0 %collective-permute-start.9 = (bf16[32,128]{1,0:T(8,128)(2,1)S(1)}, bf16[32,128]{1,0:T(8,128)(2,1)S(1)}, u32[]{:S(2)}, u32[]{:S(2)}) collective-permute-start(bf16[32,128]{1,0:T(8,128)(2,1)S(1)} %get-tuple-element.20), channel_id=1, source_target_pairs={{0,6},{1,7},{2,4},{3,5},{4,2},{5,3},{6,0},{7,1},{8,14},{9,15},{10,... | collective-permute-start | bytes 24584 | tf_op jit(solution)/shard_map/ppermute | solution.py:298
  19.8 1.3 %collective-permute-start.10 = (bf16[32,128]{1,0:T(8,128)(2,1)S(1)}, bf16[32,128]{1,0:T(8,128)(2,1)S(1)}, u32[]{:S(2)}, u32[]{:S(2)}) collective-permute-start(bf16[32,128]{1,0:T(8,128)(2,1)S(1)} %get-tuple-element.21), channel_id=1, source_target_pairs={{0,2},{1,3},{2,0},{3,1},{4,6},{5,7},{6,4},{7,5},{8,10},{9,11},{10,... | collective-permute-start | bytes 24584 | tf_op jit(solution)/shard_map/ppermute | solution.py:298
  21.2 1.1 %collective-permute-done.8.refs_0_ = bf16[32,128]{1,0:T(8,128)(2,1)S(1)} collective-permute-done((bf16[32,128]{1,0:T(8,128)(2,1)S(1)}, bf16[32,128]{1,0:T(8,128)(2,1)S(1)}, u32[]{:S(2)}, u32[]{:S(2)}) %collective-permute-start.8) | collective-permute-done | bytes 8224 | tf_op jit(solution)/shard_map/ppermute | solution.py:298
  22.2 2.1 %collective-permute-done.9.refs_1_ = bf16[32,128]{1,0:T(8,128)(2,1)S(1)} collective-permute-done((bf16[32,128]{1,0:T(8,128)(2,1)S(1)}, bf16[32,128]{1,0:T(8,128)(2,1)S(1)}, u32[]{:S(2)}, u32[]{:S(2)}) %collective-permute-start.9) | collective-permute-done | bytes 8224 | tf_op jit(solution)/shard_map/ppermute | solution.py:298
  24.3 0.0 collective-permute-done.10.refs_2_
  24.3 0.0 copy-done
  24.3 0.0 copy-done.1
  24.3 0.0 copy-done.4
  24.3 1.6 %tail.1 = bf16[12,2,640]{2,1,0:T(2,128)(2,1)} custom-call(bf16[32,128]{1,0:T(8,128)(2,1)S(1)} %collective-permute-done.8.refs_0_, bf16[32,128]{1,0:T(8,128)(2,1)S(1)} %collective-permute-done.9.refs_1_, bf16[32,128]{1,0:T(8,128)(2,1)S(1)} %collective-permute-done.10.refs_2_, bf16[32,128]{1,0:T(8,128)(2,1)S(1)} %get-tuple-element.22.refs_3_, ...), custom_call_target="tpu_custom_call" | custom-call | flops 1000000000 | bytes 1000000 | tf_op jit(solution)/shard_map/tail/pallas_call | solution.py:282
  (2 shorter events, 0.0 us)
Async XLA Ops:
  0.0 0.8 %copy-start.3 = (bf16[2,12,640]{2,0,1:T(2,128)(2,1)S(1)}, bf16[2,12,640]{2,0,1:T(2,128)(2,1)}, u32[]{:S(2)}) copy-start(bf16[2,12,640]{2,0,1:T(2,128)(2,1)} %param.7) | copy-start | bytes 92164
  0.8 5.9 %copy-start.2 = (bf16[9,80,20]{1,2,0:T(8,128)(2,1)S(1)}, bf16[9,80,20]{1,2,0:T(8,128)(2,1)}, u32[]{:S(2)}) copy-start(bf16[9,80,20]{1,2,0:T(8,128)(2,1)} %param.9) | copy-start | bytes 86404
  0.8 7.4 %copy-start.5 = (bf16[9,96]{1,0:T(8,128)(2,1)S(1)}, bf16[9,96]{1,0:T(8,128)(2,1)}, u32[]{:S(2)}) copy-start(bf16[9,96]{1,0:T(8,128)(2,1)} %filter_ref.1) | copy-start | bytes 5188
  0.8 7.4 %copy-start.6 = (bf16[9,2,3]{0,1,2:T(2,128)(2,1)S(1)}, bf16[9,2,3]{0,1,2:T(2,128)(2,1)}, u32[]{:S(2)}) copy-start(bf16[9,2,3]{0,1,2:T(2,128)(2,1)} %param.10) | copy-start | bytes 328
  0.9 7.6 %collective-permute-start = (bf16[32,128]{1,0:T(8,128)(2,1)S(1)}, bf16[32,128]{1,0:T(8,128)(2,1)S(1)}, u32[]{:S(2)}, u32[]{:S(2)}) collective-permute-start(bf16[32,128]{1,0:T(8,128)(2,1)S(1)} %get-tuple-element.14), channel_id=1, source_target_pairs={{0,4},{1,5},{2,6},{3,7},{4,0},{5,1},{6,2},{7,3},{8,12},{9,13},{10,... | collective-permute-start | bytes 24584 | tf_op jit(solution)/shard_map/ppermute | solution.py:298
  5.0 5.4 %collective-permute-start.1 = (bf16[32,128]{1,0:T(8,128)(2,1)S(1)}, bf16[32,128]{1,0:T(8,128)(2,1)S(1)}, u32[]{:S(2)}, u32[]{:S(2)}) collective-permute-start(bf16[32,128]{1,0:T(8,128)(2,1)S(1)} %get-tuple-element.15), channel_id=1, source_target_pairs={{0,6},{1,7},{2,4},{3,5},{4,2},{5,3},{6,0},{7,1},{8,14},{9,15},{10,... | collective-permute-start | bytes 24584 | tf_op jit(solution)/shard_map/ppermute | solution.py:298
  6.4 4.1 %collective-permute-start.2 = (bf16[32,128]{1,0:T(8,128)(2,1)S(1)}, bf16[32,128]{1,0:T(8,128)(2,1)S(1)}, u32[]{:S(2)}, u32[]{:S(2)}) collective-permute-start(bf16[32,128]{1,0:T(8,128)(2,1)S(1)} %get-tuple-element.16), channel_id=1, source_target_pairs={{0,2},{1,3},{2,0},{3,1},{4,6},{5,7},{6,4},{7,5},{8,10},{9,11},{10,... | collective-permute-start | bytes 24584 | tf_op jit(solution)/shard_map/ppermute | solution.py:298
  6.6 8.0 %collective-permute-start.7 = (bf16[9,20,80]{2,1,0:T(8,128)(2,1)S(1)}, bf16[9,20,80]{2,1,0:T(8,128)(2,1)S(1)}, u32[]{:S(2)}, u32[]{:S(2)}) collective-permute-start(bf16[9,20,80]{2,1,0:T(8,128)(2,1)S(1)} %bitcast.4), channel_id=1, source_target_pairs={{0,1},{1,0},{2,3},{3,2},{4,5},{5,4},{6,7},{7,6},{8,9},{9,8},{10,11... | collective-permute-start | bytes 86408 | tf_op jit(solution)/shard_map/ppermute | solution.py:303
  10.5 4.0 %collective-permute-start.5 = (bf16[4,32,128]{2,1,0:T(8,128)(2,1)S(1)}, bf16[4,32,128]{2,1,0:T(8,128)(2,1)S(1)}, u32[]{:S(2)}, u32[]{:S(2)}) collective-permute-start(bf16[4,32,128]{2,1,0:T(8,128)(2,1)S(1)} %join_columns.1.own_ref), channel_id=1, source_target_pairs={{0,1},{1,0},{2,3},{3,2},{4,5},{5,4},{6,7},{7,6},{8,9},{9,8},{10,11... | collective-permute-start | bytes 98312 | tf_op jit(solution)/shard_map/ppermute | solution.py:312
  12.1 3.9 %collective-permute-start.4 = (bf16[4,32,128]{2,1,0:T(8,128)(2,1)S(1)}, bf16[4,32,128]{2,1,0:T(8,128)(2,1)S(1)}, u32[]{:S(2)}, u32[]{:S(2)}) collective-permute-start(bf16[4,32,128]{2,1,0:T(8,128)(2,1)S(1)} %join_columns.1.own_ref), channel_id=1, source_target_pairs={{0,1},{1,0},{2,3},{3,2},{4,5},{5,4},{6,7},{7,6},{8,17},{9,16},{10,... | collective-permute-start | bytes 98312 | tf_op jit(solution)/shard_map/ppermute | solution.py:312
  12.6 4.1 %collective-permute-start.3 = (bf16[4,32,128]{2,1,0:T(8,128)(2,1)S(1)}, bf16[4,32,128]{2,1,0:T(8,128)(2,1)S(1)}, u32[]{:S(2)}, u32[]{:S(2)}) collective-permute-start(bf16[4,32,128]{2,1,0:T(8,128)(2,1)S(1)} %join_columns.1.own_ref), channel_id=1, source_target_pairs={{0,1},{1,0},{2,3},{3,2},{4,5},{5,4},{6,7},{7,6},{8,16},{9,17},{10,... | collective-permute-start | bytes 98312 | tf_op jit(solution)/shard_map/ppermute | solution.py:312
  14.5 2.2 %collective-permute-start.6 = (bf16[4,2,32,128]{3,2,1,0:T(8,128)(2,1)S(1)}, bf16[4,2,32,128]{3,2,1,0:T(8,128)(2,1)S(1)}, u32[]{:S(2)}, u32[]{:S(2)}) collective-permute-start(bf16[4,2,32,128]{3,2,1,0:T(8,128)(2,1)S(1)} %join_sides.1), channel_id=1, source_target_pairs={{0,8},{1,9},{2,10},{3,11},{4,12},{5,13},{6,14},{7,15},{8,0},{9,1},... | collective-permute-start | bytes 196616 | tf_op jit(solution)/shard_map/ppermute | solution.py:312
  15.5 8.8 %copy-start = (bf16[640,1280]{1,0:T(8,128)(2,1)S(1)}, bf16[640,1280]{1,0:T(8,128)(2,1)}, u32[]{:S(2)}) copy-start(bf16[640,1280]{1,0:T(8,128)(2,1)} %refs_5_.1) | copy-start | bytes 4915204
  15.5 8.8 %copy-start.1 = (bf16[1280,640]{1,0:T(8,128)(2,1)S(1)}, bf16[1280,640]{1,0:T(8,128)(2,1)}, u32[]{:S(2)}) copy-start(bf16[1280,640]{1,0:T(8,128)(2,1)} %refs_6_.1) | copy-start | bytes 4915204
  15.5 8.8 %copy-start.4 = (bf16[2,12,640]{2,0,1:T(2,128)(2,1)S(1)}, bf16[2,12,640]{2,0,1:T(2,128)(2,1)}, u32[]{:S(2)}) copy-start(bf16[2,12,640]{2,0,1:T(2,128)(2,1)} %param.7) | copy-start | bytes 92164
  17.6 4.6 %collective-permute-start.8 = (bf16[32,128]{1,0:T(8,128)(2,1)S(1)}, bf16[32,128]{1,0:T(8,128)(2,1)S(1)}, u32[]{:S(2)}, u32[]{:S(2)}) collective-permute-start(bf16[32,128]{1,0:T(8,128)(2,1)S(1)} %get-tuple-element.19), channel_id=1, source_target_pairs={{0,4},{1,5},{2,6},{3,7},{4,0},{5,1},{6,2},{7,3},{8,12},{9,13},{10,... | collective-permute-start | bytes 24584 | tf_op jit(solution)/shard_map/ppermute | solution.py:298
  18.9 5.4 %collective-permute-start.9 = (bf16[32,128]{1,0:T(8,128)(2,1)S(1)}, bf16[32,128]{1,0:T(8,128)(2,1)S(1)}, u32[]{:S(2)}, u32[]{:S(2)}) collective-permute-start(bf16[32,128]{1,0:T(8,128)(2,1)S(1)} %get-tuple-element.20), channel_id=1, source_target_pairs={{0,6},{1,7},{2,4},{3,5},{4,2},{5,3},{6,0},{7,1},{8,14},{9,15},{10,... | collective-permute-start | bytes 24584 | tf_op jit(solution)/shard_map/ppermute | solution.py:298
  19.8 4.5 %collective-permute-start.10 = (bf16[32,128]{1,0:T(8,128)(2,1)S(1)}, bf16[32,128]{1,0:T(8,128)(2,1)S(1)}, u32[]{:S(2)}, u32[]{:S(2)}) collective-permute-start(bf16[32,128]{1,0:T(8,128)(2,1)S(1)} %get-tuple-element.21), channel_id=1, source_target_pairs={{0,2},{1,3},{2,0},{3,1},{4,6},{5,7},{6,4},{7,5},{8,10},{9,11},{10,... | collective-permute-start | bytes 24584 | tf_op jit(solution)/shard_map/ppermute | solution.py:298

commit v2 on v1

--- a/solution.py
+++ b/solution.py
@@ -261,11 +261,19 @@
             piece = jnp.concatenate([piece, gap], axis=1)
         piece = pltpu.roll(piece, target * block, 1) if target else piece
         convolved = piece if convolved is None else convolved + piece
-    summed = (points[...] + convolved).astype(BF16).astype(F32)
-    centred = summed - jnp.mean(summed, axis=1, keepdims=True)
-    variance = jnp.mean(centred * centred, axis=1, keepdims=True)
-    normed = (centred * lax.rsqrt(variance + 1e-05)).astype(BF16)
-    hidden = jnp.dot(normed, up_ref[...], preferred_element_type=F32)
+    summed = (points[...] + convolved).astype(BF16)
+    ones = jnp.ones((2 * SUBLANES, chans), BF16)
+    count = summed.shape[0]
+    raised = jnp.dot(
+        jnp.concatenate([summed, ones[: up_to(count, 2 * SUBLANES) - count]], axis=0),
+        up_ref[...],
+        preferred_element_type=F32,
+    )
+    summed = summed.astype(F32)
+    mean = jnp.mean(summed, axis=1, keepdims=True)
+    centred = summed - mean
+    scale = lax.rsqrt(jnp.mean(centred * centred, axis=1, keepdims=True) + 1e-05)
+    hidden = scale * (raised[:count] - mean * raised[count : count + 1])
     hidden = (0.5 * hidden * (1.0 + lax.erf(hidden * 0.5**0.5))).astype(BF16)
     result = summed + jnp.dot(hidden, down_ref[...], preferred_element_type=F32)
     for row in range(rows):
@@ -335,8 +343,9 @@
     assert 3 * (block % LANES) <= LANES
 
     far_first = tuple(reversed(range(columns)))
+    inward = far_first
     if columns > 3:
-        far_first = (far_first[1], far_first[0]) + far_first[2:]
+        inward = (far_first[1], far_first[0]) + far_first[2:]
     message = jax.ShapeDtypeStruct((height, LANES), BF16)
     messages = (message,) * columns
     stage = pltpu.VMEM((columns, height, LANES), BF16)
@@ -358,12 +367,12 @@
     )
     gathered = jax.ShapeDtypeStruct((columns, height, LANES), BF16)
     own_side = call(
-        functools.partial(column_kernel, far_first),
+        functools.partial(column_kernel, inward),
         "join_columns",
         gathered,
         [],
         10**8,
-        *[arrived[apart] for apart in far_first],
+        *[arrived[apart] for apart in inward],
     )
     lats = lax.axis_size("lat")
     mate_side = swap(own_side, count, lambda lat, lon: (lat, lon ^ 1))

time: 26.1 us -> 25.8 us (0.989)
  waiting for transfers between devices: 6.55 us -> 5.54 us
  starting transfers between devices: 14.4 us -> 15.3 us
    ppermute x6, waiting for transfers between devices: 5.09 us -> 4.07 us  [over_columns(): arrived[apart] = lax.ppermute(messages[apart], 'lon', pairs)]
    ppermute x6, starting transfers between devices: 9.23 us -> 10.1 us  [over_columns(): arrived[apart] = lax.ppermute(messages[apart], 'lon', pairs)]
  transfers between devices with their start and end apart: 11 -> 11, of which waited for: 6 -> 6; matrix products, arithmetic and copies ran while one was open for 0% -> 0% of each run, Pallas kernels for 5% -> 6%
where the time goes in v2:
time: 25.8 us; the launch traced here: 25.6 us
  starting transfers between devices  15.3 us (59%)
  waiting for transfers between devices  5.54 us (21%)
  Pallas kernels  3.92 us (15%)
  local copies, waits for them, and re-layouts  0.78 us (3%)
    ppermute x6, starting transfers between devices, over_columns(): arrived[apart] = lax.ppermute(messages[apart], 'lon', pairs)  10.1 us
    ppermute x6, waiting for transfers between devices, over_columns(): arrived[apart] = lax.ppermute(messages[apart], 'lon', pairs)  4.07 us
    pallas_call x9, Pallas kernels, call(): pl.pallas_call(kernel, out_shape=out_shape, in_specs=[VMEM] * len(operand...  3.92 us
    ppermute x4, starting transfers between devices, swap(): return lax.ppermute(block, ('lat', 'lon'), pairs)  3.65 us
    ppermute x1, starting transfers between devices, over_sides(): return lax.ppermute(block, 'lon', [(i, i ^ 1) for i in range(count)])  1.49 us
    ppermute x4, waiting for transfers between devices, swap(): return lax.ppermute(block, ('lat', 'lon'), pairs)  1.46 us
    unnamed x14, local copies, waits for them, and re-layouts  0.78 us
  transfers between devices with their start and end apart: 11, of which 6 were waited for; matrix products, arithmetic and copies ran while one was open for 0% of the time, Pallas kernels for 6%

profile of v2, /device:TPU:0, one launch (start us, length us, event | category | flops | bytes accessed | tf_op | source)
XLA Modules:
  0.0 25.6 jit_solution(14988037199429777874)
XLA Ops:
  0.0 0.0 copy-start.3
  0.0 0.8 %copy-done.3 = bf16[2,12,640]{2,0,1:T(2,128)(2,1)S(1)} copy-done((bf16[2,12,640]{2,0,1:T(2,128)(2,1)S(1)}, bf16[2,12,640]{2,0,1:T(2,128)(2,1)}, u32[]{:S(2)}) %copy-start.3) | copy-done | bytes 30744
  0.8 0.0 copy-start.2
  0.8 0.0 copy-start.5
  0.8 0.0 copy-start.6
  0.8 0.2 pack.1
  0.9 4.1 %collective-permute-start = (bf16[32,128]{1,0:T(8,128)(2,1)S(1)}, bf16[32,128]{1,0:T(8,128)(2,1)S(1)}, u32[]{:S(2)}, u32[]{:S(2)}) collective-permute-start(bf16[32,128]{1,0:T(8,128)(2,1)S(1)} %get-tuple-element.14), channel_id=1, source_target_pairs={{0,4},{1,5},{2,6},{3,7},{4,0},{5,1},{6,2},{7,3},{8,12},{9,13},{10,... | collective-permute-start | bytes 24584 | tf_op jit(solution)/shard_map/ppermute | solution.py:306
  5.0 1.3 %collective-permute-start.1 = (bf16[32,128]{1,0:T(8,128)(2,1)S(1)}, bf16[32,128]{1,0:T(8,128)(2,1)S(1)}, u32[]{:S(2)}, u32[]{:S(2)}) collective-permute-start(bf16[32,128]{1,0:T(8,128)(2,1)S(1)} %get-tuple-element.15), channel_id=1, source_target_pairs={{0,6},{1,7},{2,4},{3,5},{4,2},{5,3},{6,0},{7,1},{8,14},{9,15},{10,... | collective-permute-start | bytes 24584 | tf_op jit(solution)/shard_map/ppermute | solution.py:306
  6.4 0.2 collective-permute-start.2
  6.6 0.0 copy-done.2
  6.6 1.5 %collective-permute-start.7 = (bf16[9,20,80]{2,1,0:T(8,128)(2,1)S(1)}, bf16[9,20,80]{2,1,0:T(8,128)(2,1)S(1)}, u32[]{:S(2)}, u32[]{:S(2)}) collective-permute-start(bf16[9,20,80]{2,1,0:T(8,128)(2,1)S(1)} %bitcast.4), channel_id=1, source_target_pairs={{0,1},{1,0},{2,3},{3,2},{4,5},{5,4},{6,7},{7,6},{8,9},{9,8},{10,11... | collective-permute-start | bytes 86408 | tf_op jit(solution)/shard_map/ppermute | solution.py:311
  8.1 0.0 copy-done.5
  8.1 0.0 copy-done.6
  8.1 0.4 %tables.1.table_ref = bf16[2,576,384]{2,1,0:T(8,128)(2,1)S(1)} custom-call(bf16[9,96]{1,0:T(8,128)(2,1)S(1)} %copy-done.5, bf16[3,2,9]{2,1,0:T(2,128)(2,1)S(1)} %bitcast.8), custom_call_target="tpu_custom_call" | custom-call | flops 1000000000 | bytes 1000000 | tf_op jit(solution)/shard_map/tables/pallas_call | solution.py:290
  8.5 0.0 collective-permute-done.refs_0_
  8.5 1.9 %collective-permute-done.1.refs_1_ = bf16[32,128]{1,0:T(8,128)(2,1)S(1)} collective-permute-done((bf16[32,128]{1,0:T(8,128)(2,1)S(1)}, bf16[32,128]{1,0:T(8,128)(2,1)S(1)}, u32[]{:S(2)}, u32[]{:S(2)}) %collective-permute-start.1) | collective-permute-done | bytes 8224 | tf_op jit(solution)/shard_map/ppermute | solution.py:306
  10.5 0.0 collective-permute-done.2.refs_2_
  10.5 1.6 %collective-permute-start.5 = (bf16[4,32,128]{2,1,0:T(8,128)(2,1)S(1)}, bf16[4,32,128]{2,1,0:T(8,128)(2,1)S(1)}, u32[]{:S(2)}, u32[]{:S(2)}) collective-permute-start(bf16[4,32,128]{2,1,0:T(8,128)(2,1)S(1)} %join_columns.1.own_ref), channel_id=1, source_target_pairs={{0,1},{1,0},{2,3},{3,2},{4,5},{5,4},{6,7},{7,6},{8,9},{9,8},{10,11... | collective-permute-start | bytes 98312 | tf_op jit(solution)/shard_map/ppermute | solution.py:320
  12.1 0.5 %collective-permute-start.4 = (bf16[4,32,128]{2,1,0:T(8,128)(2,1)S(1)}, bf16[4,32,128]{2,1,0:T(8,128)(2,1)S(1)}, u32[]{:S(2)}, u32[]{:S(2)}) collective-permute-start(bf16[4,32,128]{2,1,0:T(8,128)(2,1)S(1)} %join_columns.1.own_ref), channel_id=1, source_target_pairs={{0,1},{1,0},{2,3},{3,2},{4,5},{5,4},{6,7},{7,6},{8,17},{9,16},{10,... | collective-permute-start | bytes 98312 | tf_op jit(solution)/shard_map/ppermute | solution.py:320
  12.6 1.5 %collective-permute-start.3 = (bf16[4,32,128]{2,1,0:T(8,128)(2,1)S(1)}, bf16[4,32,128]{2,1,0:T(8,128)(2,1)S(1)}, u32[]{:S(2)}, u32[]{:S(2)}) collective-permute-start(bf16[4,32,128]{2,1,0:T(8,128)(2,1)S(1)} %join_columns.1.own_ref), channel_id=1, source_target_pairs={{0,1},{1,0},{2,3},{3,2},{4,5},{5,4},{6,7},{7,6},{8,16},{9,17},{10,... | collective-permute-start | bytes 98312 | tf_op jit(solution)/shard_map/ppermute | solution.py:320
  14.1 0.1 unpack.1.own
  14.2 0.3 %collective-permute-done.5.mate_ref.mate = bf16[4,32,128]{2,1,0:T(8,128)(2,1)S(1)} collective-permute-done((bf16[4,32,128]{2,1,0:T(8,128)(2,1)S(1)}, bf16[4,32,128]{2,1,0:T(8,128)(2,1)S(1)}, u32[]{:S(2)}, u32[]{:S(2)}) %collective-permute-start.5) | collective-permute-done | bytes 32800 | tf_op jit(solution)/shard_map/ppermute | solution.py:320
  14.5 0.1 collective-permute-start.6
  14.6 0.0 collective-permute-done.7.mate_ref
  14.6 0.6 %squares.1.squares_ref = bf16[2304,256]{1,0:T(8,128)(2,1)S(1)} custom-call(bf16[9,20,80]{2,1,0:T(8,128)(2,1)S(1)} %bitcast.5, bf16[9,20,80]{2,1,0:T(8,128)(2,1)S(1)} %collective-permute-done.7.mate_ref), custom_call_target="tpu_custom_call" | custom-call | flops 1000000000 | bytes 1000000 | tf_op jit(solution)/shard_map/squares/pallas_call | solution.py:290
  15.1 0.4 %conv_own.1.part_ref = f32[2,576,256]{2,1,0:T(8,128)S(1)} custom-call(bf16[4,32,128]{2,1,0:T(8,128)(2,1)S(1)} %collective-permute-done.5.mate_ref.mate, bf16[2,4,16,256]{3,2,1,0:T(8,128)(2,1)S(1)} %unpack.1.own, bf16[2,576,384]{2,1,0:T(8,128)(2,1)S(1)} %tables.1.table_ref), custom_call_target="tpu_custom_call" | custom-call | flops 1000000000 | bytes 1000000 | tf_op jit(solution)/shard_map/conv_own/pallas_call | solution.py:290
  15.5 0.0 copy-start
  15.5 0.0 copy-start.1
  15.5 0.0 copy-start.4
  15.6 0.4 %collective-permute-done.4.odd_mate = bf16[4,32,128]{2,1,0:T(8,128)(2,1)S(1)} collective-permute-done((bf16[4,32,128]{2,1,0:T(8,128)(2,1)S(1)}, bf16[4,32,128]{2,1,0:T(8,128)(2,1)S(1)}, u32[]{:S(2)}, u32[]{:S(2)}) %collective-permute-start.4) | collective-permute-done | bytes 32800 | tf_op jit(solution)/shard_map/ppermute | solution.py:320
  16.0 0.7 %collective-permute-done.3.odd_own = bf16[4,32,128]{2,1,0:T(8,128)(2,1)S(1)} collective-permute-done((bf16[4,32,128]{2,1,0:T(8,128)(2,1)S(1)}, bf16[4,32,128]{2,1,0:T(8,128)(2,1)S(1)}, u32[]{:S(2)}, u32[]{:S(2)}) %collective-permute-start.3) | collective-permute-done | bytes 32800 | tf_op jit(solution)/shard_map/ppermute | solution.py:320
  16.7 0.0 collective-permute-done.6.even
  16.7 0.9 %conv.1 = (bf16[32,128]{1,0:T(8,128)(2,1)S(1)}, bf16[32,128]{1,0:T(8,128)(2,1)S(1)}, bf16[32,128]{1,0:T(8,128)(2,1)S(1)}, bf16[32,128]{1,0:T(8,128)(2,1)S(1)}) custom-call(bf16[4,32,128]{2,1,0:T(8,128)(2,1)S(1)} %collective-permute-done.3.odd_own, bf16[4,32,128]{2,1,0:T(8,128)(2,1)S(1)} %collective-permute-done.4.odd_mate, ...), custom_call_target="tpu_custom_call" | custom-call | flops 10000000000 | bytes 1000000 | tf_op jit(solution)/shard_map/conv/pallas_call | solution.py:290
  17.6 2.0 %collective-permute-start.8 = (bf16[32,128]{1,0:T(8,128)(2,1)S(1)}, bf16[32,128]{1,0:T(8,128)(2,1)S(1)}, u32[]{:S(2)}, u32[]{:S(2)}) collective-permute-start(bf16[32,128]{1,0:T(8,128)(2,1)S(1)} %get-tuple-element.19), channel_id=1, source_target_pairs={{0,6},{1,7},{2,4},{3,5},{4,2},{5,3},{6,0},{7,1},{8,14},{9,15},{10,... | collective-permute-start | bytes 24584 | tf_op jit(solution)/shard_map/ppermute | solution.py:306
  19.6 0.0 collective-permute-start.9
  19.6 2.4 %collective-permute-start.10 = (bf16[32,128]{1,0:T(8,128)(2,1)S(1)}, bf16[32,128]{1,0:T(8,128)(2,1)S(1)}, u32[]{:S(2)}, u32[]{:S(2)}) collective-permute-start(bf16[32,128]{1,0:T(8,128)(2,1)S(1)} %get-tuple-element.21), channel_id=1, source_target_pairs={{0,2},{1,3},{2,0},{3,1},{4,6},{5,7},{6,4},{7,5},{8,10},{9,11},{10,... | collective-permute-start | bytes 24584 | tf_op jit(solution)/shard_map/ppermute | solution.py:306
  22.1 1.1 %collective-permute-done.8.refs_0_ = bf16[32,128]{1,0:T(8,128)(2,1)S(1)} collective-permute-done((bf16[32,128]{1,0:T(8,128)(2,1)S(1)}, bf16[32,128]{1,0:T(8,128)(2,1)S(1)}, u32[]{:S(2)}, u32[]{:S(2)}) %collective-permute-start.8) | collective-permute-done | bytes 8224 | tf_op jit(solution)/shard_map/ppermute | solution.py:306
  23.1 1.1 %collective-permute-done.9.refs_1_ = bf16[32,128]{1,0:T(8,128)(2,1)S(1)} collective-permute-done((bf16[32,128]{1,0:T(8,128)(2,1)S(1)}, bf16[32,128]{1,0:T(8,128)(2,1)S(1)}, u32[]{:S(2)}, u32[]{:S(2)}) %collective-permute-start.9) | collective-permute-done | bytes 8224 | tf_op jit(solution)/shard_map/ppermute | solution.py:306
  24.2 0.0 collective-permute-done.10.refs_2_
  24.2 0.0 copy-done
  24.2 0.0 copy-done.1
  24.2 0.0 copy-done.4
  24.2 1.4 %tail.1 = bf16[12,2,640]{2,1,0:T(2,128)(2,1)} custom-call(bf16[32,128]{1,0:T(8,128)(2,1)S(1)} %collective-permute-done.8.refs_0_, bf16[32,128]{1,0:T(8,128)(2,1)S(1)} %collective-permute-done.9.refs_1_, bf16[32,128]{1,0:T(8,128)(2,1)S(1)} %collective-permute-done.10.refs_2_, bf16[32,128]{1,0:T(8,128)(2,1)S(1)} %get-tuple-element.22.refs_3_, ...), custom_call_target="tpu_custom_call" | custom-call | flops 1000000000 | bytes 1000000 | tf_op jit(solution)/shard_map/tail/pallas_call | solution.py:290
  (2 shorter events, 0.0 us)
Async XLA Ops:
  0.0 0.8 %copy-start.3 = (bf16[2,12,640]{2,0,1:T(2,128)(2,1)S(1)}, bf16[2,12,640]{2,0,1:T(2,128)(2,1)}, u32[]{:S(2)}) copy-start(bf16[2,12,640]{2,0,1:T(2,128)(2,1)} %param.7) | copy-start | bytes 92164
  0.8 5.9 %copy-start.2 = (bf16[9,80,20]{1,2,0:T(8,128)(2,1)S(1)}, bf16[9,80,20]{1,2,0:T(8,128)(2,1)}, u32[]{:S(2)}) copy-start(bf16[9,80,20]{1,2,0:T(8,128)(2,1)} %param.9) | copy-start | bytes 86404
  0.8 7.4 %copy-start.5 = (bf16[9,96]{1,0:T(8,128)(2,1)S(1)}, bf16[9,96]{1,0:T(8,128)(2,1)}, u32[]{:S(2)}) copy-start(bf16[9,96]{1,0:T(8,128)(2,1)} %filter_ref.1) | copy-start | bytes 5188
  0.8 7.4 %copy-start.6 = (bf16[9,2,3]{0,1,2:T(2,128)(2,1)S(1)}, bf16[9,2,3]{0,1,2:T(2,128)(2,1)}, u32[]{:S(2)}) copy-start(bf16[9,2,3]{0,1,2:T(2,128)(2,1)} %param.10) | copy-start | bytes 328
  0.9 7.6 %collective-permute-start = (bf16[32,128]{1,0:T(8,128)(2,1)S(1)}, bf16[32,128]{1,0:T(8,128)(2,1)S(1)}, u32[]{:S(2)}, u32[]{:S(2)}) collective-permute-start(bf16[32,128]{1,0:T(8,128)(2,1)S(1)} %get-tuple-element.14), channel_id=1, source_target_pairs={{0,4},{1,5},{2,6},{3,7},{4,0},{5,1},{6,2},{7,3},{8,12},{9,13},{10,... | collective-permute-start | bytes 24584 | tf_op jit(solution)/shard_map/ppermute | solution.py:306
  5.0 5.4 %collective-permute-start.1 = (bf16[32,128]{1,0:T(8,128)(2,1)S(1)}, bf16[32,128]{1,0:T(8,128)(2,1)S(1)}, u32[]{:S(2)}, u32[]{:S(2)}) collective-permute-start(bf16[32,128]{1,0:T(8,128)(2,1)S(1)} %get-tuple-element.15), channel_id=1, source_target_pairs={{0,6},{1,7},{2,4},{3,5},{4,2},{5,3},{6,0},{7,1},{8,14},{9,15},{10,... | collective-permute-start | bytes 24584 | tf_op jit(solution)/shard_map/ppermute | solution.py:306
  6.4 4.1 %collective-permute-start.2 = (bf16[32,128]{1,0:T(8,128)(2,1)S(1)}, bf16[32,128]{1,0:T(8,128)(2,1)S(1)}, u32[]{:S(2)}, u32[]{:S(2)}) collective-permute-start(bf16[32,128]{1,0:T(8,128)(2,1)S(1)} %get-tuple-element.16), channel_id=1, source_target_pairs={{0,2},{1,3},{2,0},{3,1},{4,6},{5,7},{6,4},{7,5},{8,10},{9,11},{10,... | collective-permute-start | bytes 24584 | tf_op jit(solution)/shard_map/ppermute | solution.py:306
  6.6 8.0 %collective-permute-start.7 = (bf16[9,20,80]{2,1,0:T(8,128)(2,1)S(1)}, bf16[9,20,80]{2,1,0:T(8,128)(2,1)S(1)}, u32[]{:S(2)}, u32[]{:S(2)}) collective-permute-start(bf16[9,20,80]{2,1,0:T(8,128)(2,1)S(1)} %bitcast.4), channel_id=1, source_target_pairs={{0,1},{1,0},{2,3},{3,2},{4,5},{5,4},{6,7},{7,6},{8,9},{9,8},{10,11... | collective-permute-start | bytes 86408 | tf_op jit(solution)/shard_map/ppermute | solution.py:311
  10.5 4.0 %collective-permute-start.5 = (bf16[4,32,128]{2,1,0:T(8,128)(2,1)S(1)}, bf16[4,32,128]{2,1,0:T(8,128)(2,1)S(1)}, u32[]{:S(2)}, u32[]{:S(2)}) collective-permute-start(bf16[4,32,128]{2,1,0:T(8,128)(2,1)S(1)} %join_columns.1.own_ref), channel_id=1, source_target_pairs={{0,1},{1,0},{2,3},{3,2},{4,5},{5,4},{6,7},{7,6},{8,9},{9,8},{10,11... | collective-permute-start | bytes 98312 | tf_op jit(solution)/shard_map/ppermute | solution.py:320
  12.1 3.9 %collective-permute-start.4 = (bf16[4,32,128]{2,1,0:T(8,128)(2,1)S(1)}, bf16[4,32,128]{2,1,0:T(8,128)(2,1)S(1)}, u32[]{:S(2)}, u32[]{:S(2)}) collective-permute-start(bf16[4,32,128]{2,1,0:T(8,128)(2,1)S(1)} %join_columns.1.own_ref), channel_id=1, source_target_pairs={{0,1},{1,0},{2,3},{3,2},{4,5},{5,4},{6,7},{7,6},{8,17},{9,16},{10,... | collective-permute-start | bytes 98312 | tf_op jit(solution)/shard_map/ppermute | solution.py:320
  12.6 4.1 %collective-permute-start.3 = (bf16[4,32,128]{2,1,0:T(8,128)(2,1)S(1)}, bf16[4,32,128]{2,1,0:T(8,128)(2,1)S(1)}, u32[]{:S(2)}, u32[]{:S(2)}) collective-permute-start(bf16[4,32,128]{2,1,0:T(8,128)(2,1)S(1)} %join_columns.1.own_ref), channel_id=1, source_target_pairs={{0,1},{1,0},{2,3},{3,2},{4,5},{5,4},{6,7},{7,6},{8,16},{9,17},{10,... | collective-permute-start | bytes 98312 | tf_op jit(solution)/shard_map/ppermute | solution.py:320
  14.5 2.2 %collective-permute-start.6 = (bf16[4,2,32,128]{3,2,1,0:T(8,128)(2,1)S(1)}, bf16[4,2,32,128]{3,2,1,0:T(8,128)(2,1)S(1)}, u32[]{:S(2)}, u32[]{:S(2)}) collective-permute-start(bf16[4,2,32,128]{3,2,1,0:T(8,128)(2,1)S(1)} %join_sides.1), channel_id=1, source_target_pairs={{0,8},{1,9},{2,10},{3,11},{4,12},{5,13},{6,14},{7,15},{8,0},{9,1},... | collective-permute-start | bytes 196616 | tf_op jit(solution)/shard_map/ppermute | solution.py:320
  15.5 8.7 %copy-start = (bf16[640,1280]{1,0:T(8,128)(2,1)S(1)}, bf16[640,1280]{1,0:T(8,128)(2,1)}, u32[]{:S(2)}) copy-start(bf16[640,1280]{1,0:T(8,128)(2,1)} %refs_5_.1) | copy-start | bytes 4915204
  15.5 8.7 %copy-start.1 = (bf16[1280,640]{1,0:T(8,128)(2,1)S(1)}, bf16[1280,640]{1,0:T(8,128)(2,1)}, u32[]{:S(2)}) copy-start(bf16[1280,640]{1,0:T(8,128)(2,1)} %refs_6_.1) | copy-start | bytes 4915204
  15.5 8.6 %copy-start.4 = (bf16[2,12,640]{2,0,1:T(2,128)(2,1)S(1)}, bf16[2,12,640]{2,0,1:T(2,128)(2,1)}, u32[]{:S(2)}) copy-start(bf16[2,12,640]{2,0,1:T(2,128)(2,1)} %param.7) | copy-start | bytes 92164
  17.6 5.5 %collective-permute-start.8 = (bf16[32,128]{1,0:T(8,128)(2,1)S(1)}, bf16[32,128]{1,0:T(8,128)(2,1)S(1)}, u32[]{:S(2)}, u32[]{:S(2)}) collective-permute-start(bf16[32,128]{1,0:T(8,128)(2,1)S(1)} %get-tuple-element.19), channel_id=1, source_target_pairs={{0,6},{1,7},{2,4},{3,5},{4,2},{5,3},{6,0},{7,1},{8,14},{9,15},{10,... | collective-permute-start | bytes 24584 | tf_op jit(solution)/shard_map/ppermute | solution.py:306
  19.6 4.5 %collective-permute-start.9 = (bf16[32,128]{1,0:T(8,128)(2,1)S(1)}, bf16[32,128]{1,0:T(8,128)(2,1)S(1)}, u32[]{:S(2)}, u32[]{:S(2)}) collective-permute-start(bf16[32,128]{1,0:T(8,128)(2,1)S(1)} %get-tuple-element.20), channel_id=1, source_target_pairs={{0,4},{1,5},{2,6},{3,7},{4,0},{5,1},{6,2},{7,3},{8,12},{9,13},{10,... | collective-permute-start | bytes 24584 | tf_op jit(solution)/shard_map/ppermute | solution.py:306
  19.6 4.5 %collective-permute-start.10 = (bf16[32,128]{1,0:T(8,128)(2,1)S(1)}, bf16[32,128]{1,0:T(8,128)(2,1)S(1)}, u32[]{:S(2)}, u32[]{:S(2)}) collective-permute-start(bf16[32,128]{1,0:T(8,128)(2,1)S(1)} %get-tuple-element.21), channel_id=1, source_target_pairs={{0,2},{1,3},{2,0},{3,1},{4,6},{5,7},{6,4},{7,5},{8,10},{9,11},{10,... | collective-permute-start | bytes 24584 | tf_op jit(solution)/shard_map/ppermute | solution.py:306

commit v3 on v2

--- a/solution.py
+++ b/solution.py
@@ -196,7 +196,7 @@
 def conv_kernel(
     block, width, odd_own, odd_mate, even, part_ref, table_ref, squares_ref, *refs
 ):
-    *out_refs, field, spread, stage = refs
+    *out_refs, field, stage = refs
     columns = len(out_refs)
     lanes = squares_ref.shape[1]
     bases = squares_ref.shape[0] // lanes
@@ -218,16 +218,19 @@
         place(1 - odd, 2 * at + 1, even[at, 1])
         place(odd, 2 * at + side, odd_own[at])
         place(odd, 2 * at + 1 - side, odd_mate[at])
-    for row in range(rows):
-        over = jnp.dot(
-            table_ref[row, :, : 2 * places], field[row], preferred_element_type=F32
+    over = [
+        jnp.dot(table_ref[row, :, : 2 * places], field[row], preferred_element_type=F32)
+        for row in range(rows)
+    ]
+    mixed = None
+    for basis in range(bases):
+        taken = slice(basis * half, (basis + 1) * half)
+        both = [(over[row][taken] + part_ref[row, taken]).astype(BF16) for row in range(rows)]
+        square = squares_ref[basis * lanes : (basis + 1) * lanes]
+        product = jnp.dot(
+            jnp.concatenate(both, axis=0), square, preferred_element_type=F32
         )
-        over = (over + part_ref[row]).astype(BF16)
-        for basis in range(bases):
-            spread[row * half : (row + 1) * half, basis * lanes : (basis + 1) * lanes] = over[
-                basis * half : (basis + 1) * half
-            ]
-    mixed = jnp.dot(spread[...], squares_ref[...], preferred_element_type=F32)
+        mixed = product if mixed is None else mixed + product
     upper = lax.broadcasted_iota(jnp.int32, (SUBLANES, lanes), 0) < rest
     for target in range(columns):
         top = mixed[target * step : (target + 1) * step]
@@ -262,20 +265,21 @@
         piece = pltpu.roll(piece, target * block, 1) if target else piece
         convolved = piece if convolved is None else convolved + piece
     summed = (points[...] + convolved).astype(BF16)
-    ones = jnp.ones((2 * SUBLANES, chans), BF16)
     count = summed.shape[0]
-    raised = jnp.dot(
-        jnp.concatenate([summed, ones[: up_to(count, 2 * SUBLANES) - count]], axis=0),
-        up_ref[...],
-        preferred_element_type=F32,
-    )
+    ones = jnp.ones((up_to(count, 2 * SUBLANES) - count, chans), BF16)
+    rows_and_ones = jnp.concatenate([summed, ones], axis=0)
     summed = summed.astype(F32)
     mean = jnp.mean(summed, axis=1, keepdims=True)
     centred = summed - mean
     scale = lax.rsqrt(jnp.mean(centred * centred, axis=1, keepdims=True) + 1e-05)
-    hidden = scale * (raised[:count] - mean * raised[count : count + 1])
-    hidden = (0.5 * hidden * (1.0 + lax.erf(hidden * 0.5**0.5))).astype(BF16)
-    result = summed + jnp.dot(hidden, down_ref[...], preferred_element_type=F32)
+    result = summed
+    units = up_ref.shape[1]
+    for first in range(0, units, 2 * LANES):
+        taken = slice(first, min(first + 2 * LANES, units))
+        raised = jnp.dot(rows_and_ones, up_ref[:, taken], preferred_element_type=F32)
+        hidden = scale * (raised[:count] - mean * raised[count : count + 1])
+        hidden = (0.5 * hidden * (1.0 + lax.erf(hidden * 0.5**0.5))).astype(BF16)
+        result = result + jnp.dot(hidden, down_ref[taken], preferred_element_type=F32)
     for row in range(rows):
         out_ref[:SUBLANES, row, :] = result[row * SUBLANES : (row + 1) * SUBLANES].astype(BF16)
         at = rows * SUBLANES + row * rest
@@ -415,7 +419,6 @@
         messages,
         [
             pltpu.VMEM((rows, 2 * places, lanes), BF16),
-            pltpu.VMEM((rows * places // 2, bases * lanes), BF16),
             pltpu.VMEM((columns, height, LANES), BF16),
         ],
         10**10,

time: 25.8 us -> 25.9 us (level)
  no operation moved by 1% of the time
where the time goes in v3:
time: 25.9 us; the launch traced here: 25.7 us
  starting transfers between devices  15.3 us (59%)
  waiting for transfers between devices  5.54 us (21%)
  Pallas kernels  4.01 us (15%)
  local copies, waits for them, and re-layouts  0.78 us (3%)
    ppermute x6, starting transfers between devices, over_columns(): arrived[apart] = lax.ppermute(messages[apart], 'lon', pairs)  10.1 us
    ppermute x6, waiting for transfers between devices, over_columns(): arrived[apart] = lax.ppermute(messages[apart], 'lon', pairs)  4.07 us
    pallas_call x9, Pallas kernels, call(): pl.pallas_call(kernel, out_shape=out_shape, in_specs=[VMEM] * len(operand...  4.01 us
    ppermute x4, starting transfers between devices, swap(): return lax.ppermute(block, ('lat', 'lon'), pairs)  3.65 us
    ppermute x1, starting transfers between devices, over_sides(): return lax.ppermute(block, 'lon', [(i, i ^ 1) for i in range(count)])  1.49 us
    ppermute x4, waiting for transfers between devices, swap(): return lax.ppermute(block, ('lat', 'lon'), pairs)  1.46 us
    unnamed x14, local copies, waits for them, and re-layouts  0.78 us
  transfers between devices with their start and end apart: 11, of which 6 were waited for; matrix products, arithmetic and copies ran while one was open for 0% of the time, Pallas kernels for 6%

profile of v3, /device:TPU:0, one launch (start us, length us, event | category | flops | bytes accessed | tf_op | source)
XLA Modules:
  0.0 25.7 jit_solution(16756104427333017613)
XLA Ops:
  0.0 0.0 copy-start.3
  0.0 0.8 %copy-done.3 = bf16[2,12,640]{2,0,1:T(2,128)(2,1)S(1)} copy-done((bf16[2,12,640]{2,0,1:T(2,128)(2,1)S(1)}, bf16[2,12,640]{2,0,1:T(2,128)(2,1)}, u32[]{:S(2)}) %copy-start.3) | copy-done | bytes 30744
  0.8 0.0 copy-start.2
  0.8 0.0 copy-start.5
  0.8 0.0 copy-start.6
  0.8 0.2 pack.1
  0.9 4.1 %collective-permute-start = (bf16[32,128]{1,0:T(8,128)(2,1)S(1)}, bf16[32,128]{1,0:T(8,128)(2,1)S(1)}, u32[]{:S(2)}, u32[]{:S(2)}) collective-permute-start(bf16[32,128]{1,0:T(8,128)(2,1)S(1)} %get-tuple-element.14), channel_id=1, source_target_pairs={{0,4},{1,5},{2,6},{3,7},{4,0},{5,1},{6,2},{7,3},{8,12},{9,13},{10,... | collective-permute-start | bytes 24584 | tf_op jit(solution)/shard_map/ppermute | solution.py:310
  5.0 1.3 %collective-permute-start.1 = (bf16[32,128]{1,0:T(8,128)(2,1)S(1)}, bf16[32,128]{1,0:T(8,128)(2,1)S(1)}, u32[]{:S(2)}, u32[]{:S(2)}) collective-permute-start(bf16[32,128]{1,0:T(8,128)(2,1)S(1)} %get-tuple-element.15), channel_id=1, source_target_pairs={{0,6},{1,7},{2,4},{3,5},{4,2},{5,3},{6,0},{7,1},{8,14},{9,15},{10,... | collective-permute-start | bytes 24584 | tf_op jit(solution)/shard_map/ppermute | solution.py:310
  6.4 0.2 collective-permute-start.2
  6.6 0.0 copy-done.2
  6.6 1.5 %collective-permute-start.7 = (bf16[9,20,80]{2,1,0:T(8,128)(2,1)S(1)}, bf16[9,20,80]{2,1,0:T(8,128)(2,1)S(1)}, u32[]{:S(2)}, u32[]{:S(2)}) collective-permute-start(bf16[9,20,80]{2,1,0:T(8,128)(2,1)S(1)} %bitcast.4), channel_id=1, source_target_pairs={{0,1},{1,0},{2,3},{3,2},{4,5},{5,4},{6,7},{7,6},{8,9},{9,8},{10,11... | collective-permute-start | bytes 86408 | tf_op jit(solution)/shard_map/ppermute | solution.py:315
  8.1 0.0 copy-done.5
  8.1 0.0 copy-done.6
  8.1 0.4 %tables.1.table_ref = bf16[2,576,384]{2,1,0:T(8,128)(2,1)S(1)} custom-call(bf16[9,96]{1,0:T(8,128)(2,1)S(1)} %copy-done.5, bf16[3,2,9]{2,1,0:T(2,128)(2,1)S(1)} %bitcast.8), custom_call_target="tpu_custom_call" | custom-call | flops 1000000000 | bytes 1000000 | tf_op jit(solution)/shard_map/tables/pallas_call | solution.py:294
  8.5 0.0 collective-permute-done.refs_0_
  8.5 1.9 %collective-permute-done.1.refs_1_ = bf16[32,128]{1,0:T(8,128)(2,1)S(1)} collective-permute-done((bf16[32,128]{1,0:T(8,128)(2,1)S(1)}, bf16[32,128]{1,0:T(8,128)(2,1)S(1)}, u32[]{:S(2)}, u32[]{:S(2)}) %collective-permute-start.1) | collective-permute-done | bytes 8224 | tf_op jit(solution)/shard_map/ppermute | solution.py:310
  10.5 0.0 collective-permute-done.2.refs_2_
  10.5 1.6 %collective-permute-start.5 = (bf16[4,32,128]{2,1,0:T(8,128)(2,1)S(1)}, bf16[4,32,128]{2,1,0:T(8,128)(2,1)S(1)}, u32[]{:S(2)}, u32[]{:S(2)}) collective-permute-start(bf16[4,32,128]{2,1,0:T(8,128)(2,1)S(1)} %join_columns.1.own_ref), channel_id=1, source_target_pairs={{0,1},{1,0},{2,3},{3,2},{4,5},{5,4},{6,7},{7,6},{8,9},{9,8},{10,11... | collective-permute-start | bytes 98312 | tf_op jit(solution)/shard_map/ppermute | solution.py:324
  12.1 0.5 %collective-permute-start.4 = (bf16[4,32,128]{2,1,0:T(8,128)(2,1)S(1)}, bf16[4,32,128]{2,1,0:T(8,128)(2,1)S(1)}, u32[]{:S(2)}, u32[]{:S(2)}) collective-permute-start(bf16[4,32,128]{2,1,0:T(8,128)(2,1)S(1)} %join_columns.1.own_ref), channel_id=1, source_target_pairs={{0,1},{1,0},{2,3},{3,2},{4,5},{5,4},{6,7},{7,6},{8,17},{9,16},{10,... | collective-permute-start | bytes 98312 | tf_op jit(solution)/shard_map/ppermute | solution.py:324
  12.6 1.5 %collective-permute-start.3 = (bf16[4,32,128]{2,1,0:T(8,128)(2,1)S(1)}, bf16[4,32,128]{2,1,0:T(8,128)(2,1)S(1)}, u32[]{:S(2)}, u32[]{:S(2)}) collective-permute-start(bf16[4,32,128]{2,1,0:T(8,128)(2,1)S(1)} %join_columns.1.own_ref), channel_id=1, source_target_pairs={{0,1},{1,0},{2,3},{3,2},{4,5},{5,4},{6,7},{7,6},{8,16},{9,17},{10,... | collective-permute-start | bytes 98312 | tf_op jit(solution)/shard_map/ppermute | solution.py:324
  14.1 0.1 unpack.1.own
  14.2 0.3 %collective-permute-done.5.mate_ref.mate = bf16[4,32,128]{2,1,0:T(8,128)(2,1)S(1)} collective-permute-done((bf16[4,32,128]{2,1,0:T(8,128)(2,1)S(1)}, bf16[4,32,128]{2,1,0:T(8,128)(2,1)S(1)}, u32[]{:S(2)}, u32[]{:S(2)}) %collective-permute-start.5) | collective-permute-done | bytes 32800 | tf_op jit(solution)/shard_map/ppermute | solution.py:324
  14.5 0.1 collective-permute-start.6
  14.6 0.0 collective-permute-done.7.mate_ref
  14.6 0.6 %squares.1.squares_ref = bf16[2304,256]{1,0:T(8,128)(2,1)S(1)} custom-call(bf16[9,20,80]{2,1,0:T(8,128)(2,1)S(1)} %bitcast.5, bf16[9,20,80]{2,1,0:T(8,128)(2,1)S(1)} %collective-permute-done.7.mate_ref), custom_call_target="tpu_custom_call" | custom-call | flops 1000000000 | bytes 1000000 | tf_op jit(solution)/shard_map/squares/pallas_call | solution.py:294
  15.1 0.4 %conv_own.1.part_ref = f32[2,576,256]{2,1,0:T(8,128)S(1)} custom-call(bf16[4,32,128]{2,1,0:T(8,128)(2,1)S(1)} %collective-permute-done.5.mate_ref.mate, bf16[2,4,16,256]{3,2,1,0:T(8,128)(2,1)S(1)} %unpack.1.own, bf16[2,576,384]{2,1,0:T(8,128)(2,1)S(1)} %tables.1.table_ref), custom_call_target="tpu_custom_call" | custom-call | flops 1000000000 | bytes 1000000 | tf_op jit(solution)/shard_map/conv_own/pallas_call | solution.py:294
  15.5 0.0 copy-start
  15.5 0.0 copy-start.1
  15.5 0.0 copy-start.4
  15.6 0.4 %collective-permute-done.4.odd_mate = bf16[4,32,128]{2,1,0:T(8,128)(2,1)S(1)} collective-permute-done((bf16[4,32,128]{2,1,0:T(8,128)(2,1)S(1)}, bf16[4,32,128]{2,1,0:T(8,128)(2,1)S(1)}, u32[]{:S(2)}, u32[]{:S(2)}) %collective-permute-start.4) | collective-permute-done | bytes 32800 | tf_op jit(solution)/shard_map/ppermute | solution.py:324
  16.0 0.7 %collective-permute-done.3.odd_own = bf16[4,32,128]{2,1,0:T(8,128)(2,1)S(1)} collective-permute-done((bf16[4,32,128]{2,1,0:T(8,128)(2,1)S(1)}, bf16[4,32,128]{2,1,0:T(8,128)(2,1)S(1)}, u32[]{:S(2)}, u32[]{:S(2)}) %collective-permute-start.3) | collective-permute-done | bytes 32800 | tf_op jit(solution)/shard_map/ppermute | solution.py:324
  16.7 0.0 collective-permute-done.6.even
  16.7 0.9 %conv.1 = (bf16[32,128]{1,0:T(8,128)(2,1)S(1)}, bf16[32,128]{1,0:T(8,128)(2,1)S(1)}, bf16[32,128]{1,0:T(8,128)(2,1)S(1)}, bf16[32,128]{1,0:T(8,128)(2,1)S(1)}) custom-call(bf16[4,32,128]{2,1,0:T(8,128)(2,1)S(1)} %collective-permute-done.3.odd_own, bf16[4,32,128]{2,1,0:T(8,128)(2,1)S(1)} %collective-permute-done.4.odd_mate, ...), custom_call_target="tpu_custom_call" | custom-call | flops 10000000000 | bytes 1000000 | tf_op jit(solution)/shard_map/conv/pallas_call | solution.py:294
  17.6 2.0 %collective-permute-start.8 = (bf16[32,128]{1,0:T(8,128)(2,1)S(1)}, bf16[32,128]{1,0:T(8,128)(2,1)S(1)}, u32[]{:S(2)}, u32[]{:S(2)}) collective-permute-start(bf16[32,128]{1,0:T(8,128)(2,1)S(1)} %get-tuple-element.19), channel_id=1, source_target_pairs={{0,6},{1,7},{2,4},{3,5},{4,2},{5,3},{6,0},{7,1},{8,14},{9,15},{10,... | collective-permute-start | bytes 24584 | tf_op jit(solution)/shard_map/ppermute | solution.py:310
  19.6 0.0 collective-permute-start.9
  19.6 2.4 %collective-permute-start.10 = (bf16[32,128]{1,0:T(8,128)(2,1)S(1)}, bf16[32,128]{1,0:T(8,128)(2,1)S(1)}, u32[]{:S(2)}, u32[]{:S(2)}) collective-permute-start(bf16[32,128]{1,0:T(8,128)(2,1)S(1)} %get-tuple-element.21), channel_id=1, source_target_pairs={{0,2},{1,3},{2,0},{3,1},{4,6},{5,7},{6,4},{7,5},{8,10},{9,11},{10,... | collective-permute-start | bytes 24584 | tf_op jit(solution)/shard_map/ppermute | solution.py:310
  22.1 1.1 %collective-permute-done.8.refs_0_ = bf16[32,128]{1,0:T(8,128)(2,1)S(1)} collective-permute-done((bf16[32,128]{1,0:T(8,128)(2,1)S(1)}, bf16[32,128]{1,0:T(8,128)(2,1)S(1)}, u32[]{:S(2)}, u32[]{:S(2)}) %collective-permute-start.8) | collective-permute-done | bytes 8224 | tf_op jit(solution)/shard_map/ppermute | solution.py:310
  23.1 1.1 %collective-permute-done.9.refs_1_ = bf16[32,128]{1,0:T(8,128)(2,1)S(1)} collective-permute-done((bf16[32,128]{1,0:T(8,128)(2,1)S(1)}, bf16[32,128]{1,0:T(8,128)(2,1)S(1)}, u32[]{:S(2)}, u32[]{:S(2)}) %collective-permute-start.9) | collective-permute-done | bytes 8224 | tf_op jit(solution)/shard_map/ppermute | solution.py:310
  24.2 0.0 collective-permute-done.10.refs_2_
  24.2 0.0 copy-done
  24.2 0.0 copy-done.1
  24.2 0.0 copy-done.4
  24.2 1.5 %tail.1 = bf16[12,2,640]{2,1,0:T(2,128)(2,1)} custom-call(bf16[32,128]{1,0:T(8,128)(2,1)S(1)} %collective-permute-done.8.refs_0_, bf16[32,128]{1,0:T(8,128)(2,1)S(1)} %collective-permute-done.9.refs_1_, bf16[32,128]{1,0:T(8,128)(2,1)S(1)} %collective-permute-done.10.refs_2_, bf16[32,128]{1,0:T(8,128)(2,1)S(1)} %get-tuple-element.22.refs_3_, ...), custom_call_target="tpu_custom_call" | custom-call | flops 1000000000 | bytes 1000000 | tf_op jit(solution)/shard_map/tail/pallas_call | solution.py:294
  (2 shorter events, 0.0 us)
Async XLA Ops:
  0.0 0.8 %copy-start.3 = (bf16[2,12,640]{2,0,1:T(2,128)(2,1)S(1)}, bf16[2,12,640]{2,0,1:T(2,128)(2,1)}, u32[]{:S(2)}) copy-start(bf16[2,12,640]{2,0,1:T(2,128)(2,1)} %param.7) | copy-start | bytes 92164
  0.8 5.9 %copy-start.2 = (bf16[9,80,20]{1,2,0:T(8,128)(2,1)S(1)}, bf16[9,80,20]{1,2,0:T(8,128)(2,1)}, u32[]{:S(2)}) copy-start(bf16[9,80,20]{1,2,0:T(8,128)(2,1)} %param.9) | copy-start | bytes 86404
  0.8 7.4 %copy-start.5 = (bf16[9,96]{1,0:T(8,128)(2,1)S(1)}, bf16[9,96]{1,0:T(8,128)(2,1)}, u32[]{:S(2)}) copy-start(bf16[9,96]{1,0:T(8,128)(2,1)} %filter_ref.1) | copy-start | bytes 5188
  0.8 7.4 %copy-start.6 = (bf16[9,2,3]{0,1,2:T(2,128)(2,1)S(1)}, bf16[9,2,3]{0,1,2:T(2,128)(2,1)}, u32[]{:S(2)}) copy-start(bf16[9,2,3]{0,1,2:T(2,128)(2,1)} %param.10) | copy-start | bytes 328
  0.9 7.6 %collective-permute-start = (bf16[32,128]{1,0:T(8,128)(2,1)S(1)}, bf16[32,128]{1,0:T(8,128)(2,1)S(1)}, u32[]{:S(2)}, u32[]{:S(2)}) collective-permute-start(bf16[32,128]{1,0:T(8,128)(2,1)S(1)} %get-tuple-element.14), channel_id=1, source_target_pairs={{0,4},{1,5},{2,6},{3,7},{4,0},{5,1},{6,2},{7,3},{8,12},{9,13},{10,... | collective-permute-start | bytes 24584 | tf_op jit(solution)/shard_map/ppermute | solution.py:310
  5.0 5.4 %collective-permute-start.1 = (bf16[32,128]{1,0:T(8,128)(2,1)S(1)}, bf16[32,128]{1,0:T(8,128)(2,1)S(1)}, u32[]{:S(2)}, u32[]{:S(2)}) collective-permute-start(bf16[32,128]{1,0:T(8,128)(2,1)S(1)} %get-tuple-element.15), channel_id=1, source_target_pairs={{0,6},{1,7},{2,4},{3,5},{4,2},{5,3},{6,0},{7,1},{8,14},{9,15},{10,... | collective-permute-start | bytes 24584 | tf_op jit(solution)/shard_map/ppermute | solution.py:310
  6.4 4.1 %collective-permute-start.2 = (bf16[32,128]{1,0:T(8,128)(2,1)S(1)}, bf16[32,128]{1,0:T(8,128)(2,1)S(1)}, u32[]{:S(2)}, u32[]{:S(2)}) collective-permute-start(bf16[32,128]{1,0:T(8,128)(2,1)S(1)} %get-tuple-element.16), channel_id=1, source_target_pairs={{0,2},{1,3},{2,0},{3,1},{4,6},{5,7},{6,4},{7,5},{8,10},{9,11},{10,... | collective-permute-start | bytes 24584 | tf_op jit(solution)/shard_map/ppermute | solution.py:310
  6.6 8.0 %collective-permute-start.7 = (bf16[9,20,80]{2,1,0:T(8,128)(2,1)S(1)}, bf16[9,20,80]{2,1,0:T(8,128)(2,1)S(1)}, u32[]{:S(2)}, u32[]{:S(2)}) collective-permute-start(bf16[9,20,80]{2,1,0:T(8,128)(2,1)S(1)} %bitcast.4), channel_id=1, source_target_pairs={{0,1},{1,0},{2,3},{3,2},{4,5},{5,4},{6,7},{7,6},{8,9},{9,8},{10,11... | collective-permute-start | bytes 86408 | tf_op jit(solution)/shard_map/ppermute | solution.py:315
  10.5 4.0 %collective-permute-start.5 = (bf16[4,32,128]{2,1,0:T(8,128)(2,1)S(1)}, bf16[4,32,128]{2,1,0:T(8,128)(2,1)S(1)}, u32[]{:S(2)}, u32[]{:S(2)}) collective-permute-start(bf16[4,32,128]{2,1,0:T(8,128)(2,1)S(1)} %join_columns.1.own_ref), channel_id=1, source_target_pairs={{0,1},{1,0},{2,3},{3,2},{4,5},{5,4},{6,7},{7,6},{8,9},{9,8},{10,11... | collective-permute-start | bytes 98312 | tf_op jit(solution)/shard_map/ppermute | solution.py:324
  12.1 3.9 %collective-permute-start.4 = (bf16[4,32,128]{2,1,0:T(8,128)(2,1)S(1)}, bf16[4,32,128]{2,1,0:T(8,128)(2,1)S(1)}, u32[]{:S(2)}, u32[]{:S(2)}) collective-permute-start(bf16[4,32,128]{2,1,0:T(8,128)(2,1)S(1)} %join_columns.1.own_ref), channel_id=1, source_target_pairs={{0,1},{1,0},{2,3},{3,2},{4,5},{5,4},{6,7},{7,6},{8,17},{9,16},{10,... | collective-permute-start | bytes 98312 | tf_op jit(solution)/shard_map/ppermute | solution.py:324
  12.6 4.1 %collective-permute-start.3 = (bf16[4,32,128]{2,1,0:T(8,128)(2,1)S(1)}, bf16[4,32,128]{2,1,0:T(8,128)(2,1)S(1)}, u32[]{:S(2)}, u32[]{:S(2)}) collective-permute-start(bf16[4,32,128]{2,1,0:T(8,128)(2,1)S(1)} %join_columns.1.own_ref), channel_id=1, source_target_pairs={{0,1},{1,0},{2,3},{3,2},{4,5},{5,4},{6,7},{7,6},{8,16},{9,17},{10,... | collective-permute-start | bytes 98312 | tf_op jit(solution)/shard_map/ppermute | solution.py:324
  14.5 2.2 %collective-permute-start.6 = (bf16[4,2,32,128]{3,2,1,0:T(8,128)(2,1)S(1)}, bf16[4,2,32,128]{3,2,1,0:T(8,128)(2,1)S(1)}, u32[]{:S(2)}, u32[]{:S(2)}) collective-permute-start(bf16[4,2,32,128]{3,2,1,0:T(8,128)(2,1)S(1)} %join_sides.1), channel_id=1, source_target_pairs={{0,8},{1,9},{2,10},{3,11},{4,12},{5,13},{6,14},{7,15},{8,0},{9,1},... | collective-permute-start | bytes 196616 | tf_op jit(solution)/shard_map/ppermute | solution.py:324
  15.5 8.7 %copy-start = (bf16[640,1280]{1,0:T(8,128)(2,1)S(1)}, bf16[640,1280]{1,0:T(8,128)(2,1)}, u32[]{:S(2)}) copy-start(bf16[640,1280]{1,0:T(8,128)(2,1)} %refs_5_.1) | copy-start | bytes 4915204
  15.5 8.7 %copy-start.1 = (bf16[1280,640]{1,0:T(8,128)(2,1)S(1)}, bf16[1280,640]{1,0:T(8,128)(2,1)}, u32[]{:S(2)}) copy-start(bf16[1280,640]{1,0:T(8,128)(2,1)} %refs_6_.1) | copy-start | bytes 4915204
  15.5 8.7 %copy-start.4 = (bf16[2,12,640]{2,0,1:T(2,128)(2,1)S(1)}, bf16[2,12,640]{2,0,1:T(2,128)(2,1)}, u32[]{:S(2)}) copy-start(bf16[2,12,640]{2,0,1:T(2,128)(2,1)} %param.7) | copy-start | bytes 92164
  17.6 5.5 %collective-permute-start.8 = (bf16[32,128]{1,0:T(8,128)(2,1)S(1)}, bf16[32,128]{1,0:T(8,128)(2,1)S(1)}, u32[]{:S(2)}, u32[]{:S(2)}) collective-permute-start(bf16[32,128]{1,0:T(8,128)(2,1)S(1)} %get-tuple-element.19), channel_id=1, source_target_pairs={{0,6},{1,7},{2,4},{3,5},{4,2},{5,3},{6,0},{7,1},{8,14},{9,15},{10,... | collective-permute-start | bytes 24584 | tf_op jit(solution)/shard_map/ppermute | solution.py:310
  19.6 4.5 %collective-permute-start.9 = (bf16[32,128]{1,0:T(8,128)(2,1)S(1)}, bf16[32,128]{1,0:T(8,128)(2,1)S(1)}, u32[]{:S(2)}, u32[]{:S(2)}) collective-permute-start(bf16[32,128]{1,0:T(8,128)(2,1)S(1)} %get-tuple-element.20), channel_id=1, source_target_pairs={{0,4},{1,5},{2,6},{3,7},{4,0},{5,1},{6,2},{7,3},{8,12},{9,13},{10,... | collective-permute-start | bytes 24584 | tf_op jit(solution)/shard_map/ppermute | solution.py:310
  19.6 4.5 %collective-permute-start.10 = (bf16[32,128]{1,0:T(8,128)(2,1)S(1)}, bf16[32,128]{1,0:T(8,128)(2,1)S(1)}, u32[]{:S(2)}, u32[]{:S(2)}) collective-permute-start(bf16[32,128]{1,0:T(8,128)(2,1)S(1)} %get-tuple-element.21), channel_id=1, source_target_pairs={{0,2},{1,3},{2,0},{3,1},{4,6},{5,7},{6,4},{7,5},{8,10},{9,11},{10,... | collective-permute-start | bytes 24584 | tf_op jit(solution)/shard_map/ppermute | solution.py:310

commit v4 on v2

--- a/solution.py
+++ b/solution.py
@@ -74,9 +74,9 @@
         points[at : at + rest] = latent_ref[SUBLANES:, row, :].astype(F32)
 
 
-def pack_kernel(latent_ref, *refs):
+def pack_kernel(order, latent_ref, *refs):
     *out_refs, points, stage = refs
-    columns = len(out_refs)
+    columns = stage.shape[0]
     chans = latent_ref.shape[2]
     block = chans // columns
     column, _ = column_and_side()
@@ -85,8 +85,17 @@
     for target in range(columns):
         turned = pltpu.roll(own, chans - target * block, 1) if target else own
         stage[target] = fold(turned[:, : lanes_of(block)], block)
-    for apart in range(columns):
-        out_refs[apart][...] = stage[column ^ apart]
+    for apart, ref in zip(order, out_refs):
+        ref[...] = stage[column ^ apart]
+
+
+def cut_kernel(raw_ref, out_ref, points):
+    chans = raw_ref.shape[2]
+    block = chans // (lax.axis_size("lon") // 2)
+    column, _ = column_and_side()
+    group_points(raw_ref, points)
+    turned = pltpu.roll(points[...], (chans - column * block) % chans, 1)
+    out_ref[...] = fold(turned[:, : lanes_of(block)], block)
 
 
 def column_kernel(order, *refs):
@@ -102,12 +111,23 @@
     out_ref[:, 1 - side] = mate_ref[...]
 
 
-def tables_kernel(width, filter_ref, band_ref, table_ref, first):
+def apart_kernel(width, step, out_ref):
+    lons = out_ref.shape[0]
+    side = lax.axis_index("lon") % 2
+    source = lax.broadcasted_iota(jnp.int32, out_ref.shape, 0)
+    place = lax.broadcasted_iota(jnp.int32, out_ref.shape, 1)
+    within = place % step
+    apart = source + (place // step) * width + within + (lons - side * width)
+    for _ in range(3):
+        apart = jnp.where(apart >= lons, apart - lons, apart)
+    out_ref[...] = jnp.where(within < width, apart, -1)
+
+
+def tables_kernel(width, filter_ref, band_ref, apart_ref, table_ref, first):
     bases, lons = filter_ref.shape
     taps, rows, _ = band_ref.shape
     step, places = first.shape[1:]
     columns = places // (2 * step)
-    _, side = column_and_side()
     lat = lax.axis_index("lat")
     below = (lat > 0).astype(F32)
     above = (lat < lax.axis_size("lat") - 1).astype(F32)
@@ -115,13 +135,7 @@
     slots = [[0, 1, 2], [2, 0, 1]]
     profile = filter_ref[...]
     band = band_ref[...].astype(F32)
-    source = lax.broadcasted_iota(jnp.int32, (lons, places), 0)
-    place = lax.broadcasted_iota(jnp.int32, (lons, places), 1)
-    within = place % step
-    apart = source + (place // step) * width + within + (lons - side * width)
-    for _ in range(3):
-        apart = jnp.where(apart >= lons, apart - lons, apart)
-    apart = jnp.where(within < width, apart, -1)
+    apart = apart_ref[...]
     first[...] = jnp.zeros_like(first)
     for lon in range(width):
         pick = (apart == lon).astype(F32).astype(BF16)
@@ -194,7 +208,7 @@
 
 
 def conv_kernel(
-    block, width, odd_own, odd_mate, even, part_ref, table_ref, squares_ref, *refs
+    block, width, odd_mate, odd_own, even, part_ref, table_ref, squares_ref, *refs
 ):
     *out_refs, field, spread, stage = refs
     columns = len(out_refs)
@@ -299,12 +313,9 @@
     )(*operands)
 
 
-def over_columns(messages, count):
-    arrived = {0: messages[0]}
-    for apart in reversed(range(1, count // 2)):
-        pairs = [(i, ((i // 2) ^ apart) * 2 + i % 2) for i in range(count)]
-        arrived[apart] = lax.ppermute(messages[apart], "lon", pairs)
-    return arrived
+def over_columns(message, count, apart):
+    pairs = [(i, ((i // 2) ^ apart) * 2 + i % 2) for i in range(count)]
+    return lax.ppermute(message, "lon", pairs) if apart else message
 
 
 def over_sides(block, count):
@@ -353,17 +364,35 @@
     lon_first = jnp.transpose(latent, (1, 0, 2))
     mix_own = jnp.transpose(mix_weight, (0, 2, 1))
 
-    packed = call(pack_kernel, "pack", messages, [points, stage], 10**9, lon_first)
-    arrived = over_columns(packed, count)
+    raw = over_columns(lon_first, count, inward[0])
+    apart = call(
+        functools.partial(apart_kernel, width, step),
+        "apart",
+        jax.ShapeDtypeStruct((lons, places), jnp.int32),
+        [],
+        10**9,
+    )
+    loaded, apart = lax.optimization_barrier((lon_first, apart))
+    packed = call(
+        functools.partial(pack_kernel, inward[1:]),
+        "pack",
+        (message,) * (columns - 1),
+        [points, stage],
+        10**9,
+        loaded,
+    )
+    arrived = [call(cut_kernel, "cut", message, [points], 5 * 10**9, raw)]
+    arrived += [over_columns(*pair) for pair in zip(packed, [count] * columns, inward[1:])]
     mix_mate = over_sides(mix_own, count)
     table = call(
         functools.partial(tables_kernel, width),
         "tables",
         jax.ShapeDtypeStruct((rows, bases * places // 2, taps * places), BF16),
         [pltpu.VMEM((bases, step, places), F32)],
-        10**9,
+        10**6,
         lon_filter,
         jnp.transpose(band_weight, (2, 1, 0)),
+        apart,
     )
     gathered = jax.ShapeDtypeStruct((columns, height, LANES), BF16)
     own_side = call(
@@ -372,7 +401,7 @@
         gathered,
         [],
         10**8,
-        *[arrived[apart] for apart in inward],
+        *arrived,
     )
     lats = lax.axis_size("lat")
     mate_side = swap(own_side, count, lambda lat, lon: (lat, lon ^ 1))
@@ -419,21 +448,22 @@
             pltpu.VMEM((columns, height, LANES), BF16),
         ],
         10**10,
+        odd_mate,
         odd_own,
-        odd_mate,
         even,
         part,
         table,
         squares,
     )
-    back = over_columns(mixed, count)
+    outward = far_first[1:-1] + far_first[:1] + far_first[-1:]
+    back = [over_columns(mixed[apart], count, apart) for apart in outward]
     result = call(
-        functools.partial(tail_kernel, far_first),
+        functools.partial(tail_kernel, outward),
         "tail",
         jax.ShapeDtypeStruct(lon_first.shape, BF16),
         [points, stage],
         10**9,
-        *[back[apart] for apart in far_first],
+        *back,
         lon_first,
         w_up,
         w_down,

time: 25.8 us -> 25.2 us (0.977)
  local copies, waits for them, and re-layouts: 0.78 us -> 0.04 us
    unnamed x14 -> x12, local copies, waits for them, and re-layouts: 0.78 us -> 0.04 us
    ppermute x6, waiting for transfers between devices: 4.07 us -> 3.8 us  [over_columns(): return lax.ppermute(message, 'lon', pairs) if apart else message]
    pallas_call x9 -> x11, Pallas kernels: 3.92 us -> 4.12 us  [call(): pl.pallas_call(kernel, out_shape=out_shape, in_specs=[VMEM] * len(operand...]
  transfers between devices with their start and end apart: 11 -> 11, of which waited for: 6 -> 6; matrix products, arithmetic and copies ran while one was open for 0% -> 0% of each run, Pallas kernels for 6% -> 7%
where the time goes in v4:
time: 25.2 us; the launch traced here: 25 us
  starting transfers between devices  15.4 us (61%)
  waiting for transfers between devices  5.36 us (21%)
  Pallas kernels  4.12 us (16%)
    ppermute x6, starting transfers between devices, over_columns(): return lax.ppermute(message, 'lon', pairs) if apart else message  10.2 us
    pallas_call x11, Pallas kernels, call(): pl.pallas_call(kernel, out_shape=out_shape, in_specs=[VMEM] * len(operand...  4.12 us
    ppermute x6, waiting for transfers between devices, over_columns(): return lax.ppermute(message, 'lon', pairs) if apart else message  3.8 us
    ppermute x4, starting transfers between devices, swap(): return lax.ppermute(block, ('lat', 'lon'), pairs)  3.66 us
    ppermute x4, waiting for transfers between devices, swap(): return lax.ppermute(block, ('lat', 'lon'), pairs)  1.55 us
    ppermute x1, starting transfers between devices, over_sides(): return lax.ppermute(block, 'lon', [(i, i ^ 1) for i in range(count)])  1.49 us
  transfers between devices with their start and end apart: 11, of which 6 were waited for; matrix products, arithmetic and copies ran while one was open for 0% of the time, Pallas kernels for 7%

profile of v4, /device:TPU:0, one launch (start us, length us, event | category | flops | bytes accessed | tf_op | source)
XLA Modules:
  0.0 25.0 jit_solution(16762664489414928329)
XLA Ops:
  0.0 0.0 copy-start.5
  0.0 4.0 %collective-permute-start = (bf16[12,2,640]{2,1,0:T(2,128)(2,1)}, bf16[12,2,640]{2,1,0:T(2,128)(2,1)S(1)}, u32[]{:S(2)}, u32[]{:S(2)}) collective-permute-start(bf16[12,2,640]{2,1,0:T(2,128)(2,1)} %bitcast.7), channel_id=1, source_target_pairs={{0,4},{1,5},{2,6},{3,7},{4,0},{5,1},{6,2},{7,3},{8,12},{9,13},{10,... | collective-permute-start | bytes 92168 | tf_op jit(solution)/shard_map/ppermute | solution.py:318
  4.1 0.0 copy-done.5
  4.1 0.0 copy-start.4
  4.1 0.0 copy-start
  4.1 0.0 copy-start.1
  4.1 0.2 pack.1
  4.3 1.7 %collective-permute-start.1 = (bf16[32,128]{1,0:T(8,128)(2,1)S(1)}, bf16[32,128]{1,0:T(8,128)(2,1)S(1)}, u32[]{:S(2)}, u32[]{:S(2)}) collective-permute-start(bf16[32,128]{1,0:T(8,128)(2,1)S(1)} %get-tuple-element.16), channel_id=1, source_target_pairs={{0,6},{1,7},{2,4},{3,5},{4,2},{5,3},{6,0},{7,1},{8,14},{9,15},{10,... | collective-permute-start | bytes 24584 | tf_op jit(solution)/shard_map/ppermute | solution.py:318
  6.0 0.0 collective-permute-start.2
  6.0 0.0 copy-done.4
  6.0 1.5 %collective-permute-start.7 = (bf16[9,20,80]{2,1,0:T(8,128)(2,1)S(1)}, bf16[9,20,80]{2,1,0:T(8,128)(2,1)S(1)}, u32[]{:S(2)}, u32[]{:S(2)}) collective-permute-start(bf16[9,20,80]{2,1,0:T(8,128)(2,1)S(1)} %bitcast.5), channel_id=1, source_target_pairs={{0,1},{1,0},{2,3},{3,2},{4,5},{5,4},{6,7},{7,6},{8,9},{9,8},{10,11... | collective-permute-start | bytes 86408 | tf_op jit(solution)/shard_map/ppermute | solution.py:322
  7.5 0.0 copy-done
  7.5 0.0 copy-done.1
  7.5 0.4 %tables.1.table_ref = bf16[2,576,384]{2,1,0:T(8,128)(2,1)S(1)} custom-call(bf16[9,96]{1,0:T(8,128)(2,1)S(1)} %copy-done, bf16[3,2,9]{2,1,0:T(2,128)(2,1)S(1)} %bitcast.4, s32[96,128]{1,0:T(8,128)S(1)} %apart.1.apart_ref), custom_call_target="tpu_custom_call" | custom-call | flops 1000000 | bytes 1000000 | tf_op jit(solution)/shard_map/tables/pallas_call | solution.py:304
  7.9 0.0 collective-permute-done.raw_ref
  8.0 0.2 cut.1.refs_0_
  8.1 1.7 %collective-permute-done.1.refs_1_ = bf16[32,128]{1,0:T(8,128)(2,1)S(1)} collective-permute-done((bf16[32,128]{1,0:T(8,128)(2,1)S(1)}, bf16[32,128]{1,0:T(8,128)(2,1)S(1)}, u32[]{:S(2)}, u32[]{:S(2)}) %collective-permute-start.1) | collective-permute-done | bytes 8224 | tf_op jit(solution)/shard_map/ppermute | solution.py:318
  9.8 0.0 collective-permute-done.2.refs_2_
  9.8 1.6 %collective-permute-start.5 = (bf16[4,32,128]{2,1,0:T(8,128)(2,1)S(1)}, bf16[4,32,128]{2,1,0:T(8,128)(2,1)S(1)}, u32[]{:S(2)}, u32[]{:S(2)}) collective-permute-start(bf16[4,32,128]{2,1,0:T(8,128)(2,1)S(1)} %join_columns.1.own_ref), channel_id=1, source_target_pairs={{0,1},{1,0},{2,3},{3,2},{4,5},{5,4},{6,7},{7,6},{8,9},{9,8},{10,11... | collective-permute-start | bytes 98312 | tf_op jit(solution)/shard_map/ppermute | solution.py:331
  11.4 0.1 unpack.1.own
  11.5 0.5 %collective-permute-start.3 = (bf16[4,32,128]{2,1,0:T(8,128)(2,1)S(1)}, bf16[4,32,128]{2,1,0:T(8,128)(2,1)S(1)}, u32[]{:S(2)}, u32[]{:S(2)}) collective-permute-start(bf16[4,32,128]{2,1,0:T(8,128)(2,1)S(1)} %join_columns.1.own_ref), channel_id=1, source_target_pairs={{0,1},{1,0},{2,3},{3,2},{4,5},{5,4},{6,7},{7,6},{8,17},{9,16},{10,... | collective-permute-start | bytes 98312 | tf_op jit(solution)/shard_map/ppermute | solution.py:331
  12.0 1.5 %collective-permute-start.4 = (bf16[4,32,128]{2,1,0:T(8,128)(2,1)S(1)}, bf16[4,32,128]{2,1,0:T(8,128)(2,1)S(1)}, u32[]{:S(2)}, u32[]{:S(2)}) collective-permute-start(bf16[4,32,128]{2,1,0:T(8,128)(2,1)S(1)} %join_columns.1.own_ref), channel_id=1, source_target_pairs={{0,1},{1,0},{2,3},{3,2},{4,5},{5,4},{6,7},{7,6},{8,16},{9,17},{10,... | collective-permute-start | bytes 98312 | tf_op jit(solution)/shard_map/ppermute | solution.py:331
  13.5 0.3 %collective-permute-done.5.mate_ref.mate = bf16[4,32,128]{2,1,0:T(8,128)(2,1)S(1)} collective-permute-done((bf16[4,32,128]{2,1,0:T(8,128)(2,1)S(1)}, bf16[4,32,128]{2,1,0:T(8,128)(2,1)S(1)}, u32[]{:S(2)}, u32[]{:S(2)}) %collective-permute-start.5) | collective-permute-done | bytes 32800 | tf_op jit(solution)/shard_map/ppermute | solution.py:331
  13.8 0.1 collective-permute-start.6
  13.9 0.0 collective-permute-done.7.mate_ref
  13.9 0.5 %squares.1.squares_ref = bf16[2304,256]{1,0:T(8,128)(2,1)S(1)} custom-call(bf16[9,20,80]{2,1,0:T(8,128)(2,1)S(1)} %bitcast.6, bf16[9,20,80]{2,1,0:T(8,128)(2,1)S(1)} %collective-permute-done.7.mate_ref), custom_call_target="tpu_custom_call" | custom-call | flops 1000000000 | bytes 1000000 | tf_op jit(solution)/shard_map/squares/pallas_call | solution.py:304
  14.5 0.4 %conv_own.1.part_ref = f32[2,576,256]{2,1,0:T(8,128)S(1)} custom-call(bf16[4,32,128]{2,1,0:T(8,128)(2,1)S(1)} %collective-permute-done.5.mate_ref.mate, bf16[2,4,16,256]{3,2,1,0:T(8,128)(2,1)S(1)} %unpack.1.own, bf16[2,576,384]{2,1,0:T(8,128)(2,1)S(1)} %tables.1.table_ref), custom_call_target="tpu_custom_call" | custom-call | flops 1000000000 | bytes 1000000 | tf_op jit(solution)/shard_map/conv_own/pallas_call | solution.py:304
  14.8 0.0 copy-start.2
  14.9 0.0 copy-start.3
  14.9 0.5 %collective-permute-done.3.odd_mate = bf16[4,32,128]{2,1,0:T(8,128)(2,1)S(1)} collective-permute-done((bf16[4,32,128]{2,1,0:T(8,128)(2,1)S(1)}, bf16[4,32,128]{2,1,0:T(8,128)(2,1)S(1)}, u32[]{:S(2)}, u32[]{:S(2)}) %collective-permute-start.3) | collective-permute-done | bytes 32800 | tf_op jit(solution)/shard_map/ppermute | solution.py:331
  15.4 0.7 %collective-permute-done.4.odd_own = bf16[4,32,128]{2,1,0:T(8,128)(2,1)S(1)} collective-permute-done((bf16[4,32,128]{2,1,0:T(8,128)(2,1)S(1)}, bf16[4,32,128]{2,1,0:T(8,128)(2,1)S(1)}, u32[]{:S(2)}, u32[]{:S(2)}) %collective-permute-start.4) | collective-permute-done | bytes 32800 | tf_op jit(solution)/shard_map/ppermute | solution.py:331
  16.1 0.0 collective-permute-done.6.even
  16.1 0.9 %conv.1 = (bf16[32,128]{1,0:T(8,128)(2,1)S(1)}, bf16[32,128]{1,0:T(8,128)(2,1)S(1)}, bf16[32,128]{1,0:T(8,128)(2,1)S(1)}, bf16[32,128]{1,0:T(8,128)(2,1)S(1)}) custom-call(bf16[4,32,128]{2,1,0:T(8,128)(2,1)S(1)} %collective-permute-done.3.odd_mate, bf16[4,32,128]{2,1,0:T(8,128)(2,1)S(1)} %collective-permute-done.4.odd_own, ...), custom_call_target="tpu_custom_call" | custom-call | flops 10000000000 | bytes 1000000 | tf_op jit(solution)/shard_map/conv/pallas_call | solution.py:304
  17.0 2.0 %collective-permute-start.10 = (bf16[32,128]{1,0:T(8,128)(2,1)S(1)}, bf16[32,128]{1,0:T(8,128)(2,1)S(1)}, u32[]{:S(2)}, u32[]{:S(2)}) collective-permute-start(bf16[32,128]{1,0:T(8,128)(2,1)S(1)} %get-tuple-element.23), channel_id=1, source_target_pairs={{0,6},{1,7},{2,4},{3,5},{4,2},{5,3},{6,0},{7,1},{8,14},{9,15},{10,... | collective-permute-start | bytes 24584 | tf_op jit(solution)/shard_map/ppermute | solution.py:318
  19.0 0.0 collective-permute-start.8
  19.0 2.4 %collective-permute-start.9 = (bf16[32,128]{1,0:T(8,128)(2,1)S(1)}, bf16[32,128]{1,0:T(8,128)(2,1)S(1)}, u32[]{:S(2)}, u32[]{:S(2)}) collective-permute-start(bf16[32,128]{1,0:T(8,128)(2,1)S(1)} %get-tuple-element.22), channel_id=1, source_target_pairs={{0,2},{1,3},{2,0},{3,1},{4,6},{5,7},{6,4},{7,5},{8,10},{9,11},{10,... | collective-permute-start | bytes 24584 | tf_op jit(solution)/shard_map/ppermute | solution.py:318
  21.5 1.1 %collective-permute-done.10.refs_2_ = bf16[32,128]{1,0:T(8,128)(2,1)S(1)} collective-permute-done((bf16[32,128]{1,0:T(8,128)(2,1)S(1)}, bf16[32,128]{1,0:T(8,128)(2,1)S(1)}, u32[]{:S(2)}, u32[]{:S(2)}) %collective-permute-start.10) | collective-permute-done | bytes 8224 | tf_op jit(solution)/shard_map/ppermute | solution.py:318
  22.5 1.1 %collective-permute-done.8.refs_0_ = bf16[32,128]{1,0:T(8,128)(2,1)S(1)} collective-permute-done((bf16[32,128]{1,0:T(8,128)(2,1)S(1)}, bf16[32,128]{1,0:T(8,128)(2,1)S(1)}, u32[]{:S(2)}, u32[]{:S(2)}) %collective-permute-start.8) | collective-permute-done | bytes 8224 | tf_op jit(solution)/shard_map/ppermute | solution.py:318
  23.6 0.0 collective-permute-done.9.refs_1_
  23.6 0.0 copy-done.2
  23.6 0.0 copy-done.3
  23.6 1.4 %tail.1 = bf16[12,2,640]{2,1,0:T(2,128)(2,1)} custom-call(bf16[32,128]{1,0:T(8,128)(2,1)S(1)} %collective-permute-done.8.refs_0_, bf16[32,128]{1,0:T(8,128)(2,1)S(1)} %collective-permute-done.9.refs_1_, bf16[32,128]{1,0:T(8,128)(2,1)S(1)} %collective-permute-done.10.refs_2_, bf16[32,128]{1,0:T(8,128)(2,1)S(1)} %get-tuple-element.24.refs_3_, ...), custom_call_target="tpu_custom_call" | custom-call | flops 1000000000 | bytes 1000000 | tf_op jit(solution)/shard_map/tail/pallas_call | solution.py:304
  (3 shorter events, 0.0 us)
Async XLA Ops:
  0.0 4.1 %copy-start.5 = (bf16[2,12,640]{2,0,1:T(2,128)(2,1)S(1)}, bf16[2,12,640]{2,0,1:T(2,128)(2,1)}, u32[]{:S(2)}) copy-start(bf16[2,12,640]{2,0,1:T(2,128)(2,1)} %param.7) | copy-start | bytes 92164
  0.0 7.9 %collective-permute-start = (bf16[12,2,640]{2,1,0:T(2,128)(2,1)}, bf16[12,2,640]{2,1,0:T(2,128)(2,1)S(1)}, u32[]{:S(2)}, u32[]{:S(2)}) collective-permute-start(bf16[12,2,640]{2,1,0:T(2,128)(2,1)} %bitcast.7), channel_id=1, source_target_pairs={{0,4},{1,5},{2,6},{3,7},{4,0},{5,1},{6,2},{7,3},{8,12},{9,13},{10,... | collective-permute-start | bytes 92168 | tf_op jit(solution)/shard_map/ppermute | solution.py:318
  4.1 2.0 %copy-start.4 = (bf16[9,80,20]{1,2,0:T(8,128)(2,1)S(1)}, bf16[9,80,20]{1,2,0:T(8,128)(2,1)}, u32[]{:S(2)}) copy-start(bf16[9,80,20]{1,2,0:T(8,128)(2,1)} %param.9) | copy-start | bytes 86404
  4.1 3.4 %copy-start = (bf16[9,96]{1,0:T(8,128)(2,1)S(1)}, bf16[9,96]{1,0:T(8,128)(2,1)}, u32[]{:S(2)}) copy-start(bf16[9,96]{1,0:T(8,128)(2,1)} %filter_ref.1) | copy-start | bytes 5188
  4.1 3.4 %copy-start.1 = (bf16[9,2,3]{0,1,2:T(2,128)(2,1)S(1)}, bf16[9,2,3]{0,1,2:T(2,128)(2,1)}, u32[]{:S(2)}) copy-start(bf16[9,2,3]{0,1,2:T(2,128)(2,1)} %param.10) | copy-start | bytes 328
  4.3 5.5 %collective-permute-start.1 = (bf16[32,128]{1,0:T(8,128)(2,1)S(1)}, bf16[32,128]{1,0:T(8,128)(2,1)S(1)}, u32[]{:S(2)}, u32[]{:S(2)}) collective-permute-start(bf16[32,128]{1,0:T(8,128)(2,1)S(1)} %get-tuple-element.16), channel_id=1, source_target_pairs={{0,6},{1,7},{2,4},{3,5},{4,2},{5,3},{6,0},{7,1},{8,14},{9,15},{10,... | collective-permute-start | bytes 24584 | tf_op jit(solution)/shard_map/ppermute | solution.py:318
  6.0 3.8 %collective-permute-start.2 = (bf16[32,128]{1,0:T(8,128)(2,1)S(1)}, bf16[32,128]{1,0:T(8,128)(2,1)S(1)}, u32[]{:S(2)}, u32[]{:S(2)}) collective-permute-start(bf16[32,128]{1,0:T(8,128)(2,1)S(1)} %get-tuple-element.17), channel_id=1, source_target_pairs={{0,2},{1,3},{2,0},{3,1},{4,6},{5,7},{6,4},{7,5},{8,10},{9,11},{10,... | collective-permute-start | bytes 24584 | tf_op jit(solution)/shard_map/ppermute | solution.py:318
  6.0 7.8 %collective-permute-start.7 = (bf16[9,20,80]{2,1,0:T(8,128)(2,1)S(1)}, bf16[9,20,80]{2,1,0:T(8,128)(2,1)S(1)}, u32[]{:S(2)}, u32[]{:S(2)}) collective-permute-start(bf16[9,20,80]{2,1,0:T(8,128)(2,1)S(1)} %bitcast.5), channel_id=1, source_target_pairs={{0,1},{1,0},{2,3},{3,2},{4,5},{5,4},{6,7},{7,6},{8,9},{9,8},{10,11... | collective-permute-start | bytes 86408 | tf_op jit(solution)/shard_map/ppermute | solution.py:322
  9.8 4.0 %collective-permute-start.5 = (bf16[4,32,128]{2,1,0:T(8,128)(2,1)S(1)}, bf16[4,32,128]{2,1,0:T(8,128)(2,1)S(1)}, u32[]{:S(2)}, u32[]{:S(2)}) collective-permute-start(bf16[4,32,128]{2,1,0:T(8,128)(2,1)S(1)} %join_columns.1.own_ref), channel_id=1, source_target_pairs={{0,1},{1,0},{2,3},{3,2},{4,5},{5,4},{6,7},{7,6},{8,9},{9,8},{10,11... | collective-permute-start | bytes 98312 | tf_op jit(solution)/shard_map/ppermute | solution.py:331
  11.5 3.9 %collective-permute-start.3 = (bf16[4,32,128]{2,1,0:T(8,128)(2,1)S(1)}, bf16[4,32,128]{2,1,0:T(8,128)(2,1)S(1)}, u32[]{:S(2)}, u32[]{:S(2)}) collective-permute-start(bf16[4,32,128]{2,1,0:T(8,128)(2,1)S(1)} %join_columns.1.own_ref), channel_id=1, source_target_pairs={{0,1},{1,0},{2,3},{3,2},{4,5},{5,4},{6,7},{7,6},{8,17},{9,16},{10,... | collective-permute-start | bytes 98312 | tf_op jit(solution)/shard_map/ppermute | solution.py:331
  12.0 4.1 %collective-permute-start.4 = (bf16[4,32,128]{2,1,0:T(8,128)(2,1)S(1)}, bf16[4,32,128]{2,1,0:T(8,128)(2,1)S(1)}, u32[]{:S(2)}, u32[]{:S(2)}) collective-permute-start(bf16[4,32,128]{2,1,0:T(8,128)(2,1)S(1)} %join_columns.1.own_ref), channel_id=1, source_target_pairs={{0,1},{1,0},{2,3},{3,2},{4,5},{5,4},{6,7},{7,6},{8,16},{9,17},{10,... | collective-permute-start | bytes 98312 | tf_op jit(solution)/shard_map/ppermute | solution.py:331
  13.8 2.3 %collective-permute-start.6 = (bf16[4,2,32,128]{3,2,1,0:T(8,128)(2,1)S(1)}, bf16[4,2,32,128]{3,2,1,0:T(8,128)(2,1)S(1)}, u32[]{:S(2)}, u32[]{:S(2)}) collective-permute-start(bf16[4,2,32,128]{3,2,1,0:T(8,128)(2,1)S(1)} %join_sides.1), channel_id=1, source_target_pairs={{0,8},{1,9},{2,10},{3,11},{4,12},{5,13},{6,14},{7,15},{8,0},{9,1},... | collective-permute-start | bytes 196616 | tf_op jit(solution)/shard_map/ppermute | solution.py:331
  14.8 8.7 %copy-start.2 = (bf16[640,1280]{1,0:T(8,128)(2,1)S(1)}, bf16[640,1280]{1,0:T(8,128)(2,1)}, u32[]{:S(2)}) copy-start(bf16[640,1280]{1,0:T(8,128)(2,1)} %refs_5_.1) | copy-start | bytes 4915204
  14.9 8.7 %copy-start.3 = (bf16[1280,640]{1,0:T(8,128)(2,1)S(1)}, bf16[1280,640]{1,0:T(8,128)(2,1)}, u32[]{:S(2)}) copy-start(bf16[1280,640]{1,0:T(8,128)(2,1)} %refs_6_.1) | copy-start | bytes 4915204
  17.0 5.5 %collective-permute-start.10 = (bf16[32,128]{1,0:T(8,128)(2,1)S(1)}, bf16[32,128]{1,0:T(8,128)(2,1)S(1)}, u32[]{:S(2)}, u32[]{:S(2)}) collective-permute-start(bf16[32,128]{1,0:T(8,128)(2,1)S(1)} %get-tuple-element.23), channel_id=1, source_target_pairs={{0,6},{1,7},{2,4},{3,5},{4,2},{5,3},{6,0},{7,1},{8,14},{9,15},{10,... | collective-permute-start | bytes 24584 | tf_op jit(solution)/shard_map/ppermute | solution.py:318
  19.0 4.5 %collective-permute-start.8 = (bf16[32,128]{1,0:T(8,128)(2,1)S(1)}, bf16[32,128]{1,0:T(8,128)(2,1)S(1)}, u32[]{:S(2)}, u32[]{:S(2)}) collective-permute-start(bf16[32,128]{1,0:T(8,128)(2,1)S(1)} %get-tuple-element.21), channel_id=1, source_target_pairs={{0,4},{1,5},{2,6},{3,7},{4,0},{5,1},{6,2},{7,3},{8,12},{9,13},{10,... | collective-permute-start | bytes 24584 | tf_op jit(solution)/shard_map/ppermute | solution.py:318
  19.0 4.5 %collective-permute-start.9 = (bf16[32,128]{1,0:T(8,128)(2,1)S(1)}, bf16[32,128]{1,0:T(8,128)(2,1)S(1)}, u32[]{:S(2)}, u32[]{:S(2)}) collective-permute-start(bf16[32,128]{1,0:T(8,128)(2,1)S(1)} %get-tuple-element.22), channel_id=1, source_target_pairs={{0,2},{1,3},{2,0},{3,1},{4,6},{5,7},{6,4},{7,5},{8,10},{9,11},{10,... | collective-permute-start | bytes 24584 | tf_op jit(solution)/shard_map/ppermute | solution.py:318

commit v5 on v4

--- a/solution.py
+++ b/solution.py
@@ -140,18 +140,26 @@
     for lon in range(width):
         pick = (apart == lon).astype(F32).astype(BF16)
         first[:, lon, :] = jnp.dot(profile, pick, preferred_element_type=F32)
+    upper = lax.broadcasted_iota(jnp.int32, (SUBLANES, places), 0) < SUBLANES // 2
+    count = columns * width
     for basis in range(bases):
         circle = first[basis]
-        for column in range(columns):
-            turned = pltpu.roll(circle, column * 2 * step, 1) if column else circle
-            at = (basis * columns + column) * step
-            for row in range(rows):
-                for tap in range(taps):
-                    weight = band[tap, row : row + 1, basis : basis + 1] * inside[row][tap]
-                    to = slots[row][tap] * places
-                    table_ref[row, at : at + step, to : to + places] = (weight * turned).astype(
-                        BF16
-                    )
+        turned = [
+            pltpu.roll(circle, column * 2 * step, 1) if column else circle
+            for column in range(columns)
+        ]
+        last = [block[SUBLANES:] for block in turned]
+        pairs = [
+            jnp.where(upper, one, pltpu.roll(other, SUBLANES // 2, 0))
+            for one, other in zip(last[::2], last[1::2])
+        ]
+        turned = jnp.concatenate([block[:SUBLANES] for block in turned] + pairs, axis=0)
+        at = basis * count
+        for row in range(rows):
+            for tap in range(taps):
+                weight = band[tap, row : row + 1, basis : basis + 1] * inside[row][tap]
+                to = slots[row][tap] * places
+                table_ref[row, at : at + count, to : to + places] = (weight * turned).astype(BF16)
 
 
 def squares_kernel(own_ref, mate_ref, squares_ref, padded):
@@ -217,7 +225,7 @@
     rows, _, inner = table_ref.shape
     places = inner // 3
     step = places // (2 * columns)
-    half = places // 2
+    half = columns * width
     rest = width - SUBLANES
     column, side = column_and_side()
     odd = lax.axis_index("lat") % 2
@@ -243,11 +251,19 @@
             ]
     mixed = jnp.dot(spread[...], squares_ref[...], preferred_element_type=F32)
     upper = lax.broadcasted_iota(jnp.int32, (SUBLANES, lanes), 0) < rest
+    top, bottom = mixed[:half], mixed[half:]
     for target in range(columns):
-        top = mixed[target * step : (target + 1) * step]
-        bottom = mixed[half + target * step : half + (target + 1) * step]
-        last = jnp.where(upper, top[SUBLANES:], pltpu.roll(bottom[SUBLANES:], rest, 0))
-        points = jnp.concatenate([top[:SUBLANES], bottom[:SUBLANES], last], axis=0)
+        at = target * SUBLANES
+        pair = (columns + target // 2) * SUBLANES
+        first, second = top[pair : pair + SUBLANES], bottom[pair : pair + SUBLANES]
+        if target % 2:
+            first = pltpu.roll(first, rest, 0)
+        else:
+            second = pltpu.roll(second, rest, 0)
+        last = jnp.where(upper, first, second)
+        points = jnp.concatenate(
+            [top[at : at + SUBLANES], bottom[at : at + SUBLANES], last], axis=0
+        )
         stage[target] = fold(points, block)
     for apart in range(columns):
         out_refs[apart][...] = stage[column ^ apart]
@@ -350,7 +366,7 @@
     height = message_rows(block)
     assert rows == 2 and taps == 3 and columns & (columns - 1) == 0
     assert lax.axis_size("lat") % 2 == 0
-    assert SUBLANES < width and rows * (width - SUBLANES) <= SUBLANES
+    assert 2 * width == 3 * SUBLANES and columns * width % (2 * SUBLANES) == 0
     assert 3 * (block % LANES) <= LANES
 
     far_first = tuple(reversed(range(columns)))
@@ -387,7 +403,7 @@
     table = call(
         functools.partial(tables_kernel, width),
         "tables",
-        jax.ShapeDtypeStruct((rows, bases * places // 2, taps * places), BF16),
+        jax.ShapeDtypeStruct((rows, bases * columns * width, taps * places), BF16),
         [pltpu.VMEM((bases, step, places), F32)],
         10**6,
         lon_filter,
@@ -431,7 +447,7 @@
     part = call(
         functools.partial(own_kernel, block, width),
         "conv_own",
-        jax.ShapeDtypeStruct((rows, bases * places // 2, lanes), F32),
+        jax.ShapeDtypeStruct((rows, bases * columns * width, lanes), F32),
         [pltpu.VMEM((rows, places, lanes), BF16)],
         10**9,
         mate_side,
@@ -444,7 +460,7 @@
         messages,
         [
             pltpu.VMEM((rows, 2 * places, lanes), BF16),
-            pltpu.VMEM((rows * places // 2, bases * lanes), BF16),
+            pltpu.VMEM((rows * columns * width, bases * lanes), BF16),
             pltpu.VMEM((columns, height, LANES), BF16),
         ],
         10**10,

time: 25.2 us -> 25.1 us (level)
  no operation moved by 1% of the time
where the time goes in v5:
time: 25.1 us; the launch traced here: 24.9 us
  starting transfers between devices  15.4 us (61%)
  waiting for transfers between devices  5.41 us (22%)
  Pallas kernels  3.97 us (16%)
    ppermute x6, starting transfers between devices, over_columns(): return lax.ppermute(message, 'lon', pairs) if apart else message  10.2 us
    pallas_call x11, Pallas kernels, call(): pl.pallas_call(kernel, out_shape=out_shape, in_specs=[VMEM] * len(operand...  3.97 us
    ppermute x6, waiting for transfers between devices, over_columns(): return lax.ppermute(message, 'lon', pairs) if apart else message  3.82 us
    ppermute x4, starting transfers between devices, swap(): return lax.ppermute(block, ('lat', 'lon'), pairs)  3.66 us
    ppermute x4, waiting for transfers between devices, swap(): return lax.ppermute(block, ('lat', 'lon'), pairs)  1.59 us
    ppermute x1, starting transfers between devices, over_sides(): return lax.ppermute(block, 'lon', [(i, i ^ 1) for i in range(count)])  1.49 us
  transfers between devices with their start and end apart: 11, of which 6 were waited for; matrix products, arithmetic and copies ran while one was open for 0% of the time, Pallas kernels for 7%

profile of v5, /device:TPU:0, one launch (start us, length us, event | category | flops | bytes accessed | tf_op | source)
XLA Modules:
  0.0 24.9 jit_solution(7575431282152271724)
XLA Ops:
  0.0 0.0 copy-start.5
  0.0 4.0 %collective-permute-start = (bf16[12,2,640]{2,1,0:T(2,128)(2,1)}, bf16[12,2,640]{2,1,0:T(2,128)(2,1)S(1)}, u32[]{:S(2)}, u32[]{:S(2)}) collective-permute-start(bf16[12,2,640]{2,1,0:T(2,128)(2,1)} %bitcast.7), channel_id=1, source_target_pairs={{0,4},{1,5},{2,6},{3,7},{4,0},{5,1},{6,2},{7,3},{8,12},{9,13},{10,... | collective-permute-start | bytes 92168 | tf_op jit(solution)/shard_map/ppermute | solution.py:334
  4.1 0.0 copy-done.5
  4.1 0.0 copy-start.4
  4.1 0.0 copy-start
  4.1 0.0 copy-start.1
  4.1 0.2 pack.1
  4.3 1.7 %collective-permute-start.1 = (bf16[32,128]{1,0:T(8,128)(2,1)S(1)}, bf16[32,128]{1,0:T(8,128)(2,1)S(1)}, u32[]{:S(2)}, u32[]{:S(2)}) collective-permute-start(bf16[32,128]{1,0:T(8,128)(2,1)S(1)} %get-tuple-element.16), channel_id=1, source_target_pairs={{0,6},{1,7},{2,4},{3,5},{4,2},{5,3},{6,0},{7,1},{8,14},{9,15},{10,... | collective-permute-start | bytes 24584 | tf_op jit(solution)/shard_map/ppermute | solution.py:334
  6.0 0.0 collective-permute-start.2
  6.0 0.0 copy-done.4
  6.0 1.5 %collective-permute-start.7 = (bf16[9,20,80]{2,1,0:T(8,128)(2,1)S(1)}, bf16[9,20,80]{2,1,0:T(8,128)(2,1)S(1)}, u32[]{:S(2)}, u32[]{:S(2)}) collective-permute-start(bf16[9,20,80]{2,1,0:T(8,128)(2,1)S(1)} %bitcast.5), channel_id=1, source_target_pairs={{0,1},{1,0},{2,3},{3,2},{4,5},{5,4},{6,7},{7,6},{8,9},{9,8},{10,11... | collective-permute-start | bytes 86408 | tf_op jit(solution)/shard_map/ppermute | solution.py:338
  7.5 0.0 copy-done
  7.5 0.0 copy-done.1
  7.5 0.4 %tables.1.table_ref = bf16[2,432,384]{2,1,0:T(8,128)(2,1)S(1)} custom-call(bf16[9,96]{1,0:T(8,128)(2,1)S(1)} %copy-done, bf16[3,2,9]{2,1,0:T(2,128)(2,1)S(1)} %bitcast.4, s32[96,128]{1,0:T(8,128)S(1)} %apart.1.apart_ref), custom_call_target="tpu_custom_call" | custom-call | flops 1000000 | bytes 1000000 | tf_op jit(solution)/shard_map/tables/pallas_call | solution.py:320
  7.9 0.0 collective-permute-done.raw_ref
  7.9 0.2 cut.1.refs_0_
  8.1 1.7 %collective-permute-done.1.refs_1_ = bf16[32,128]{1,0:T(8,128)(2,1)S(1)} collective-permute-done((bf16[32,128]{1,0:T(8,128)(2,1)S(1)}, bf16[32,128]{1,0:T(8,128)(2,1)S(1)}, u32[]{:S(2)}, u32[]{:S(2)}) %collective-permute-start.1) | collective-permute-done | bytes 8224 | tf_op jit(solution)/shard_map/ppermute | solution.py:334
  9.8 0.0 collective-permute-done.2.refs_2_
  9.8 1.6 %collective-permute-start.5 = (bf16[4,32,128]{2,1,0:T(8,128)(2,1)S(1)}, bf16[4,32,128]{2,1,0:T(8,128)(2,1)S(1)}, u32[]{:S(2)}, u32[]{:S(2)}) collective-permute-start(bf16[4,32,128]{2,1,0:T(8,128)(2,1)S(1)} %join_columns.1.own_ref), channel_id=1, source_target_pairs={{0,1},{1,0},{2,3},{3,2},{4,5},{5,4},{6,7},{7,6},{8,9},{9,8},{10,11... | collective-permute-start | bytes 98312 | tf_op jit(solution)/shard_map/ppermute | solution.py:347
  11.4 0.1 unpack.1.own
  11.5 0.5 %collective-permute-start.3 = (bf16[4,32,128]{2,1,0:T(8,128)(2,1)S(1)}, bf16[4,32,128]{2,1,0:T(8,128)(2,1)S(1)}, u32[]{:S(2)}, u32[]{:S(2)}) collective-permute-start(bf16[4,32,128]{2,1,0:T(8,128)(2,1)S(1)} %join_columns.1.own_ref), channel_id=1, source_target_pairs={{0,1},{1,0},{2,3},{3,2},{4,5},{5,4},{6,7},{7,6},{8,17},{9,16},{10,... | collective-permute-start | bytes 98312 | tf_op jit(solution)/shard_map/ppermute | solution.py:347
  12.0 1.5 %collective-permute-start.4 = (bf16[4,32,128]{2,1,0:T(8,128)(2,1)S(1)}, bf16[4,32,128]{2,1,0:T(8,128)(2,1)S(1)}, u32[]{:S(2)}, u32[]{:S(2)}) collective-permute-start(bf16[4,32,128]{2,1,0:T(8,128)(2,1)S(1)} %join_columns.1.own_ref), channel_id=1, source_target_pairs={{0,1},{1,0},{2,3},{3,2},{4,5},{5,4},{6,7},{7,6},{8,16},{9,17},{10,... | collective-permute-start | bytes 98312 | tf_op jit(solution)/shard_map/ppermute | solution.py:347
  13.5 0.3 %collective-permute-done.5.mate_ref.mate = bf16[4,32,128]{2,1,0:T(8,128)(2,1)S(1)} collective-permute-done((bf16[4,32,128]{2,1,0:T(8,128)(2,1)S(1)}, bf16[4,32,128]{2,1,0:T(8,128)(2,1)S(1)}, u32[]{:S(2)}, u32[]{:S(2)}) %collective-permute-start.5) | collective-permute-done | bytes 32800 | tf_op jit(solution)/shard_map/ppermute | solution.py:347
  13.8 0.1 collective-permute-start.6
  13.9 0.0 collective-permute-done.7.mate_ref
  13.9 0.5 %squares.1.squares_ref = bf16[2304,256]{1,0:T(8,128)(2,1)S(1)} custom-call(bf16[9,20,80]{2,1,0:T(8,128)(2,1)S(1)} %bitcast.6, bf16[9,20,80]{2,1,0:T(8,128)(2,1)S(1)} %collective-permute-done.7.mate_ref), custom_call_target="tpu_custom_call" | custom-call | flops 1000000000 | bytes 1000000 | tf_op jit(solution)/shard_map/squares/pallas_call | solution.py:320
  14.5 0.3 %conv_own.1.part_ref = f32[2,432,256]{2,1,0:T(8,128)S(1)} custom-call(bf16[4,32,128]{2,1,0:T(8,128)(2,1)S(1)} %collective-permute-done.5.mate_ref.mate, bf16[2,4,16,256]{3,2,1,0:T(8,128)(2,1)S(1)} %unpack.1.own, bf16[2,432,384]{2,1,0:T(8,128)(2,1)S(1)} %tables.1.table_ref), custom_call_target="tpu_custom_call" | custom-call | flops 1000000000 | bytes 1000000 | tf_op jit(solution)/shard_map/conv_own/pallas_call | solution.py:320
  14.8 0.0 copy-start.2
  14.8 0.0 copy-start.3
  14.8 0.5 %collective-permute-done.3.odd_mate = bf16[4,32,128]{2,1,0:T(8,128)(2,1)S(1)} collective-permute-done((bf16[4,32,128]{2,1,0:T(8,128)(2,1)S(1)}, bf16[4,32,128]{2,1,0:T(8,128)(2,1)S(1)}, u32[]{:S(2)}, u32[]{:S(2)}) %collective-permute-start.3) | collective-permute-done | bytes 32800 | tf_op jit(solution)/shard_map/ppermute | solution.py:347
  15.4 0.7 %collective-permute-done.4.odd_own = bf16[4,32,128]{2,1,0:T(8,128)(2,1)S(1)} collective-permute-done((bf16[4,32,128]{2,1,0:T(8,128)(2,1)S(1)}, bf16[4,32,128]{2,1,0:T(8,128)(2,1)S(1)}, u32[]{:S(2)}, u32[]{:S(2)}) %collective-permute-start.4) | collective-permute-done | bytes 32800 | tf_op jit(solution)/shard_map/ppermute | solution.py:347
  16.1 0.0 collective-permute-done.6.even
  16.1 0.8 %conv.1 = (bf16[32,128]{1,0:T(8,128)(2,1)S(1)}, bf16[32,128]{1,0:T(8,128)(2,1)S(1)}, bf16[32,128]{1,0:T(8,128)(2,1)S(1)}, bf16[32,128]{1,0:T(8,128)(2,1)S(1)}) custom-call(bf16[4,32,128]{2,1,0:T(8,128)(2,1)S(1)} %collective-permute-done.3.odd_mate, bf16[4,32,128]{2,1,0:T(8,128)(2,1)S(1)} %collective-permute-done.4.odd_own, ...), custom_call_target="tpu_custom_call" | custom-call | flops 10000000000 | bytes 1000000 | tf_op jit(solution)/shard_map/conv/pallas_call | solution.py:320
  16.9 2.0 %collective-permute-start.10 = (bf16[32,128]{1,0:T(8,128)(2,1)S(1)}, bf16[32,128]{1,0:T(8,128)(2,1)S(1)}, u32[]{:S(2)}, u32[]{:S(2)}) collective-permute-start(bf16[32,128]{1,0:T(8,128)(2,1)S(1)} %get-tuple-element.23), channel_id=1, source_target_pairs={{0,6},{1,7},{2,4},{3,5},{4,2},{5,3},{6,0},{7,1},{8,14},{9,15},{10,... | collective-permute-start | bytes 24584 | tf_op jit(solution)/shard_map/ppermute | solution.py:334
  18.9 0.0 collective-permute-start.8
  18.9 2.4 %collective-permute-start.9 = (bf16[32,128]{1,0:T(8,128)(2,1)S(1)}, bf16[32,128]{1,0:T(8,128)(2,1)S(1)}, u32[]{:S(2)}, u32[]{:S(2)}) collective-permute-start(bf16[32,128]{1,0:T(8,128)(2,1)S(1)} %get-tuple-element.22), channel_id=1, source_target_pairs={{0,2},{1,3},{2,0},{3,1},{4,6},{5,7},{6,4},{7,5},{8,10},{9,11},{10,... | collective-permute-start | bytes 24584 | tf_op jit(solution)/shard_map/ppermute | solution.py:334
  21.4 1.1 %collective-permute-done.10.refs_2_ = bf16[32,128]{1,0:T(8,128)(2,1)S(1)} collective-permute-done((bf16[32,128]{1,0:T(8,128)(2,1)S(1)}, bf16[32,128]{1,0:T(8,128)(2,1)S(1)}, u32[]{:S(2)}, u32[]{:S(2)}) %collective-permute-start.10) | collective-permute-done | bytes 8224 | tf_op jit(solution)/shard_map/ppermute | solution.py:334
  22.4 1.1 %collective-permute-done.8.refs_0_ = bf16[32,128]{1,0:T(8,128)(2,1)S(1)} collective-permute-done((bf16[32,128]{1,0:T(8,128)(2,1)S(1)}, bf16[32,128]{1,0:T(8,128)(2,1)S(1)}, u32[]{:S(2)}, u32[]{:S(2)}) %collective-permute-start.8) | collective-permute-done | bytes 8224 | tf_op jit(solution)/shard_map/ppermute | solution.py:334
  23.5 0.0 collective-permute-done.9.refs_1_
  23.5 0.0 copy-done.2
  23.5 0.0 copy-done.3
  23.5 1.4 %tail.1 = bf16[12,2,640]{2,1,0:T(2,128)(2,1)} custom-call(bf16[32,128]{1,0:T(8,128)(2,1)S(1)} %collective-permute-done.8.refs_0_, bf16[32,128]{1,0:T(8,128)(2,1)S(1)} %collective-permute-done.9.refs_1_, bf16[32,128]{1,0:T(8,128)(2,1)S(1)} %collective-permute-done.10.refs_2_, bf16[32,128]{1,0:T(8,128)(2,1)S(1)} %get-tuple-element.24.refs_3_, ...), custom_call_target="tpu_custom_call" | custom-call | flops 1000000000 | bytes 1000000 | tf_op jit(solution)/shard_map/tail/pallas_call | solution.py:320
  (3 shorter events, 0.0 us)
Async XLA Ops:
  0.0 4.1 %copy-start.5 = (bf16[2,12,640]{2,0,1:T(2,128)(2,1)S(1)}, bf16[2,12,640]{2,0,1:T(2,128)(2,1)}, u32[]{:S(2)}) copy-start(bf16[2,12,640]{2,0,1:T(2,128)(2,1)} %param.7) | copy-start | bytes 92164
  0.0 7.9 %collective-permute-start = (bf16[12,2,640]{2,1,0:T(2,128)(2,1)}, bf16[12,2,640]{2,1,0:T(2,128)(2,1)S(1)}, u32[]{:S(2)}, u32[]{:S(2)}) collective-permute-start(bf16[12,2,640]{2,1,0:T(2,128)(2,1)} %bitcast.7), channel_id=1, source_target_pairs={{0,4},{1,5},{2,6},{3,7},{4,0},{5,1},{6,2},{7,3},{8,12},{9,13},{10,... | collective-permute-start | bytes 92168 | tf_op jit(solution)/shard_map/ppermute | solution.py:334
  4.1 2.0 %copy-start.4 = (bf16[9,80,20]{1,2,0:T(8,128)(2,1)S(1)}, bf16[9,80,20]{1,2,0:T(8,128)(2,1)}, u32[]{:S(2)}) copy-start(bf16[9,80,20]{1,2,0:T(8,128)(2,1)} %param.9) | copy-start | bytes 86404
  4.1 3.4 %copy-start = (bf16[9,96]{1,0:T(8,128)(2,1)S(1)}, bf16[9,96]{1,0:T(8,128)(2,1)}, u32[]{:S(2)}) copy-start(bf16[9,96]{1,0:T(8,128)(2,1)} %filter_ref.1) | copy-start | bytes 5188
  4.1 3.4 %copy-start.1 = (bf16[9,2,3]{0,1,2:T(2,128)(2,1)S(1)}, bf16[9,2,3]{0,1,2:T(2,128)(2,1)}, u32[]{:S(2)}) copy-start(bf16[9,2,3]{0,1,2:T(2,128)(2,1)} %param.10) | copy-start | bytes 328
  4.3 5.5 %collective-permute-start.1 = (bf16[32,128]{1,0:T(8,128)(2,1)S(1)}, bf16[32,128]{1,0:T(8,128)(2,1)S(1)}, u32[]{:S(2)}, u32[]{:S(2)}) collective-permute-start(bf16[32,128]{1,0:T(8,128)(2,1)S(1)} %get-tuple-element.16), channel_id=1, source_target_pairs={{0,6},{1,7},{2,4},{3,5},{4,2},{5,3},{6,0},{7,1},{8,14},{9,15},{10,... | collective-permute-start | bytes 24584 | tf_op jit(solution)/shard_map/ppermute | solution.py:334
  6.0 3.8 %collective-permute-start.2 = (bf16[32,128]{1,0:T(8,128)(2,1)S(1)}, bf16[32,128]{1,0:T(8,128)(2,1)S(1)}, u32[]{:S(2)}, u32[]{:S(2)}) collective-permute-start(bf16[32,128]{1,0:T(8,128)(2,1)S(1)} %get-tuple-element.17), channel_id=1, source_target_pairs={{0,2},{1,3},{2,0},{3,1},{4,6},{5,7},{6,4},{7,5},{8,10},{9,11},{10,... | collective-permute-start | bytes 24584 | tf_op jit(solution)/shard_map/ppermute | solution.py:334
  6.0 7.8 %collective-permute-start.7 = (bf16[9,20,80]{2,1,0:T(8,128)(2,1)S(1)}, bf16[9,20,80]{2,1,0:T(8,128)(2,1)S(1)}, u32[]{:S(2)}, u32[]{:S(2)}) collective-permute-start(bf16[9,20,80]{2,1,0:T(8,128)(2,1)S(1)} %bitcast.5), channel_id=1, source_target_pairs={{0,1},{1,0},{2,3},{3,2},{4,5},{5,4},{6,7},{7,6},{8,9},{9,8},{10,11... | collective-permute-start | bytes 86408 | tf_op jit(solution)/shard_map/ppermute | solution.py:338
  9.8 4.0 %collective-permute-start.5 = (bf16[4,32,128]{2,1,0:T(8,128)(2,1)S(1)}, bf16[4,32,128]{2,1,0:T(8,128)(2,1)S(1)}, u32[]{:S(2)}, u32[]{:S(2)}) collective-permute-start(bf16[4,32,128]{2,1,0:T(8,128)(2,1)S(1)} %join_columns.1.own_ref), channel_id=1, source_target_pairs={{0,1},{1,0},{2,3},{3,2},{4,5},{5,4},{6,7},{7,6},{8,9},{9,8},{10,11... | collective-permute-start | bytes 98312 | tf_op jit(solution)/shard_map/ppermute | solution.py:347
  11.5 3.9 %collective-permute-start.3 = (bf16[4,32,128]{2,1,0:T(8,128)(2,1)S(1)}, bf16[4,32,128]{2,1,0:T(8,128)(2,1)S(1)}, u32[]{:S(2)}, u32[]{:S(2)}) collective-permute-start(bf16[4,32,128]{2,1,0:T(8,128)(2,1)S(1)} %join_columns.1.own_ref), channel_id=1, source_target_pairs={{0,1},{1,0},{2,3},{3,2},{4,5},{5,4},{6,7},{7,6},{8,17},{9,16},{10,... | collective-permute-start | bytes 98312 | tf_op jit(solution)/shard_map/ppermute | solution.py:347
  12.0 4.1 %collective-permute-start.4 = (bf16[4,32,128]{2,1,0:T(8,128)(2,1)S(1)}, bf16[4,32,128]{2,1,0:T(8,128)(2,1)S(1)}, u32[]{:S(2)}, u32[]{:S(2)}) collective-permute-start(bf16[4,32,128]{2,1,0:T(8,128)(2,1)S(1)} %join_columns.1.own_ref), channel_id=1, source_target_pairs={{0,1},{1,0},{2,3},{3,2},{4,5},{5,4},{6,7},{7,6},{8,16},{9,17},{10,... | collective-permute-start | bytes 98312 | tf_op jit(solution)/shard_map/ppermute | solution.py:347
  13.8 2.3 %collective-permute-start.6 = (bf16[4,2,32,128]{3,2,1,0:T(8,128)(2,1)S(1)}, bf16[4,2,32,128]{3,2,1,0:T(8,128)(2,1)S(1)}, u32[]{:S(2)}, u32[]{:S(2)}) collective-permute-start(bf16[4,2,32,128]{3,2,1,0:T(8,128)(2,1)S(1)} %join_sides.1), channel_id=1, source_target_pairs={{0,8},{1,9},{2,10},{3,11},{4,12},{5,13},{6,14},{7,15},{8,0},{9,1},... | collective-permute-start | bytes 196616 | tf_op jit(solution)/shard_map/ppermute | solution.py:347
  14.8 8.7 %copy-start.2 = (bf16[640,1280]{1,0:T(8,128)(2,1)S(1)}, bf16[640,1280]{1,0:T(8,128)(2,1)}, u32[]{:S(2)}) copy-start(bf16[640,1280]{1,0:T(8,128)(2,1)} %refs_5_.1) | copy-start | bytes 4915204
  14.8 8.7 %copy-start.3 = (bf16[1280,640]{1,0:T(8,128)(2,1)S(1)}, bf16[1280,640]{1,0:T(8,128)(2,1)}, u32[]{:S(2)}) copy-start(bf16[1280,640]{1,0:T(8,128)(2,1)} %refs_6_.1) | copy-start | bytes 4915204
  16.9 5.5 %collective-permute-start.10 = (bf16[32,128]{1,0:T(8,128)(2,1)S(1)}, bf16[32,128]{1,0:T(8,128)(2,1)S(1)}, u32[]{:S(2)}, u32[]{:S(2)}) collective-permute-start(bf16[32,128]{1,0:T(8,128)(2,1)S(1)} %get-tuple-element.23), channel_id=1, source_target_pairs={{0,6},{1,7},{2,4},{3,5},{4,2},{5,3},{6,0},{7,1},{8,14},{9,15},{10,... | collective-permute-start | bytes 24584 | tf_op jit(solution)/shard_map/ppermute | solution.py:334
  18.9 4.5 %collective-permute-start.8 = (bf16[32,128]{1,0:T(8,128)(2,1)S(1)}, bf16[32,128]{1,0:T(8,128)(2,1)S(1)}, u32[]{:S(2)}, u32[]{:S(2)}) collective-permute-start(bf16[32,128]{1,0:T(8,128)(2,1)S(1)} %get-tuple-element.21), channel_id=1, source_target_pairs={{0,4},{1,5},{2,6},{3,7},{4,0},{5,1},{6,2},{7,3},{8,12},{9,13},{10,... | collective-permute-start | bytes 24584 | tf_op jit(solution)/shard_map/ppermute | solution.py:334
  18.9 4.5 %collective-permute-start.9 = (bf16[32,128]{1,0:T(8,128)(2,1)S(1)}, bf16[32,128]{1,0:T(8,128)(2,1)S(1)}, u32[]{:S(2)}, u32[]{:S(2)}) collective-permute-start(bf16[32,128]{1,0:T(8,128)(2,1)S(1)} %get-tuple-element.22), channel_id=1, source_target_pairs={{0,2},{1,3},{2,0},{3,1},{4,6},{5,7},{6,4},{7,5},{8,10},{9,11},{10,... | collective-permute-start | bytes 24584 | tf_op jit(solution)/shard_map/ppermute | solution.py:334

commit v6 on v5

--- a/solution.py
+++ b/solution.py
@@ -269,29 +269,35 @@
         out_refs[apart][...] = stage[column ^ apart]
 
 
+def placed(message, column, chans, block):
+    lanes = lanes_of(block)
+    kept = lax.broadcasted_iota(jnp.int32, (3 * SUBLANES, lanes), 1) < block
+    piece = jnp.concatenate(unfold(message.astype(F32), block), axis=0)
+    piece = jnp.where(kept, piece, 0.0)
+    if chans > lanes:
+        gap = jnp.zeros((3 * SUBLANES, chans - lanes), F32)
+        piece = jnp.concatenate([piece, gap], axis=1)
+    return pltpu.roll(piece, column * block, 1)
+
+
+def residual_kernel(columns, own_ref, latent_ref, out_ref, points):
+    chans = latent_ref.shape[2]
+    column, _ = column_and_side()
+    group_points(latent_ref, points)
+    out_ref[...] = points[...] + placed(own_ref[...], column, chans, chans // columns)
+
+
 def tail_kernel(order, *refs):
-    columns = len(order)
-    back_refs = refs[:columns]
-    latent_ref, up_ref, down_ref, out_ref, points, stage = refs[columns:]
-    width, rows, chans = latent_ref.shape
+    columns = len(order) + 1
+    back_refs = refs[: columns - 1]
+    residual_ref, up_ref, down_ref, out_ref = refs[columns - 1 :]
+    width, rows, chans = out_ref.shape
     rest = width - SUBLANES
-    block = chans // columns
-    lanes = lanes_of(block)
     column, _ = column_and_side()
+    convolved = residual_ref[...]
     for apart, ref in zip(order, back_refs):
-        stage[column ^ apart] = ref[...]
-    group_points(latent_ref, points)
-    kept = lax.broadcasted_iota(jnp.int32, (3 * SUBLANES, lanes), 1) < block
-    convolved = None
-    for target in range(columns):
-        piece = jnp.concatenate(unfold(stage[target].astype(F32), block), axis=0)
-        piece = jnp.where(kept, piece, 0.0)
-        if chans > lanes:
-            gap = jnp.zeros((3 * SUBLANES, chans - lanes), F32)
-            piece = jnp.concatenate([piece, gap], axis=1)
-        piece = pltpu.roll(piece, target * block, 1) if target else piece
-        convolved = piece if convolved is None else convolved + piece
-    summed = (points[...] + convolved).astype(BF16)
+        convolved = convolved + placed(ref[...], column ^ apart, chans, chans // columns)
+    summed = convolved.astype(BF16)
     ones = jnp.ones((2 * SUBLANES, chans), BF16)
     count = summed.shape[0]
     raised = jnp.dot(
@@ -471,16 +477,25 @@
         table,
         squares,
     )
-    outward = far_first[1:-1] + far_first[:1] + far_first[-1:]
+    outward = far_first[1:-1] + far_first[:1]
     back = [over_columns(mixed[apart], count, apart) for apart in outward]
+    residual = call(
+        functools.partial(residual_kernel, columns),
+        "residual",
+        jax.ShapeDtypeStruct((3 * SUBLANES, chans), F32),
+        [points],
+        10**9,
+        mixed[0],
+        lon_first,
+    )
     result = call(
         functools.partial(tail_kernel, outward),
         "tail",
         jax.ShapeDtypeStruct(lon_first.shape, BF16),
-        [points, stage],
+        [],
         10**9,
         *back,
-        lon_first,
+        residual,
         w_up,
         w_down,
     )

time: 25.1 us -> 25.1 us (level)
    pallas_call x11 -> x12, Pallas kernels: 3.97 us -> 4.13 us  [call(): pl.pallas_call(kernel, out_shape=out_shape, in_specs=[VMEM] * len(operand...]
  transfers between devices with their start and end apart: 11 -> 11, of which waited for: 6 -> 6; matrix products, arithmetic and copies ran while one was open for 0% -> 0% of each run, Pallas kernels for 7% -> 8%
where the time goes in v6:
time: 25.1 us; the launch traced here: 24.9 us
  starting transfers between devices  15.4 us (61%)
  waiting for transfers between devices  5.28 us (21%)
  Pallas kernels  4.13 us (16%)
    ppermute x6, starting transfers between devices, over_columns(): return lax.ppermute(message, 'lon', pairs) if apart else message  10.2 us
    pallas_call x12, Pallas kernels, call(): pl.pallas_call(kernel, out_shape=out_shape, in_specs=[VMEM] * len(operand...  4.13 us
    ppermute x6, waiting for transfers between devices, over_columns(): return lax.ppermute(message, 'lon', pairs) if apart else message  3.67 us
    ppermute x4, starting transfers between devices, swap(): return lax.ppermute(block, ('lat', 'lon'), pairs)  3.66 us
    ppermute x4, waiting for transfers between devices, swap(): return lax.ppermute(block, ('lat', 'lon'), pairs)  1.62 us
    ppermute x1, starting transfers between devices, over_sides(): return lax.ppermute(block, 'lon', [(i, i ^ 1) for i in range(count)])  1.49 us
  transfers between devices with their start and end apart: 11, of which 6 were waited for; matrix products, arithmetic and copies ran while one was open for 0% of the time, Pallas kernels for 8%

profile of v6, /device:TPU:0, one launch (start us, length us, event | category | flops | bytes accessed | tf_op | source)
XLA Modules:
  0.0 24.9 jit_solution(5733264207668817112)
XLA Ops:
  0.0 0.0 copy-start.5
  0.0 4.0 %collective-permute-start = (bf16[12,2,640]{2,1,0:T(2,128)(2,1)}, bf16[12,2,640]{2,1,0:T(2,128)(2,1)S(1)}, u32[]{:S(2)}, u32[]{:S(2)}) collective-permute-start(bf16[12,2,640]{2,1,0:T(2,128)(2,1)} %bitcast.7), channel_id=1, source_target_pairs={{0,4},{1,5},{2,6},{3,7},{4,0},{5,1},{6,2},{7,3},{8,12},{9,13},{10,... | collective-permute-start | bytes 92168 | tf_op jit(solution)/shard_map/ppermute | solution.py:340
  4.1 0.0 copy-done.5
  4.1 0.0 copy-start.4
  4.1 0.0 copy-start
  4.1 0.0 copy-start.1
  4.1 0.2 pack.1
  4.3 1.7 %collective-permute-start.1 = (bf16[32,128]{1,0:T(8,128)(2,1)S(1)}, bf16[32,128]{1,0:T(8,128)(2,1)S(1)}, u32[]{:S(2)}, u32[]{:S(2)}) collective-permute-start(bf16[32,128]{1,0:T(8,128)(2,1)S(1)} %get-tuple-element.16), channel_id=1, source_target_pairs={{0,6},{1,7},{2,4},{3,5},{4,2},{5,3},{6,0},{7,1},{8,14},{9,15},{10,... | collective-permute-start | bytes 24584 | tf_op jit(solution)/shard_map/ppermute | solution.py:340
  6.0 0.0 collective-permute-start.2
  6.0 0.0 copy-done.4
  6.0 1.5 %collective-permute-start.7 = (bf16[9,20,80]{2,1,0:T(8,128)(2,1)S(1)}, bf16[9,20,80]{2,1,0:T(8,128)(2,1)S(1)}, u32[]{:S(2)}, u32[]{:S(2)}) collective-permute-start(bf16[9,20,80]{2,1,0:T(8,128)(2,1)S(1)} %bitcast.5), channel_id=1, source_target_pairs={{0,1},{1,0},{2,3},{3,2},{4,5},{5,4},{6,7},{7,6},{8,9},{9,8},{10,11... | collective-permute-start | bytes 86408 | tf_op jit(solution)/shard_map/ppermute | solution.py:344
  7.5 0.0 copy-done
  7.5 0.0 copy-done.1
  7.5 0.4 %tables.1.table_ref = bf16[2,432,384]{2,1,0:T(8,128)(2,1)S(1)} custom-call(bf16[9,96]{1,0:T(8,128)(2,1)S(1)} %copy-done, bf16[3,2,9]{2,1,0:T(2,128)(2,1)S(1)} %bitcast.4, s32[96,128]{1,0:T(8,128)S(1)} %apart.1.apart_ref), custom_call_target="tpu_custom_call" | custom-call | flops 1000000 | bytes 1000000 | tf_op jit(solution)/shard_map/tables/pallas_call | solution.py:326
  7.9 0.0 collective-permute-done.raw_ref
  7.9 0.2 cut.1.refs_0_
  8.1 1.7 %collective-permute-done.1.refs_1_ = bf16[32,128]{1,0:T(8,128)(2,1)S(1)} collective-permute-done((bf16[32,128]{1,0:T(8,128)(2,1)S(1)}, bf16[32,128]{1,0:T(8,128)(2,1)S(1)}, u32[]{:S(2)}, u32[]{:S(2)}) %collective-permute-start.1) | collective-permute-done | bytes 8224 | tf_op jit(solution)/shard_map/ppermute | solution.py:340
  9.8 0.0 collective-permute-done.2.refs_2_
  9.8 1.6 %collective-permute-start.5 = (bf16[4,32,128]{2,1,0:T(8,128)(2,1)S(1)}, bf16[4,32,128]{2,1,0:T(8,128)(2,1)S(1)}, u32[]{:S(2)}, u32[]{:S(2)}) collective-permute-start(bf16[4,32,128]{2,1,0:T(8,128)(2,1)S(1)} %join_columns.1.own_ref), channel_id=1, source_target_pairs={{0,1},{1,0},{2,3},{3,2},{4,5},{5,4},{6,7},{7,6},{8,9},{9,8},{10,11... | collective-permute-start | bytes 98312 | tf_op jit(solution)/shard_map/ppermute | solution.py:353
  11.4 0.1 unpack.1.own
  11.5 0.5 %collective-permute-start.3 = (bf16[4,32,128]{2,1,0:T(8,128)(2,1)S(1)}, bf16[4,32,128]{2,1,0:T(8,128)(2,1)S(1)}, u32[]{:S(2)}, u32[]{:S(2)}) collective-permute-start(bf16[4,32,128]{2,1,0:T(8,128)(2,1)S(1)} %join_columns.1.own_ref), channel_id=1, source_target_pairs={{0,1},{1,0},{2,3},{3,2},{4,5},{5,4},{6,7},{7,6},{8,17},{9,16},{10,... | collective-permute-start | bytes 98312 | tf_op jit(solution)/shard_map/ppermute | solution.py:353
  12.0 1.5 %collective-permute-start.4 = (bf16[4,32,128]{2,1,0:T(8,128)(2,1)S(1)}, bf16[4,32,128]{2,1,0:T(8,128)(2,1)S(1)}, u32[]{:S(2)}, u32[]{:S(2)}) collective-permute-start(bf16[4,32,128]{2,1,0:T(8,128)(2,1)S(1)} %join_columns.1.own_ref), channel_id=1, source_target_pairs={{0,1},{1,0},{2,3},{3,2},{4,5},{5,4},{6,7},{7,6},{8,16},{9,17},{10,... | collective-permute-start | bytes 98312 | tf_op jit(solution)/shard_map/ppermute | solution.py:353
  13.5 0.3 %collective-permute-done.5.mate_ref.mate = bf16[4,32,128]{2,1,0:T(8,128)(2,1)S(1)} collective-permute-done((bf16[4,32,128]{2,1,0:T(8,128)(2,1)S(1)}, bf16[4,32,128]{2,1,0:T(8,128)(2,1)S(1)}, u32[]{:S(2)}, u32[]{:S(2)}) %collective-permute-start.5) | collective-permute-done | bytes 32800 | tf_op jit(solution)/shard_map/ppermute | solution.py:353
  13.8 0.1 collective-permute-start.6
  13.9 0.0 collective-permute-done.7.mate_ref
  13.9 0.5 %squares.1.squares_ref = bf16[2304,256]{1,0:T(8,128)(2,1)S(1)} custom-call(bf16[9,20,80]{2,1,0:T(8,128)(2,1)S(1)} %bitcast.6, bf16[9,20,80]{2,1,0:T(8,128)(2,1)S(1)} %collective-permute-done.7.mate_ref), custom_call_target="tpu_custom_call" | custom-call | flops 1000000000 | bytes 1000000 | tf_op jit(solution)/shard_map/squares/pallas_call | solution.py:326
  14.5 0.3 %conv_own.1.part_ref = f32[2,432,256]{2,1,0:T(8,128)S(1)} custom-call(bf16[4,32,128]{2,1,0:T(8,128)(2,1)S(1)} %collective-permute-done.5.mate_ref.mate, bf16[2,4,16,256]{3,2,1,0:T(8,128)(2,1)S(1)} %unpack.1.own, bf16[2,432,384]{2,1,0:T(8,128)(2,1)S(1)} %tables.1.table_ref), custom_call_target="tpu_custom_call" | custom-call | flops 1000000000 | bytes 1000000 | tf_op jit(solution)/shard_map/conv_own/pallas_call | solution.py:326
  14.8 0.6 %collective-permute-done.3.odd_mate = bf16[4,32,128]{2,1,0:T(8,128)(2,1)S(1)} collective-permute-done((bf16[4,32,128]{2,1,0:T(8,128)(2,1)S(1)}, bf16[4,32,128]{2,1,0:T(8,128)(2,1)S(1)}, u32[]{:S(2)}, u32[]{:S(2)}) %collective-permute-start.3) | collective-permute-done | bytes 32800 | tf_op jit(solution)/shard_map/ppermute | solution.py:353
  15.4 0.7 %collective-permute-done.4.odd_own = bf16[4,32,128]{2,1,0:T(8,128)(2,1)S(1)} collective-permute-done((bf16[4,32,128]{2,1,0:T(8,128)(2,1)S(1)}, bf16[4,32,128]{2,1,0:T(8,128)(2,1)S(1)}, u32[]{:S(2)}, u32[]{:S(2)}) %collective-permute-start.4) | collective-permute-done | bytes 32800 | tf_op jit(solution)/shard_map/ppermute | solution.py:353
  16.1 0.0 collective-permute-done.6.even
  16.1 0.8 %conv.1 = (bf16[32,128]{1,0:T(8,128)(2,1)S(1)}, bf16[32,128]{1,0:T(8,128)(2,1)S(1)}, bf16[32,128]{1,0:T(8,128)(2,1)S(1)}, bf16[32,128]{1,0:T(8,128)(2,1)S(1)}) custom-call(bf16[4,32,128]{2,1,0:T(8,128)(2,1)S(1)} %collective-permute-done.3.odd_mate, bf16[4,32,128]{2,1,0:T(8,128)(2,1)S(1)} %collective-permute-done.4.odd_own, ...), custom_call_target="tpu_custom_call" | custom-call | flops 10000000000 | bytes 1000000 | tf_op jit(solution)/shard_map/conv/pallas_call | solution.py:326
  16.9 2.0 %collective-permute-start.10 = (bf16[32,128]{1,0:T(8,128)(2,1)S(1)}, bf16[32,128]{1,0:T(8,128)(2,1)S(1)}, u32[]{:S(2)}, u32[]{:S(2)}) collective-permute-start(bf16[32,128]{1,0:T(8,128)(2,1)S(1)} %get-tuple-element.23), channel_id=1, source_target_pairs={{0,6},{1,7},{2,4},{3,5},{4,2},{5,3},{6,0},{7,1},{8,14},{9,15},{10,... | collective-permute-start | bytes 24584 | tf_op jit(solution)/shard_map/ppermute | solution.py:340
  18.9 0.0 collective-permute-start.8
  18.9 2.4 %collective-permute-start.9 = (bf16[32,128]{1,0:T(8,128)(2,1)S(1)}, bf16[32,128]{1,0:T(8,128)(2,1)S(1)}, u32[]{:S(2)}, u32[]{:S(2)}) collective-permute-start(bf16[32,128]{1,0:T(8,128)(2,1)S(1)} %get-tuple-element.22), channel_id=1, source_target_pairs={{0,2},{1,3},{2,0},{3,1},{4,6},{5,7},{6,4},{7,5},{8,10},{9,11},{10,... | collective-permute-start | bytes 24584 | tf_op jit(solution)/shard_map/ppermute | solution.py:340
  21.4 0.0 copy-start.2
  21.4 0.0 copy-start.3
  21.4 0.1 residual.1.refs_3_
  21.5 0.9 %collective-permute-done.10.refs_2_ = bf16[32,128]{1,0:T(8,128)(2,1)S(1)} collective-permute-done((bf16[32,128]{1,0:T(8,128)(2,1)S(1)}, bf16[32,128]{1,0:T(8,128)(2,1)S(1)}, u32[]{:S(2)}, u32[]{:S(2)}) %collective-permute-start.10) | collective-permute-done | bytes 8224 | tf_op jit(solution)/shard_map/ppermute | solution.py:340
  22.4 1.1 %collective-permute-done.8.refs_0_ = bf16[32,128]{1,0:T(8,128)(2,1)S(1)} collective-permute-done((bf16[32,128]{1,0:T(8,128)(2,1)S(1)}, bf16[32,128]{1,0:T(8,128)(2,1)S(1)}, u32[]{:S(2)}, u32[]{:S(2)}) %collective-permute-start.8) | collective-permute-done | bytes 8224 | tf_op jit(solution)/shard_map/ppermute | solution.py:340
  23.5 0.0 collective-permute-done.9.refs_1_
  23.5 0.0 copy-done.2
  23.5 0.0 copy-done.3
  23.5 1.4 %tail.1 = bf16[12,2,640]{2,1,0:T(2,128)(2,1)} custom-call(bf16[32,128]{1,0:T(8,128)(2,1)S(1)} %collective-permute-done.8.refs_0_, bf16[32,128]{1,0:T(8,128)(2,1)S(1)} %collective-permute-done.9.refs_1_, bf16[32,128]{1,0:T(8,128)(2,1)S(1)} %collective-permute-done.10.refs_2_, f32[24,640]{1,0:T(8,128)S(1)} %residual.1.refs_3_, ...), custom_call_target="tpu_custom_call" | custom-call | flops 1000000000 | bytes 1000000 | tf_op jit(solution)/shard_map/tail/pallas_call | solution.py:326
  (3 shorter events, 0.0 us)
Async XLA Ops:
  0.0 4.1 %copy-start.5 = (bf16[2,12,640]{2,0,1:T(2,128)(2,1)S(1)}, bf16[2,12,640]{2,0,1:T(2,128)(2,1)}, u32[]{:S(2)}) copy-start(bf16[2,12,640]{2,0,1:T(2,128)(2,1)} %param.7) | copy-start | bytes 92164
  0.0 7.9 %collective-permute-start = (bf16[12,2,640]{2,1,0:T(2,128)(2,1)}, bf16[12,2,640]{2,1,0:T(2,128)(2,1)S(1)}, u32[]{:S(2)}, u32[]{:S(2)}) collective-permute-start(bf16[12,2,640]{2,1,0:T(2,128)(2,1)} %bitcast.7), channel_id=1, source_target_pairs={{0,4},{1,5},{2,6},{3,7},{4,0},{5,1},{6,2},{7,3},{8,12},{9,13},{10,... | collective-permute-start | bytes 92168 | tf_op jit(solution)/shard_map/ppermute | solution.py:340
  4.1 2.0 %copy-start.4 = (bf16[9,80,20]{1,2,0:T(8,128)(2,1)S(1)}, bf16[9,80,20]{1,2,0:T(8,128)(2,1)}, u32[]{:S(2)}) copy-start(bf16[9,80,20]{1,2,0:T(8,128)(2,1)} %param.9) | copy-start | bytes 86404
  4.1 3.4 %copy-start = (bf16[9,96]{1,0:T(8,128)(2,1)S(1)}, bf16[9,96]{1,0:T(8,128)(2,1)}, u32[]{:S(2)}) copy-start(bf16[9,96]{1,0:T(8,128)(2,1)} %filter_ref.1) | copy-start | bytes 5188
  4.1 3.4 %copy-start.1 = (bf16[9,2,3]{0,1,2:T(2,128)(2,1)S(1)}, bf16[9,2,3]{0,1,2:T(2,128)(2,1)}, u32[]{:S(2)}) copy-start(bf16[9,2,3]{0,1,2:T(2,128)(2,1)} %param.10) | copy-start | bytes 328
  4.3 5.5 %collective-permute-start.1 = (bf16[32,128]{1,0:T(8,128)(2,1)S(1)}, bf16[32,128]{1,0:T(8,128)(2,1)S(1)}, u32[]{:S(2)}, u32[]{:S(2)}) collective-permute-start(bf16[32,128]{1,0:T(8,128)(2,1)S(1)} %get-tuple-element.16), channel_id=1, source_target_pairs={{0,6},{1,7},{2,4},{3,5},{4,2},{5,3},{6,0},{7,1},{8,14},{9,15},{10,... | collective-permute-start | bytes 24584 | tf_op jit(solution)/shard_map/ppermute | solution.py:340
  6.0 3.8 %collective-permute-start.2 = (bf16[32,128]{1,0:T(8,128)(2,1)S(1)}, bf16[32,128]{1,0:T(8,128)(2,1)S(1)}, u32[]{:S(2)}, u32[]{:S(2)}) collective-permute-start(bf16[32,128]{1,0:T(8,128)(2,1)S(1)} %get-tuple-element.17), channel_id=1, source_target_pairs={{0,2},{1,3},{2,0},{3,1},{4,6},{5,7},{6,4},{7,5},{8,10},{9,11},{10,... | collective-permute-start | bytes 24584 | tf_op jit(solution)/shard_map/ppermute | solution.py:340
  6.0 7.8 %collective-permute-start.7 = (bf16[9,20,80]{2,1,0:T(8,128)(2,1)S(1)}, bf16[9,20,80]{2,1,0:T(8,128)(2,1)S(1)}, u32[]{:S(2)}, u32[]{:S(2)}) collective-permute-start(bf16[9,20,80]{2,1,0:T(8,128)(2,1)S(1)} %bitcast.5), channel_id=1, source_target_pairs={{0,1},{1,0},{2,3},{3,2},{4,5},{5,4},{6,7},{7,6},{8,9},{9,8},{10,11... | collective-permute-start | bytes 86408 | tf_op jit(solution)/shard_map/ppermute | solution.py:344
  9.8 4.0 %collective-permute-start.5 = (bf16[4,32,128]{2,1,0:T(8,128)(2,1)S(1)}, bf16[4,32,128]{2,1,0:T(8,128)(2,1)S(1)}, u32[]{:S(2)}, u32[]{:S(2)}) collective-permute-start(bf16[4,32,128]{2,1,0:T(8,128)(2,1)S(1)} %join_columns.1.own_ref), channel_id=1, source_target_pairs={{0,1},{1,0},{2,3},{3,2},{4,5},{5,4},{6,7},{7,6},{8,9},{9,8},{10,11... | collective-permute-start | bytes 98312 | tf_op jit(solution)/shard_map/ppermute | solution.py:353
  11.5 3.9 %collective-permute-start.3 = (bf16[4,32,128]{2,1,0:T(8,128)(2,1)S(1)}, bf16[4,32,128]{2,1,0:T(8,128)(2,1)S(1)}, u32[]{:S(2)}, u32[]{:S(2)}) collective-permute-start(bf16[4,32,128]{2,1,0:T(8,128)(2,1)S(1)} %join_columns.1.own_ref), channel_id=1, source_target_pairs={{0,1},{1,0},{2,3},{3,2},{4,5},{5,4},{6,7},{7,6},{8,17},{9,16},{10,... | collective-permute-start | bytes 98312 | tf_op jit(solution)/shard_map/ppermute | solution.py:353
  12.0 4.1 %collective-permute-start.4 = (bf16[4,32,128]{2,1,0:T(8,128)(2,1)S(1)}, bf16[4,32,128]{2,1,0:T(8,128)(2,1)S(1)}, u32[]{:S(2)}, u32[]{:S(2)}) collective-permute-start(bf16[4,32,128]{2,1,0:T(8,128)(2,1)S(1)} %join_columns.1.own_ref), channel_id=1, source_target_pairs={{0,1},{1,0},{2,3},{3,2},{4,5},{5,4},{6,7},{7,6},{8,16},{9,17},{10,... | collective-permute-start | bytes 98312 | tf_op jit(solution)/shard_map/ppermute | solution.py:353
  13.8 2.3 %collective-permute-start.6 = (bf16[4,2,32,128]{3,2,1,0:T(8,128)(2,1)S(1)}, bf16[4,2,32,128]{3,2,1,0:T(8,128)(2,1)S(1)}, u32[]{:S(2)}, u32[]{:S(2)}) collective-permute-start(bf16[4,2,32,128]{3,2,1,0:T(8,128)(2,1)S(1)} %join_sides.1), channel_id=1, source_target_pairs={{0,8},{1,9},{2,10},{3,11},{4,12},{5,13},{6,14},{7,15},{8,0},{9,1},... | collective-permute-start | bytes 196616 | tf_op jit(solution)/shard_map/ppermute | solution.py:353
  16.9 5.5 %collective-permute-start.10 = (bf16[32,128]{1,0:T(8,128)(2,1)S(1)}, bf16[32,128]{1,0:T(8,128)(2,1)S(1)}, u32[]{:S(2)}, u32[]{:S(2)}) collective-permute-start(bf16[32,128]{1,0:T(8,128)(2,1)S(1)} %get-tuple-element.23), channel_id=1, source_target_pairs={{0,6},{1,7},{2,4},{3,5},{4,2},{5,3},{6,0},{7,1},{8,14},{9,15},{10,... | collective-permute-start | bytes 24584 | tf_op jit(solution)/shard_map/ppermute | solution.py:340
  18.9 4.5 %collective-permute-start.8 = (bf16[32,128]{1,0:T(8,128)(2,1)S(1)}, bf16[32,128]{1,0:T(8,128)(2,1)S(1)}, u32[]{:S(2)}, u32[]{:S(2)}) collective-permute-start(bf16[32,128]{1,0:T(8,128)(2,1)S(1)} %get-tuple-element.21), channel_id=1, source_target_pairs={{0,4},{1,5},{2,6},{3,7},{4,0},{5,1},{6,2},{7,3},{8,12},{9,13},{10,... | collective-permute-start | bytes 24584 | tf_op jit(solution)/shard_map/ppermute | solution.py:340
  18.9 4.5 %collective-permute-start.9 = (bf16[32,128]{1,0:T(8,128)(2,1)S(1)}, bf16[32,128]{1,0:T(8,128)(2,1)S(1)}, u32[]{:S(2)}, u32[]{:S(2)}) collective-permute-start(bf16[32,128]{1,0:T(8,128)(2,1)S(1)} %get-tuple-element.22), channel_id=1, source_target_pairs={{0,2},{1,3},{2,0},{3,1},{4,6},{5,7},{6,4},{7,5},{8,10},{9,11},{10,... | collective-permute-start | bytes 24584 | tf_op jit(solution)/shard_map/ppermute | solution.py:340
  21.4 2.1 %copy-start.2 = (bf16[640,1280]{1,0:T(8,128)(2,1)S(1)}, bf16[640,1280]{1,0:T(8,128)(2,1)}, u32[]{:S(2)}) copy-start(bf16[640,1280]{1,0:T(8,128)(2,1)} %refs_4_.1) | copy-start | bytes 4915204
  21.4 2.1 %copy-start.3 = (bf16[1280,640]{1,0:T(8,128)(2,1)S(1)}, bf16[1280,640]{1,0:T(8,128)(2,1)}, u32[]{:S(2)}) copy-start(bf16[1280,640]{1,0:T(8,128)(2,1)} %refs_5_.1) | copy-start | bytes 4915204

commit v7 on v6

--- a/solution.py
+++ b/solution.py
@@ -269,43 +269,67 @@
         out_refs[apart][...] = stage[column ^ apart]
 
 
-def placed(message, column, chans, block):
-    lanes = lanes_of(block)
-    kept = lax.broadcasted_iota(jnp.int32, (3 * SUBLANES, lanes), 1) < block
-    piece = jnp.concatenate(unfold(message.astype(F32), block), axis=0)
-    piece = jnp.where(kept, piece, 0.0)
-    if chans > lanes:
-        gap = jnp.zeros((3 * SUBLANES, chans - lanes), F32)
+def summed_block(latent_block, message, block):
+    convolved = jnp.concatenate(unfold(message.astype(F32), block), axis=0)
+    kept = lax.broadcasted_iota(jnp.int32, convolved.shape, 1) < block
+    return jnp.where(kept, latent_block + convolved, 0.0).astype(BF16)
+
+
+def raised_block(summed, column, block, up_ref):
+    count = summed.shape[0]
+    ones = jnp.ones((up_to(count, 2 * SUBLANES) - count, block), BF16)
+    rows = pl.multiple_of(column * block, block)
+    return jnp.dot(
+        jnp.concatenate([summed[:, :block], ones], axis=0),
+        up_ref[pl.ds(rows, block), :],
+        preferred_element_type=F32,
+    )
+
+
+def placed(summed, column, chans, block):
+    piece = summed.astype(F32)
+    if chans > piece.shape[1]:
+        gap = jnp.zeros((piece.shape[0], chans - piece.shape[1]), F32)
         piece = jnp.concatenate([piece, gap], axis=1)
     return pltpu.roll(piece, column * block, 1)
 
 
-def residual_kernel(columns, own_ref, latent_ref, out_ref, points):
+def lift_kernel(
+    apart, own_ref, first_ref, latent_ref, up_ref, blocks_ref, summed_ref, raised_ref, points
+):
+    columns = blocks_ref.shape[0]
     chans = latent_ref.shape[2]
+    block = chans // columns
     column, _ = column_and_side()
     group_points(latent_ref, points)
-    out_ref[...] = points[...] + placed(own_ref[...], column, chans, chans // columns)
+    own = points[...]
+    for target in range(columns):
+        turned = pltpu.roll(own, chans - target * block, 1) if target else own
+        blocks_ref[target] = turned[:, : lanes_of(block)]
+    other = column ^ apart
+    here = summed_block(blocks_ref[column], own_ref[...], block)
+    there = summed_block(blocks_ref[other], first_ref[...], block)
+    summed_ref[...] = placed(here, column, chans, block) + placed(there, other, chans, block)
+    raised_ref[...] = raised_block(here, column, block, up_ref) + raised_block(
+        there, other, block, up_ref
+    )
 
 
 def tail_kernel(order, *refs):
-    columns = len(order) + 1
-    back_refs = refs[: columns - 1]
-    residual_ref, up_ref, down_ref, out_ref = refs[columns - 1 :]
+    back_refs = refs[: len(order)]
+    blocks_ref, summed_ref, raised_ref, up_ref, down_ref, out_ref = refs[len(order) :]
     width, rows, chans = out_ref.shape
     rest = width - SUBLANES
+    block = chans // blocks_ref.shape[0]
     column, _ = column_and_side()
-    convolved = residual_ref[...]
+    summed = summed_ref[...]
+    raised = raised_ref[...]
     for apart, ref in zip(order, back_refs):
-        convolved = convolved + placed(ref[...], column ^ apart, chans, chans // columns)
-    summed = convolved.astype(BF16)
-    ones = jnp.ones((2 * SUBLANES, chans), BF16)
+        other = column ^ apart
+        there = summed_block(blocks_ref[other], ref[...], block)
+        raised = raised + raised_block(there, other, block, up_ref)
+        summed = summed + placed(there, other, chans, block)
     count = summed.shape[0]
-    raised = jnp.dot(
-        jnp.concatenate([summed, ones[: up_to(count, 2 * SUBLANES) - count]], axis=0),
-        up_ref[...],
-        preferred_element_type=F32,
-    )
-    summed = summed.astype(F32)
     mean = jnp.mean(summed, axis=1, keepdims=True)
     centred = summed - mean
     scale = lax.rsqrt(jnp.mean(centred * centred, axis=1, keepdims=True) + 1e-05)
@@ -479,23 +503,31 @@
     )
     outward = far_first[1:-1] + far_first[:1]
     back = [over_columns(mixed[apart], count, apart) for apart in outward]
-    residual = call(
-        functools.partial(residual_kernel, columns),
-        "residual",
-        jax.ShapeDtypeStruct((3 * SUBLANES, chans), F32),
+    first = outward.index(far_first[0])
+    lifted = call(
+        functools.partial(lift_kernel, far_first[0]),
+        "lift",
+        (
+            jax.ShapeDtypeStruct((columns, 3 * SUBLANES, lanes), F32),
+            jax.ShapeDtypeStruct((3 * SUBLANES, chans), F32),
+            jax.ShapeDtypeStruct((up_to(3 * SUBLANES, 2 * SUBLANES), w_up.shape[1]), F32),
+        ),
         [points],
-        10**9,
+        10**8,
         mixed[0],
+        back[first],
         lon_first,
+        w_up,
     )
     result = call(
-        functools.partial(tail_kernel, outward),
+        functools.partial(tail_kernel, outward[:first] + outward[first + 1 :]),
         "tail",
         jax.ShapeDtypeStruct(lon_first.shape, BF16),
         [],
         10**9,
-        *back,
-        residual,
+        *back[:first],
+        *back[first + 1 :],
+        *lifted,
         w_up,
         w_down,
     )

time: 25.1 us -> 25.1 us (level)
  no operation moved by 1% of the time
where the time goes in v7:
time: 25.1 us; the launch traced here: 24.9 us
  starting transfers between devices  15.4 us (61%)
  waiting for transfers between devices  5.05 us (20%)
  Pallas kernels  4.33 us (17%)
    ppermute x6, starting transfers between devices, over_columns(): return lax.ppermute(message, 'lon', pairs) if apart else message  10.2 us
    pallas_call x12, Pallas kernels, call(): pl.pallas_call(kernel, out_shape=out_shape, in_specs=[VMEM] * len(operand...  4.33 us
    ppermute x4, starting transfers between devices, swap(): return lax.ppermute(block, ('lat', 'lon'), pairs)  3.66 us
    ppermute x6, waiting for transfers between devices, over_columns(): return lax.ppermute(message, 'lon', pairs) if apart else message  3.44 us
    ppermute x4, waiting for transfers between devices, swap(): return lax.ppermute(block, ('lat', 'lon'), pairs)  1.6 us
    ppermute x1, starting transfers between devices, over_sides(): return lax.ppermute(block, 'lon', [(i, i ^ 1) for i in range(count)])  1.49 us
  transfers between devices with their start and end apart: 11, of which 6 were waited for; matrix products, arithmetic and copies ran while one was open for 0% of the time, Pallas kernels for 8%

profile of v7, /device:TPU:0, one launch (start us, length us, event | category | flops | bytes accessed | tf_op | source)
XLA Modules:
  0.0 24.9 jit_solution(12957257759074690894)
XLA Ops:
  0.0 0.0 copy-start.1
  0.0 4.0 %collective-permute-start = (bf16[12,2,640]{2,1,0:T(2,128)(2,1)}, bf16[12,2,640]{2,1,0:T(2,128)(2,1)S(1)}, u32[]{:S(2)}, u32[]{:S(2)}) collective-permute-start(bf16[12,2,640]{2,1,0:T(2,128)(2,1)} %bitcast.4), channel_id=1, source_target_pairs={{0,4},{1,5},{2,6},{3,7},{4,0},{5,1},{6,2},{7,3},{8,12},{9,13},{10,... | collective-permute-start | bytes 92168 | tf_op jit(solution)/shard_map/ppermute | solution.py:364
  4.1 0.0 copy-done.1
  4.1 0.0 copy-start.5
  4.1 0.0 copy-start.2
  4.1 0.0 copy-start.3
  4.1 0.2 pack.1
  4.3 1.7 %collective-permute-start.1 = (bf16[32,128]{1,0:T(8,128)(2,1)S(1)}, bf16[32,128]{1,0:T(8,128)(2,1)S(1)}, u32[]{:S(2)}, u32[]{:S(2)}) collective-permute-start(bf16[32,128]{1,0:T(8,128)(2,1)S(1)} %get-tuple-element.19), channel_id=1, source_target_pairs={{0,6},{1,7},{2,4},{3,5},{4,2},{5,3},{6,0},{7,1},{8,14},{9,15},{10,... | collective-permute-start | bytes 24584 | tf_op jit(solution)/shard_map/ppermute | solution.py:364
  6.0 0.0 collective-permute-start.2
  6.0 0.0 copy-done.5
  6.0 1.5 %collective-permute-start.7 = (bf16[9,20,80]{2,1,0:T(8,128)(2,1)S(1)}, bf16[9,20,80]{2,1,0:T(8,128)(2,1)S(1)}, u32[]{:S(2)}, u32[]{:S(2)}) collective-permute-start(bf16[9,20,80]{2,1,0:T(8,128)(2,1)S(1)} %bitcast.8), channel_id=1, source_target_pairs={{0,1},{1,0},{2,3},{3,2},{4,5},{5,4},{6,7},{7,6},{8,9},{9,8},{10,11... | collective-permute-start | bytes 86408 | tf_op jit(solution)/shard_map/ppermute | solution.py:368
  7.5 0.0 copy-done.2
  7.5 0.0 copy-done.3
  7.5 0.4 %tables.1.table_ref = bf16[2,432,384]{2,1,0:T(8,128)(2,1)S(1)} custom-call(bf16[9,96]{1,0:T(8,128)(2,1)S(1)} %copy-done.2, bf16[3,2,9]{2,1,0:T(2,128)(2,1)S(1)} %bitcast.7, s32[96,128]{1,0:T(8,128)S(1)} %apart.1.apart_ref), custom_call_target="tpu_custom_call" | custom-call | flops 1000000 | bytes 1000000 | tf_op jit(solution)/shard_map/tables/pallas_call | solution.py:350
  7.9 0.0 collective-permute-done.raw_ref
  7.9 0.2 cut.1.refs_0_
  8.1 1.7 %collective-permute-done.1.refs_1_ = bf16[32,128]{1,0:T(8,128)(2,1)S(1)} collective-permute-done((bf16[32,128]{1,0:T(8,128)(2,1)S(1)}, bf16[32,128]{1,0:T(8,128)(2,1)S(1)}, u32[]{:S(2)}, u32[]{:S(2)}) %collective-permute-start.1) | collective-permute-done | bytes 8224 | tf_op jit(solution)/shard_map/ppermute | solution.py:364
  9.8 0.0 collective-permute-done.2.refs_2_
  9.8 1.6 %collective-permute-start.5 = (bf16[4,32,128]{2,1,0:T(8,128)(2,1)S(1)}, bf16[4,32,128]{2,1,0:T(8,128)(2,1)S(1)}, u32[]{:S(2)}, u32[]{:S(2)}) collective-permute-start(bf16[4,32,128]{2,1,0:T(8,128)(2,1)S(1)} %join_columns.1.own_ref), channel_id=1, source_target_pairs={{0,1},{1,0},{2,3},{3,2},{4,5},{5,4},{6,7},{7,6},{8,9},{9,8},{10,11... | collective-permute-start | bytes 98312 | tf_op jit(solution)/shard_map/ppermute | solution.py:377
  11.4 0.1 unpack.1.own
  11.5 0.5 %collective-permute-start.3 = (bf16[4,32,128]{2,1,0:T(8,128)(2,1)S(1)}, bf16[4,32,128]{2,1,0:T(8,128)(2,1)S(1)}, u32[]{:S(2)}, u32[]{:S(2)}) collective-permute-start(bf16[4,32,128]{2,1,0:T(8,128)(2,1)S(1)} %join_columns.1.own_ref), channel_id=1, source_target_pairs={{0,1},{1,0},{2,3},{3,2},{4,5},{5,4},{6,7},{7,6},{8,17},{9,16},{10,... | collective-permute-start | bytes 98312 | tf_op jit(solution)/shard_map/ppermute | solution.py:377
  12.0 1.5 %collective-permute-start.4 = (bf16[4,32,128]{2,1,0:T(8,128)(2,1)S(1)}, bf16[4,32,128]{2,1,0:T(8,128)(2,1)S(1)}, u32[]{:S(2)}, u32[]{:S(2)}) collective-permute-start(bf16[4,32,128]{2,1,0:T(8,128)(2,1)S(1)} %join_columns.1.own_ref), channel_id=1, source_target_pairs={{0,1},{1,0},{2,3},{3,2},{4,5},{5,4},{6,7},{7,6},{8,16},{9,17},{10,... | collective-permute-start | bytes 98312 | tf_op jit(solution)/shard_map/ppermute | solution.py:377
  13.5 0.3 %collective-permute-done.5.mate_ref.mate = bf16[4,32,128]{2,1,0:T(8,128)(2,1)S(1)} collective-permute-done((bf16[4,32,128]{2,1,0:T(8,128)(2,1)S(1)}, bf16[4,32,128]{2,1,0:T(8,128)(2,1)S(1)}, u32[]{:S(2)}, u32[]{:S(2)}) %collective-permute-start.5) | collective-permute-done | bytes 32800 | tf_op jit(solution)/shard_map/ppermute | solution.py:377
  13.8 0.1 collective-permute-start.6
  13.9 0.0 collective-permute-done.7.mate_ref
  13.9 0.5 %squares.1.squares_ref = bf16[2304,256]{1,0:T(8,128)(2,1)S(1)} custom-call(bf16[9,20,80]{2,1,0:T(8,128)(2,1)S(1)} %bitcast.9, bf16[9,20,80]{2,1,0:T(8,128)(2,1)S(1)} %collective-permute-done.7.mate_ref), custom_call_target="tpu_custom_call" | custom-call | flops 1000000000 | bytes 1000000 | tf_op jit(solution)/shard_map/squares/pallas_call | solution.py:350
  14.5 0.3 %conv_own.1.part_ref = f32[2,432,256]{2,1,0:T(8,128)S(1)} custom-call(bf16[4,32,128]{2,1,0:T(8,128)(2,1)S(1)} %collective-permute-done.5.mate_ref.mate, bf16[2,4,16,256]{3,2,1,0:T(8,128)(2,1)S(1)} %unpack.1.own, bf16[2,432,384]{2,1,0:T(8,128)(2,1)S(1)} %tables.1.table_ref), custom_call_target="tpu_custom_call" | custom-call | flops 1000000000 | bytes 1000000 | tf_op jit(solution)/shard_map/conv_own/pallas_call | solution.py:350
  14.8 0.0 copy-start
  14.8 0.6 %collective-permute-done.3.odd_mate = bf16[4,32,128]{2,1,0:T(8,128)(2,1)S(1)} collective-permute-done((bf16[4,32,128]{2,1,0:T(8,128)(2,1)S(1)}, bf16[4,32,128]{2,1,0:T(8,128)(2,1)S(1)}, u32[]{:S(2)}, u32[]{:S(2)}) %collective-permute-start.3) | collective-permute-done | bytes 32800 | tf_op jit(solution)/shard_map/ppermute | solution.py:377
  15.4 0.7 %collective-permute-done.4.odd_own = bf16[4,32,128]{2,1,0:T(8,128)(2,1)S(1)} collective-permute-done((bf16[4,32,128]{2,1,0:T(8,128)(2,1)S(1)}, bf16[4,32,128]{2,1,0:T(8,128)(2,1)S(1)}, u32[]{:S(2)}, u32[]{:S(2)}) %collective-permute-start.4) | collective-permute-done | bytes 32800 | tf_op jit(solution)/shard_map/ppermute | solution.py:377
  16.1 0.0 collective-permute-done.6.even
  16.1 0.8 %conv.1 = (bf16[32,128]{1,0:T(8,128)(2,1)S(1)}, bf16[32,128]{1,0:T(8,128)(2,1)S(1)}, bf16[32,128]{1,0:T(8,128)(2,1)S(1)}, bf16[32,128]{1,0:T(8,128)(2,1)S(1)}) custom-call(bf16[4,32,128]{2,1,0:T(8,128)(2,1)S(1)} %collective-permute-done.3.odd_mate, bf16[4,32,128]{2,1,0:T(8,128)(2,1)S(1)} %collective-permute-done.4.odd_own, ...), custom_call_target="tpu_custom_call" | custom-call | flops 10000000000 | bytes 1000000 | tf_op jit(solution)/shard_map/conv/pallas_call | solution.py:350
  16.9 0.0 copy-start.4
  16.9 2.0 %collective-permute-start.10 = (bf16[32,128]{1,0:T(8,128)(2,1)S(1)}, bf16[32,128]{1,0:T(8,128)(2,1)S(1)}, u32[]{:S(2)}, u32[]{:S(2)}) collective-permute-start(bf16[32,128]{1,0:T(8,128)(2,1)S(1)} %get-tuple-element.27), channel_id=1, source_target_pairs={{0,6},{1,7},{2,4},{3,5},{4,2},{5,3},{6,0},{7,1},{8,14},{9,15},{10,... | collective-permute-start | bytes 24584 | tf_op jit(solution)/shard_map/ppermute | solution.py:364
  19.0 0.0 collective-permute-start.8
  19.0 2.4 %collective-permute-start.9 = (bf16[32,128]{1,0:T(8,128)(2,1)S(1)}, bf16[32,128]{1,0:T(8,128)(2,1)S(1)}, u32[]{:S(2)}, u32[]{:S(2)}) collective-permute-start(bf16[32,128]{1,0:T(8,128)(2,1)S(1)} %get-tuple-element.25), channel_id=1, source_target_pairs={{0,2},{1,3},{2,0},{3,1},{4,6},{5,7},{6,4},{7,5},{8,10},{9,11},{10,... | collective-permute-start | bytes 24584 | tf_op jit(solution)/shard_map/ppermute | solution.py:364
  21.4 1.1 %collective-permute-done.10.first_ref = bf16[32,128]{1,0:T(8,128)(2,1)S(1)} collective-permute-done((bf16[32,128]{1,0:T(8,128)(2,1)S(1)}, bf16[32,128]{1,0:T(8,128)(2,1)S(1)}, u32[]{:S(2)}, u32[]{:S(2)}) %collective-permute-start.10) | collective-permute-done | bytes 8224 | tf_op jit(solution)/shard_map/ppermute | solution.py:364
  22.5 0.0 copy-done
  22.5 0.4 %lift.1 = (f32[4,24,256]{2,1,0:T(8,128)S(1)}, f32[24,640]{1,0:T(8,128)S(1)}, f32[32,1280]{1,0:T(8,128)S(1)}) custom-call(bf16[32,128]{1,0:T(8,128)(2,1)S(1)} %get-tuple-element.26.own_ref, bf16[32,128]{1,0:T(8,128)(2,1)S(1)} %collective-permute-done.10.first_ref, bf16[12,2,640]{2,1,0:T(2,128)(2,1)S(1)} %bitcast.6, bf16[640,1280]{1,0:T(8,128)(2,1)S(1)} %copy-done), custom_call_target="tpu_custom_call" | custom-call | flops 100000000 | bytes 1000000 | tf_op jit(solution)/shard_map/lift/pallas_call | solution.py:350
  22.8 0.7 %collective-permute-done.8.refs_0_ = bf16[32,128]{1,0:T(8,128)(2,1)S(1)} collective-permute-done((bf16[32,128]{1,0:T(8,128)(2,1)S(1)}, bf16[32,128]{1,0:T(8,128)(2,1)S(1)}, u32[]{:S(2)}, u32[]{:S(2)}) %collective-permute-start.8) | collective-permute-done | bytes 8224 | tf_op jit(solution)/shard_map/ppermute | solution.py:364
  23.5 0.0 collective-permute-done.9.refs_1_
  23.5 0.0 copy-done.4
  23.5 1.4 %tail.1 = bf16[12,2,640]{2,1,0:T(2,128)(2,1)} custom-call(bf16[32,128]{1,0:T(8,128)(2,1)S(1)} %collective-permute-done.8.refs_0_, bf16[32,128]{1,0:T(8,128)(2,1)S(1)} %collective-permute-done.9.refs_1_, f32[4,24,256]{2,1,0:T(8,128)S(1)} %get-tuple-element.28.refs_2_, f32[24,640]{1,0:T(8,128)S(1)} %get-tuple-element.29.refs_3_, ...), custom_call_target="tpu_custom_call" | custom-call | flops 1000000000 | bytes 1000000 | tf_op jit(solution)/shard_map/tail/pallas_call | solution.py:350
  (3 shorter events, 0.0 us)
Async XLA Ops:
  0.0 4.1 %copy-start.1 = (bf16[2,12,640]{2,0,1:T(2,128)(2,1)S(1)}, bf16[2,12,640]{2,0,1:T(2,128)(2,1)}, u32[]{:S(2)}) copy-start(bf16[2,12,640]{2,0,1:T(2,128)(2,1)} %param.7) | copy-start | bytes 92164
  0.0 7.9 %collective-permute-start = (bf16[12,2,640]{2,1,0:T(2,128)(2,1)}, bf16[12,2,640]{2,1,0:T(2,128)(2,1)S(1)}, u32[]{:S(2)}, u32[]{:S(2)}) collective-permute-start(bf16[12,2,640]{2,1,0:T(2,128)(2,1)} %bitcast.4), channel_id=1, source_target_pairs={{0,4},{1,5},{2,6},{3,7},{4,0},{5,1},{6,2},{7,3},{8,12},{9,13},{10,... | collective-permute-start | bytes 92168 | tf_op jit(solution)/shard_map/ppermute | solution.py:364
  4.1 2.0 %copy-start.5 = (bf16[9,80,20]{1,2,0:T(8,128)(2,1)S(1)}, bf16[9,80,20]{1,2,0:T(8,128)(2,1)}, u32[]{:S(2)}) copy-start(bf16[9,80,20]{1,2,0:T(8,128)(2,1)} %param.9) | copy-start | bytes 86404
  4.1 3.4 %copy-start.2 = (bf16[9,96]{1,0:T(8,128)(2,1)S(1)}, bf16[9,96]{1,0:T(8,128)(2,1)}, u32[]{:S(2)}) copy-start(bf16[9,96]{1,0:T(8,128)(2,1)} %filter_ref.1) | copy-start | bytes 5188
  4.1 3.4 %copy-start.3 = (bf16[9,2,3]{0,1,2:T(2,128)(2,1)S(1)}, bf16[9,2,3]{0,1,2:T(2,128)(2,1)}, u32[]{:S(2)}) copy-start(bf16[9,2,3]{0,1,2:T(2,128)(2,1)} %param.10) | copy-start | bytes 328
  4.3 5.5 %collective-permute-start.1 = (bf16[32,128]{1,0:T(8,128)(2,1)S(1)}, bf16[32,128]{1,0:T(8,128)(2,1)S(1)}, u32[]{:S(2)}, u32[]{:S(2)}) collective-permute-start(bf16[32,128]{1,0:T(8,128)(2,1)S(1)} %get-tuple-element.19), channel_id=1, source_target_pairs={{0,6},{1,7},{2,4},{3,5},{4,2},{5,3},{6,0},{7,1},{8,14},{9,15},{10,... | collective-permute-start | bytes 24584 | tf_op jit(solution)/shard_map/ppermute | solution.py:364
  6.0 3.8 %collective-permute-start.2 = (bf16[32,128]{1,0:T(8,128)(2,1)S(1)}, bf16[32,128]{1,0:T(8,128)(2,1)S(1)}, u32[]{:S(2)}, u32[]{:S(2)}) collective-permute-start(bf16[32,128]{1,0:T(8,128)(2,1)S(1)} %get-tuple-element.20), channel_id=1, source_target_pairs={{0,2},{1,3},{2,0},{3,1},{4,6},{5,7},{6,4},{7,5},{8,10},{9,11},{10,... | collective-permute-start | bytes 24584 | tf_op jit(solution)/shard_map/ppermute | solution.py:364
  6.0 7.8 %collective-permute-start.7 = (bf16[9,20,80]{2,1,0:T(8,128)(2,1)S(1)}, bf16[9,20,80]{2,1,0:T(8,128)(2,1)S(1)}, u32[]{:S(2)}, u32[]{:S(2)}) collective-permute-start(bf16[9,20,80]{2,1,0:T(8,128)(2,1)S(1)} %bitcast.8), channel_id=1, source_target_pairs={{0,1},{1,0},{2,3},{3,2},{4,5},{5,4},{6,7},{7,6},{8,9},{9,8},{10,11... | collective-permute-start | bytes 86408 | tf_op jit(solution)/shard_map/ppermute | solution.py:368
  9.8 4.0 %collective-permute-start.5 = (bf16[4,32,128]{2,1,0:T(8,128)(2,1)S(1)}, bf16[4,32,128]{2,1,0:T(8,128)(2,1)S(1)}, u32[]{:S(2)}, u32[]{:S(2)}) collective-permute-start(bf16[4,32,128]{2,1,0:T(8,128)(2,1)S(1)} %join_columns.1.own_ref), channel_id=1, source_target_pairs={{0,1},{1,0},{2,3},{3,2},{4,5},{5,4},{6,7},{7,6},{8,9},{9,8},{10,11... | collective-permute-start | bytes 98312 | tf_op jit(solution)/shard_map/ppermute | solution.py:377
  11.5 3.9 %collective-permute-start.3 = (bf16[4,32,128]{2,1,0:T(8,128)(2,1)S(1)}, bf16[4,32,128]{2,1,0:T(8,128)(2,1)S(1)}, u32[]{:S(2)}, u32[]{:S(2)}) collective-permute-start(bf16[4,32,128]{2,1,0:T(8,128)(2,1)S(1)} %join_columns.1.own_ref), channel_id=1, source_target_pairs={{0,1},{1,0},{2,3},{3,2},{4,5},{5,4},{6,7},{7,6},{8,17},{9,16},{10,... | collective-permute-start | bytes 98312 | tf_op jit(solution)/shard_map/ppermute | solution.py:377
  12.0 4.1 %collective-permute-start.4 = (bf16[4,32,128]{2,1,0:T(8,128)(2,1)S(1)}, bf16[4,32,128]{2,1,0:T(8,128)(2,1)S(1)}, u32[]{:S(2)}, u32[]{:S(2)}) collective-permute-start(bf16[4,32,128]{2,1,0:T(8,128)(2,1)S(1)} %join_columns.1.own_ref), channel_id=1, source_target_pairs={{0,1},{1,0},{2,3},{3,2},{4,5},{5,4},{6,7},{7,6},{8,16},{9,17},{10,... | collective-permute-start | bytes 98312 | tf_op jit(solution)/shard_map/ppermute | solution.py:377
  13.8 2.3 %collective-permute-start.6 = (bf16[4,2,32,128]{3,2,1,0:T(8,128)(2,1)S(1)}, bf16[4,2,32,128]{3,2,1,0:T(8,128)(2,1)S(1)}, u32[]{:S(2)}, u32[]{:S(2)}) collective-permute-start(bf16[4,2,32,128]{3,2,1,0:T(8,128)(2,1)S(1)} %join_sides.1), channel_id=1, source_target_pairs={{0,8},{1,9},{2,10},{3,11},{4,12},{5,13},{6,14},{7,15},{8,0},{9,1},... | collective-permute-start | bytes 196616 | tf_op jit(solution)/shard_map/ppermute | solution.py:377
  14.8 7.7 %copy-start = (bf16[640,1280]{1,0:T(8,128)(2,1)S(1)}, bf16[640,1280]{1,0:T(8,128)(2,1)}, u32[]{:S(2)}) copy-start(bf16[640,1280]{1,0:T(8,128)(2,1)} %refs_5_.1) | copy-start | bytes 4915204
  16.9 6.6 %copy-start.4 = (bf16[1280,640]{1,0:T(8,128)(2,1)S(1)}, bf16[1280,640]{1,0:T(8,128)(2,1)}, u32[]{:S(2)}) copy-start(bf16[1280,640]{1,0:T(8,128)(2,1)} %refs_6_.1) | copy-start | bytes 4915204
  16.9 5.5 %collective-permute-start.10 = (bf16[32,128]{1,0:T(8,128)(2,1)S(1)}, bf16[32,128]{1,0:T(8,128)(2,1)S(1)}, u32[]{:S(2)}, u32[]{:S(2)}) collective-permute-start(bf16[32,128]{1,0:T(8,128)(2,1)S(1)} %get-tuple-element.27), channel_id=1, source_target_pairs={{0,6},{1,7},{2,4},{3,5},{4,2},{5,3},{6,0},{7,1},{8,14},{9,15},{10,... | collective-permute-start | bytes 24584 | tf_op jit(solution)/shard_map/ppermute | solution.py:364
  19.0 4.5 %collective-permute-start.8 = (bf16[32,128]{1,0:T(8,128)(2,1)S(1)}, bf16[32,128]{1,0:T(8,128)(2,1)S(1)}, u32[]{:S(2)}, u32[]{:S(2)}) collective-permute-start(bf16[32,128]{1,0:T(8,128)(2,1)S(1)} %get-tuple-element.24), channel_id=1, source_target_pairs={{0,4},{1,5},{2,6},{3,7},{4,0},{5,1},{6,2},{7,3},{8,12},{9,13},{10,... | collective-permute-start | bytes 24584 | tf_op jit(solution)/shard_map/ppermute | solution.py:364
  19.0 4.5 %collective-permute-start.9 = (bf16[32,128]{1,0:T(8,128)(2,1)S(1)}, bf16[32,128]{1,0:T(8,128)(2,1)S(1)}, u32[]{:S(2)}, u32[]{:S(2)}) collective-permute-start(bf16[32,128]{1,0:T(8,128)(2,1)S(1)} %get-tuple-element.25), channel_id=1, source_target_pairs={{0,2},{1,3},{2,0},{3,1},{4,6},{5,7},{6,4},{7,5},{8,10},{9,11},{10,... | collective-permute-start | bytes 24584 | tf_op jit(solution)/shard_map/ppermute | solution.py:364

commit v8 on v7

--- a/solution.py
+++ b/solution.py
@@ -294,8 +294,26 @@
     return pltpu.roll(piece, column * block, 1)
 
 
+def deviations(summed, mean, block):
+    kept = lax.broadcasted_iota(jnp.int32, summed.shape, 1) < block
+    return jnp.where(kept, summed.astype(F32) - mean, 0.0)
+
+
+def over_lanes(values):
+    return jnp.sum(values, axis=1, keepdims=True)
+
+
 def lift_kernel(
-    apart, own_ref, first_ref, latent_ref, up_ref, blocks_ref, summed_ref, raised_ref, points
+    apart,
+    own_ref,
+    first_ref,
+    latent_ref,
+    up_ref,
+    blocks_ref,
+    summed_ref,
+    raised_ref,
+    stats_ref,
+    points,
 ):
     columns = blocks_ref.shape[0]
     chans = latent_ref.shape[2]
@@ -313,28 +331,41 @@
     raised_ref[...] = raised_block(here, column, block, up_ref) + raised_block(
         there, other, block, up_ref
     )
+    mean = over_lanes(here.astype(F32) + there.astype(F32)) / (2 * block)
+    squares = sum(deviations(summed, mean, block) ** 2 for summed in (here, there))
+    stats_ref[0] = jnp.broadcast_to(mean, stats_ref.shape[1:])
+    stats_ref[1] = jnp.broadcast_to(over_lanes(squares), stats_ref.shape[1:])
 
 
 def tail_kernel(order, *refs):
     back_refs = refs[: len(order)]
-    blocks_ref, summed_ref, raised_ref, up_ref, down_ref, out_ref = refs[len(order) :]
+    blocks_ref, summed_ref, raised_ref, stats_ref, up_ref, down_ref, out_ref = refs[len(order) :]
     width, rows, chans = out_ref.shape
     rest = width - SUBLANES
     block = chans // blocks_ref.shape[0]
     column, _ = column_and_side()
-    summed = summed_ref[...]
     raised = raised_ref[...]
+    early_mean, early_squares = stats_ref[0, :, :1], stats_ref[1, :, :1]
+    theirs = []
+    away = squares = None
     for apart, ref in zip(order, back_refs):
         other = column ^ apart
         there = summed_block(blocks_ref[other], ref[...], block)
+        theirs.append((there, other))
         raised = raised + raised_block(there, other, block, up_ref)
-        summed = summed + placed(there, other, chans, block)
-    count = summed.shape[0]
-    mean = jnp.mean(summed, axis=1, keepdims=True)
-    centred = summed - mean
-    scale = lax.rsqrt(jnp.mean(centred * centred, axis=1, keepdims=True) + 1e-05)
+        apart_from = deviations(there, early_mean, block)
+        away = apart_from if away is None else away + apart_from
+        squares = apart_from**2 if squares is None else squares + apart_from**2
+    away, squares = over_lanes(away), over_lanes(squares)
+    mean = early_mean + away / chans
+    variance = (early_squares + squares - away * away / chans) / chans
+    scale = lax.rsqrt(variance + 1e-05)
+    count = summed_ref.shape[0]
     hidden = scale * (raised[:count] - mean * raised[count : count + 1])
     hidden = (0.5 * hidden * (1.0 + lax.erf(hidden * 0.5**0.5))).astype(BF16)
+    summed = summed_ref[...]
+    for there, other in theirs:
+        summed = summed + placed(there, other, chans, block)
     result = summed + jnp.dot(hidden, down_ref[...], preferred_element_type=F32)
     for row in range(rows):
         out_ref[:SUBLANES, row, :] = result[row * SUBLANES : (row + 1) * SUBLANES].astype(BF16)
@@ -511,6 +542,7 @@
             jax.ShapeDtypeStruct((columns, 3 * SUBLANES, lanes), F32),
             jax.ShapeDtypeStruct((3 * SUBLANES, chans), F32),
             jax.ShapeDtypeStruct((up_to(3 * SUBLANES, 2 * SUBLANES), w_up.shape[1]), F32),
+            jax.ShapeDtypeStruct((2, 3 * SUBLANES, LANES), F32),
         ),
         [points],
         10**8,

time: 25.1 us -> 25 us (level)
  no operation moved by 1% of the time
where the time goes in v8:
time: 25 us; the launch traced here: 24.9 us
  starting transfers between devices  15.4 us (62%)
  waiting for transfers between devices  5.05 us (20%)
  Pallas kernels  4.27 us (17%)
    ppermute x6, starting transfers between devices, over_columns(): return lax.ppermute(message, 'lon', pairs) if apart else message  10.2 us
    pallas_call x12, Pallas kernels, call(): pl.pallas_call(kernel, out_shape=out_shape, in_specs=[VMEM] * len(operand...  4.27 us
    ppermute x4, starting transfers between devices, swap(): return lax.ppermute(block, ('lat', 'lon'), pairs)  3.66 us
    ppermute x6, waiting for transfers between devices, over_columns(): return lax.ppermute(message, 'lon', pairs) if apart else message  3.44 us
    ppermute x4, waiting for transfers between devices, swap(): return lax.ppermute(block, ('lat', 'lon'), pairs)  1.6 us
    ppermute x1, starting transfers between devices, over_sides(): return lax.ppermute(block, 'lon', [(i, i ^ 1) for i in range(count)])  1.49 us
  transfers between devices with their start and end apart: 11, of which 6 were waited for; matrix products, arithmetic and copies ran while one was open for 0% of the time, Pallas kernels for 8%

profile of v8, /device:TPU:0, one launch (start us, length us, event | category | flops | bytes accessed | tf_op | source)
XLA Modules:
  0.0 24.9 jit_solution(3057863788910129231)
XLA Ops:
  0.0 0.0 copy-start.1
  0.0 4.0 %collective-permute-start = (bf16[12,2,640]{2,1,0:T(2,128)(2,1)}, bf16[12,2,640]{2,1,0:T(2,128)(2,1)S(1)}, u32[]{:S(2)}, u32[]{:S(2)}) collective-permute-start(bf16[12,2,640]{2,1,0:T(2,128)(2,1)} %bitcast.4), channel_id=1, source_target_pairs={{0,4},{1,5},{2,6},{3,7},{4,0},{5,1},{6,2},{7,3},{8,12},{9,13},{10,... | collective-permute-start | bytes 92168 | tf_op jit(solution)/shard_map/ppermute | solution.py:395
  4.1 0.0 copy-done.1
  4.1 0.0 copy-start.5
  4.1 0.0 copy-start.2
  4.1 0.0 copy-start.3
  4.1 0.2 pack.1
  4.3 1.7 %collective-permute-start.1 = (bf16[32,128]{1,0:T(8,128)(2,1)S(1)}, bf16[32,128]{1,0:T(8,128)(2,1)S(1)}, u32[]{:S(2)}, u32[]{:S(2)}) collective-permute-start(bf16[32,128]{1,0:T(8,128)(2,1)S(1)} %get-tuple-element.20), channel_id=1, source_target_pairs={{0,6},{1,7},{2,4},{3,5},{4,2},{5,3},{6,0},{7,1},{8,14},{9,15},{10,... | collective-permute-start | bytes 24584 | tf_op jit(solution)/shard_map/ppermute | solution.py:395
  6.0 0.0 collective-permute-start.2
  6.0 0.0 copy-done.5
  6.0 1.5 %collective-permute-start.7 = (bf16[9,20,80]{2,1,0:T(8,128)(2,1)S(1)}, bf16[9,20,80]{2,1,0:T(8,128)(2,1)S(1)}, u32[]{:S(2)}, u32[]{:S(2)}) collective-permute-start(bf16[9,20,80]{2,1,0:T(8,128)(2,1)S(1)} %bitcast.8), channel_id=1, source_target_pairs={{0,1},{1,0},{2,3},{3,2},{4,5},{5,4},{6,7},{7,6},{8,9},{9,8},{10,11... | collective-permute-start | bytes 86408 | tf_op jit(solution)/shard_map/ppermute | solution.py:399
  7.5 0.0 copy-done.2
  7.5 0.0 copy-done.3
  7.5 0.4 %tables.1.table_ref = bf16[2,432,384]{2,1,0:T(8,128)(2,1)S(1)} custom-call(bf16[9,96]{1,0:T(8,128)(2,1)S(1)} %copy-done.2, bf16[3,2,9]{2,1,0:T(2,128)(2,1)S(1)} %bitcast.7, s32[96,128]{1,0:T(8,128)S(1)} %apart.1.apart_ref), custom_call_target="tpu_custom_call" | custom-call | flops 1000000 | bytes 1000000 | tf_op jit(solution)/shard_map/tables/pallas_call | solution.py:381
  7.9 0.0 collective-permute-done.raw_ref
  7.9 0.2 cut.1.refs_0_
  8.1 1.7 %collective-permute-done.1.refs_1_ = bf16[32,128]{1,0:T(8,128)(2,1)S(1)} collective-permute-done((bf16[32,128]{1,0:T(8,128)(2,1)S(1)}, bf16[32,128]{1,0:T(8,128)(2,1)S(1)}, u32[]{:S(2)}, u32[]{:S(2)}) %collective-permute-start.1) | collective-permute-done | bytes 8224 | tf_op jit(solution)/shard_map/ppermute | solution.py:395
  9.8 0.0 collective-permute-done.2.refs_2_
  9.8 1.6 %collective-permute-start.5 = (bf16[4,32,128]{2,1,0:T(8,128)(2,1)S(1)}, bf16[4,32,128]{2,1,0:T(8,128)(2,1)S(1)}, u32[]{:S(2)}, u32[]{:S(2)}) collective-permute-start(bf16[4,32,128]{2,1,0:T(8,128)(2,1)S(1)} %join_columns.1.own_ref), channel_id=1, source_target_pairs={{0,1},{1,0},{2,3},{3,2},{4,5},{5,4},{6,7},{7,6},{8,9},{9,8},{10,11... | collective-permute-start | bytes 98312 | tf_op jit(solution)/shard_map/ppermute | solution.py:408
  11.4 0.1 unpack.1.own
  11.5 0.5 %collective-permute-start.3 = (bf16[4,32,128]{2,1,0:T(8,128)(2,1)S(1)}, bf16[4,32,128]{2,1,0:T(8,128)(2,1)S(1)}, u32[]{:S(2)}, u32[]{:S(2)}) collective-permute-start(bf16[4,32,128]{2,1,0:T(8,128)(2,1)S(1)} %join_columns.1.own_ref), channel_id=1, source_target_pairs={{0,1},{1,0},{2,3},{3,2},{4,5},{5,4},{6,7},{7,6},{8,17},{9,16},{10,... | collective-permute-start | bytes 98312 | tf_op jit(solution)/shard_map/ppermute | solution.py:408
  12.0 1.5 %collective-permute-start.4 = (bf16[4,32,128]{2,1,0:T(8,128)(2,1)S(1)}, bf16[4,32,128]{2,1,0:T(8,128)(2,1)S(1)}, u32[]{:S(2)}, u32[]{:S(2)}) collective-permute-start(bf16[4,32,128]{2,1,0:T(8,128)(2,1)S(1)} %join_columns.1.own_ref), channel_id=1, source_target_pairs={{0,1},{1,0},{2,3},{3,2},{4,5},{5,4},{6,7},{7,6},{8,16},{9,17},{10,... | collective-permute-start | bytes 98312 | tf_op jit(solution)/shard_map/ppermute | solution.py:408
  13.5 0.3 %collective-permute-done.5.mate_ref.mate = bf16[4,32,128]{2,1,0:T(8,128)(2,1)S(1)} collective-permute-done((bf16[4,32,128]{2,1,0:T(8,128)(2,1)S(1)}, bf16[4,32,128]{2,1,0:T(8,128)(2,1)S(1)}, u32[]{:S(2)}, u32[]{:S(2)}) %collective-permute-start.5) | collective-permute-done | bytes 32800 | tf_op jit(solution)/shard_map/ppermute | solution.py:408
  13.8 0.1 collective-permute-start.6
  13.9 0.0 collective-permute-done.7.mate_ref
  13.9 0.5 %squares.1.squares_ref = bf16[2304,256]{1,0:T(8,128)(2,1)S(1)} custom-call(bf16[9,20,80]{2,1,0:T(8,128)(2,1)S(1)} %bitcast.9, bf16[9,20,80]{2,1,0:T(8,128)(2,1)S(1)} %collective-permute-done.7.mate_ref), custom_call_target="tpu_custom_call" | custom-call | flops 1000000000 | bytes 1000000 | tf_op jit(solution)/shard_map/squares/pallas_call | solution.py:381
  14.5 0.3 %conv_own.1.part_ref = f32[2,432,256]{2,1,0:T(8,128)S(1)} custom-call(bf16[4,32,128]{2,1,0:T(8,128)(2,1)S(1)} %collective-permute-done.5.mate_ref.mate, bf16[2,4,16,256]{3,2,1,0:T(8,128)(2,1)S(1)} %unpack.1.own, bf16[2,432,384]{2,1,0:T(8,128)(2,1)S(1)} %tables.1.table_ref), custom_call_target="tpu_custom_call" | custom-call | flops 1000000000 | bytes 1000000 | tf_op jit(solution)/shard_map/conv_own/pallas_call | solution.py:381
  14.8 0.0 copy-start
  14.8 0.6 %collective-permute-done.3.odd_mate = bf16[4,32,128]{2,1,0:T(8,128)(2,1)S(1)} collective-permute-done((bf16[4,32,128]{2,1,0:T(8,128)(2,1)S(1)}, bf16[4,32,128]{2,1,0:T(8,128)(2,1)S(1)}, u32[]{:S(2)}, u32[]{:S(2)}) %collective-permute-start.3) | collective-permute-done | bytes 32800 | tf_op jit(solution)/shard_map/ppermute | solution.py:408
  15.4 0.7 %collective-permute-done.4.odd_own = bf16[4,32,128]{2,1,0:T(8,128)(2,1)S(1)} collective-permute-done((bf16[4,32,128]{2,1,0:T(8,128)(2,1)S(1)}, bf16[4,32,128]{2,1,0:T(8,128)(2,1)S(1)}, u32[]{:S(2)}, u32[]{:S(2)}) %collective-permute-start.4) | collective-permute-done | bytes 32800 | tf_op jit(solution)/shard_map/ppermute | solution.py:408
  16.1 0.0 collective-permute-done.6.even
  16.1 0.8 %conv.1 = (bf16[32,128]{1,0:T(8,128)(2,1)S(1)}, bf16[32,128]{1,0:T(8,128)(2,1)S(1)}, bf16[32,128]{1,0:T(8,128)(2,1)S(1)}, bf16[32,128]{1,0:T(8,128)(2,1)S(1)}) custom-call(bf16[4,32,128]{2,1,0:T(8,128)(2,1)S(1)} %collective-permute-done.3.odd_mate, bf16[4,32,128]{2,1,0:T(8,128)(2,1)S(1)} %collective-permute-done.4.odd_own, ...), custom_call_target="tpu_custom_call" | custom-call | flops 10000000000 | bytes 1000000 | tf_op jit(solution)/shard_map/conv/pallas_call | solution.py:381
  16.9 0.0 copy-start.4
  16.9 2.0 %collective-permute-start.10 = (bf16[32,128]{1,0:T(8,128)(2,1)S(1)}, bf16[32,128]{1,0:T(8,128)(2,1)S(1)}, u32[]{:S(2)}, u32[]{:S(2)}) collective-permute-start(bf16[32,128]{1,0:T(8,128)(2,1)S(1)} %get-tuple-element.28), channel_id=1, source_target_pairs={{0,6},{1,7},{2,4},{3,5},{4,2},{5,3},{6,0},{7,1},{8,14},{9,15},{10,... | collective-permute-start | bytes 24584 | tf_op jit(solution)/shard_map/ppermute | solution.py:395
  19.0 0.0 collective-permute-start.8
  19.0 2.4 %collective-permute-start.9 = (bf16[32,128]{1,0:T(8,128)(2,1)S(1)}, bf16[32,128]{1,0:T(8,128)(2,1)S(1)}, u32[]{:S(2)}, u32[]{:S(2)}) collective-permute-start(bf16[32,128]{1,0:T(8,128)(2,1)S(1)} %get-tuple-element.26), channel_id=1, source_target_pairs={{0,2},{1,3},{2,0},{3,1},{4,6},{5,7},{6,4},{7,5},{8,10},{9,11},{10,... | collective-permute-start | bytes 24584 | tf_op jit(solution)/shard_map/ppermute | solution.py:395
  21.4 1.1 %collective-permute-done.10.first_ref = bf16[32,128]{1,0:T(8,128)(2,1)S(1)} collective-permute-done((bf16[32,128]{1,0:T(8,128)(2,1)S(1)}, bf16[32,128]{1,0:T(8,128)(2,1)S(1)}, u32[]{:S(2)}, u32[]{:S(2)}) %collective-permute-start.10) | collective-permute-done | bytes 8224 | tf_op jit(solution)/shard_map/ppermute | solution.py:395
  22.5 0.0 copy-done
  22.5 0.4 %lift.1 = (f32[4,24,256]{2,1,0:T(8,128)S(1)}, f32[24,640]{1,0:T(8,128)S(1)}, f32[32,1280]{1,0:T(8,128)S(1)}, f32[2,24,128]{2,1,0:T(8,128)S(1)}) custom-call(bf16[32,128]{1,0:T(8,128)(2,1)S(1)} %get-tuple-element.27.own_ref, bf16[32,128]{1,0:T(8,128)(2,1)S(1)} %collective-permute-done.10.first_ref, bf16[12,2,640]{2,1,0:T(2,128)(2,1)S(1)} %bitcast.6, ...), custom_call_target="tpu_custom_call" | custom-call | flops 100000000 | bytes 1000000 | tf_op jit(solution)/shard_map/lift/pallas_call | solution.py:381
  22.8 0.7 %collective-permute-done.8.refs_0_ = bf16[32,128]{1,0:T(8,128)(2,1)S(1)} collective-permute-done((bf16[32,128]{1,0:T(8,128)(2,1)S(1)}, bf16[32,128]{1,0:T(8,128)(2,1)S(1)}, u32[]{:S(2)}, u32[]{:S(2)}) %collective-permute-start.8) | collective-permute-done | bytes 8224 | tf_op jit(solution)/shard_map/ppermute | solution.py:395
  23.5 0.0 collective-permute-done.9.refs_1_
  23.5 0.0 copy-done.4
  23.5 1.3 %tail.1 = bf16[12,2,640]{2,1,0:T(2,128)(2,1)} custom-call(bf16[32,128]{1,0:T(8,128)(2,1)S(1)} %collective-permute-done.8.refs_0_, bf16[32,128]{1,0:T(8,128)(2,1)S(1)} %collective-permute-done.9.refs_1_, f32[4,24,256]{2,1,0:T(8,128)S(1)} %get-tuple-element.29.refs_2_, f32[24,640]{1,0:T(8,128)S(1)} %get-tuple-element.30.refs_3_, ...), custom_call_target="tpu_custom_call" | custom-call | flops 1000000000 | bytes 1000000 | tf_op jit(solution)/shard_map/tail/pallas_call | solution.py:381
  (3 shorter events, 0.0 us)
Async XLA Ops:
  0.0 4.1 %copy-start.1 = (bf16[2,12,640]{2,0,1:T(2,128)(2,1)S(1)}, bf16[2,12,640]{2,0,1:T(2,128)(2,1)}, u32[]{:S(2)}) copy-start(bf16[2,12,640]{2,0,1:T(2,128)(2,1)} %param.7) | copy-start | bytes 92164
  0.0 7.9 %collective-permute-start = (bf16[12,2,640]{2,1,0:T(2,128)(2,1)}, bf16[12,2,640]{2,1,0:T(2,128)(2,1)S(1)}, u32[]{:S(2)}, u32[]{:S(2)}) collective-permute-start(bf16[12,2,640]{2,1,0:T(2,128)(2,1)} %bitcast.4), channel_id=1, source_target_pairs={{0,4},{1,5},{2,6},{3,7},{4,0},{5,1},{6,2},{7,3},{8,12},{9,13},{10,... | collective-permute-start | bytes 92168 | tf_op jit(solution)/shard_map/ppermute | solution.py:395
  4.1 2.0 %copy-start.5 = (bf16[9,80,20]{1,2,0:T(8,128)(2,1)S(1)}, bf16[9,80,20]{1,2,0:T(8,128)(2,1)}, u32[]{:S(2)}) copy-start(bf16[9,80,20]{1,2,0:T(8,128)(2,1)} %param.9) | copy-start | bytes 86404
  4.1 3.4 %copy-start.2 = (bf16[9,96]{1,0:T(8,128)(2,1)S(1)}, bf16[9,96]{1,0:T(8,128)(2,1)}, u32[]{:S(2)}) copy-start(bf16[9,96]{1,0:T(8,128)(2,1)} %filter_ref.1) | copy-start | bytes 5188
  4.1 3.4 %copy-start.3 = (bf16[9,2,3]{0,1,2:T(2,128)(2,1)S(1)}, bf16[9,2,3]{0,1,2:T(2,128)(2,1)}, u32[]{:S(2)}) copy-start(bf16[9,2,3]{0,1,2:T(2,128)(2,1)} %param.10) | copy-start | bytes 328
  4.3 5.5 %collective-permute-start.1 = (bf16[32,128]{1,0:T(8,128)(2,1)S(1)}, bf16[32,128]{1,0:T(8,128)(2,1)S(1)}, u32[]{:S(2)}, u32[]{:S(2)}) collective-permute-start(bf16[32,128]{1,0:T(8,128)(2,1)S(1)} %get-tuple-element.20), channel_id=1, source_target_pairs={{0,6},{1,7},{2,4},{3,5},{4,2},{5,3},{6,0},{7,1},{8,14},{9,15},{10,... | collective-permute-start | bytes 24584 | tf_op jit(solution)/shard_map/ppermute | solution.py:395
  6.0 3.8 %collective-permute-start.2 = (bf16[32,128]{1,0:T(8,128)(2,1)S(1)}, bf16[32,128]{1,0:T(8,128)(2,1)S(1)}, u32[]{:S(2)}, u32[]{:S(2)}) collective-permute-start(bf16[32,128]{1,0:T(8,128)(2,1)S(1)} %get-tuple-element.21), channel_id=1, source_target_pairs={{0,2},{1,3},{2,0},{3,1},{4,6},{5,7},{6,4},{7,5},{8,10},{9,11},{10,... | collective-permute-start | bytes 24584 | tf_op jit(solution)/shard_map/ppermute | solution.py:395
  6.0 7.8 %collective-permute-start.7 = (bf16[9,20,80]{2,1,0:T(8,128)(2,1)S(1)}, bf16[9,20,80]{2,1,0:T(8,128)(2,1)S(1)}, u32[]{:S(2)}, u32[]{:S(2)}) collective-permute-start(bf16[9,20,80]{2,1,0:T(8,128)(2,1)S(1)} %bitcast.8), channel_id=1, source_target_pairs={{0,1},{1,0},{2,3},{3,2},{4,5},{5,4},{6,7},{7,6},{8,9},{9,8},{10,11... | collective-permute-start | bytes 86408 | tf_op jit(solution)/shard_map/ppermute | solution.py:399
  9.8 4.0 %collective-permute-start.5 = (bf16[4,32,128]{2,1,0:T(8,128)(2,1)S(1)}, bf16[4,32,128]{2,1,0:T(8,128)(2,1)S(1)}, u32[]{:S(2)}, u32[]{:S(2)}) collective-permute-start(bf16[4,32,128]{2,1,0:T(8,128)(2,1)S(1)} %join_columns.1.own_ref), channel_id=1, source_target_pairs={{0,1},{1,0},{2,3},{3,2},{4,5},{5,4},{6,7},{7,6},{8,9},{9,8},{10,11... | collective-permute-start | bytes 98312 | tf_op jit(solution)/shard_map/ppermute | solution.py:408
  11.5 3.9 %collective-permute-start.3 = (bf16[4,32,128]{2,1,0:T(8,128)(2,1)S(1)}, bf16[4,32,128]{2,1,0:T(8,128)(2,1)S(1)}, u32[]{:S(2)}, u32[]{:S(2)}) collective-permute-start(bf16[4,32,128]{2,1,0:T(8,128)(2,1)S(1)} %join_columns.1.own_ref), channel_id=1, source_target_pairs={{0,1},{1,0},{2,3},{3,2},{4,5},{5,4},{6,7},{7,6},{8,17},{9,16},{10,... | collective-permute-start | bytes 98312 | tf_op jit(solution)/shard_map/ppermute | solution.py:408
  12.0 4.1 %collective-permute-start.4 = (bf16[4,32,128]{2,1,0:T(8,128)(2,1)S(1)}, bf16[4,32,128]{2,1,0:T(8,128)(2,1)S(1)}, u32[]{:S(2)}, u32[]{:S(2)}) collective-permute-start(bf16[4,32,128]{2,1,0:T(8,128)(2,1)S(1)} %join_columns.1.own_ref), channel_id=1, source_target_pairs={{0,1},{1,0},{2,3},{3,2},{4,5},{5,4},{6,7},{7,6},{8,16},{9,17},{10,... | collective-permute-start | bytes 98312 | tf_op jit(solution)/shard_map/ppermute | solution.py:408
  13.8 2.3 %collective-permute-start.6 = (bf16[4,2,32,128]{3,2,1,0:T(8,128)(2,1)S(1)}, bf16[4,2,32,128]{3,2,1,0:T(8,128)(2,1)S(1)}, u32[]{:S(2)}, u32[]{:S(2)}) collective-permute-start(bf16[4,2,32,128]{3,2,1,0:T(8,128)(2,1)S(1)} %join_sides.1), channel_id=1, source_target_pairs={{0,8},{1,9},{2,10},{3,11},{4,12},{5,13},{6,14},{7,15},{8,0},{9,1},... | collective-permute-start | bytes 196616 | tf_op jit(solution)/shard_map/ppermute | solution.py:408
  14.8 7.7 %copy-start = (bf16[640,1280]{1,0:T(8,128)(2,1)S(1)}, bf16[640,1280]{1,0:T(8,128)(2,1)}, u32[]{:S(2)}) copy-start(bf16[640,1280]{1,0:T(8,128)(2,1)} %refs_6_.1) | copy-start | bytes 4915204
  16.9 6.6 %copy-start.4 = (bf16[1280,640]{1,0:T(8,128)(2,1)S(1)}, bf16[1280,640]{1,0:T(8,128)(2,1)}, u32[]{:S(2)}) copy-start(bf16[1280,640]{1,0:T(8,128)(2,1)} %refs_7_.1) | copy-start | bytes 4915204
  16.9 5.5 %collective-permute-start.10 = (bf16[32,128]{1,0:T(8,128)(2,1)S(1)}, bf16[32,128]{1,0:T(8,128)(2,1)S(1)}, u32[]{:S(2)}, u32[]{:S(2)}) collective-permute-start(bf16[32,128]{1,0:T(8,128)(2,1)S(1)} %get-tuple-element.28), channel_id=1, source_target_pairs={{0,6},{1,7},{2,4},{3,5},{4,2},{5,3},{6,0},{7,1},{8,14},{9,15},{10,... | collective-permute-start | bytes 24584 | tf_op jit(solution)/shard_map/ppermute | solution.py:395
  19.0 4.5 %collective-permute-start.8 = (bf16[32,128]{1,0:T(8,128)(2,1)S(1)}, bf16[32,128]{1,0:T(8,128)(2,1)S(1)}, u32[]{:S(2)}, u32[]{:S(2)}) collective-permute-start(bf16[32,128]{1,0:T(8,128)(2,1)S(1)} %get-tuple-element.25), channel_id=1, source_target_pairs={{0,4},{1,5},{2,6},{3,7},{4,0},{5,1},{6,2},{7,3},{8,12},{9,13},{10,... | collective-permute-start | bytes 24584 | tf_op jit(solution)/shard_map/ppermute | solution.py:395
  19.0 4.5 %collective-permute-start.9 = (bf16[32,128]{1,0:T(8,128)(2,1)S(1)}, bf16[32,128]{1,0:T(8,128)(2,1)S(1)}, u32[]{:S(2)}, u32[]{:S(2)}) collective-permute-start(bf16[32,128]{1,0:T(8,128)(2,1)S(1)} %get-tuple-element.26), channel_id=1, source_target_pairs={{0,2},{1,3},{2,0},{3,1},{4,6},{5,7},{6,4},{7,5},{8,10},{9,11},{10,... | collective-permute-start | bytes 24584 | tf_op jit(solution)/shard_map/ppermute | solution.py:395

commit v9 on v8

--- a/solution.py
+++ b/solution.py
@@ -103,12 +103,6 @@
     column, _ = column_and_side()
     for apart, ref in zip(order, in_refs):
         out_ref[column ^ apart] = ref[...]
-
-
-def sides_kernel(own_ref, mate_ref, out_ref):
-    _, side = column_and_side()
-    out_ref[:, side] = own_ref[...]
-    out_ref[:, 1 - side] = mate_ref[...]
 
 
 def apart_kernel(width, step, out_ref):
@@ -216,7 +210,16 @@
 
 
 def conv_kernel(
-    block, width, odd_mate, odd_own, even, part_ref, table_ref, squares_ref, *refs
+    block,
+    width,
+    odd_mate,
+    odd_own,
+    even_own,
+    even_mate,
+    part_ref,
+    table_ref,
+    squares_ref,
+    *refs,
 ):
     *out_refs, field, spread, stage = refs
     columns = len(out_refs)
@@ -236,8 +239,8 @@
             field[row, pl.ds(first, step)] = read
 
     for at in range(columns):
-        place(1 - odd, 2 * at, even[at, 0])
-        place(1 - odd, 2 * at + 1, even[at, 1])
+        place(1 - odd, 2 * at + side, even_own[at])
+        place(1 - odd, 2 * at + 1 - side, even_mate[at])
         place(odd, 2 * at + side, odd_own[at])
         place(odd, 2 * at + 1 - side, odd_mate[at])
     for row in range(rows):
@@ -492,16 +495,15 @@
         10**9,
         own_side,
     )
-    circle = jax.ShapeDtypeStruct((columns, 2, height, LANES), BF16)
-    home = call(sides_kernel, "join_sides", circle, [], 10**8, own_side, mate_side)
-    even = swap(home, count, lambda lat, lon: (lat ^ 1, lon))
-    mix_mate, _ = lax.optimization_barrier((mix_mate, home))
+    even_own = swap(own_side, count, lambda lat, lon: (lat ^ 1, lon))
+    even_mate = swap(mate_side, count, lambda lat, lon: (lat ^ 1, lon))
+    mix_mate, _ = lax.optimization_barrier((mix_mate, mate_side))
     squares = call(
         squares_kernel,
         "squares",
         jax.ShapeDtypeStruct((bases * lanes, lanes), BF16),
         [pltpu.VMEM((2, bases, up_to(group, 2 * SUBLANES), lanes), F32)],
-        10**9,
+        3 * 10**8,
         mix_own,
         mix_mate,
     )
@@ -510,7 +512,7 @@
         "conv_own",
         jax.ShapeDtypeStruct((rows, bases * columns * width, lanes), F32),
         [pltpu.VMEM((rows, places, lanes), BF16)],
-        10**9,
+        3 * 10**8,
         mate_side,
         own_rows,
         table,
@@ -527,12 +529,13 @@
         10**10,
         odd_mate,
         odd_own,
-        even,
+        even_own,
+        even_mate,
         part,
         table,
         squares,
     )
-    outward = far_first[1:-1] + far_first[:1]
+    outward = tuple(reversed(far_first[:-1]))
     back = [over_columns(mixed[apart], count, apart) for apart in outward]
     first = outward.index(far_first[0])
     lifted = call(

time: 25 us -> 25 us (level)
    ppermute x4 -> x5, starting transfers between devices: 3.66 us -> 3.79 us  [swap(): return lax.ppermute(block, ('lat', 'lon'), pairs)]
    ppermute x4 -> x5, waiting for transfers between devices: 1.6 us -> 1.5 us  [swap(): return lax.ppermute(block, ('lat', 'lon'), pairs)]
    pallas_call x12 -> x11, Pallas kernels: 4.27 us -> 4.26 us  [call(): pl.pallas_call(kernel, out_shape=out_shape, in_specs=[VMEM] * len(operand...]
  transfers between devices with their start and end apart: 11 -> 12, of which waited for: 6 -> 6; matrix products, arithmetic and copies ran while one was open for 0% -> 0% of each run, Pallas kernels for 8% -> 8%
where the time goes in v9:
time: 25 us; the launch traced here: 24.9 us
  starting transfers between devices  15.5 us (62%)
  waiting for transfers between devices  4.94 us (20%)
  Pallas kernels  4.26 us (17%)
    ppermute x6, starting transfers between devices, over_columns(): return lax.ppermute(message, 'lon', pairs) if apart else message  10.2 us
    pallas_call x11, Pallas kernels, call(): pl.pallas_call(kernel, out_shape=out_shape, in_specs=[VMEM] * len(operand...  4.26 us
    ppermute x5, starting transfers between devices, swap(): return lax.ppermute(block, ('lat', 'lon'), pairs)  3.79 us
    ppermute x6, waiting for transfers between devices, over_columns(): return lax.ppermute(message, 'lon', pairs) if apart else message  3.43 us
    ppermute x5, waiting for transfers between devices, swap(): return lax.ppermute(block, ('lat', 'lon'), pairs)  1.5 us
    ppermute x1, starting transfers between devices, over_sides(): return lax.ppermute(block, 'lon', [(i, i ^ 1) for i in range(count)])  1.49 us
  transfers between devices with their start and end apart: 12, of which 6 were waited for; matrix products, arithmetic and copies ran while one was open for 0% of the time, Pallas kernels for 8%

profile of v9, /device:TPU:0, one launch (start us, length us, event | category | flops | bytes accessed | tf_op | source)
XLA Modules:
  0.0 24.9 jit_solution(4734736404996630062)
XLA Ops:
  0.0 0.0 copy-start.2
  0.0 4.0 %collective-permute-start = (bf16[12,2,640]{2,1,0:T(2,128)(2,1)}, bf16[12,2,640]{2,1,0:T(2,128)(2,1)S(1)}, u32[]{:S(2)}, u32[]{:S(2)}) collective-permute-start(bf16[12,2,640]{2,1,0:T(2,128)(2,1)} %bitcast.6), channel_id=1, source_target_pairs={{0,4},{1,5},{2,6},{3,7},{4,0},{5,1},{6,2},{7,3},{8,12},{9,13},{10,... | collective-permute-start | bytes 92168 | tf_op jit(solution)/shard_map/ppermute | solution.py:398
  4.1 0.0 copy-done.2
  4.1 0.0 copy-start.1
  4.1 0.0 copy-start.3
  4.1 0.0 copy-start.4
  4.1 0.2 pack.1
  4.3 1.7 %collective-permute-start.1 = (bf16[32,128]{1,0:T(8,128)(2,1)S(1)}, bf16[32,128]{1,0:T(8,128)(2,1)S(1)}, u32[]{:S(2)}, u32[]{:S(2)}) collective-permute-start(bf16[32,128]{1,0:T(8,128)(2,1)S(1)} %get-tuple-element.20), channel_id=1, source_target_pairs={{0,6},{1,7},{2,4},{3,5},{4,2},{5,3},{6,0},{7,1},{8,14},{9,15},{10,... | collective-permute-start | bytes 24584 | tf_op jit(solution)/shard_map/ppermute | solution.py:398
  6.0 0.0 collective-permute-start.2
  6.0 0.0 copy-done.1
  6.0 1.5 %collective-permute-start.8 = (bf16[9,20,80]{2,1,0:T(8,128)(2,1)S(1)}, bf16[9,20,80]{2,1,0:T(8,128)(2,1)S(1)}, u32[]{:S(2)}, u32[]{:S(2)}) collective-permute-start(bf16[9,20,80]{2,1,0:T(8,128)(2,1)S(1)} %bitcast.4), channel_id=1, source_target_pairs={{0,1},{1,0},{2,3},{3,2},{4,5},{5,4},{6,7},{7,6},{8,9},{9,8},{10,11... | collective-permute-start | bytes 86408 | tf_op jit(solution)/shard_map/ppermute | solution.py:402
  7.5 0.0 copy-done.3
  7.5 0.0 copy-done.4
  7.5 0.4 %tables.1.table_ref = bf16[2,432,384]{2,1,0:T(8,128)(2,1)S(1)} custom-call(bf16[9,96]{1,0:T(8,128)(2,1)S(1)} %copy-done.3, bf16[3,2,9]{2,1,0:T(2,128)(2,1)S(1)} %bitcast.9, s32[96,128]{1,0:T(8,128)S(1)} %apart.1.apart_ref), custom_call_target="tpu_custom_call" | custom-call | flops 1000000 | bytes 1000000 | tf_op jit(solution)/shard_map/tables/pallas_call | solution.py:384
  7.9 0.0 collective-permute-done.raw_ref
  7.9 0.2 cut.1.refs_0_
  8.1 1.7 %collective-permute-done.1.refs_1_ = bf16[32,128]{1,0:T(8,128)(2,1)S(1)} collective-permute-done((bf16[32,128]{1,0:T(8,128)(2,1)S(1)}, bf16[32,128]{1,0:T(8,128)(2,1)S(1)}, u32[]{:S(2)}, u32[]{:S(2)}) %collective-permute-start.1) | collective-permute-done | bytes 8224 | tf_op jit(solution)/shard_map/ppermute | solution.py:398
  9.8 0.0 collective-permute-done.2.refs_2_
  9.8 1.6 %collective-permute-start.6 = (bf16[4,32,128]{2,1,0:T(8,128)(2,1)S(1)}, bf16[4,32,128]{2,1,0:T(8,128)(2,1)S(1)}, u32[]{:S(2)}, u32[]{:S(2)}) collective-permute-start(bf16[4,32,128]{2,1,0:T(8,128)(2,1)S(1)} %join_columns.1.own_ref), channel_id=1, source_target_pairs={{0,1},{1,0},{2,3},{3,2},{4,5},{5,4},{6,7},{7,6},{8,9},{9,8},{10,11... | collective-permute-start | bytes 98312 | tf_op jit(solution)/shard_map/ppermute | solution.py:411
  11.4 0.1 unpack.1.own
  11.5 0.5 %collective-permute-start.3 = (bf16[4,32,128]{2,1,0:T(8,128)(2,1)S(1)}, bf16[4,32,128]{2,1,0:T(8,128)(2,1)S(1)}, u32[]{:S(2)}, u32[]{:S(2)}) collective-permute-start(bf16[4,32,128]{2,1,0:T(8,128)(2,1)S(1)} %join_columns.1.own_ref), channel_id=1, source_target_pairs={{0,1},{1,0},{2,3},{3,2},{4,5},{5,4},{6,7},{7,6},{8,17},{9,16},{10,... | collective-permute-start | bytes 98312 | tf_op jit(solution)/shard_map/ppermute | solution.py:411
  12.0 1.5 %collective-permute-start.4 = (bf16[4,32,128]{2,1,0:T(8,128)(2,1)S(1)}, bf16[4,32,128]{2,1,0:T(8,128)(2,1)S(1)}, u32[]{:S(2)}, u32[]{:S(2)}) collective-permute-start(bf16[4,32,128]{2,1,0:T(8,128)(2,1)S(1)} %join_columns.1.own_ref), channel_id=1, source_target_pairs={{0,1},{1,0},{2,3},{3,2},{4,5},{5,4},{6,7},{7,6},{8,16},{9,17},{10,... | collective-permute-start | bytes 98312 | tf_op jit(solution)/shard_map/ppermute | solution.py:411
  13.5 0.0 collective-permute-start.5
  13.5 0.0 collective-permute-done.8.mate_ref
  13.5 0.3 %collective-permute-done.6.mate = bf16[4,32,128]{2,1,0:T(8,128)(2,1)S(1)} collective-permute-done((bf16[4,32,128]{2,1,0:T(8,128)(2,1)S(1)}, bf16[4,32,128]{2,1,0:T(8,128)(2,1)S(1)}, u32[]{:S(2)}, u32[]{:S(2)}) %collective-permute-start.6) | collective-permute-done | bytes 32800 | tf_op jit(solution)/shard_map/ppermute | solution.py:411
  13.8 0.2 collective-permute-start.7
  14.0 0.5 %squares.1.squares_ref = bf16[2304,256]{1,0:T(8,128)(2,1)S(1)} custom-call(bf16[9,20,80]{2,1,0:T(8,128)(2,1)S(1)} %bitcast.5, bf16[9,20,80]{2,1,0:T(8,128)(2,1)S(1)} %collective-permute-done.8.mate_ref), custom_call_target="tpu_custom_call" | custom-call | flops 300000000 | bytes 1000000 | tf_op jit(solution)/shard_map/squares/pallas_call | solution.py:384
  14.6 0.3 %conv_own.1.part_ref = f32[2,432,256]{2,1,0:T(8,128)S(1)} custom-call(bf16[4,32,128]{2,1,0:T(8,128)(2,1)S(1)} %collective-permute-done.6.mate, bf16[2,4,16,256]{3,2,1,0:T(8,128)(2,1)S(1)} %unpack.1.own, bf16[2,432,384]{2,1,0:T(8,128)(2,1)S(1)} %tables.1.table_ref), custom_call_target="tpu_custom_call" | custom-call | flops 300000000 | bytes 1000000 | tf_op jit(solution)/shard_map/conv_own/pallas_call | solution.py:384
  14.9 0.0 copy-start
  14.9 0.5 %collective-permute-done.3.odd_mate = bf16[4,32,128]{2,1,0:T(8,128)(2,1)S(1)} collective-permute-done((bf16[4,32,128]{2,1,0:T(8,128)(2,1)S(1)}, bf16[4,32,128]{2,1,0:T(8,128)(2,1)S(1)}, u32[]{:S(2)}, u32[]{:S(2)}) %collective-permute-start.3) | collective-permute-done | bytes 32800 | tf_op jit(solution)/shard_map/ppermute | solution.py:411
  15.4 0.7 %collective-permute-done.4.odd_own = bf16[4,32,128]{2,1,0:T(8,128)(2,1)S(1)} collective-permute-done((bf16[4,32,128]{2,1,0:T(8,128)(2,1)S(1)}, bf16[4,32,128]{2,1,0:T(8,128)(2,1)S(1)}, u32[]{:S(2)}, u32[]{:S(2)}) %collective-permute-start.4) | collective-permute-done | bytes 32800 | tf_op jit(solution)/shard_map/ppermute | solution.py:411
  16.1 0.0 collective-permute-done.5.even_own
  16.1 0.0 collective-permute-done.7.even_mate
  16.1 0.8 %conv.1 = (bf16[32,128]{1,0:T(8,128)(2,1)S(1)}, bf16[32,128]{1,0:T(8,128)(2,1)S(1)}, bf16[32,128]{1,0:T(8,128)(2,1)S(1)}, bf16[32,128]{1,0:T(8,128)(2,1)S(1)}) custom-call(bf16[4,32,128]{2,1,0:T(8,128)(2,1)S(1)} %collective-permute-done.3.odd_mate, bf16[4,32,128]{2,1,0:T(8,128)(2,1)S(1)} %collective-permute-done.4.odd_own, ...), custom_call_target="tpu_custom_call" | custom-call | flops 10000000000 | bytes 1000000 | tf_op jit(solution)/shard_map/conv/pallas_call | solution.py:384
  16.9 0.0 copy-start.5
  16.9 2.0 %collective-permute-start.11 = (bf16[32,128]{1,0:T(8,128)(2,1)S(1)}, bf16[32,128]{1,0:T(8,128)(2,1)S(1)}, u32[]{:S(2)}, u32[]{:S(2)}) collective-permute-start(bf16[32,128]{1,0:T(8,128)(2,1)S(1)} %get-tuple-element.28), channel_id=1, source_target_pairs={{0,6},{1,7},{2,4},{3,5},{4,2},{5,3},{6,0},{7,1},{8,14},{9,15},{10,... | collective-permute-start | bytes 24584 | tf_op jit(solution)/shard_map/ppermute | solution.py:398
  19.0 0.0 collective-permute-start.10
  19.0 2.4 %collective-permute-start.9 = (bf16[32,128]{1,0:T(8,128)(2,1)S(1)}, bf16[32,128]{1,0:T(8,128)(2,1)S(1)}, u32[]{:S(2)}, u32[]{:S(2)}) collective-permute-start(bf16[32,128]{1,0:T(8,128)(2,1)S(1)} %get-tuple-element.25), channel_id=1, source_target_pairs={{0,2},{1,3},{2,0},{3,1},{4,6},{5,7},{6,4},{7,5},{8,10},{9,11},{10,... | collective-permute-start | bytes 24584 | tf_op jit(solution)/shard_map/ppermute | solution.py:398
  21.4 1.1 %collective-permute-done.11.first_ref = bf16[32,128]{1,0:T(8,128)(2,1)S(1)} collective-permute-done((bf16[32,128]{1,0:T(8,128)(2,1)S(1)}, bf16[32,128]{1,0:T(8,128)(2,1)S(1)}, u32[]{:S(2)}, u32[]{:S(2)}) %collective-permute-start.11) | collective-permute-done | bytes 8224 | tf_op jit(solution)/shard_map/ppermute | solution.py:398
  22.5 0.0 copy-done
  22.5 0.4 %lift.1 = (f32[4,24,256]{2,1,0:T(8,128)S(1)}, f32[24,640]{1,0:T(8,128)S(1)}, f32[32,1280]{1,0:T(8,128)S(1)}, f32[2,24,128]{2,1,0:T(8,128)S(1)}) custom-call(bf16[32,128]{1,0:T(8,128)(2,1)S(1)} %get-tuple-element.27.own_ref, bf16[32,128]{1,0:T(8,128)(2,1)S(1)} %collective-permute-done.11.first_ref, bf16[12,2,640]{2,1,0:T(2,128)(2,1)S(1)} %bitcast.8, ...), custom_call_target="tpu_custom_call" | custom-call | flops 100000000 | bytes 1000000 | tf_op jit(solution)/shard_map/lift/pallas_call | solution.py:384
  22.8 0.7 %collective-permute-done.10.refs_1_ = bf16[32,128]{1,0:T(8,128)(2,1)S(1)} collective-permute-done((bf16[32,128]{1,0:T(8,128)(2,1)S(1)}, bf16[32,128]{1,0:T(8,128)(2,1)S(1)}, u32[]{:S(2)}, u32[]{:S(2)}) %collective-permute-start.10) | collective-permute-done | bytes 8224 | tf_op jit(solution)/shard_map/ppermute | solution.py:398
  23.5 0.0 collective-permute-done.9.refs_0_
  23.5 0.0 copy-done.5
  23.5 1.3 %tail.1 = bf16[12,2,640]{2,1,0:T(2,128)(2,1)} custom-call(bf16[32,128]{1,0:T(8,128)(2,1)S(1)} %collective-permute-done.9.refs_0_, bf16[32,128]{1,0:T(8,128)(2,1)S(1)} %collective-permute-done.10.refs_1_, f32[4,24,256]{2,1,0:T(8,128)S(1)} %get-tuple-element.29.refs_2_, f32[24,640]{1,0:T(8,128)S(1)} %get-tuple-element.30.refs_3_, ...), custom_call_target="tpu_custom_call" | custom-call | flops 1000000000 | bytes 1000000 | tf_op jit(solution)/shard_map/tail/pallas_call | solution.py:384
  (2 shorter events, 0.0 us)
Async XLA Ops:
  0.0 4.1 %copy-start.2 = (bf16[2,12,640]{2,0,1:T(2,128)(2,1)S(1)}, bf16[2,12,640]{2,0,1:T(2,128)(2,1)}, u32[]{:S(2)}) copy-start(bf16[2,12,640]{2,0,1:T(2,128)(2,1)} %param.7) | copy-start | bytes 92164
  0.0 7.9 %collective-permute-start = (bf16[12,2,640]{2,1,0:T(2,128)(2,1)}, bf16[12,2,640]{2,1,0:T(2,128)(2,1)S(1)}, u32[]{:S(2)}, u32[]{:S(2)}) collective-permute-start(bf16[12,2,640]{2,1,0:T(2,128)(2,1)} %bitcast.6), channel_id=1, source_target_pairs={{0,4},{1,5},{2,6},{3,7},{4,0},{5,1},{6,2},{7,3},{8,12},{9,13},{10,... | collective-permute-start | bytes 92168 | tf_op jit(solution)/shard_map/ppermute | solution.py:398
  4.1 2.0 %copy-start.1 = (bf16[9,80,20]{1,2,0:T(8,128)(2,1)S(1)}, bf16[9,80,20]{1,2,0:T(8,128)(2,1)}, u32[]{:S(2)}) copy-start(bf16[9,80,20]{1,2,0:T(8,128)(2,1)} %param.9) | copy-start | bytes 86404
  4.1 3.4 %copy-start.3 = (bf16[9,96]{1,0:T(8,128)(2,1)S(1)}, bf16[9,96]{1,0:T(8,128)(2,1)}, u32[]{:S(2)}) copy-start(bf16[9,96]{1,0:T(8,128)(2,1)} %filter_ref.1) | copy-start | bytes 5188
  4.1 3.4 %copy-start.4 = (bf16[9,2,3]{0,1,2:T(2,128)(2,1)S(1)}, bf16[9,2,3]{0,1,2:T(2,128)(2,1)}, u32[]{:S(2)}) copy-start(bf16[9,2,3]{0,1,2:T(2,128)(2,1)} %param.10) | copy-start | bytes 328
  4.3 5.5 %collective-permute-start.1 = (bf16[32,128]{1,0:T(8,128)(2,1)S(1)}, bf16[32,128]{1,0:T(8,128)(2,1)S(1)}, u32[]{:S(2)}, u32[]{:S(2)}) collective-permute-start(bf16[32,128]{1,0:T(8,128)(2,1)S(1)} %get-tuple-element.20), channel_id=1, source_target_pairs={{0,6},{1,7},{2,4},{3,5},{4,2},{5,3},{6,0},{7,1},{8,14},{9,15},{10,... | collective-permute-start | bytes 24584 | tf_op jit(solution)/shard_map/ppermute | solution.py:398
  6.0 3.8 %collective-permute-start.2 = (bf16[32,128]{1,0:T(8,128)(2,1)S(1)}, bf16[32,128]{1,0:T(8,128)(2,1)S(1)}, u32[]{:S(2)}, u32[]{:S(2)}) collective-permute-start(bf16[32,128]{1,0:T(8,128)(2,1)S(1)} %get-tuple-element.21), channel_id=1, source_target_pairs={{0,2},{1,3},{2,0},{3,1},{4,6},{5,7},{6,4},{7,5},{8,10},{9,11},{10,... | collective-permute-start | bytes 24584 | tf_op jit(solution)/shard_map/ppermute | solution.py:398
  6.0 7.4 %collective-permute-start.8 = (bf16[9,20,80]{2,1,0:T(8,128)(2,1)S(1)}, bf16[9,20,80]{2,1,0:T(8,128)(2,1)S(1)}, u32[]{:S(2)}, u32[]{:S(2)}) collective-permute-start(bf16[9,20,80]{2,1,0:T(8,128)(2,1)S(1)} %bitcast.4), channel_id=1, source_target_pairs={{0,1},{1,0},{2,3},{3,2},{4,5},{5,4},{6,7},{7,6},{8,9},{9,8},{10,11... | collective-permute-start | bytes 86408 | tf_op jit(solution)/shard_map/ppermute | solution.py:402
  9.8 4.0 %collective-permute-start.6 = (bf16[4,32,128]{2,1,0:T(8,128)(2,1)S(1)}, bf16[4,32,128]{2,1,0:T(8,128)(2,1)S(1)}, u32[]{:S(2)}, u32[]{:S(2)}) collective-permute-start(bf16[4,32,128]{2,1,0:T(8,128)(2,1)S(1)} %join_columns.1.own_ref), channel_id=1, source_target_pairs={{0,1},{1,0},{2,3},{3,2},{4,5},{5,4},{6,7},{7,6},{8,9},{9,8},{10,11... | collective-permute-start | bytes 98312 | tf_op jit(solution)/shard_map/ppermute | solution.py:411
  11.5 3.9 %collective-permute-start.3 = (bf16[4,32,128]{2,1,0:T(8,128)(2,1)S(1)}, bf16[4,32,128]{2,1,0:T(8,128)(2,1)S(1)}, u32[]{:S(2)}, u32[]{:S(2)}) collective-permute-start(bf16[4,32,128]{2,1,0:T(8,128)(2,1)S(1)} %join_columns.1.own_ref), channel_id=1, source_target_pairs={{0,1},{1,0},{2,3},{3,2},{4,5},{5,4},{6,7},{7,6},{8,17},{9,16},{10,... | collective-permute-start | bytes 98312 | tf_op jit(solution)/shard_map/ppermute | solution.py:411
  12.0 4.1 %collective-permute-start.4 = (bf16[4,32,128]{2,1,0:T(8,128)(2,1)S(1)}, bf16[4,32,128]{2,1,0:T(8,128)(2,1)S(1)}, u32[]{:S(2)}, u32[]{:S(2)}) collective-permute-start(bf16[4,32,128]{2,1,0:T(8,128)(2,1)S(1)} %join_columns.1.own_ref), channel_id=1, source_target_pairs={{0,1},{1,0},{2,3},{3,2},{4,5},{5,4},{6,7},{7,6},{8,16},{9,17},{10,... | collective-permute-start | bytes 98312 | tf_op jit(solution)/shard_map/ppermute | solution.py:411
  13.5 2.6 %collective-permute-start.5 = (bf16[4,32,128]{2,1,0:T(8,128)(2,1)S(1)}, bf16[4,32,128]{2,1,0:T(8,128)(2,1)S(1)}, u32[]{:S(2)}, u32[]{:S(2)}) collective-permute-start(bf16[4,32,128]{2,1,0:T(8,128)(2,1)S(1)} %join_columns.1.own_ref), channel_id=1, source_target_pairs={{0,8},{1,9},{2,10},{3,11},{4,12},{5,13},{6,14},{7,15},{8,0},{9,1},... | collective-permute-start | bytes 98312 | tf_op jit(solution)/shard_map/ppermute | solution.py:411
  13.8 2.3 %collective-permute-start.7 = (bf16[4,32,128]{2,1,0:T(8,128)(2,1)S(1)}, bf16[4,32,128]{2,1,0:T(8,128)(2,1)S(1)}, u32[]{:S(2)}, u32[]{:S(2)}) collective-permute-start(bf16[4,32,128]{2,1,0:T(8,128)(2,1)S(1)} %collective-permute-done.6.mate), channel_id=1, source_target_pairs={{0,8},{1,9},{2,10},{3,11},{4,12},{5,13},{6,14},{7,15},{8,0},{9,1},... | collective-permute-start | bytes 98312 | tf_op jit(solution)/shard_map/ppermute | solution.py:411
  14.9 7.6 %copy-start = (bf16[640,1280]{1,0:T(8,128)(2,1)S(1)}, bf16[640,1280]{1,0:T(8,128)(2,1)}, u32[]{:S(2)}) copy-start(bf16[640,1280]{1,0:T(8,128)(2,1)} %refs_6_.1) | copy-start | bytes 4915204
  16.9 6.6 %copy-start.5 = (bf16[1280,640]{1,0:T(8,128)(2,1)S(1)}, bf16[1280,640]{1,0:T(8,128)(2,1)}, u32[]{:S(2)}) copy-start(bf16[1280,640]{1,0:T(8,128)(2,1)} %refs_7_.1) | copy-start | bytes 4915204
  16.9 5.5 %collective-permute-start.11 = (bf16[32,128]{1,0:T(8,128)(2,1)S(1)}, bf16[32,128]{1,0:T(8,128)(2,1)S(1)}, u32[]{:S(2)}, u32[]{:S(2)}) collective-permute-start(bf16[32,128]{1,0:T(8,128)(2,1)S(1)} %get-tuple-element.28), channel_id=1, source_target_pairs={{0,6},{1,7},{2,4},{3,5},{4,2},{5,3},{6,0},{7,1},{8,14},{9,15},{10,... | collective-permute-start | bytes 24584 | tf_op jit(solution)/shard_map/ppermute | solution.py:398
  19.0 4.5 %collective-permute-start.10 = (bf16[32,128]{1,0:T(8,128)(2,1)S(1)}, bf16[32,128]{1,0:T(8,128)(2,1)S(1)}, u32[]{:S(2)}, u32[]{:S(2)}) collective-permute-start(bf16[32,128]{1,0:T(8,128)(2,1)S(1)} %get-tuple-element.26), channel_id=1, source_target_pairs={{0,4},{1,5},{2,6},{3,7},{4,0},{5,1},{6,2},{7,3},{8,12},{9,13},{10,... | collective-permute-start | bytes 24584 | tf_op jit(solution)/shard_map/ppermute | solution.py:398
  19.0 4.5 %collective-permute-start.9 = (bf16[32,128]{1,0:T(8,128)(2,1)S(1)}, bf16[32,128]{1,0:T(8,128)(2,1)S(1)}, u32[]{:S(2)}, u32[]{:S(2)}) collective-permute-start(bf16[32,128]{1,0:T(8,128)(2,1)S(1)} %get-tuple-element.25), channel_id=1, source_target_pairs={{0,2},{1,3},{2,0},{3,1},{4,6},{5,7},{6,4},{7,5},{8,10},{9,11},{10,... | collective-permute-start | bytes 24584 | tf_op jit(solution)/shard_map/ppermute | solution.py:398

commit v10 on v9

--- a/solution.py
+++ b/solution.py
@@ -221,7 +221,7 @@
     squares_ref,
     *refs,
 ):
-    *out_refs, field, spread, stage = refs
+    *out_refs, field, stage = refs
     columns = len(out_refs)
     lanes = squares_ref.shape[1]
     bases = squares_ref.shape[0] // lanes
@@ -243,16 +243,20 @@
         place(1 - odd, 2 * at + 1 - side, even_mate[at])
         place(odd, 2 * at + side, odd_own[at])
         place(odd, 2 * at + 1 - side, odd_mate[at])
-    for row in range(rows):
-        over = jnp.dot(
-            table_ref[row, :, : 2 * places], field[row], preferred_element_type=F32
+    over = [
+        jnp.dot(table_ref[row, :, : 2 * places], field[row], preferred_element_type=F32)
+        for row in range(rows)
+    ]
+    mixed = None
+    for basis in range(bases):
+        taken = slice(basis * half, (basis + 1) * half)
+        both = [(over[row][taken] + part_ref[row, taken]).astype(BF16) for row in range(rows)]
+        product = jnp.dot(
+            jnp.concatenate(both, axis=0)[:, :block],
+            squares_ref[basis * lanes : basis * lanes + block],
+            preferred_element_type=F32,
         )
-        over = (over + part_ref[row]).astype(BF16)
-        for basis in range(bases):
-            spread[row * half : (row + 1) * half, basis * lanes : (basis + 1) * lanes] = over[
-                basis * half : (basis + 1) * half
-            ]
-    mixed = jnp.dot(spread[...], squares_ref[...], preferred_element_type=F32)
+        mixed = product if mixed is None else mixed + product
     upper = lax.broadcasted_iota(jnp.int32, (SUBLANES, lanes), 0) < rest
     top, bottom = mixed[:half], mixed[half:]
     for target in range(columns):
@@ -523,7 +527,6 @@
         messages,
         [
             pltpu.VMEM((rows, 2 * places, lanes), BF16),
-            pltpu.VMEM((rows * columns * width, bases * lanes), BF16),
             pltpu.VMEM((columns, height, LANES), BF16),
         ],
         10**10,

time: 25 us -> 25 us (level)
  no operation moved by 1% of the time
where the time goes in v10:
time: 25 us; the launch traced here: 24.8 us
  starting transfers between devices  15.5 us (62%)
  waiting for transfers between devices  4.94 us (20%)
  Pallas kernels  4.23 us (17%)
    ppermute x6, starting transfers between devices, over_columns(): return lax.ppermute(message, 'lon', pairs) if apart else message  10.2 us
    pallas_call x11, Pallas kernels, call(): pl.pallas_call(kernel, out_shape=out_shape, in_specs=[VMEM] * len(operand...  4.23 us
    ppermute x5, starting transfers between devices, swap(): return lax.ppermute(block, ('lat', 'lon'), pairs)  3.79 us
    ppermute x6, waiting for transfers between devices, over_columns(): return lax.ppermute(message, 'lon', pairs) if apart else message  3.43 us
    ppermute x5, waiting for transfers between devices, swap(): return lax.ppermute(block, ('lat', 'lon'), pairs)  1.5 us
    ppermute x1, starting transfers between devices, over_sides(): return lax.ppermute(block, 'lon', [(i, i ^ 1) for i in range(count)])  1.49 us
  transfers between devices with their start and end apart: 12, of which 6 were waited for; matrix products, arithmetic and copies ran while one was open for 0% of the time, Pallas kernels for 8%

profile of v10, /device:TPU:0, one launch (start us, length us, event | category | flops | bytes accessed | tf_op | source)
XLA Modules:
  0.0 24.8 jit_solution(1656430813841836714)
XLA Ops:
  0.0 0.0 copy-start.2
  0.0 4.0 %collective-permute-start = (bf16[12,2,640]{2,1,0:T(2,128)(2,1)}, bf16[12,2,640]{2,1,0:T(2,128)(2,1)S(1)}, u32[]{:S(2)}, u32[]{:S(2)}) collective-permute-start(bf16[12,2,640]{2,1,0:T(2,128)(2,1)} %bitcast.6), channel_id=1, source_target_pairs={{0,4},{1,5},{2,6},{3,7},{4,0},{5,1},{6,2},{7,3},{8,12},{9,13},{10,... | collective-permute-start | bytes 92168 | tf_op jit(solution)/shard_map/ppermute | solution.py:402
  4.1 0.0 copy-done.2
  4.1 0.0 copy-start.1
  4.1 0.0 copy-start.3
  4.1 0.0 copy-start.4
  4.1 0.2 pack.1
  4.3 1.7 %collective-permute-start.1 = (bf16[32,128]{1,0:T(8,128)(2,1)S(1)}, bf16[32,128]{1,0:T(8,128)(2,1)S(1)}, u32[]{:S(2)}, u32[]{:S(2)}) collective-permute-start(bf16[32,128]{1,0:T(8,128)(2,1)S(1)} %get-tuple-element.20), channel_id=1, source_target_pairs={{0,6},{1,7},{2,4},{3,5},{4,2},{5,3},{6,0},{7,1},{8,14},{9,15},{10,... | collective-permute-start | bytes 24584 | tf_op jit(solution)/shard_map/ppermute | solution.py:402
  6.0 0.0 collective-permute-start.2
  6.0 0.0 copy-done.1
  6.0 1.5 %collective-permute-start.8 = (bf16[9,20,80]{2,1,0:T(8,128)(2,1)S(1)}, bf16[9,20,80]{2,1,0:T(8,128)(2,1)S(1)}, u32[]{:S(2)}, u32[]{:S(2)}) collective-permute-start(bf16[9,20,80]{2,1,0:T(8,128)(2,1)S(1)} %bitcast.4), channel_id=1, source_target_pairs={{0,1},{1,0},{2,3},{3,2},{4,5},{5,4},{6,7},{7,6},{8,9},{9,8},{10,11... | collective-permute-start | bytes 86408 | tf_op jit(solution)/shard_map/ppermute | solution.py:406
  7.5 0.0 copy-done.3
  7.5 0.0 copy-done.4
  7.5 0.4 %tables.1.table_ref = bf16[2,432,384]{2,1,0:T(8,128)(2,1)S(1)} custom-call(bf16[9,96]{1,0:T(8,128)(2,1)S(1)} %copy-done.3, bf16[3,2,9]{2,1,0:T(2,128)(2,1)S(1)} %bitcast.9, s32[96,128]{1,0:T(8,128)S(1)} %apart.1.apart_ref), custom_call_target="tpu_custom_call" | custom-call | flops 1000000 | bytes 1000000 | tf_op jit(solution)/shard_map/tables/pallas_call | solution.py:388
  7.9 0.0 collective-permute-done.raw_ref
  7.9 0.2 cut.1.refs_0_
  8.1 1.7 %collective-permute-done.1.refs_1_ = bf16[32,128]{1,0:T(8,128)(2,1)S(1)} collective-permute-done((bf16[32,128]{1,0:T(8,128)(2,1)S(1)}, bf16[32,128]{1,0:T(8,128)(2,1)S(1)}, u32[]{:S(2)}, u32[]{:S(2)}) %collective-permute-start.1) | collective-permute-done | bytes 8224 | tf_op jit(solution)/shard_map/ppermute | solution.py:402
  9.8 0.0 collective-permute-done.2.refs_2_
  9.8 1.6 %collective-permute-start.6 = (bf16[4,32,128]{2,1,0:T(8,128)(2,1)S(1)}, bf16[4,32,128]{2,1,0:T(8,128)(2,1)S(1)}, u32[]{:S(2)}, u32[]{:S(2)}) collective-permute-start(bf16[4,32,128]{2,1,0:T(8,128)(2,1)S(1)} %join_columns.1.own_ref), channel_id=1, source_target_pairs={{0,1},{1,0},{2,3},{3,2},{4,5},{5,4},{6,7},{7,6},{8,9},{9,8},{10,11... | collective-permute-start | bytes 98312 | tf_op jit(solution)/shard_map/ppermute | solution.py:415
  11.4 0.1 unpack.1.own
  11.5 0.5 %collective-permute-start.3 = (bf16[4,32,128]{2,1,0:T(8,128)(2,1)S(1)}, bf16[4,32,128]{2,1,0:T(8,128)(2,1)S(1)}, u32[]{:S(2)}, u32[]{:S(2)}) collective-permute-start(bf16[4,32,128]{2,1,0:T(8,128)(2,1)S(1)} %join_columns.1.own_ref), channel_id=1, source_target_pairs={{0,1},{1,0},{2,3},{3,2},{4,5},{5,4},{6,7},{7,6},{8,17},{9,16},{10,... | collective-permute-start | bytes 98312 | tf_op jit(solution)/shard_map/ppermute | solution.py:415
  12.0 1.5 %collective-permute-start.4 = (bf16[4,32,128]{2,1,0:T(8,128)(2,1)S(1)}, bf16[4,32,128]{2,1,0:T(8,128)(2,1)S(1)}, u32[]{:S(2)}, u32[]{:S(2)}) collective-permute-start(bf16[4,32,128]{2,1,0:T(8,128)(2,1)S(1)} %join_columns.1.own_ref), channel_id=1, source_target_pairs={{0,1},{1,0},{2,3},{3,2},{4,5},{5,4},{6,7},{7,6},{8,16},{9,17},{10,... | collective-permute-start | bytes 98312 | tf_op jit(solution)/shard_map/ppermute | solution.py:415
  13.5 0.0 collective-permute-start.5
  13.5 0.0 collective-permute-done.8.mate_ref
  13.5 0.3 %collective-permute-done.6.mate = bf16[4,32,128]{2,1,0:T(8,128)(2,1)S(1)} collective-permute-done((bf16[4,32,128]{2,1,0:T(8,128)(2,1)S(1)}, bf16[4,32,128]{2,1,0:T(8,128)(2,1)S(1)}, u32[]{:S(2)}, u32[]{:S(2)}) %collective-permute-start.6) | collective-permute-done | bytes 32800 | tf_op jit(solution)/shard_map/ppermute | solution.py:415
  13.8 0.2 collective-permute-start.7
  14.0 0.5 %squares.1.squares_ref = bf16[2304,256]{1,0:T(8,128)(2,1)S(1)} custom-call(bf16[9,20,80]{2,1,0:T(8,128)(2,1)S(1)} %bitcast.5, bf16[9,20,80]{2,1,0:T(8,128)(2,1)S(1)} %collective-permute-done.8.mate_ref), custom_call_target="tpu_custom_call" | custom-call | flops 300000000 | bytes 1000000 | tf_op jit(solution)/shard_map/squares/pallas_call | solution.py:388
  14.6 0.3 %conv_own.1.part_ref = f32[2,432,256]{2,1,0:T(8,128)S(1)} custom-call(bf16[4,32,128]{2,1,0:T(8,128)(2,1)S(1)} %collective-permute-done.6.mate, bf16[2,4,16,256]{3,2,1,0:T(8,128)(2,1)S(1)} %unpack.1.own, bf16[2,432,384]{2,1,0:T(8,128)(2,1)S(1)} %tables.1.table_ref), custom_call_target="tpu_custom_call" | custom-call | flops 300000000 | bytes 1000000 | tf_op jit(solution)/shard_map/conv_own/pallas_call | solution.py:388
  14.9 0.0 copy-start
  14.9 0.5 %collective-permute-done.3.odd_mate = bf16[4,32,128]{2,1,0:T(8,128)(2,1)S(1)} collective-permute-done((bf16[4,32,128]{2,1,0:T(8,128)(2,1)S(1)}, bf16[4,32,128]{2,1,0:T(8,128)(2,1)S(1)}, u32[]{:S(2)}, u32[]{:S(2)}) %collective-permute-start.3) | collective-permute-done | bytes 32800 | tf_op jit(solution)/shard_map/ppermute | solution.py:415
  15.4 0.7 %collective-permute-done.4.odd_own = bf16[4,32,128]{2,1,0:T(8,128)(2,1)S(1)} collective-permute-done((bf16[4,32,128]{2,1,0:T(8,128)(2,1)S(1)}, bf16[4,32,128]{2,1,0:T(8,128)(2,1)S(1)}, u32[]{:S(2)}, u32[]{:S(2)}) %collective-permute-start.4) | collective-permute-done | bytes 32800 | tf_op jit(solution)/shard_map/ppermute | solution.py:415
  16.1 0.0 collective-permute-done.5.even_own
  16.1 0.0 collective-permute-done.7.even_mate
  16.1 0.8 %conv.1 = (bf16[32,128]{1,0:T(8,128)(2,1)S(1)}, bf16[32,128]{1,0:T(8,128)(2,1)S(1)}, bf16[32,128]{1,0:T(8,128)(2,1)S(1)}, bf16[32,128]{1,0:T(8,128)(2,1)S(1)}) custom-call(bf16[4,32,128]{2,1,0:T(8,128)(2,1)S(1)} %collective-permute-done.3.odd_mate, bf16[4,32,128]{2,1,0:T(8,128)(2,1)S(1)} %collective-permute-done.4.odd_own, ...), custom_call_target="tpu_custom_call" | custom-call | flops 10000000000 | bytes 1000000 | tf_op jit(solution)/shard_map/conv/pallas_call | solution.py:388
  16.9 0.0 copy-start.5
  16.9 2.0 %collective-permute-start.11 = (bf16[32,128]{1,0:T(8,128)(2,1)S(1)}, bf16[32,128]{1,0:T(8,128)(2,1)S(1)}, u32[]{:S(2)}, u32[]{:S(2)}) collective-permute-start(bf16[32,128]{1,0:T(8,128)(2,1)S(1)} %get-tuple-element.28), channel_id=1, source_target_pairs={{0,6},{1,7},{2,4},{3,5},{4,2},{5,3},{6,0},{7,1},{8,14},{9,15},{10,... | collective-permute-start | bytes 24584 | tf_op jit(solution)/shard_map/ppermute | solution.py:402
  18.9 0.0 collective-permute-start.10
  18.9 2.4 %collective-permute-start.9 = (bf16[32,128]{1,0:T(8,128)(2,1)S(1)}, bf16[32,128]{1,0:T(8,128)(2,1)S(1)}, u32[]{:S(2)}, u32[]{:S(2)}) collective-permute-start(bf16[32,128]{1,0:T(8,128)(2,1)S(1)} %get-tuple-element.25), channel_id=1, source_target_pairs={{0,2},{1,3},{2,0},{3,1},{4,6},{5,7},{6,4},{7,5},{8,10},{9,11},{10,... | collective-permute-start | bytes 24584 | tf_op jit(solution)/shard_map/ppermute | solution.py:402
  21.4 1.1 %collective-permute-done.11.first_ref = bf16[32,128]{1,0:T(8,128)(2,1)S(1)} collective-permute-done((bf16[32,128]{1,0:T(8,128)(2,1)S(1)}, bf16[32,128]{1,0:T(8,128)(2,1)S(1)}, u32[]{:S(2)}, u32[]{:S(2)}) %collective-permute-start.11) | collective-permute-done | bytes 8224 | tf_op jit(solution)/shard_map/ppermute | solution.py:402
  22.4 0.0 copy-done
  22.4 0.4 %lift.1 = (f32[4,24,256]{2,1,0:T(8,128)S(1)}, f32[24,640]{1,0:T(8,128)S(1)}, f32[32,1280]{1,0:T(8,128)S(1)}, f32[2,24,128]{2,1,0:T(8,128)S(1)}) custom-call(bf16[32,128]{1,0:T(8,128)(2,1)S(1)} %get-tuple-element.27.own_ref, bf16[32,128]{1,0:T(8,128)(2,1)S(1)} %collective-permute-done.11.first_ref, bf16[12,2,640]{2,1,0:T(2,128)(2,1)S(1)} %bitcast.8, ...), custom_call_target="tpu_custom_call" | custom-call | flops 100000000 | bytes 1000000 | tf_op jit(solution)/shard_map/lift/pallas_call | solution.py:388
  22.8 0.7 %collective-permute-done.10.refs_1_ = bf16[32,128]{1,0:T(8,128)(2,1)S(1)} collective-permute-done((bf16[32,128]{1,0:T(8,128)(2,1)S(1)}, bf16[32,128]{1,0:T(8,128)(2,1)S(1)}, u32[]{:S(2)}, u32[]{:S(2)}) %collective-permute-start.10) | collective-permute-done | bytes 8224 | tf_op jit(solution)/shard_map/ppermute | solution.py:402
  23.5 0.0 collective-permute-done.9.refs_0_
  23.5 0.0 copy-done.5
  23.5 1.3 %tail.1 = bf16[12,2,640]{2,1,0:T(2,128)(2,1)} custom-call(bf16[32,128]{1,0:T(8,128)(2,1)S(1)} %collective-permute-done.9.refs_0_, bf16[32,128]{1,0:T(8,128)(2,1)S(1)} %collective-permute-done.10.refs_1_, f32[4,24,256]{2,1,0:T(8,128)S(1)} %get-tuple-element.29.refs_2_, f32[24,640]{1,0:T(8,128)S(1)} %get-tuple-element.30.refs_3_, ...), custom_call_target="tpu_custom_call" | custom-call | flops 1000000000 | bytes 1000000 | tf_op jit(solution)/shard_map/tail/pallas_call | solution.py:388
  (2 shorter events, 0.0 us)
Async XLA Ops:
  0.0 4.1 %copy-start.2 = (bf16[2,12,640]{2,0,1:T(2,128)(2,1)S(1)}, bf16[2,12,640]{2,0,1:T(2,128)(2,1)}, u32[]{:S(2)}) copy-start(bf16[2,12,640]{2,0,1:T(2,128)(2,1)} %param.7) | copy-start | bytes 92164
  0.0 7.9 %collective-permute-start = (bf16[12,2,640]{2,1,0:T(2,128)(2,1)}, bf16[12,2,640]{2,1,0:T(2,128)(2,1)S(1)}, u32[]{:S(2)}, u32[]{:S(2)}) collective-permute-start(bf16[12,2,640]{2,1,0:T(2,128)(2,1)} %bitcast.6), channel_id=1, source_target_pairs={{0,4},{1,5},{2,6},{3,7},{4,0},{5,1},{6,2},{7,3},{8,12},{9,13},{10,... | collective-permute-start | bytes 92168 | tf_op jit(solution)/shard_map/ppermute | solution.py:402
  4.1 2.0 %copy-start.1 = (bf16[9,80,20]{1,2,0:T(8,128)(2,1)S(1)}, bf16[9,80,20]{1,2,0:T(8,128)(2,1)}, u32[]{:S(2)}) copy-start(bf16[9,80,20]{1,2,0:T(8,128)(2,1)} %param.9) | copy-start | bytes 86404
  4.1 3.4 %copy-start.3 = (bf16[9,96]{1,0:T(8,128)(2,1)S(1)}, bf16[9,96]{1,0:T(8,128)(2,1)}, u32[]{:S(2)}) copy-start(bf16[9,96]{1,0:T(8,128)(2,1)} %filter_ref.1) | copy-start | bytes 5188
  4.1 3.4 %copy-start.4 = (bf16[9,2,3]{0,1,2:T(2,128)(2,1)S(1)}, bf16[9,2,3]{0,1,2:T(2,128)(2,1)}, u32[]{:S(2)}) copy-start(bf16[9,2,3]{0,1,2:T(2,128)(2,1)} %param.10) | copy-start | bytes 328
  4.3 5.5 %collective-permute-start.1 = (bf16[32,128]{1,0:T(8,128)(2,1)S(1)}, bf16[32,128]{1,0:T(8,128)(2,1)S(1)}, u32[]{:S(2)}, u32[]{:S(2)}) collective-permute-start(bf16[32,128]{1,0:T(8,128)(2,1)S(1)} %get-tuple-element.20), channel_id=1, source_target_pairs={{0,6},{1,7},{2,4},{3,5},{4,2},{5,3},{6,0},{7,1},{8,14},{9,15},{10,... | collective-permute-start | bytes 24584 | tf_op jit(solution)/shard_map/ppermute | solution.py:402
  6.0 3.8 %collective-permute-start.2 = (bf16[32,128]{1,0:T(8,128)(2,1)S(1)}, bf16[32,128]{1,0:T(8,128)(2,1)S(1)}, u32[]{:S(2)}, u32[]{:S(2)}) collective-permute-start(bf16[32,128]{1,0:T(8,128)(2,1)S(1)} %get-tuple-element.21), channel_id=1, source_target_pairs={{0,2},{1,3},{2,0},{3,1},{4,6},{5,7},{6,4},{7,5},{8,10},{9,11},{10,... | collective-permute-start | bytes 24584 | tf_op jit(solution)/shard_map/ppermute | solution.py:402
  6.0 7.4 %collective-permute-start.8 = (bf16[9,20,80]{2,1,0:T(8,128)(2,1)S(1)}, bf16[9,20,80]{2,1,0:T(8,128)(2,1)S(1)}, u32[]{:S(2)}, u32[]{:S(2)}) collective-permute-start(bf16[9,20,80]{2,1,0:T(8,128)(2,1)S(1)} %bitcast.4), channel_id=1, source_target_pairs={{0,1},{1,0},{2,3},{3,2},{4,5},{5,4},{6,7},{7,6},{8,9},{9,8},{10,11... | collective-permute-start | bytes 86408 | tf_op jit(solution)/shard_map/ppermute | solution.py:406
  9.8 4.0 %collective-permute-start.6 = (bf16[4,32,128]{2,1,0:T(8,128)(2,1)S(1)}, bf16[4,32,128]{2,1,0:T(8,128)(2,1)S(1)}, u32[]{:S(2)}, u32[]{:S(2)}) collective-permute-start(bf16[4,32,128]{2,1,0:T(8,128)(2,1)S(1)} %join_columns.1.own_ref), channel_id=1, source_target_pairs={{0,1},{1,0},{2,3},{3,2},{4,5},{5,4},{6,7},{7,6},{8,9},{9,8},{10,11... | collective-permute-start | bytes 98312 | tf_op jit(solution)/shard_map/ppermute | solution.py:415
  11.5 3.9 %collective-permute-start.3 = (bf16[4,32,128]{2,1,0:T(8,128)(2,1)S(1)}, bf16[4,32,128]{2,1,0:T(8,128)(2,1)S(1)}, u32[]{:S(2)}, u32[]{:S(2)}) collective-permute-start(bf16[4,32,128]{2,1,0:T(8,128)(2,1)S(1)} %join_columns.1.own_ref), channel_id=1, source_target_pairs={{0,1},{1,0},{2,3},{3,2},{4,5},{5,4},{6,7},{7,6},{8,17},{9,16},{10,... | collective-permute-start | bytes 98312 | tf_op jit(solution)/shard_map/ppermute | solution.py:415
  12.0 4.1 %collective-permute-start.4 = (bf16[4,32,128]{2,1,0:T(8,128)(2,1)S(1)}, bf16[4,32,128]{2,1,0:T(8,128)(2,1)S(1)}, u32[]{:S(2)}, u32[]{:S(2)}) collective-permute-start(bf16[4,32,128]{2,1,0:T(8,128)(2,1)S(1)} %join_columns.1.own_ref), channel_id=1, source_target_pairs={{0,1},{1,0},{2,3},{3,2},{4,5},{5,4},{6,7},{7,6},{8,16},{9,17},{10,... | collective-permute-start | bytes 98312 | tf_op jit(solution)/shard_map/ppermute | solution.py:415
  13.5 2.6 %collective-permute-start.5 = (bf16[4,32,128]{2,1,0:T(8,128)(2,1)S(1)}, bf16[4,32,128]{2,1,0:T(8,128)(2,1)S(1)}, u32[]{:S(2)}, u32[]{:S(2)}) collective-permute-start(bf16[4,32,128]{2,1,0:T(8,128)(2,1)S(1)} %join_columns.1.own_ref), channel_id=1, source_target_pairs={{0,8},{1,9},{2,10},{3,11},{4,12},{5,13},{6,14},{7,15},{8,0},{9,1},... | collective-permute-start | bytes 98312 | tf_op jit(solution)/shard_map/ppermute | solution.py:415
  13.8 2.3 %collective-permute-start.7 = (bf16[4,32,128]{2,1,0:T(8,128)(2,1)S(1)}, bf16[4,32,128]{2,1,0:T(8,128)(2,1)S(1)}, u32[]{:S(2)}, u32[]{:S(2)}) collective-permute-start(bf16[4,32,128]{2,1,0:T(8,128)(2,1)S(1)} %collective-permute-done.6.mate), channel_id=1, source_target_pairs={{0,8},{1,9},{2,10},{3,11},{4,12},{5,13},{6,14},{7,15},{8,0},{9,1},... | collective-permute-start | bytes 98312 | tf_op jit(solution)/shard_map/ppermute | solution.py:415
  14.9 7.5 %copy-start = (bf16[640,1280]{1,0:T(8,128)(2,1)S(1)}, bf16[640,1280]{1,0:T(8,128)(2,1)}, u32[]{:S(2)}) copy-start(bf16[640,1280]{1,0:T(8,128)(2,1)} %refs_6_.1) | copy-start | bytes 4915204
  16.9 6.6 %copy-start.5 = (bf16[1280,640]{1,0:T(8,128)(2,1)S(1)}, bf16[1280,640]{1,0:T(8,128)(2,1)}, u32[]{:S(2)}) copy-start(bf16[1280,640]{1,0:T(8,128)(2,1)} %refs_7_.1) | copy-start | bytes 4915204
  16.9 5.5 %collective-permute-start.11 = (bf16[32,128]{1,0:T(8,128)(2,1)S(1)}, bf16[32,128]{1,0:T(8,128)(2,1)S(1)}, u32[]{:S(2)}, u32[]{:S(2)}) collective-permute-start(bf16[32,128]{1,0:T(8,128)(2,1)S(1)} %get-tuple-element.28), channel_id=1, source_target_pairs={{0,6},{1,7},{2,4},{3,5},{4,2},{5,3},{6,0},{7,1},{8,14},{9,15},{10,... | collective-permute-start | bytes 24584 | tf_op jit(solution)/shard_map/ppermute | solution.py:402
  18.9 4.5 %collective-permute-start.10 = (bf16[32,128]{1,0:T(8,128)(2,1)S(1)}, bf16[32,128]{1,0:T(8,128)(2,1)S(1)}, u32[]{:S(2)}, u32[]{:S(2)}) collective-permute-start(bf16[32,128]{1,0:T(8,128)(2,1)S(1)} %get-tuple-element.26), channel_id=1, source_target_pairs={{0,4},{1,5},{2,6},{3,7},{4,0},{5,1},{6,2},{7,3},{8,12},{9,13},{10,... | collective-permute-start | bytes 24584 | tf_op jit(solution)/shard_map/ppermute | solution.py:402
  18.9 4.5 %collective-permute-start.9 = (bf16[32,128]{1,0:T(8,128)(2,1)S(1)}, bf16[32,128]{1,0:T(8,128)(2,1)S(1)}, u32[]{:S(2)}, u32[]{:S(2)}) collective-permute-start(bf16[32,128]{1,0:T(8,128)(2,1)S(1)} %get-tuple-element.25), channel_id=1, source_target_pairs={{0,2},{1,3},{2,0},{3,1},{4,6},{5,7},{6,4},{7,5},{8,10},{9,11},{10,... | collective-permute-start | bytes 24584 | tf_op jit(solution)/shard_map/ppermute | solution.py:402

commit v11 on v10

--- a/solution.py
+++ b/solution.py
@@ -415,9 +415,11 @@
     return lax.ppermute(block, ("lat", "lon"), pairs)
 
 
-def odd_pair(lat, lon, to_lon, rows):
+def odd_pair(lat, lon, other_side, rows):
     to = lat + 1 if lat % 2 else lat - 1
-    return (to, to_lon) if 0 <= to < rows else (lat, lon ^ 1)
+    if 0 <= to < rows:
+        return to, lon ^ other_side
+    return (lat, lon ^ 1) if other_side else (rows - 1 - lat, lon)
 
 
 def local(latent, lon_filter, mix_weight, band_weight, offsets, w_up, w_down):
@@ -489,8 +491,8 @@
     )
     lats = lax.axis_size("lat")
     mate_side = swap(own_side, count, lambda lat, lon: (lat, lon ^ 1))
-    odd_mate = swap(own_side, count, lambda lat, lon: odd_pair(lat, lon, lon ^ 1, lats))
-    odd_own = swap(own_side, count, lambda lat, lon: odd_pair(lat, lon, lon, lats))
+    odd_mate = swap(own_side, count, lambda lat, lon: odd_pair(lat, lon, 1, lats))
+    odd_own = swap(own_side, count, lambda lat, lon: odd_pair(lat, lon, 0, lats))
     own_rows = call(
         functools.partial(unpack_kernel, block, width),
         "unpack",

time: 25 us -> 24.3 us (0.972)
  starting transfers between devices: 15.5 us -> 15 us
    ppermute x5, starting transfers between devices: 3.79 us -> 3.27 us  [swap(): return lax.ppermute(block, ('lat', 'lon'), pairs)]
  transfers between devices with their start and end apart: 12 -> 12, of which waited for: 6 -> 6; matrix products, arithmetic and copies ran while one was open for 0% -> 0% of each run, Pallas kernels for 8% -> 9%
where the time goes in v11:
time: 24.3 us; the launch traced here: 24.2 us
  starting transfers between devices  15 us (62%)
  waiting for transfers between devices  4.8 us (20%)
  Pallas kernels  4.22 us (17%)
    ppermute x6, starting transfers between devices, over_columns(): return lax.ppermute(message, 'lon', pairs) if apart else message  10.3 us
    pallas_call x11, Pallas kernels, call(): pl.pallas_call(kernel, out_shape=out_shape, in_specs=[VMEM] * len(operand...  4.22 us
    ppermute x6, waiting for transfers between devices, over_columns(): return lax.ppermute(message, 'lon', pairs) if apart else message  3.42 us
    ppermute x5, starting transfers between devices, swap(): return lax.ppermute(block, ('lat', 'lon'), pairs)  3.27 us
    ppermute x1, starting transfers between devices, over_sides(): return lax.ppermute(block, 'lon', [(i, i ^ 1) for i in range(count)])  1.49 us
    ppermute x5, waiting for transfers between devices, swap(): return lax.ppermute(block, ('lat', 'lon'), pairs)  1.37 us
  transfers between devices with their start and end apart: 12, of which 6 were waited for; matrix products, arithmetic and copies ran while one was open for 0% of the time, Pallas kernels for 9%

profile of v11, /device:TPU:0, one launch (start us, length us, event | category | flops | bytes accessed | tf_op | source)
XLA Modules:
  0.0 24.2 jit_solution(360189173269669849)
XLA Ops:
  0.0 0.0 copy-start.2
  0.0 4.0 %collective-permute-start = (bf16[12,2,640]{2,1,0:T(2,128)(2,1)}, bf16[12,2,640]{2,1,0:T(2,128)(2,1)S(1)}, u32[]{:S(2)}, u32[]{:S(2)}) collective-permute-start(bf16[12,2,640]{2,1,0:T(2,128)(2,1)} %bitcast.6), channel_id=1, source_target_pairs={{0,4},{1,5},{2,6},{3,7},{4,0},{5,1},{6,2},{7,3},{8,12},{9,13},{10,... | collective-permute-start | bytes 92168 | tf_op jit(solution)/shard_map/ppermute | solution.py:402
  4.1 0.0 copy-done.2
  4.1 0.0 copy-start.1
  4.1 0.0 copy-start.3
  4.1 0.0 copy-start.4
  4.1 0.2 pack.1
  4.3 1.7 %collective-permute-start.1 = (bf16[32,128]{1,0:T(8,128)(2,1)S(1)}, bf16[32,128]{1,0:T(8,128)(2,1)S(1)}, u32[]{:S(2)}, u32[]{:S(2)}) collective-permute-start(bf16[32,128]{1,0:T(8,128)(2,1)S(1)} %get-tuple-element.20), channel_id=1, source_target_pairs={{0,6},{1,7},{2,4},{3,5},{4,2},{5,3},{6,0},{7,1},{8,14},{9,15},{10,... | collective-permute-start | bytes 24584 | tf_op jit(solution)/shard_map/ppermute | solution.py:402
  6.0 0.0 collective-permute-start.2
  6.0 0.0 copy-done.1
  6.0 1.5 %collective-permute-start.8 = (bf16[9,20,80]{2,1,0:T(8,128)(2,1)S(1)}, bf16[9,20,80]{2,1,0:T(8,128)(2,1)S(1)}, u32[]{:S(2)}, u32[]{:S(2)}) collective-permute-start(bf16[9,20,80]{2,1,0:T(8,128)(2,1)S(1)} %bitcast.4), channel_id=1, source_target_pairs={{0,1},{1,0},{2,3},{3,2},{4,5},{5,4},{6,7},{7,6},{8,9},{9,8},{10,11... | collective-permute-start | bytes 86408 | tf_op jit(solution)/shard_map/ppermute | solution.py:406
  7.5 0.0 copy-done.3
  7.5 0.0 copy-done.4
  7.5 0.4 %tables.1.table_ref = bf16[2,432,384]{2,1,0:T(8,128)(2,1)S(1)} custom-call(bf16[9,96]{1,0:T(8,128)(2,1)S(1)} %copy-done.3, bf16[3,2,9]{2,1,0:T(2,128)(2,1)S(1)} %bitcast.9, s32[96,128]{1,0:T(8,128)S(1)} %apart.1.apart_ref), custom_call_target="tpu_custom_call" | custom-call | flops 1000000 | bytes 1000000 | tf_op jit(solution)/shard_map/tables/pallas_call | solution.py:388
  7.9 0.0 collective-permute-done.raw_ref
  7.9 0.2 cut.1.refs_0_
  8.1 1.7 %collective-permute-done.1.refs_1_ = bf16[32,128]{1,0:T(8,128)(2,1)S(1)} collective-permute-done((bf16[32,128]{1,0:T(8,128)(2,1)S(1)}, bf16[32,128]{1,0:T(8,128)(2,1)S(1)}, u32[]{:S(2)}, u32[]{:S(2)}) %collective-permute-start.1) | collective-permute-done | bytes 8224 | tf_op jit(solution)/shard_map/ppermute | solution.py:402
  9.8 0.0 collective-permute-done.2.refs_2_
  9.8 1.6 %collective-permute-start.6 = (bf16[4,32,128]{2,1,0:T(8,128)(2,1)S(1)}, bf16[4,32,128]{2,1,0:T(8,128)(2,1)S(1)}, u32[]{:S(2)}, u32[]{:S(2)}) collective-permute-start(bf16[4,32,128]{2,1,0:T(8,128)(2,1)S(1)} %join_columns.1.own_ref), channel_id=1, source_target_pairs={{0,1},{1,0},{2,3},{3,2},{4,5},{5,4},{6,7},{7,6},{8,9},{9,8},{10,11... | collective-permute-start | bytes 98312 | tf_op jit(solution)/shard_map/ppermute | solution.py:415
  11.4 0.1 unpack.1.own
  11.5 0.5 %collective-permute-start.3 = (bf16[4,32,128]{2,1,0:T(8,128)(2,1)S(1)}, bf16[4,32,128]{2,1,0:T(8,128)(2,1)S(1)}, u32[]{:S(2)}, u32[]{:S(2)}) collective-permute-start(bf16[4,32,128]{2,1,0:T(8,128)(2,1)S(1)} %join_columns.1.own_ref), channel_id=1, source_target_pairs={{0,1},{1,0},{2,3},{3,2},{4,5},{5,4},{6,7},{7,6},{8,17},{9,16},{10,... | collective-permute-start | bytes 98312 | tf_op jit(solution)/shard_map/ppermute | solution.py:415
  12.0 0.0 collective-permute-start.4
  12.0 1.2 %collective-permute-start.5 = (bf16[4,32,128]{2,1,0:T(8,128)(2,1)S(1)}, bf16[4,32,128]{2,1,0:T(8,128)(2,1)S(1)}, u32[]{:S(2)}, u32[]{:S(2)}) collective-permute-start(bf16[4,32,128]{2,1,0:T(8,128)(2,1)S(1)} %join_columns.1.own_ref), channel_id=1, source_target_pairs={{0,8},{1,9},{2,10},{3,11},{4,12},{5,13},{6,14},{7,15},{8,0},{9,1},... | collective-permute-start | bytes 98312 | tf_op jit(solution)/shard_map/ppermute | solution.py:415
  13.2 0.0 collective-permute-done.8.mate_ref
  13.2 0.6 %collective-permute-done.6.mate = bf16[4,32,128]{2,1,0:T(8,128)(2,1)S(1)} collective-permute-done((bf16[4,32,128]{2,1,0:T(8,128)(2,1)S(1)}, bf16[4,32,128]{2,1,0:T(8,128)(2,1)S(1)}, u32[]{:S(2)}, u32[]{:S(2)}) %collective-permute-start.6) | collective-permute-done | bytes 32800 | tf_op jit(solution)/shard_map/ppermute | solution.py:415
  13.8 0.0 collective-permute-start.7
  13.8 0.5 %squares.1.squares_ref = bf16[2304,256]{1,0:T(8,128)(2,1)S(1)} custom-call(bf16[9,20,80]{2,1,0:T(8,128)(2,1)S(1)} %bitcast.5, bf16[9,20,80]{2,1,0:T(8,128)(2,1)S(1)} %collective-permute-done.8.mate_ref), custom_call_target="tpu_custom_call" | custom-call | flops 300000000 | bytes 1000000 | tf_op jit(solution)/shard_map/squares/pallas_call | solution.py:388
  14.4 0.3 %conv_own.1.part_ref = f32[2,432,256]{2,1,0:T(8,128)S(1)} custom-call(bf16[4,32,128]{2,1,0:T(8,128)(2,1)S(1)} %collective-permute-done.6.mate, bf16[2,4,16,256]{3,2,1,0:T(8,128)(2,1)S(1)} %unpack.1.own, bf16[2,432,384]{2,1,0:T(8,128)(2,1)S(1)} %tables.1.table_ref), custom_call_target="tpu_custom_call" | custom-call | flops 300000000 | bytes 1000000 | tf_op jit(solution)/shard_map/conv_own/pallas_call | solution.py:388
  14.7 0.0 copy-start
  14.7 0.7 %collective-permute-done.3.odd_mate = bf16[4,32,128]{2,1,0:T(8,128)(2,1)S(1)} collective-permute-done((bf16[4,32,128]{2,1,0:T(8,128)(2,1)S(1)}, bf16[4,32,128]{2,1,0:T(8,128)(2,1)S(1)}, u32[]{:S(2)}, u32[]{:S(2)}) %collective-permute-start.3) | collective-permute-done | bytes 32800 | tf_op jit(solution)/shard_map/ppermute | solution.py:415
  15.4 0.1 collective-permute-done.4.odd_own
  15.5 0.0 collective-permute-done.5.even_own
  15.5 0.0 collective-permute-done.7.even_mate
  15.5 0.8 %conv.1 = (bf16[32,128]{1,0:T(8,128)(2,1)S(1)}, bf16[32,128]{1,0:T(8,128)(2,1)S(1)}, bf16[32,128]{1,0:T(8,128)(2,1)S(1)}, bf16[32,128]{1,0:T(8,128)(2,1)S(1)}) custom-call(bf16[4,32,128]{2,1,0:T(8,128)(2,1)S(1)} %collective-permute-done.3.odd_mate, bf16[4,32,128]{2,1,0:T(8,128)(2,1)S(1)} %collective-permute-done.4.odd_own, ...), custom_call_target="tpu_custom_call" | custom-call | flops 10000000000 | bytes 1000000 | tf_op jit(solution)/shard_map/conv/pallas_call | solution.py:388
  16.3 0.0 copy-start.5
  16.3 2.0 %collective-permute-start.11 = (bf16[32,128]{1,0:T(8,128)(2,1)S(1)}, bf16[32,128]{1,0:T(8,128)(2,1)S(1)}, u32[]{:S(2)}, u32[]{:S(2)}) collective-permute-start(bf16[32,128]{1,0:T(8,128)(2,1)S(1)} %get-tuple-element.28), channel_id=1, source_target_pairs={{0,6},{1,7},{2,4},{3,5},{4,2},{5,3},{6,0},{7,1},{8,14},{9,15},{10,... | collective-permute-start | bytes 24584 | tf_op jit(solution)/shard_map/ppermute | solution.py:402
  18.3 0.0 collective-permute-start.10
  18.3 2.5 %collective-permute-start.9 = (bf16[32,128]{1,0:T(8,128)(2,1)S(1)}, bf16[32,128]{1,0:T(8,128)(2,1)S(1)}, u32[]{:S(2)}, u32[]{:S(2)}) collective-permute-start(bf16[32,128]{1,0:T(8,128)(2,1)S(1)} %get-tuple-element.25), channel_id=1, source_target_pairs={{0,2},{1,3},{2,0},{3,1},{4,6},{5,7},{6,4},{7,5},{8,10},{9,11},{10,... | collective-permute-start | bytes 24584 | tf_op jit(solution)/shard_map/ppermute | solution.py:402
  20.7 1.1 %collective-permute-done.11.first_ref = bf16[32,128]{1,0:T(8,128)(2,1)S(1)} collective-permute-done((bf16[32,128]{1,0:T(8,128)(2,1)S(1)}, bf16[32,128]{1,0:T(8,128)(2,1)S(1)}, u32[]{:S(2)}, u32[]{:S(2)}) %collective-permute-start.11) | collective-permute-done | bytes 8224 | tf_op jit(solution)/shard_map/ppermute | solution.py:402
  21.9 0.0 copy-done
  21.9 0.4 %lift.1 = (f32[4,24,256]{2,1,0:T(8,128)S(1)}, f32[24,640]{1,0:T(8,128)S(1)}, f32[32,1280]{1,0:T(8,128)S(1)}, f32[2,24,128]{2,1,0:T(8,128)S(1)}) custom-call(bf16[32,128]{1,0:T(8,128)(2,1)S(1)} %get-tuple-element.27.own_ref, bf16[32,128]{1,0:T(8,128)(2,1)S(1)} %collective-permute-done.11.first_ref, bf16[12,2,640]{2,1,0:T(2,128)(2,1)S(1)} %bitcast.8, ...), custom_call_target="tpu_custom_call" | custom-call | flops 100000000 | bytes 1000000 | tf_op jit(solution)/shard_map/lift/pallas_call | solution.py:388
  22.2 0.6 %collective-permute-done.10.refs_1_ = bf16[32,128]{1,0:T(8,128)(2,1)S(1)} collective-permute-done((bf16[32,128]{1,0:T(8,128)(2,1)S(1)}, bf16[32,128]{1,0:T(8,128)(2,1)S(1)}, u32[]{:S(2)}, u32[]{:S(2)}) %collective-permute-start.10) | collective-permute-done | bytes 8224 | tf_op jit(solution)/shard_map/ppermute | solution.py:402
  22.8 0.0 collective-permute-done.9.refs_0_
  22.8 0.0 copy-done.5
  22.8 1.3 %tail.1 = bf16[12,2,640]{2,1,0:T(2,128)(2,1)} custom-call(bf16[32,128]{1,0:T(8,128)(2,1)S(1)} %collective-permute-done.9.refs_0_, bf16[32,128]{1,0:T(8,128)(2,1)S(1)} %collective-permute-done.10.refs_1_, f32[4,24,256]{2,1,0:T(8,128)S(1)} %get-tuple-element.29.refs_2_, f32[24,640]{1,0:T(8,128)S(1)} %get-tuple-element.30.refs_3_, ...), custom_call_target="tpu_custom_call" | custom-call | flops 1000000000 | bytes 1000000 | tf_op jit(solution)/shard_map/tail/pallas_call | solution.py:388
  (2 shorter events, 0.0 us)
Async XLA Ops:
  0.0 4.1 %copy-start.2 = (bf16[2,12,640]{2,0,1:T(2,128)(2,1)S(1)}, bf16[2,12,640]{2,0,1:T(2,128)(2,1)}, u32[]{:S(2)}) copy-start(bf16[2,12,640]{2,0,1:T(2,128)(2,1)} %param.7) | copy-start | bytes 92164
  0.0 7.9 %collective-permute-start = (bf16[12,2,640]{2,1,0:T(2,128)(2,1)}, bf16[12,2,640]{2,1,0:T(2,128)(2,1)S(1)}, u32[]{:S(2)}, u32[]{:S(2)}) collective-permute-start(bf16[12,2,640]{2,1,0:T(2,128)(2,1)} %bitcast.6), channel_id=1, source_target_pairs={{0,4},{1,5},{2,6},{3,7},{4,0},{5,1},{6,2},{7,3},{8,12},{9,13},{10,... | collective-permute-start | bytes 92168 | tf_op jit(solution)/shard_map/ppermute | solution.py:402
  4.1 2.0 %copy-start.1 = (bf16[9,80,20]{1,2,0:T(8,128)(2,1)S(1)}, bf16[9,80,20]{1,2,0:T(8,128)(2,1)}, u32[]{:S(2)}) copy-start(bf16[9,80,20]{1,2,0:T(8,128)(2,1)} %param.9) | copy-start | bytes 86404
  4.1 3.4 %copy-start.3 = (bf16[9,96]{1,0:T(8,128)(2,1)S(1)}, bf16[9,96]{1,0:T(8,128)(2,1)}, u32[]{:S(2)}) copy-start(bf16[9,96]{1,0:T(8,128)(2,1)} %filter_ref.1) | copy-start | bytes 5188
  4.1 3.4 %copy-start.4 = (bf16[9,2,3]{0,1,2:T(2,128)(2,1)S(1)}, bf16[9,2,3]{0,1,2:T(2,128)(2,1)}, u32[]{:S(2)}) copy-start(bf16[9,2,3]{0,1,2:T(2,128)(2,1)} %param.10) | copy-start | bytes 328
  4.3 5.5 %collective-permute-start.1 = (bf16[32,128]{1,0:T(8,128)(2,1)S(1)}, bf16[32,128]{1,0:T(8,128)(2,1)S(1)}, u32[]{:S(2)}, u32[]{:S(2)}) collective-permute-start(bf16[32,128]{1,0:T(8,128)(2,1)S(1)} %get-tuple-element.20), channel_id=1, source_target_pairs={{0,6},{1,7},{2,4},{3,5},{4,2},{5,3},{6,0},{7,1},{8,14},{9,15},{10,... | collective-permute-start | bytes 24584 | tf_op jit(solution)/shard_map/ppermute | solution.py:402
  6.0 3.8 %collective-permute-start.2 = (bf16[32,128]{1,0:T(8,128)(2,1)S(1)}, bf16[32,128]{1,0:T(8,128)(2,1)S(1)}, u32[]{:S(2)}, u32[]{:S(2)}) collective-permute-start(bf16[32,128]{1,0:T(8,128)(2,1)S(1)} %get-tuple-element.21), channel_id=1, source_target_pairs={{0,2},{1,3},{2,0},{3,1},{4,6},{5,7},{6,4},{7,5},{8,10},{9,11},{10,... | collective-permute-start | bytes 24584 | tf_op jit(solution)/shard_map/ppermute | solution.py:402
  6.0 7.1 %collective-permute-start.8 = (bf16[9,20,80]{2,1,0:T(8,128)(2,1)S(1)}, bf16[9,20,80]{2,1,0:T(8,128)(2,1)S(1)}, u32[]{:S(2)}, u32[]{:S(2)}) collective-permute-start(bf16[9,20,80]{2,1,0:T(8,128)(2,1)S(1)} %bitcast.4), channel_id=1, source_target_pairs={{0,1},{1,0},{2,3},{3,2},{4,5},{5,4},{6,7},{7,6},{8,9},{9,8},{10,11... | collective-permute-start | bytes 86408 | tf_op jit(solution)/shard_map/ppermute | solution.py:406
  9.8 4.0 %collective-permute-start.6 = (bf16[4,32,128]{2,1,0:T(8,128)(2,1)S(1)}, bf16[4,32,128]{2,1,0:T(8,128)(2,1)S(1)}, u32[]{:S(2)}, u32[]{:S(2)}) collective-permute-start(bf16[4,32,128]{2,1,0:T(8,128)(2,1)S(1)} %join_columns.1.own_ref), channel_id=1, source_target_pairs={{0,1},{1,0},{2,3},{3,2},{4,5},{5,4},{6,7},{7,6},{8,9},{9,8},{10,11... | collective-permute-start | bytes 98312 | tf_op jit(solution)/shard_map/ppermute | solution.py:415
  11.5 3.9 %collective-permute-start.3 = (bf16[4,32,128]{2,1,0:T(8,128)(2,1)S(1)}, bf16[4,32,128]{2,1,0:T(8,128)(2,1)S(1)}, u32[]{:S(2)}, u32[]{:S(2)}) collective-permute-start(bf16[4,32,128]{2,1,0:T(8,128)(2,1)S(1)} %join_columns.1.own_ref), channel_id=1, source_target_pairs={{0,1},{1,0},{2,3},{3,2},{4,5},{5,4},{6,7},{7,6},{8,17},{9,16},{10,... | collective-permute-start | bytes 98312 | tf_op jit(solution)/shard_map/ppermute | solution.py:415
  12.0 3.5 %collective-permute-start.4 = (bf16[4,32,128]{2,1,0:T(8,128)(2,1)S(1)}, bf16[4,32,128]{2,1,0:T(8,128)(2,1)S(1)}, u32[]{:S(2)}, u32[]{:S(2)}) collective-permute-start(bf16[4,32,128]{2,1,0:T(8,128)(2,1)S(1)} %join_columns.1.own_ref), channel_id=1, source_target_pairs={{0,24},{1,25},{2,26},{3,27},{4,28},{5,29},{6,30},{7,31},{8,16},{9,... | collective-permute-start | bytes 98312 | tf_op jit(solution)/shard_map/ppermute | solution.py:415
  12.0 3.5 %collective-permute-start.5 = (bf16[4,32,128]{2,1,0:T(8,128)(2,1)S(1)}, bf16[4,32,128]{2,1,0:T(8,128)(2,1)S(1)}, u32[]{:S(2)}, u32[]{:S(2)}) collective-permute-start(bf16[4,32,128]{2,1,0:T(8,128)(2,1)S(1)} %join_columns.1.own_ref), channel_id=1, source_target_pairs={{0,8},{1,9},{2,10},{3,11},{4,12},{5,13},{6,14},{7,15},{8,0},{9,1},... | collective-permute-start | bytes 98312 | tf_op jit(solution)/shard_map/ppermute | solution.py:415
  13.8 1.7 %collective-permute-start.7 = (bf16[4,32,128]{2,1,0:T(8,128)(2,1)S(1)}, bf16[4,32,128]{2,1,0:T(8,128)(2,1)S(1)}, u32[]{:S(2)}, u32[]{:S(2)}) collective-permute-start(bf16[4,32,128]{2,1,0:T(8,128)(2,1)S(1)} %collective-permute-done.6.mate), channel_id=1, source_target_pairs={{0,8},{1,9},{2,10},{3,11},{4,12},{5,13},{6,14},{7,15},{8,0},{9,1},... | collective-permute-start | bytes 98312 | tf_op jit(solution)/shard_map/ppermute | solution.py:415
  14.7 7.2 %copy-start = (bf16[640,1280]{1,0:T(8,128)(2,1)S(1)}, bf16[640,1280]{1,0:T(8,128)(2,1)}, u32[]{:S(2)}) copy-start(bf16[640,1280]{1,0:T(8,128)(2,1)} %refs_6_.1) | copy-start | bytes 4915204
  16.3 6.6 %copy-start.5 = (bf16[1280,640]{1,0:T(8,128)(2,1)S(1)}, bf16[1280,640]{1,0:T(8,128)(2,1)}, u32[]{:S(2)}) copy-start(bf16[1280,640]{1,0:T(8,128)(2,1)} %refs_7_.1) | copy-start | bytes 4915204
  16.3 5.6 %collective-permute-start.11 = (bf16[32,128]{1,0:T(8,128)(2,1)S(1)}, bf16[32,128]{1,0:T(8,128)(2,1)S(1)}, u32[]{:S(2)}, u32[]{:S(2)}) collective-permute-start(bf16[32,128]{1,0:T(8,128)(2,1)S(1)} %get-tuple-element.28), channel_id=1, source_target_pairs={{0,6},{1,7},{2,4},{3,5},{4,2},{5,3},{6,0},{7,1},{8,14},{9,15},{10,... | collective-permute-start | bytes 24584 | tf_op jit(solution)/shard_map/ppermute | solution.py:402
  18.3 4.5 %collective-permute-start.10 = (bf16[32,128]{1,0:T(8,128)(2,1)S(1)}, bf16[32,128]{1,0:T(8,128)(2,1)S(1)}, u32[]{:S(2)}, u32[]{:S(2)}) collective-permute-start(bf16[32,128]{1,0:T(8,128)(2,1)S(1)} %get-tuple-element.26), channel_id=1, source_target_pairs={{0,4},{1,5},{2,6},{3,7},{4,0},{5,1},{6,2},{7,3},{8,12},{9,13},{10,... | collective-permute-start | bytes 24584 | tf_op jit(solution)/shard_map/ppermute | solution.py:402
  18.3 4.5 %collective-permute-start.9 = (bf16[32,128]{1,0:T(8,128)(2,1)S(1)}, bf16[32,128]{1,0:T(8,128)(2,1)S(1)}, u32[]{:S(2)}, u32[]{:S(2)}) collective-permute-start(bf16[32,128]{1,0:T(8,128)(2,1)S(1)} %get-tuple-element.25), channel_id=1, source_target_pairs={{0,2},{1,3},{2,0},{3,1},{4,6},{5,7},{6,4},{7,5},{8,10},{9,11},{10,... | collective-permute-start | bytes 24584 | tf_op jit(solution)/shard_map/ppermute | solution.py:402

commit v12 on v11

--- a/solution.py
+++ b/solution.py
@@ -419,7 +419,7 @@
     to = lat + 1 if lat % 2 else lat - 1
     if 0 <= to < rows:
         return to, lon ^ other_side
-    return (lat, lon ^ 1) if other_side else (rows - 1 - lat, lon)
+    return rows - 1 - lat, lon
 
 
 def local(latent, lon_filter, mix_weight, band_weight, offsets, w_up, w_down):

time: 24.3 us -> 24.4 us (level)
  no operation moved by 1% of the time
where the time goes in v12:
time: 24.4 us; the launch traced here: 24.2 us
  starting transfers between devices  15 us (61%)
  waiting for transfers between devices  4.82 us (20%)
  Pallas kernels  4.22 us (17%)
    ppermute x6, starting transfers between devices, over_columns(): return lax.ppermute(message, 'lon', pairs) if apart else message  10.2 us
    pallas_call x11, Pallas kernels, call(): pl.pallas_call(kernel, out_shape=out_shape, in_specs=[VMEM] * len(operand...  4.22 us
    ppermute x6, waiting for transfers between devices, over_columns(): return lax.ppermute(message, 'lon', pairs) if apart else message  3.43 us
    ppermute x5, starting transfers between devices, swap(): return lax.ppermute(block, ('lat', 'lon'), pairs)  3.3 us
    ppermute x1, starting transfers between devices, over_sides(): return lax.ppermute(block, 'lon', [(i, i ^ 1) for i in range(count)])  1.49 us
    ppermute x5, waiting for transfers between devices, swap(): return lax.ppermute(block, ('lat', 'lon'), pairs)  1.38 us
  transfers between devices with their start and end apart: 12, of which 6 were waited for; matrix products, arithmetic and copies ran while one was open for 0% of the time, Pallas kernels for 9%

profile of v12, /device:TPU:0, one launch (start us, length us, event | category | flops | bytes accessed | tf_op | source)
XLA Modules:
  0.0 24.2 jit_solution(11542911189523416782)
XLA Ops:
  0.0 0.0 copy-start.2
  0.0 4.0 %collective-permute-start = (bf16[12,2,640]{2,1,0:T(2,128)(2,1)}, bf16[12,2,640]{2,1,0:T(2,128)(2,1)S(1)}, u32[]{:S(2)}, u32[]{:S(2)}) collective-permute-start(bf16[12,2,640]{2,1,0:T(2,128)(2,1)} %bitcast.6), channel_id=1, source_target_pairs={{0,4},{1,5},{2,6},{3,7},{4,0},{5,1},{6,2},{7,3},{8,12},{9,13},{10,... | collective-permute-start | bytes 92168 | tf_op jit(solution)/shard_map/ppermute | solution.py:402
  4.1 0.0 copy-done.2
  4.1 0.0 copy-start.1
  4.1 0.0 copy-start.3
  4.1 0.0 copy-start.4
  4.1 0.2 pack.1
  4.3 1.7 %collective-permute-start.1 = (bf16[32,128]{1,0:T(8,128)(2,1)S(1)}, bf16[32,128]{1,0:T(8,128)(2,1)S(1)}, u32[]{:S(2)}, u32[]{:S(2)}) collective-permute-start(bf16[32,128]{1,0:T(8,128)(2,1)S(1)} %get-tuple-element.20), channel_id=1, source_target_pairs={{0,6},{1,7},{2,4},{3,5},{4,2},{5,3},{6,0},{7,1},{8,14},{9,15},{10,... | collective-permute-start | bytes 24584 | tf_op jit(solution)/shard_map/ppermute | solution.py:402
  6.0 0.0 collective-permute-start.2
  6.0 0.0 copy-done.1
  6.0 1.5 %collective-permute-start.8 = (bf16[9,20,80]{2,1,0:T(8,128)(2,1)S(1)}, bf16[9,20,80]{2,1,0:T(8,128)(2,1)S(1)}, u32[]{:S(2)}, u32[]{:S(2)}) collective-permute-start(bf16[9,20,80]{2,1,0:T(8,128)(2,1)S(1)} %bitcast.4), channel_id=1, source_target_pairs={{0,1},{1,0},{2,3},{3,2},{4,5},{5,4},{6,7},{7,6},{8,9},{9,8},{10,11... | collective-permute-start | bytes 86408 | tf_op jit(solution)/shard_map/ppermute | solution.py:406
  7.5 0.0 copy-done.3
  7.5 0.0 copy-done.4
  7.5 0.4 %tables.1.table_ref = bf16[2,432,384]{2,1,0:T(8,128)(2,1)S(1)} custom-call(bf16[9,96]{1,0:T(8,128)(2,1)S(1)} %copy-done.3, bf16[3,2,9]{2,1,0:T(2,128)(2,1)S(1)} %bitcast.9, s32[96,128]{1,0:T(8,128)S(1)} %apart.1.apart_ref), custom_call_target="tpu_custom_call" | custom-call | flops 1000000 | bytes 1000000 | tf_op jit(solution)/shard_map/tables/pallas_call | solution.py:388
  7.9 0.0 collective-permute-done.raw_ref
  7.9 0.2 cut.1.refs_0_
  8.1 1.7 %collective-permute-done.1.refs_1_ = bf16[32,128]{1,0:T(8,128)(2,1)S(1)} collective-permute-done((bf16[32,128]{1,0:T(8,128)(2,1)S(1)}, bf16[32,128]{1,0:T(8,128)(2,1)S(1)}, u32[]{:S(2)}, u32[]{:S(2)}) %collective-permute-start.1) | collective-permute-done | bytes 8224 | tf_op jit(solution)/shard_map/ppermute | solution.py:402
  9.8 0.0 collective-permute-done.2.refs_2_
  9.8 1.6 %collective-permute-start.6 = (bf16[4,32,128]{2,1,0:T(8,128)(2,1)S(1)}, bf16[4,32,128]{2,1,0:T(8,128)(2,1)S(1)}, u32[]{:S(2)}, u32[]{:S(2)}) collective-permute-start(bf16[4,32,128]{2,1,0:T(8,128)(2,1)S(1)} %join_columns.1.own_ref), channel_id=1, source_target_pairs={{0,1},{1,0},{2,3},{3,2},{4,5},{5,4},{6,7},{7,6},{8,9},{9,8},{10,11... | collective-permute-start | bytes 98312 | tf_op jit(solution)/shard_map/ppermute | solution.py:415
  11.4 0.1 unpack.1.own
  11.5 0.0 collective-permute-start.3
  11.5 1.7 %collective-permute-start.4 = (bf16[4,32,128]{2,1,0:T(8,128)(2,1)S(1)}, bf16[4,32,128]{2,1,0:T(8,128)(2,1)S(1)}, u32[]{:S(2)}, u32[]{:S(2)}) collective-permute-start(bf16[4,32,128]{2,1,0:T(8,128)(2,1)S(1)} %join_columns.1.own_ref), channel_id=1, source_target_pairs={{0,24},{1,25},{2,26},{3,27},{4,28},{5,29},{6,30},{7,31},{8,16},{9,... | collective-permute-start | bytes 98312 | tf_op jit(solution)/shard_map/ppermute | solution.py:415
  13.2 0.0 collective-permute-start.5
  13.2 0.0 collective-permute-done.8.mate_ref
  13.2 0.6 %collective-permute-done.6.mate = bf16[4,32,128]{2,1,0:T(8,128)(2,1)S(1)} collective-permute-done((bf16[4,32,128]{2,1,0:T(8,128)(2,1)S(1)}, bf16[4,32,128]{2,1,0:T(8,128)(2,1)S(1)}, u32[]{:S(2)}, u32[]{:S(2)}) %collective-permute-start.6) | collective-permute-done | bytes 32800 | tf_op jit(solution)/shard_map/ppermute | solution.py:415
  13.8 0.0 collective-permute-start.7
  13.8 0.5 %squares.1.squares_ref = bf16[2304,256]{1,0:T(8,128)(2,1)S(1)} custom-call(bf16[9,20,80]{2,1,0:T(8,128)(2,1)S(1)} %bitcast.5, bf16[9,20,80]{2,1,0:T(8,128)(2,1)S(1)} %collective-permute-done.8.mate_ref), custom_call_target="tpu_custom_call" | custom-call | flops 300000000 | bytes 1000000 | tf_op jit(solution)/shard_map/squares/pallas_call | solution.py:388
  14.4 0.3 %conv_own.1.part_ref = f32[2,432,256]{2,1,0:T(8,128)S(1)} custom-call(bf16[4,32,128]{2,1,0:T(8,128)(2,1)S(1)} %collective-permute-done.6.mate, bf16[2,4,16,256]{3,2,1,0:T(8,128)(2,1)S(1)} %unpack.1.own, bf16[2,432,384]{2,1,0:T(8,128)(2,1)S(1)} %tables.1.table_ref), custom_call_target="tpu_custom_call" | custom-call | flops 300000000 | bytes 1000000 | tf_op jit(solution)/shard_map/conv_own/pallas_call | solution.py:388
  14.7 0.0 copy-start
  14.7 0.1 collective-permute-done.3.odd_mate
  14.8 0.7 %collective-permute-done.4.odd_own = bf16[4,32,128]{2,1,0:T(8,128)(2,1)S(1)} collective-permute-done((bf16[4,32,128]{2,1,0:T(8,128)(2,1)S(1)}, bf16[4,32,128]{2,1,0:T(8,128)(2,1)S(1)}, u32[]{:S(2)}, u32[]{:S(2)}) %collective-permute-start.4) | collective-permute-done | bytes 32800 | tf_op jit(solution)/shard_map/ppermute | solution.py:415
  15.5 0.0 collective-permute-done.5.even_own
  15.5 0.0 collective-permute-done.7.even_mate
  15.5 0.8 %conv.1 = (bf16[32,128]{1,0:T(8,128)(2,1)S(1)}, bf16[32,128]{1,0:T(8,128)(2,1)S(1)}, bf16[32,128]{1,0:T(8,128)(2,1)S(1)}, bf16[32,128]{1,0:T(8,128)(2,1)S(1)}) custom-call(bf16[4,32,128]{2,1,0:T(8,128)(2,1)S(1)} %collective-permute-done.3.odd_mate, bf16[4,32,128]{2,1,0:T(8,128)(2,1)S(1)} %collective-permute-done.4.odd_own, ...), custom_call_target="tpu_custom_call" | custom-call | flops 10000000000 | bytes 1000000 | tf_op jit(solution)/shard_map/conv/pallas_call | solution.py:388
  16.3 0.0 copy-start.5
  16.3 2.0 %collective-permute-start.11 = (bf16[32,128]{1,0:T(8,128)(2,1)S(1)}, bf16[32,128]{1,0:T(8,128)(2,1)S(1)}, u32[]{:S(2)}, u32[]{:S(2)}) collective-permute-start(bf16[32,128]{1,0:T(8,128)(2,1)S(1)} %get-tuple-element.28), channel_id=1, source_target_pairs={{0,6},{1,7},{2,4},{3,5},{4,2},{5,3},{6,0},{7,1},{8,14},{9,15},{10,... | collective-permute-start | bytes 24584 | tf_op jit(solution)/shard_map/ppermute | solution.py:402
  18.3 0.0 collective-permute-start.10
  18.3 2.4 %collective-permute-start.9 = (bf16[32,128]{1,0:T(8,128)(2,1)S(1)}, bf16[32,128]{1,0:T(8,128)(2,1)S(1)}, u32[]{:S(2)}, u32[]{:S(2)}) collective-permute-start(bf16[32,128]{1,0:T(8,128)(2,1)S(1)} %get-tuple-element.25), channel_id=1, source_target_pairs={{0,2},{1,3},{2,0},{3,1},{4,6},{5,7},{6,4},{7,5},{8,10},{9,11},{10,... | collective-permute-start | bytes 24584 | tf_op jit(solution)/shard_map/ppermute | solution.py:402
  20.8 1.1 %collective-permute-done.11.first_ref = bf16[32,128]{1,0:T(8,128)(2,1)S(1)} collective-permute-done((bf16[32,128]{1,0:T(8,128)(2,1)S(1)}, bf16[32,128]{1,0:T(8,128)(2,1)S(1)}, u32[]{:S(2)}, u32[]{:S(2)}) %collective-permute-start.11) | collective-permute-done | bytes 8224 | tf_op jit(solution)/shard_map/ppermute | solution.py:402
  21.9 0.0 copy-done
  21.9 0.4 %lift.1 = (f32[4,24,256]{2,1,0:T(8,128)S(1)}, f32[24,640]{1,0:T(8,128)S(1)}, f32[32,1280]{1,0:T(8,128)S(1)}, f32[2,24,128]{2,1,0:T(8,128)S(1)}) custom-call(bf16[32,128]{1,0:T(8,128)(2,1)S(1)} %get-tuple-element.27.own_ref, bf16[32,128]{1,0:T(8,128)(2,1)S(1)} %collective-permute-done.11.first_ref, bf16[12,2,640]{2,1,0:T(2,128)(2,1)S(1)} %bitcast.8, ...), custom_call_target="tpu_custom_call" | custom-call | flops 100000000 | bytes 1000000 | tf_op jit(solution)/shard_map/lift/pallas_call | solution.py:388
  22.3 0.6 %collective-permute-done.10.refs_1_ = bf16[32,128]{1,0:T(8,128)(2,1)S(1)} collective-permute-done((bf16[32,128]{1,0:T(8,128)(2,1)S(1)}, bf16[32,128]{1,0:T(8,128)(2,1)S(1)}, u32[]{:S(2)}, u32[]{:S(2)}) %collective-permute-start.10) | collective-permute-done | bytes 8224 | tf_op jit(solution)/shard_map/ppermute | solution.py:402
  22.9 0.0 collective-permute-done.9.refs_0_
  22.9 0.0 copy-done.5
  22.9 1.3 %tail.1 = bf16[12,2,640]{2,1,0:T(2,128)(2,1)} custom-call(bf16[32,128]{1,0:T(8,128)(2,1)S(1)} %collective-permute-done.9.refs_0_, bf16[32,128]{1,0:T(8,128)(2,1)S(1)} %collective-permute-done.10.refs_1_, f32[4,24,256]{2,1,0:T(8,128)S(1)} %get-tuple-element.29.refs_2_, f32[24,640]{1,0:T(8,128)S(1)} %get-tuple-element.30.refs_3_, ...), custom_call_target="tpu_custom_call" | custom-call | flops 1000000000 | bytes 1000000 | tf_op jit(solution)/shard_map/tail/pallas_call | solution.py:388
  (2 shorter events, 0.0 us)
Async XLA Ops:
  0.0 4.1 %copy-start.2 = (bf16[2,12,640]{2,0,1:T(2,128)(2,1)S(1)}, bf16[2,12,640]{2,0,1:T(2,128)(2,1)}, u32[]{:S(2)}) copy-start(bf16[2,12,640]{2,0,1:T(2,128)(2,1)} %param.7) | copy-start | bytes 92164
  0.0 7.9 %collective-permute-start = (bf16[12,2,640]{2,1,0:T(2,128)(2,1)}, bf16[12,2,640]{2,1,0:T(2,128)(2,1)S(1)}, u32[]{:S(2)}, u32[]{:S(2)}) collective-permute-start(bf16[12,2,640]{2,1,0:T(2,128)(2,1)} %bitcast.6), channel_id=1, source_target_pairs={{0,4},{1,5},{2,6},{3,7},{4,0},{5,1},{6,2},{7,3},{8,12},{9,13},{10,... | collective-permute-start | bytes 92168 | tf_op jit(solution)/shard_map/ppermute | solution.py:402
  4.1 2.0 %copy-start.1 = (bf16[9,80,20]{1,2,0:T(8,128)(2,1)S(1)}, bf16[9,80,20]{1,2,0:T(8,128)(2,1)}, u32[]{:S(2)}) copy-start(bf16[9,80,20]{1,2,0:T(8,128)(2,1)} %param.9) | copy-start | bytes 86404
  4.1 3.4 %copy-start.3 = (bf16[9,96]{1,0:T(8,128)(2,1)S(1)}, bf16[9,96]{1,0:T(8,128)(2,1)}, u32[]{:S(2)}) copy-start(bf16[9,96]{1,0:T(8,128)(2,1)} %filter_ref.1) | copy-start | bytes 5188
  4.1 3.4 %copy-start.4 = (bf16[9,2,3]{0,1,2:T(2,128)(2,1)S(1)}, bf16[9,2,3]{0,1,2:T(2,128)(2,1)}, u32[]{:S(2)}) copy-start(bf16[9,2,3]{0,1,2:T(2,128)(2,1)} %param.10) | copy-start | bytes 328
  4.3 5.5 %collective-permute-start.1 = (bf16[32,128]{1,0:T(8,128)(2,1)S(1)}, bf16[32,128]{1,0:T(8,128)(2,1)S(1)}, u32[]{:S(2)}, u32[]{:S(2)}) collective-permute-start(bf16[32,128]{1,0:T(8,128)(2,1)S(1)} %get-tuple-element.20), channel_id=1, source_target_pairs={{0,6},{1,7},{2,4},{3,5},{4,2},{5,3},{6,0},{7,1},{8,14},{9,15},{10,... | collective-permute-start | bytes 24584 | tf_op jit(solution)/shard_map/ppermute | solution.py:402
  6.0 3.8 %collective-permute-start.2 = (bf16[32,128]{1,0:T(8,128)(2,1)S(1)}, bf16[32,128]{1,0:T(8,128)(2,1)S(1)}, u32[]{:S(2)}, u32[]{:S(2)}) collective-permute-start(bf16[32,128]{1,0:T(8,128)(2,1)S(1)} %get-tuple-element.21), channel_id=1, source_target_pairs={{0,2},{1,3},{2,0},{3,1},{4,6},{5,7},{6,4},{7,5},{8,10},{9,11},{10,... | collective-permute-start | bytes 24584 | tf_op jit(solution)/shard_map/ppermute | solution.py:402
  6.0 7.2 %collective-permute-start.8 = (bf16[9,20,80]{2,1,0:T(8,128)(2,1)S(1)}, bf16[9,20,80]{2,1,0:T(8,128)(2,1)S(1)}, u32[]{:S(2)}, u32[]{:S(2)}) collective-permute-start(bf16[9,20,80]{2,1,0:T(8,128)(2,1)S(1)} %bitcast.4), channel_id=1, source_target_pairs={{0,1},{1,0},{2,3},{3,2},{4,5},{5,4},{6,7},{7,6},{8,9},{9,8},{10,11... | collective-permute-start | bytes 86408 | tf_op jit(solution)/shard_map/ppermute | solution.py:406
  9.8 4.0 %collective-permute-start.6 = (bf16[4,32,128]{2,1,0:T(8,128)(2,1)S(1)}, bf16[4,32,128]{2,1,0:T(8,128)(2,1)S(1)}, u32[]{:S(2)}, u32[]{:S(2)}) collective-permute-start(bf16[4,32,128]{2,1,0:T(8,128)(2,1)S(1)} %join_columns.1.own_ref), channel_id=1, source_target_pairs={{0,1},{1,0},{2,3},{3,2},{4,5},{5,4},{6,7},{7,6},{8,9},{9,8},{10,11... | collective-permute-start | bytes 98312 | tf_op jit(solution)/shard_map/ppermute | solution.py:415
  11.5 3.4 %collective-permute-start.3 = (bf16[4,32,128]{2,1,0:T(8,128)(2,1)S(1)}, bf16[4,32,128]{2,1,0:T(8,128)(2,1)S(1)}, u32[]{:S(2)}, u32[]{:S(2)}) collective-permute-start(bf16[4,32,128]{2,1,0:T(8,128)(2,1)S(1)} %join_columns.1.own_ref), channel_id=1, source_target_pairs={{0,24},{1,25},{2,26},{3,27},{4,28},{5,29},{6,30},{7,31},{8,17},{9,... | collective-permute-start | bytes 98312 | tf_op jit(solution)/shard_map/ppermute | solution.py:415
  11.5 4.0 %collective-permute-start.4 = (bf16[4,32,128]{2,1,0:T(8,128)(2,1)S(1)}, bf16[4,32,128]{2,1,0:T(8,128)(2,1)S(1)}, u32[]{:S(2)}, u32[]{:S(2)}) collective-permute-start(bf16[4,32,128]{2,1,0:T(8,128)(2,1)S(1)} %join_columns.1.own_ref), channel_id=1, source_target_pairs={{0,24},{1,25},{2,26},{3,27},{4,28},{5,29},{6,30},{7,31},{8,16},{9,... | collective-permute-start | bytes 98312 | tf_op jit(solution)/shard_map/ppermute | solution.py:415
  13.2 2.3 %collective-permute-start.5 = (bf16[4,32,128]{2,1,0:T(8,128)(2,1)S(1)}, bf16[4,32,128]{2,1,0:T(8,128)(2,1)S(1)}, u32[]{:S(2)}, u32[]{:S(2)}) collective-permute-start(bf16[4,32,128]{2,1,0:T(8,128)(2,1)S(1)} %join_columns.1.own_ref), channel_id=1, source_target_pairs={{0,8},{1,9},{2,10},{3,11},{4,12},{5,13},{6,14},{7,15},{8,0},{9,1},... | collective-permute-start | bytes 98312 | tf_op jit(solution)/shard_map/ppermute | solution.py:415
  13.8 1.7 %collective-permute-start.7 = (bf16[4,32,128]{2,1,0:T(8,128)(2,1)S(1)}, bf16[4,32,128]{2,1,0:T(8,128)(2,1)S(1)}, u32[]{:S(2)}, u32[]{:S(2)}) collective-permute-start(bf16[4,32,128]{2,1,0:T(8,128)(2,1)S(1)} %collective-permute-done.6.mate), channel_id=1, source_target_pairs={{0,8},{1,9},{2,10},{3,11},{4,12},{5,13},{6,14},{7,15},{8,0},{9,1},... | collective-permute-start | bytes 98312 | tf_op jit(solution)/shard_map/ppermute | solution.py:415
  14.7 7.2 %copy-start = (bf16[640,1280]{1,0:T(8,128)(2,1)S(1)}, bf16[640,1280]{1,0:T(8,128)(2,1)}, u32[]{:S(2)}) copy-start(bf16[640,1280]{1,0:T(8,128)(2,1)} %refs_6_.1) | copy-start | bytes 4915204
  16.3 6.6 %copy-start.5 = (bf16[1280,640]{1,0:T(8,128)(2,1)S(1)}, bf16[1280,640]{1,0:T(8,128)(2,1)}, u32[]{:S(2)}) copy-start(bf16[1280,640]{1,0:T(8,128)(2,1)} %refs_7_.1) | copy-start | bytes 4915204
  16.3 5.6 %collective-permute-start.11 = (bf16[32,128]{1,0:T(8,128)(2,1)S(1)}, bf16[32,128]{1,0:T(8,128)(2,1)S(1)}, u32[]{:S(2)}, u32[]{:S(2)}) collective-permute-start(bf16[32,128]{1,0:T(8,128)(2,1)S(1)} %get-tuple-element.28), channel_id=1, source_target_pairs={{0,6},{1,7},{2,4},{3,5},{4,2},{5,3},{6,0},{7,1},{8,14},{9,15},{10,... | collective-permute-start | bytes 24584 | tf_op jit(solution)/shard_map/ppermute | solution.py:402
  18.3 4.5 %collective-permute-start.10 = (bf16[32,128]{1,0:T(8,128)(2,1)S(1)}, bf16[32,128]{1,0:T(8,128)(2,1)S(1)}, u32[]{:S(2)}, u32[]{:S(2)}) collective-permute-start(bf16[32,128]{1,0:T(8,128)(2,1)S(1)} %get-tuple-element.26), channel_id=1, source_target_pairs={{0,4},{1,5},{2,6},{3,7},{4,0},{5,1},{6,2},{7,3},{8,12},{9,13},{10,... | collective-permute-start | bytes 24584 | tf_op jit(solution)/shard_map/ppermute | solution.py:402
  18.3 4.5 %collective-permute-start.9 = (bf16[32,128]{1,0:T(8,128)(2,1)S(1)}, bf16[32,128]{1,0:T(8,128)(2,1)S(1)}, u32[]{:S(2)}, u32[]{:S(2)}) collective-permute-start(bf16[32,128]{1,0:T(8,128)(2,1)S(1)} %get-tuple-element.25), channel_id=1, source_target_pairs={{0,2},{1,3},{2,0},{3,1},{4,6},{5,7},{6,4},{7,5},{8,10},{9,11},{10,... | collective-permute-start | bytes 24584 | tf_op jit(solution)/shard_map/ppermute | solution.py:402

commit v13 on v11

--- a/solution.py
+++ b/solution.py
@@ -346,7 +346,9 @@
 
 def tail_kernel(order, *refs):
     back_refs = refs[: len(order)]
-    blocks_ref, summed_ref, raised_ref, stats_ref, up_ref, down_ref, out_ref = refs[len(order) :]
+    blocks_ref, summed_ref, raised_ref, stats_ref, up_ref, down_ref, out_ref, ordered = refs[
+        len(order) :
+    ]
     width, rows, chans = out_ref.shape
     rest = width - SUBLANES
     block = chans // blocks_ref.shape[0]
@@ -374,10 +376,16 @@
     for there, other in theirs:
         summed = summed + placed(there, other, chans, block)
     result = summed + jnp.dot(hidden, down_ref[...], preferred_element_type=F32)
-    for row in range(rows):
-        out_ref[:SUBLANES, row, :] = result[row * SUBLANES : (row + 1) * SUBLANES].astype(BF16)
-        at = rows * SUBLANES + row * rest
-        out_ref[SUBLANES:, row, :] = result[at : at + rest].astype(BF16)
+    for tile in range(chans // LANES):
+        part = result[:, tile * LANES : (tile + 1) * LANES]
+        for row in range(rows):
+            first = part[row * SUBLANES : (row + 1) * SUBLANES]
+            ordered[tile, pl.ds(row, SUBLANES, rows), :] = first
+            at = rows * SUBLANES + row * rest
+            ordered[tile, pl.ds(rows * SUBLANES + row, rest, rows), :] = part[at : at + rest]
+        for lon in range(width):
+            taken = ordered[tile, lon * rows : (lon + 1) * rows].astype(BF16)
+            out_ref[lon, :, tile * LANES : (tile + 1) * LANES] = taken
 
 
 VMEM = pl.BlockSpec(memory_space=pltpu.VMEM)
@@ -563,7 +571,7 @@
         functools.partial(tail_kernel, outward[:first] + outward[first + 1 :]),
         "tail",
         jax.ShapeDtypeStruct(lon_first.shape, BF16),
-        [],
+        [pltpu.VMEM((chans // LANES, 3 * SUBLANES, LANES), F32)],
         10**9,
         *back[:first],
         *back[first + 1 :],

time: 24.3 us -> 24.3 us (level)
  no operation moved by 1% of the time
where the time goes in v13:
time: 24.3 us; the launch traced here: 24.2 us
  starting transfers between devices  15 us (62%)
  waiting for transfers between devices  4.8 us (20%)
  Pallas kernels  4.21 us (17%)
    ppermute x6, starting transfers between devices, over_columns(): return lax.ppermute(message, 'lon', pairs) if apart else message  10.3 us
    pallas_call x11, Pallas kernels, call(): pl.pallas_call(kernel, out_shape=out_shape, in_specs=[VMEM] * len(operand...  4.21 us
    ppermute x6, waiting for transfers between devices, over_columns(): return lax.ppermute(message, 'lon', pairs) if apart else message  3.42 us
    ppermute x5, starting transfers between devices, swap(): return lax.ppermute(block, ('lat', 'lon'), pairs)  3.27 us
    ppermute x1, starting transfers between devices, over_sides(): return lax.ppermute(block, 'lon', [(i, i ^ 1) for i in range(count)])  1.49 us
    ppermute x5, waiting for transfers between devices, swap(): return lax.ppermute(block, ('lat', 'lon'), pairs)  1.37 us
  transfers between devices with their start and end apart: 12, of which 6 were waited for; matrix products, arithmetic and copies ran while one was open for 0% of the time, Pallas kernels for 9%

profile of v13, /device:TPU:0, one launch (start us, length us, event | category | flops | bytes accessed | tf_op | source)
XLA Modules:
  0.0 24.2 jit_solution(7178171709346592172)
XLA Ops:
  0.0 0.0 copy-start.2
  0.0 4.0 %collective-permute-start = (bf16[12,2,640]{2,1,0:T(2,128)(2,1)}, bf16[12,2,640]{2,1,0:T(2,128)(2,1)S(1)}, u32[]{:S(2)}, u32[]{:S(2)}) collective-permute-start(bf16[12,2,640]{2,1,0:T(2,128)(2,1)} %bitcast.6), channel_id=1, source_target_pairs={{0,4},{1,5},{2,6},{3,7},{4,0},{5,1},{6,2},{7,3},{8,12},{9,13},{10,... | collective-permute-start | bytes 92168 | tf_op jit(solution)/shard_map/ppermute | solution.py:410
  4.1 0.0 copy-done.2
  4.1 0.0 copy-start.1
  4.1 0.0 copy-start.3
  4.1 0.0 copy-start.4
  4.1 0.2 pack.1
  4.3 1.7 %collective-permute-start.1 = (bf16[32,128]{1,0:T(8,128)(2,1)S(1)}, bf16[32,128]{1,0:T(8,128)(2,1)S(1)}, u32[]{:S(2)}, u32[]{:S(2)}) collective-permute-start(bf16[32,128]{1,0:T(8,128)(2,1)S(1)} %get-tuple-element.20), channel_id=1, source_target_pairs={{0,6},{1,7},{2,4},{3,5},{4,2},{5,3},{6,0},{7,1},{8,14},{9,15},{10,... | collective-permute-start | bytes 24584 | tf_op jit(solution)/shard_map/ppermute | solution.py:410
  6.0 0.0 collective-permute-start.2
  6.0 0.0 copy-done.1
  6.0 1.5 %collective-permute-start.8 = (bf16[9,20,80]{2,1,0:T(8,128)(2,1)S(1)}, bf16[9,20,80]{2,1,0:T(8,128)(2,1)S(1)}, u32[]{:S(2)}, u32[]{:S(2)}) collective-permute-start(bf16[9,20,80]{2,1,0:T(8,128)(2,1)S(1)} %bitcast.4), channel_id=1, source_target_pairs={{0,1},{1,0},{2,3},{3,2},{4,5},{5,4},{6,7},{7,6},{8,9},{9,8},{10,11... | collective-permute-start | bytes 86408 | tf_op jit(solution)/shard_map/ppermute | solution.py:414
  7.5 0.0 copy-done.3
  7.5 0.0 copy-done.4
  7.5 0.4 %tables.1.table_ref = bf16[2,432,384]{2,1,0:T(8,128)(2,1)S(1)} custom-call(bf16[9,96]{1,0:T(8,128)(2,1)S(1)} %copy-done.3, bf16[3,2,9]{2,1,0:T(2,128)(2,1)S(1)} %bitcast.9, s32[96,128]{1,0:T(8,128)S(1)} %apart.1.apart_ref), custom_call_target="tpu_custom_call" | custom-call | flops 1000000 | bytes 1000000 | tf_op jit(solution)/shard_map/tables/pallas_call | solution.py:396
  7.9 0.0 collective-permute-done.raw_ref
  7.9 0.2 cut.1.refs_0_
  8.1 1.7 %collective-permute-done.1.refs_1_ = bf16[32,128]{1,0:T(8,128)(2,1)S(1)} collective-permute-done((bf16[32,128]{1,0:T(8,128)(2,1)S(1)}, bf16[32,128]{1,0:T(8,128)(2,1)S(1)}, u32[]{:S(2)}, u32[]{:S(2)}) %collective-permute-start.1) | collective-permute-done | bytes 8224 | tf_op jit(solution)/shard_map/ppermute | solution.py:410
  9.8 0.0 collective-permute-done.2.refs_2_
  9.8 1.6 %collective-permute-start.6 = (bf16[4,32,128]{2,1,0:T(8,128)(2,1)S(1)}, bf16[4,32,128]{2,1,0:T(8,128)(2,1)S(1)}, u32[]{:S(2)}, u32[]{:S(2)}) collective-permute-start(bf16[4,32,128]{2,1,0:T(8,128)(2,1)S(1)} %join_columns.1.own_ref), channel_id=1, source_target_pairs={{0,1},{1,0},{2,3},{3,2},{4,5},{5,4},{6,7},{7,6},{8,9},{9,8},{10,11... | collective-permute-start | bytes 98312 | tf_op jit(solution)/shard_map/ppermute | solution.py:423
  11.4 0.1 unpack.1.own
  11.5 0.5 %collective-permute-start.3 = (bf16[4,32,128]{2,1,0:T(8,128)(2,1)S(1)}, bf16[4,32,128]{2,1,0:T(8,128)(2,1)S(1)}, u32[]{:S(2)}, u32[]{:S(2)}) collective-permute-start(bf16[4,32,128]{2,1,0:T(8,128)(2,1)S(1)} %join_columns.1.own_ref), channel_id=1, source_target_pairs={{0,1},{1,0},{2,3},{3,2},{4,5},{5,4},{6,7},{7,6},{8,17},{9,16},{10,... | collective-permute-start | bytes 98312 | tf_op jit(solution)/shard_map/ppermute | solution.py:423
  12.0 0.0 collective-permute-start.4
  12.0 1.2 %collective-permute-start.5 = (bf16[4,32,128]{2,1,0:T(8,128)(2,1)S(1)}, bf16[4,32,128]{2,1,0:T(8,128)(2,1)S(1)}, u32[]{:S(2)}, u32[]{:S(2)}) collective-permute-start(bf16[4,32,128]{2,1,0:T(8,128)(2,1)S(1)} %join_columns.1.own_ref), channel_id=1, source_target_pairs={{0,8},{1,9},{2,10},{3,11},{4,12},{5,13},{6,14},{7,15},{8,0},{9,1},... | collective-permute-start | bytes 98312 | tf_op jit(solution)/shard_map/ppermute | solution.py:423
  13.2 0.0 collective-permute-done.8.mate_ref
  13.2 0.6 %collective-permute-done.6.mate = bf16[4,32,128]{2,1,0:T(8,128)(2,1)S(1)} collective-permute-done((bf16[4,32,128]{2,1,0:T(8,128)(2,1)S(1)}, bf16[4,32,128]{2,1,0:T(8,128)(2,1)S(1)}, u32[]{:S(2)}, u32[]{:S(2)}) %collective-permute-start.6) | collective-permute-done | bytes 32800 | tf_op jit(solution)/shard_map/ppermute | solution.py:423
  13.8 0.0 collective-permute-start.7
  13.8 0.5 %squares.1.squares_ref = bf16[2304,256]{1,0:T(8,128)(2,1)S(1)} custom-call(bf16[9,20,80]{2,1,0:T(8,128)(2,1)S(1)} %bitcast.5, bf16[9,20,80]{2,1,0:T(8,128)(2,1)S(1)} %collective-permute-done.8.mate_ref), custom_call_target="tpu_custom_call" | custom-call | flops 300000000 | bytes 1000000 | tf_op jit(solution)/shard_map/squares/pallas_call | solution.py:396
  14.4 0.3 %conv_own.1.part_ref = f32[2,432,256]{2,1,0:T(8,128)S(1)} custom-call(bf16[4,32,128]{2,1,0:T(8,128)(2,1)S(1)} %collective-permute-done.6.mate, bf16[2,4,16,256]{3,2,1,0:T(8,128)(2,1)S(1)} %unpack.1.own, bf16[2,432,384]{2,1,0:T(8,128)(2,1)S(1)} %tables.1.table_ref), custom_call_target="tpu_custom_call" | custom-call | flops 300000000 | bytes 1000000 | tf_op jit(solution)/shard_map/conv_own/pallas_call | solution.py:396
  14.7 0.0 copy-start
  14.7 0.7 %collective-permute-done.3.odd_mate = bf16[4,32,128]{2,1,0:T(8,128)(2,1)S(1)} collective-permute-done((bf16[4,32,128]{2,1,0:T(8,128)(2,1)S(1)}, bf16[4,32,128]{2,1,0:T(8,128)(2,1)S(1)}, u32[]{:S(2)}, u32[]{:S(2)}) %collective-permute-start.3) | collective-permute-done | bytes 32800 | tf_op jit(solution)/shard_map/ppermute | solution.py:423
  15.4 0.1 collective-permute-done.4.odd_own
  15.5 0.0 collective-permute-done.5.even_own
  15.5 0.0 collective-permute-done.7.even_mate
  15.5 0.8 %conv.1 = (bf16[32,128]{1,0:T(8,128)(2,1)S(1)}, bf16[32,128]{1,0:T(8,128)(2,1)S(1)}, bf16[32,128]{1,0:T(8,128)(2,1)S(1)}, bf16[32,128]{1,0:T(8,128)(2,1)S(1)}) custom-call(bf16[4,32,128]{2,1,0:T(8,128)(2,1)S(1)} %collective-permute-done.3.odd_mate, bf16[4,32,128]{2,1,0:T(8,128)(2,1)S(1)} %collective-permute-done.4.odd_own, ...), custom_call_target="tpu_custom_call" | custom-call | flops 10000000000 | bytes 1000000 | tf_op jit(solution)/shard_map/conv/pallas_call | solution.py:396
  16.3 0.0 copy-start.5
  16.3 2.0 %collective-permute-start.11 = (bf16[32,128]{1,0:T(8,128)(2,1)S(1)}, bf16[32,128]{1,0:T(8,128)(2,1)S(1)}, u32[]{:S(2)}, u32[]{:S(2)}) collective-permute-start(bf16[32,128]{1,0:T(8,128)(2,1)S(1)} %get-tuple-element.28), channel_id=1, source_target_pairs={{0,6},{1,7},{2,4},{3,5},{4,2},{5,3},{6,0},{7,1},{8,14},{9,15},{10,... | collective-permute-start | bytes 24584 | tf_op jit(solution)/shard_map/ppermute | solution.py:410
  18.3 0.0 collective-permute-start.10
  18.3 2.5 %collective-permute-start.9 = (bf16[32,128]{1,0:T(8,128)(2,1)S(1)}, bf16[32,128]{1,0:T(8,128)(2,1)S(1)}, u32[]{:S(2)}, u32[]{:S(2)}) collective-permute-start(bf16[32,128]{1,0:T(8,128)(2,1)S(1)} %get-tuple-element.25), channel_id=1, source_target_pairs={{0,2},{1,3},{2,0},{3,1},{4,6},{5,7},{6,4},{7,5},{8,10},{9,11},{10,... | collective-permute-start | bytes 24584 | tf_op jit(solution)/shard_map/ppermute | solution.py:410
  20.7 1.1 %collective-permute-done.11.first_ref = bf16[32,128]{1,0:T(8,128)(2,1)S(1)} collective-permute-done((bf16[32,128]{1,0:T(8,128)(2,1)S(1)}, bf16[32,128]{1,0:T(8,128)(2,1)S(1)}, u32[]{:S(2)}, u32[]{:S(2)}) %collective-permute-start.11) | collective-permute-done | bytes 8224 | tf_op jit(solution)/shard_map/ppermute | solution.py:410
  21.9 0.0 copy-done
  21.9 0.4 %lift.1 = (f32[4,24,256]{2,1,0:T(8,128)S(1)}, f32[24,640]{1,0:T(8,128)S(1)}, f32[32,1280]{1,0:T(8,128)S(1)}, f32[2,24,128]{2,1,0:T(8,128)S(1)}) custom-call(bf16[32,128]{1,0:T(8,128)(2,1)S(1)} %get-tuple-element.27.own_ref, bf16[32,128]{1,0:T(8,128)(2,1)S(1)} %collective-permute-done.11.first_ref, bf16[12,2,640]{2,1,0:T(2,128)(2,1)S(1)} %bitcast.8, ...), custom_call_target="tpu_custom_call" | custom-call | flops 100000000 | bytes 1000000 | tf_op jit(solution)/shard_map/lift/pallas_call | solution.py:396
  22.2 0.6 %collective-permute-done.10.refs_1_ = bf16[32,128]{1,0:T(8,128)(2,1)S(1)} collective-permute-done((bf16[32,128]{1,0:T(8,128)(2,1)S(1)}, bf16[32,128]{1,0:T(8,128)(2,1)S(1)}, u32[]{:S(2)}, u32[]{:S(2)}) %collective-permute-start.10) | collective-permute-done | bytes 8224 | tf_op jit(solution)/shard_map/ppermute | solution.py:410
  22.8 0.0 collective-permute-done.9.refs_0_
  22.8 0.0 copy-done.5
  22.8 1.3 %tail.1 = bf16[12,2,640]{2,1,0:T(2,128)(2,1)} custom-call(bf16[32,128]{1,0:T(8,128)(2,1)S(1)} %collective-permute-done.9.refs_0_, bf16[32,128]{1,0:T(8,128)(2,1)S(1)} %collective-permute-done.10.refs_1_, f32[4,24,256]{2,1,0:T(8,128)S(1)} %get-tuple-element.29.refs_2_, f32[24,640]{1,0:T(8,128)S(1)} %get-tuple-element.30.refs_3_, ...), custom_call_target="tpu_custom_call" | custom-call | flops 1000000000 | bytes 1000000 | tf_op jit(solution)/shard_map/tail/pallas_call | solution.py:396
  (2 shorter events, 0.0 us)
Async XLA Ops:
  0.0 4.1 %copy-start.2 = (bf16[2,12,640]{2,0,1:T(2,128)(2,1)S(1)}, bf16[2,12,640]{2,0,1:T(2,128)(2,1)}, u32[]{:S(2)}) copy-start(bf16[2,12,640]{2,0,1:T(2,128)(2,1)} %param.7) | copy-start | bytes 92164
  0.0 7.9 %collective-permute-start = (bf16[12,2,640]{2,1,0:T(2,128)(2,1)}, bf16[12,2,640]{2,1,0:T(2,128)(2,1)S(1)}, u32[]{:S(2)}, u32[]{:S(2)}) collective-permute-start(bf16[12,2,640]{2,1,0:T(2,128)(2,1)} %bitcast.6), channel_id=1, source_target_pairs={{0,4},{1,5},{2,6},{3,7},{4,0},{5,1},{6,2},{7,3},{8,12},{9,13},{10,... | collective-permute-start | bytes 92168 | tf_op jit(solution)/shard_map/ppermute | solution.py:410
  4.1 2.0 %copy-start.1 = (bf16[9,80,20]{1,2,0:T(8,128)(2,1)S(1)}, bf16[9,80,20]{1,2,0:T(8,128)(2,1)}, u32[]{:S(2)}) copy-start(bf16[9,80,20]{1,2,0:T(8,128)(2,1)} %param.9) | copy-start | bytes 86404
  4.1 3.4 %copy-start.3 = (bf16[9,96]{1,0:T(8,128)(2,1)S(1)}, bf16[9,96]{1,0:T(8,128)(2,1)}, u32[]{:S(2)}) copy-start(bf16[9,96]{1,0:T(8,128)(2,1)} %filter_ref.1) | copy-start | bytes 5188
  4.1 3.4 %copy-start.4 = (bf16[9,2,3]{0,1,2:T(2,128)(2,1)S(1)}, bf16[9,2,3]{0,1,2:T(2,128)(2,1)}, u32[]{:S(2)}) copy-start(bf16[9,2,3]{0,1,2:T(2,128)(2,1)} %param.10) | copy-start | bytes 328
  4.3 5.5 %collective-permute-start.1 = (bf16[32,128]{1,0:T(8,128)(2,1)S(1)}, bf16[32,128]{1,0:T(8,128)(2,1)S(1)}, u32[]{:S(2)}, u32[]{:S(2)}) collective-permute-start(bf16[32,128]{1,0:T(8,128)(2,1)S(1)} %get-tuple-element.20), channel_id=1, source_target_pairs={{0,6},{1,7},{2,4},{3,5},{4,2},{5,3},{6,0},{7,1},{8,14},{9,15},{10,... | collective-permute-start | bytes 24584 | tf_op jit(solution)/shard_map/ppermute | solution.py:410
  6.0 3.8 %collective-permute-start.2 = (bf16[32,128]{1,0:T(8,128)(2,1)S(1)}, bf16[32,128]{1,0:T(8,128)(2,1)S(1)}, u32[]{:S(2)}, u32[]{:S(2)}) collective-permute-start(bf16[32,128]{1,0:T(8,128)(2,1)S(1)} %get-tuple-element.21), channel_id=1, source_target_pairs={{0,2},{1,3},{2,0},{3,1},{4,6},{5,7},{6,4},{7,5},{8,10},{9,11},{10,... | collective-permute-start | bytes 24584 | tf_op jit(solution)/shard_map/ppermute | solution.py:410
  6.0 7.1 %collective-permute-start.8 = (bf16[9,20,80]{2,1,0:T(8,128)(2,1)S(1)}, bf16[9,20,80]{2,1,0:T(8,128)(2,1)S(1)}, u32[]{:S(2)}, u32[]{:S(2)}) collective-permute-start(bf16[9,20,80]{2,1,0:T(8,128)(2,1)S(1)} %bitcast.4), channel_id=1, source_target_pairs={{0,1},{1,0},{2,3},{3,2},{4,5},{5,4},{6,7},{7,6},{8,9},{9,8},{10,11... | collective-permute-start | bytes 86408 | tf_op jit(solution)/shard_map/ppermute | solution.py:414
  9.8 4.0 %collective-permute-start.6 = (bf16[4,32,128]{2,1,0:T(8,128)(2,1)S(1)}, bf16[4,32,128]{2,1,0:T(8,128)(2,1)S(1)}, u32[]{:S(2)}, u32[]{:S(2)}) collective-permute-start(bf16[4,32,128]{2,1,0:T(8,128)(2,1)S(1)} %join_columns.1.own_ref), channel_id=1, source_target_pairs={{0,1},{1,0},{2,3},{3,2},{4,5},{5,4},{6,7},{7,6},{8,9},{9,8},{10,11... | collective-permute-start | bytes 98312 | tf_op jit(solution)/shard_map/ppermute | solution.py:423
  11.5 3.9 %collective-permute-start.3 = (bf16[4,32,128]{2,1,0:T(8,128)(2,1)S(1)}, bf16[4,32,128]{2,1,0:T(8,128)(2,1)S(1)}, u32[]{:S(2)}, u32[]{:S(2)}) collective-permute-start(bf16[4,32,128]{2,1,0:T(8,128)(2,1)S(1)} %join_columns.1.own_ref), channel_id=1, source_target_pairs={{0,1},{1,0},{2,3},{3,2},{4,5},{5,4},{6,7},{7,6},{8,17},{9,16},{10,... | collective-permute-start | bytes 98312 | tf_op jit(solution)/shard_map/ppermute | solution.py:423
  12.0 3.5 %collective-permute-start.4 = (bf16[4,32,128]{2,1,0:T(8,128)(2,1)S(1)}, bf16[4,32,128]{2,1,0:T(8,128)(2,1)S(1)}, u32[]{:S(2)}, u32[]{:S(2)}) collective-permute-start(bf16[4,32,128]{2,1,0:T(8,128)(2,1)S(1)} %join_columns.1.own_ref), channel_id=1, source_target_pairs={{0,24},{1,25},{2,26},{3,27},{4,28},{5,29},{6,30},{7,31},{8,16},{9,... | collective-permute-start | bytes 98312 | tf_op jit(solution)/shard_map/ppermute | solution.py:423
  12.0 3.5 %collective-permute-start.5 = (bf16[4,32,128]{2,1,0:T(8,128)(2,1)S(1)}, bf16[4,32,128]{2,1,0:T(8,128)(2,1)S(1)}, u32[]{:S(2)}, u32[]{:S(2)}) collective-permute-start(bf16[4,32,128]{2,1,0:T(8,128)(2,1)S(1)} %join_columns.1.own_ref), channel_id=1, source_target_pairs={{0,8},{1,9},{2,10},{3,11},{4,12},{5,13},{6,14},{7,15},{8,0},{9,1},... | collective-permute-start | bytes 98312 | tf_op jit(solution)/shard_map/ppermute | solution.py:423
  13.8 1.7 %collective-permute-start.7 = (bf16[4,32,128]{2,1,0:T(8,128)(2,1)S(1)}, bf16[4,32,128]{2,1,0:T(8,128)(2,1)S(1)}, u32[]{:S(2)}, u32[]{:S(2)}) collective-permute-start(bf16[4,32,128]{2,1,0:T(8,128)(2,1)S(1)} %collective-permute-done.6.mate), channel_id=1, source_target_pairs={{0,8},{1,9},{2,10},{3,11},{4,12},{5,13},{6,14},{7,15},{8,0},{9,1},... | collective-permute-start | bytes 98312 | tf_op jit(solution)/shard_map/ppermute | solution.py:423
  14.7 7.2 %copy-start = (bf16[640,1280]{1,0:T(8,128)(2,1)S(1)}, bf16[640,1280]{1,0:T(8,128)(2,1)}, u32[]{:S(2)}) copy-start(bf16[640,1280]{1,0:T(8,128)(2,1)} %refs_6_.1) | copy-start | bytes 4915204
  16.3 6.6 %copy-start.5 = (bf16[1280,640]{1,0:T(8,128)(2,1)S(1)}, bf16[1280,640]{1,0:T(8,128)(2,1)}, u32[]{:S(2)}) copy-start(bf16[1280,640]{1,0:T(8,128)(2,1)} %refs_7_.1) | copy-start | bytes 4915204
  16.3 5.6 %collective-permute-start.11 = (bf16[32,128]{1,0:T(8,128)(2,1)S(1)}, bf16[32,128]{1,0:T(8,128)(2,1)S(1)}, u32[]{:S(2)}, u32[]{:S(2)}) collective-permute-start(bf16[32,128]{1,0:T(8,128)(2,1)S(1)} %get-tuple-element.28), channel_id=1, source_target_pairs={{0,6},{1,7},{2,4},{3,5},{4,2},{5,3},{6,0},{7,1},{8,14},{9,15},{10,... | collective-permute-start | bytes 24584 | tf_op jit(solution)/shard_map/ppermute | solution.py:410
  18.3 4.5 %collective-permute-start.10 = (bf16[32,128]{1,0:T(8,128)(2,1)S(1)}, bf16[32,128]{1,0:T(8,128)(2,1)S(1)}, u32[]{:S(2)}, u32[]{:S(2)}) collective-permute-start(bf16[32,128]{1,0:T(8,128)(2,1)S(1)} %get-tuple-element.26), channel_id=1, source_target_pairs={{0,4},{1,5},{2,6},{3,7},{4,0},{5,1},{6,2},{7,3},{8,12},{9,13},{10,... | collective-permute-start | bytes 24584 | tf_op jit(solution)/shard_map/ppermute | solution.py:410
  18.3 4.5 %collective-permute-start.9 = (bf16[32,128]{1,0:T(8,128)(2,1)S(1)}, bf16[32,128]{1,0:T(8,128)(2,1)S(1)}, u32[]{:S(2)}, u32[]{:S(2)}) collective-permute-start(bf16[32,128]{1,0:T(8,128)(2,1)S(1)} %get-tuple-element.25), channel_id=1, source_target_pairs={{0,2},{1,3},{2,0},{3,1},{4,6},{5,7},{6,4},{7,5},{8,10},{9,11},{10,... | collective-permute-start | bytes 24584 | tf_op jit(solution)/shard_map/ppermute | solution.py:410

commit v14 on v11

--- a/solution.py
+++ b/solution.py
@@ -66,12 +66,11 @@
 
 
 def group_points(latent_ref, points):
-    width, rows, _ = latent_ref.shape
-    rest = width - SUBLANES
-    for row in range(rows):
-        points[row * SUBLANES : (row + 1) * SUBLANES] = latent_ref[:SUBLANES, row, :].astype(F32)
-        at = rows * SUBLANES + row * rest
-        points[at : at + rest] = latent_ref[SUBLANES:, row, :].astype(F32)
+    rows = latent_ref.shape[1]
+    latent = latent_ref[...].astype(F32)
+    split = [latent[:, row, :] for row in range(rows)]
+    parts = [block[:SUBLANES] for block in split] + [block[SUBLANES:] for block in split]
+    points[...] = jnp.concatenate(parts, axis=0)
 
 
 def pack_kernel(order, latent_ref, *refs):

time: 24.3 us -> 24.3 us (level)
  no operation moved by 1% of the time
where the time goes in v14:
time: 24.3 us; the launch traced here: 24.2 us
  starting transfers between devices  15 us (62%)
  waiting for transfers between devices  4.8 us (20%)
  Pallas kernels  4.2 us (17%)
    ppermute x6, starting transfers between devices, over_columns(): return lax.ppermute(message, 'lon', pairs) if apart else message  10.3 us
    pallas_call x11, Pallas kernels, call(): pl.pallas_call(kernel, out_shape=out_shape, in_specs=[VMEM] * len(operand...  4.2 us
    ppermute x6, waiting for transfers between devices, over_columns(): return lax.ppermute(message, 'lon', pairs) if apart else message  3.43 us
    ppermute x5, starting transfers between devices, swap(): return lax.ppermute(block, ('lat', 'lon'), pairs)  3.27 us
    ppermute x1, starting transfers between devices, over_sides(): return lax.ppermute(block, 'lon', [(i, i ^ 1) for i in range(count)])  1.49 us
    ppermute x5, waiting for transfers between devices, swap(): return lax.ppermute(block, ('lat', 'lon'), pairs)  1.37 us
  transfers between devices with their start and end apart: 12, of which 6 were waited for; matrix products, arithmetic and copies ran while one was open for 0% of the time, Pallas kernels for 9%

profile of v14, /device:TPU:0, one launch (start us, length us, event | category | flops | bytes accessed | tf_op | source)
XLA Modules:
  0.0 24.2 jit_solution(6473226143232692539)
XLA Ops:
  0.0 0.0 copy-start.2
  0.0 4.0 %collective-permute-start = (bf16[12,2,640]{2,1,0:T(2,128)(2,1)}, bf16[12,2,640]{2,1,0:T(2,128)(2,1)S(1)}, u32[]{:S(2)}, u32[]{:S(2)}) collective-permute-start(bf16[12,2,640]{2,1,0:T(2,128)(2,1)} %bitcast.6), channel_id=1, source_target_pairs={{0,4},{1,5},{2,6},{3,7},{4,0},{5,1},{6,2},{7,3},{8,12},{9,13},{10,... | collective-permute-start | bytes 92168 | tf_op jit(solution)/shard_map/ppermute | solution.py:401
  4.1 0.0 copy-done.2
  4.1 0.0 copy-start.1
  4.1 0.0 copy-start.3
  4.1 0.0 copy-start.4
  4.1 0.2 pack.1
  4.3 1.7 %collective-permute-start.1 = (bf16[32,128]{1,0:T(8,128)(2,1)S(1)}, bf16[32,128]{1,0:T(8,128)(2,1)S(1)}, u32[]{:S(2)}, u32[]{:S(2)}) collective-permute-start(bf16[32,128]{1,0:T(8,128)(2,1)S(1)} %get-tuple-element.20), channel_id=1, source_target_pairs={{0,6},{1,7},{2,4},{3,5},{4,2},{5,3},{6,0},{7,1},{8,14},{9,15},{10,... | collective-permute-start | bytes 24584 | tf_op jit(solution)/shard_map/ppermute | solution.py:401
  6.0 0.0 collective-permute-start.2
  6.0 0.0 copy-done.1
  6.0 1.5 %collective-permute-start.8 = (bf16[9,20,80]{2,1,0:T(8,128)(2,1)S(1)}, bf16[9,20,80]{2,1,0:T(8,128)(2,1)S(1)}, u32[]{:S(2)}, u32[]{:S(2)}) collective-permute-start(bf16[9,20,80]{2,1,0:T(8,128)(2,1)S(1)} %bitcast.4), channel_id=1, source_target_pairs={{0,1},{1,0},{2,3},{3,2},{4,5},{5,4},{6,7},{7,6},{8,9},{9,8},{10,11... | collective-permute-start | bytes 86408 | tf_op jit(solution)/shard_map/ppermute | solution.py:405
  7.5 0.0 copy-done.3
  7.5 0.0 copy-done.4
  7.5 0.4 %tables.1.table_ref = bf16[2,432,384]{2,1,0:T(8,128)(2,1)S(1)} custom-call(bf16[9,96]{1,0:T(8,128)(2,1)S(1)} %copy-done.3, bf16[3,2,9]{2,1,0:T(2,128)(2,1)S(1)} %bitcast.9, s32[96,128]{1,0:T(8,128)S(1)} %apart.1.apart_ref), custom_call_target="tpu_custom_call" | custom-call | flops 1000000 | bytes 1000000 | tf_op jit(solution)/shard_map/tables/pallas_call | solution.py:387
  7.9 0.0 collective-permute-done.raw_ref
  7.9 0.2 cut.1.refs_0_
  8.1 1.7 %collective-permute-done.1.refs_1_ = bf16[32,128]{1,0:T(8,128)(2,1)S(1)} collective-permute-done((bf16[32,128]{1,0:T(8,128)(2,1)S(1)}, bf16[32,128]{1,0:T(8,128)(2,1)S(1)}, u32[]{:S(2)}, u32[]{:S(2)}) %collective-permute-start.1) | collective-permute-done | bytes 8224 | tf_op jit(solution)/shard_map/ppermute | solution.py:401
  9.8 0.0 collective-permute-done.2.refs_2_
  9.8 1.6 %collective-permute-start.6 = (bf16[4,32,128]{2,1,0:T(8,128)(2,1)S(1)}, bf16[4,32,128]{2,1,0:T(8,128)(2,1)S(1)}, u32[]{:S(2)}, u32[]{:S(2)}) collective-permute-start(bf16[4,32,128]{2,1,0:T(8,128)(2,1)S(1)} %join_columns.1.own_ref), channel_id=1, source_target_pairs={{0,1},{1,0},{2,3},{3,2},{4,5},{5,4},{6,7},{7,6},{8,9},{9,8},{10,11... | collective-permute-start | bytes 98312 | tf_op jit(solution)/shard_map/ppermute | solution.py:414
  11.4 0.1 unpack.1.own
  11.5 0.5 %collective-permute-start.3 = (bf16[4,32,128]{2,1,0:T(8,128)(2,1)S(1)}, bf16[4,32,128]{2,1,0:T(8,128)(2,1)S(1)}, u32[]{:S(2)}, u32[]{:S(2)}) collective-permute-start(bf16[4,32,128]{2,1,0:T(8,128)(2,1)S(1)} %join_columns.1.own_ref), channel_id=1, source_target_pairs={{0,1},{1,0},{2,3},{3,2},{4,5},{5,4},{6,7},{7,6},{8,17},{9,16},{10,... | collective-permute-start | bytes 98312 | tf_op jit(solution)/shard_map/ppermute | solution.py:414
  12.0 0.0 collective-permute-start.4
  12.0 1.2 %collective-permute-start.5 = (bf16[4,32,128]{2,1,0:T(8,128)(2,1)S(1)}, bf16[4,32,128]{2,1,0:T(8,128)(2,1)S(1)}, u32[]{:S(2)}, u32[]{:S(2)}) collective-permute-start(bf16[4,32,128]{2,1,0:T(8,128)(2,1)S(1)} %join_columns.1.own_ref), channel_id=1, source_target_pairs={{0,8},{1,9},{2,10},{3,11},{4,12},{5,13},{6,14},{7,15},{8,0},{9,1},... | collective-permute-start | bytes 98312 | tf_op jit(solution)/shard_map/ppermute | solution.py:414
  13.2 0.0 collective-permute-done.8.mate_ref
  13.2 0.6 %collective-permute-done.6.mate = bf16[4,32,128]{2,1,0:T(8,128)(2,1)S(1)} collective-permute-done((bf16[4,32,128]{2,1,0:T(8,128)(2,1)S(1)}, bf16[4,32,128]{2,1,0:T(8,128)(2,1)S(1)}, u32[]{:S(2)}, u32[]{:S(2)}) %collective-permute-start.6) | collective-permute-done | bytes 32800 | tf_op jit(solution)/shard_map/ppermute | solution.py:414
  13.8 0.0 collective-permute-start.7
  13.8 0.5 %squares.1.squares_ref = bf16[2304,256]{1,0:T(8,128)(2,1)S(1)} custom-call(bf16[9,20,80]{2,1,0:T(8,128)(2,1)S(1)} %bitcast.5, bf16[9,20,80]{2,1,0:T(8,128)(2,1)S(1)} %collective-permute-done.8.mate_ref), custom_call_target="tpu_custom_call" | custom-call | flops 300000000 | bytes 1000000 | tf_op jit(solution)/shard_map/squares/pallas_call | solution.py:387
  14.4 0.3 %conv_own.1.part_ref = f32[2,432,256]{2,1,0:T(8,128)S(1)} custom-call(bf16[4,32,128]{2,1,0:T(8,128)(2,1)S(1)} %collective-permute-done.6.mate, bf16[2,4,16,256]{3,2,1,0:T(8,128)(2,1)S(1)} %unpack.1.own, bf16[2,432,384]{2,1,0:T(8,128)(2,1)S(1)} %tables.1.table_ref), custom_call_target="tpu_custom_call" | custom-call | flops 300000000 | bytes 1000000 | tf_op jit(solution)/shard_map/conv_own/pallas_call | solution.py:387
  14.7 0.0 copy-start
  14.7 0.7 %collective-permute-done.3.odd_mate = bf16[4,32,128]{2,1,0:T(8,128)(2,1)S(1)} collective-permute-done((bf16[4,32,128]{2,1,0:T(8,128)(2,1)S(1)}, bf16[4,32,128]{2,1,0:T(8,128)(2,1)S(1)}, u32[]{:S(2)}, u32[]{:S(2)}) %collective-permute-start.3) | collective-permute-done | bytes 32800 | tf_op jit(solution)/shard_map/ppermute | solution.py:414
  15.4 0.1 collective-permute-done.4.odd_own
  15.5 0.0 collective-permute-done.5.even_own
  15.5 0.0 collective-permute-done.7.even_mate
  15.5 0.8 %conv.1 = (bf16[32,128]{1,0:T(8,128)(2,1)S(1)}, bf16[32,128]{1,0:T(8,128)(2,1)S(1)}, bf16[32,128]{1,0:T(8,128)(2,1)S(1)}, bf16[32,128]{1,0:T(8,128)(2,1)S(1)}) custom-call(bf16[4,32,128]{2,1,0:T(8,128)(2,1)S(1)} %collective-permute-done.3.odd_mate, bf16[4,32,128]{2,1,0:T(8,128)(2,1)S(1)} %collective-permute-done.4.odd_own, ...), custom_call_target="tpu_custom_call" | custom-call | flops 10000000000 | bytes 1000000 | tf_op jit(solution)/shard_map/conv/pallas_call | solution.py:387
  16.3 0.0 copy-start.5
  16.3 2.0 %collective-permute-start.11 = (bf16[32,128]{1,0:T(8,128)(2,1)S(1)}, bf16[32,128]{1,0:T(8,128)(2,1)S(1)}, u32[]{:S(2)}, u32[]{:S(2)}) collective-permute-start(bf16[32,128]{1,0:T(8,128)(2,1)S(1)} %get-tuple-element.28), channel_id=1, source_target_pairs={{0,6},{1,7},{2,4},{3,5},{4,2},{5,3},{6,0},{7,1},{8,14},{9,15},{10,... | collective-permute-start | bytes 24584 | tf_op jit(solution)/shard_map/ppermute | solution.py:401
  18.3 0.0 collective-permute-start.10
  18.3 2.5 %collective-permute-start.9 = (bf16[32,128]{1,0:T(8,128)(2,1)S(1)}, bf16[32,128]{1,0:T(8,128)(2,1)S(1)}, u32[]{:S(2)}, u32[]{:S(2)}) collective-permute-start(bf16[32,128]{1,0:T(8,128)(2,1)S(1)} %get-tuple-element.25), channel_id=1, source_target_pairs={{0,2},{1,3},{2,0},{3,1},{4,6},{5,7},{6,4},{7,5},{8,10},{9,11},{10,... | collective-permute-start | bytes 24584 | tf_op jit(solution)/shard_map/ppermute | solution.py:401
  20.7 1.1 %collective-permute-done.11.first_ref = bf16[32,128]{1,0:T(8,128)(2,1)S(1)} collective-permute-done((bf16[32,128]{1,0:T(8,128)(2,1)S(1)}, bf16[32,128]{1,0:T(8,128)(2,1)S(1)}, u32[]{:S(2)}, u32[]{:S(2)}) %collective-permute-start.11) | collective-permute-done | bytes 8224 | tf_op jit(solution)/shard_map/ppermute | solution.py:401
  21.9 0.0 copy-done
  21.9 0.4 %lift.1 = (f32[4,24,256]{2,1,0:T(8,128)S(1)}, f32[24,640]{1,0:T(8,128)S(1)}, f32[32,1280]{1,0:T(8,128)S(1)}, f32[2,24,128]{2,1,0:T(8,128)S(1)}) custom-call(bf16[32,128]{1,0:T(8,128)(2,1)S(1)} %get-tuple-element.27.own_ref, bf16[32,128]{1,0:T(8,128)(2,1)S(1)} %collective-permute-done.11.first_ref, bf16[12,2,640]{2,1,0:T(2,128)(2,1)S(1)} %bitcast.8, ...), custom_call_target="tpu_custom_call" | custom-call | flops 100000000 | bytes 1000000 | tf_op jit(solution)/shard_map/lift/pallas_call | solution.py:387
  22.2 0.6 %collective-permute-done.10.refs_1_ = bf16[32,128]{1,0:T(8,128)(2,1)S(1)} collective-permute-done((bf16[32,128]{1,0:T(8,128)(2,1)S(1)}, bf16[32,128]{1,0:T(8,128)(2,1)S(1)}, u32[]{:S(2)}, u32[]{:S(2)}) %collective-permute-start.10) | collective-permute-done | bytes 8224 | tf_op jit(solution)/shard_map/ppermute | solution.py:401
  22.8 0.0 collective-permute-done.9.refs_0_
  22.8 0.0 copy-done.5
  22.8 1.3 %tail.1 = bf16[12,2,640]{2,1,0:T(2,128)(2,1)} custom-call(bf16[32,128]{1,0:T(8,128)(2,1)S(1)} %collective-permute-done.9.refs_0_, bf16[32,128]{1,0:T(8,128)(2,1)S(1)} %collective-permute-done.10.refs_1_, f32[4,24,256]{2,1,0:T(8,128)S(1)} %get-tuple-element.29.refs_2_, f32[24,640]{1,0:T(8,128)S(1)} %get-tuple-element.30.refs_3_, ...), custom_call_target="tpu_custom_call" | custom-call | flops 1000000000 | bytes 1000000 | tf_op jit(solution)/shard_map/tail/pallas_call | solution.py:387
  (2 shorter events, 0.0 us)
Async XLA Ops:
  0.0 4.1 %copy-start.2 = (bf16[2,12,640]{2,0,1:T(2,128)(2,1)S(1)}, bf16[2,12,640]{2,0,1:T(2,128)(2,1)}, u32[]{:S(2)}) copy-start(bf16[2,12,640]{2,0,1:T(2,128)(2,1)} %param.7) | copy-start | bytes 92164
  0.0 7.9 %collective-permute-start = (bf16[12,2,640]{2,1,0:T(2,128)(2,1)}, bf16[12,2,640]{2,1,0:T(2,128)(2,1)S(1)}, u32[]{:S(2)}, u32[]{:S(2)}) collective-permute-start(bf16[12,2,640]{2,1,0:T(2,128)(2,1)} %bitcast.6), channel_id=1, source_target_pairs={{0,4},{1,5},{2,6},{3,7},{4,0},{5,1},{6,2},{7,3},{8,12},{9,13},{10,... | collective-permute-start | bytes 92168 | tf_op jit(solution)/shard_map/ppermute | solution.py:401
  4.1 2.0 %copy-start.1 = (bf16[9,80,20]{1,2,0:T(8,128)(2,1)S(1)}, bf16[9,80,20]{1,2,0:T(8,128)(2,1)}, u32[]{:S(2)}) copy-start(bf16[9,80,20]{1,2,0:T(8,128)(2,1)} %param.9) | copy-start | bytes 86404
  4.1 3.4 %copy-start.3 = (bf16[9,96]{1,0:T(8,128)(2,1)S(1)}, bf16[9,96]{1,0:T(8,128)(2,1)}, u32[]{:S(2)}) copy-start(bf16[9,96]{1,0:T(8,128)(2,1)} %filter_ref.1) | copy-start | bytes 5188
  4.1 3.4 %copy-start.4 = (bf16[9,2,3]{0,1,2:T(2,128)(2,1)S(1)}, bf16[9,2,3]{0,1,2:T(2,128)(2,1)}, u32[]{:S(2)}) copy-start(bf16[9,2,3]{0,1,2:T(2,128)(2,1)} %param.10) | copy-start | bytes 328
  4.3 5.5 %collective-permute-start.1 = (bf16[32,128]{1,0:T(8,128)(2,1)S(1)}, bf16[32,128]{1,0:T(8,128)(2,1)S(1)}, u32[]{:S(2)}, u32[]{:S(2)}) collective-permute-start(bf16[32,128]{1,0:T(8,128)(2,1)S(1)} %get-tuple-element.20), channel_id=1, source_target_pairs={{0,6},{1,7},{2,4},{3,5},{4,2},{5,3},{6,0},{7,1},{8,14},{9,15},{10,... | collective-permute-start | bytes 24584 | tf_op jit(solution)/shard_map/ppermute | solution.py:401
  6.0 3.8 %collective-permute-start.2 = (bf16[32,128]{1,0:T(8,128)(2,1)S(1)}, bf16[32,128]{1,0:T(8,128)(2,1)S(1)}, u32[]{:S(2)}, u32[]{:S(2)}) collective-permute-start(bf16[32,128]{1,0:T(8,128)(2,1)S(1)} %get-tuple-element.21), channel_id=1, source_target_pairs={{0,2},{1,3},{2,0},{3,1},{4,6},{5,7},{6,4},{7,5},{8,10},{9,11},{10,... | collective-permute-start | bytes 24584 | tf_op jit(solution)/shard_map/ppermute | solution.py:401
  6.0 7.1 %collective-permute-start.8 = (bf16[9,20,80]{2,1,0:T(8,128)(2,1)S(1)}, bf16[9,20,80]{2,1,0:T(8,128)(2,1)S(1)}, u32[]{:S(2)}, u32[]{:S(2)}) collective-permute-start(bf16[9,20,80]{2,1,0:T(8,128)(2,1)S(1)} %bitcast.4), channel_id=1, source_target_pairs={{0,1},{1,0},{2,3},{3,2},{4,5},{5,4},{6,7},{7,6},{8,9},{9,8},{10,11... | collective-permute-start | bytes 86408 | tf_op jit(solution)/shard_map/ppermute | solution.py:405
  9.8 4.0 %collective-permute-start.6 = (bf16[4,32,128]{2,1,0:T(8,128)(2,1)S(1)}, bf16[4,32,128]{2,1,0:T(8,128)(2,1)S(1)}, u32[]{:S(2)}, u32[]{:S(2)}) collective-permute-start(bf16[4,32,128]{2,1,0:T(8,128)(2,1)S(1)} %join_columns.1.own_ref), channel_id=1, source_target_pairs={{0,1},{1,0},{2,3},{3,2},{4,5},{5,4},{6,7},{7,6},{8,9},{9,8},{10,11... | collective-permute-start | bytes 98312 | tf_op jit(solution)/shard_map/ppermute | solution.py:414
  11.5 3.9 %collective-permute-start.3 = (bf16[4,32,128]{2,1,0:T(8,128)(2,1)S(1)}, bf16[4,32,128]{2,1,0:T(8,128)(2,1)S(1)}, u32[]{:S(2)}, u32[]{:S(2)}) collective-permute-start(bf16[4,32,128]{2,1,0:T(8,128)(2,1)S(1)} %join_columns.1.own_ref), channel_id=1, source_target_pairs={{0,1},{1,0},{2,3},{3,2},{4,5},{5,4},{6,7},{7,6},{8,17},{9,16},{10,... | collective-permute-start | bytes 98312 | tf_op jit(solution)/shard_map/ppermute | solution.py:414
  12.0 3.5 %collective-permute-start.4 = (bf16[4,32,128]{2,1,0:T(8,128)(2,1)S(1)}, bf16[4,32,128]{2,1,0:T(8,128)(2,1)S(1)}, u32[]{:S(2)}, u32[]{:S(2)}) collective-permute-start(bf16[4,32,128]{2,1,0:T(8,128)(2,1)S(1)} %join_columns.1.own_ref), channel_id=1, source_target_pairs={{0,24},{1,25},{2,26},{3,27},{4,28},{5,29},{6,30},{7,31},{8,16},{9,... | collective-permute-start | bytes 98312 | tf_op jit(solution)/shard_map/ppermute | solution.py:414
  12.0 3.5 %collective-permute-start.5 = (bf16[4,32,128]{2,1,0:T(8,128)(2,1)S(1)}, bf16[4,32,128]{2,1,0:T(8,128)(2,1)S(1)}, u32[]{:S(2)}, u32[]{:S(2)}) collective-permute-start(bf16[4,32,128]{2,1,0:T(8,128)(2,1)S(1)} %join_columns.1.own_ref), channel_id=1, source_target_pairs={{0,8},{1,9},{2,10},{3,11},{4,12},{5,13},{6,14},{7,15},{8,0},{9,1},... | collective-permute-start | bytes 98312 | tf_op jit(solution)/shard_map/ppermute | solution.py:414
  13.8 1.7 %collective-permute-start.7 = (bf16[4,32,128]{2,1,0:T(8,128)(2,1)S(1)}, bf16[4,32,128]{2,1,0:T(8,128)(2,1)S(1)}, u32[]{:S(2)}, u32[]{:S(2)}) collective-permute-start(bf16[4,32,128]{2,1,0:T(8,128)(2,1)S(1)} %collective-permute-done.6.mate), channel_id=1, source_target_pairs={{0,8},{1,9},{2,10},{3,11},{4,12},{5,13},{6,14},{7,15},{8,0},{9,1},... | collective-permute-start | bytes 98312 | tf_op jit(solution)/shard_map/ppermute | solution.py:414
  14.7 7.2 %copy-start = (bf16[640,1280]{1,0:T(8,128)(2,1)S(1)}, bf16[640,1280]{1,0:T(8,128)(2,1)}, u32[]{:S(2)}) copy-start(bf16[640,1280]{1,0:T(8,128)(2,1)} %refs_6_.1) | copy-start | bytes 4915204
  16.3 6.6 %copy-start.5 = (bf16[1280,640]{1,0:T(8,128)(2,1)S(1)}, bf16[1280,640]{1,0:T(8,128)(2,1)}, u32[]{:S(2)}) copy-start(bf16[1280,640]{1,0:T(8,128)(2,1)} %refs_7_.1) | copy-start | bytes 4915204
  16.3 5.6 %collective-permute-start.11 = (bf16[32,128]{1,0:T(8,128)(2,1)S(1)}, bf16[32,128]{1,0:T(8,128)(2,1)S(1)}, u32[]{:S(2)}, u32[]{:S(2)}) collective-permute-start(bf16[32,128]{1,0:T(8,128)(2,1)S(1)} %get-tuple-element.28), channel_id=1, source_target_pairs={{0,6},{1,7},{2,4},{3,5},{4,2},{5,3},{6,0},{7,1},{8,14},{9,15},{10,... | collective-permute-start | bytes 24584 | tf_op jit(solution)/shard_map/ppermute | solution.py:401
  18.3 4.5 %collective-permute-start.10 = (bf16[32,128]{1,0:T(8,128)(2,1)S(1)}, bf16[32,128]{1,0:T(8,128)(2,1)S(1)}, u32[]{:S(2)}, u32[]{:S(2)}) collective-permute-start(bf16[32,128]{1,0:T(8,128)(2,1)S(1)} %get-tuple-element.26), channel_id=1, source_target_pairs={{0,4},{1,5},{2,6},{3,7},{4,0},{5,1},{6,2},{7,3},{8,12},{9,13},{10,... | collective-permute-start | bytes 24584 | tf_op jit(solution)/shard_map/ppermute | solution.py:401
  18.3 4.5 %collective-permute-start.9 = (bf16[32,128]{1,0:T(8,128)(2,1)S(1)}, bf16[32,128]{1,0:T(8,128)(2,1)S(1)}, u32[]{:S(2)}, u32[]{:S(2)}) collective-permute-start(bf16[32,128]{1,0:T(8,128)(2,1)S(1)} %get-tuple-element.25), channel_id=1, source_target_pairs={{0,2},{1,3},{2,0},{3,1},{4,6},{5,7},{6,4},{7,5},{8,10},{9,11},{10,... | collective-permute-start | bytes 24584 | tf_op jit(solution)/shard_map/ppermute | solution.py:401

commit v15 on v11

--- a/solution.py
+++ b/solution.py
@@ -193,7 +193,7 @@
             out_ref[row, at] = read
 
 
-def own_kernel(block, width, mate, own, table_ref, part_ref, field):
+def own_kernel(block, width, mate, own, even, table_ref, part_ref, even_ref, field):
     rows, columns, step, _ = own.shape
     places = field.shape[1]
     side = lax.axis_index("lon") % 2
@@ -207,6 +207,9 @@
         part_ref[row] = jnp.dot(
             table_ref[row, :, 2 * places :], field[row], preferred_element_type=F32
         )
+    for at in range(columns):
+        for row, read in enumerate(rows_of(even[at], block, width - SUBLANES)):
+            even_ref[row, at] = read
 
 
 def conv_kernel(
@@ -214,9 +217,9 @@
     width,
     odd_mate,
     odd_own,
-    even_own,
     even_mate,
     part_ref,
+    even_rows,
     table_ref,
     squares_ref,
     *refs,
@@ -239,7 +242,9 @@
             field[row, pl.ds(first, step)] = read
 
     for at in range(columns):
-        place(1 - odd, 2 * at + side, even_own[at])
+        for slot in range(2):
+            first = pl.multiple_of(slot * places + (2 * at + side) * step, step)
+            field[1 - odd, pl.ds(first, step)] = even_rows[slot, at]
         place(1 - odd, 2 * at + 1 - side, even_mate[at])
         place(odd, 2 * at + side, odd_own[at])
         place(odd, 2 * at + 1 - side, odd_mate[at])
@@ -516,11 +521,15 @@
     part = call(
         functools.partial(own_kernel, block, width),
         "conv_own",
-        jax.ShapeDtypeStruct((rows, bases * columns * width, lanes), F32),
+        (
+            jax.ShapeDtypeStruct((rows, bases * columns * width, lanes), F32),
+            jax.ShapeDtypeStruct((rows, columns, step, lanes), BF16),
+        ),
         [pltpu.VMEM((rows, places, lanes), BF16)],
         3 * 10**8,
         mate_side,
         own_rows,
+        even_own,
         table,
     )
     mixed = call(
@@ -534,9 +543,8 @@
         10**10,
         odd_mate,
         odd_own,
-        even_own,
         even_mate,
-        part,
+        *part,
         table,
         squares,
     )

time: 24.3 us -> 24.3 us (level)
    ppermute x5, waiting for transfers between devices: 1.37 us -> 1.11 us  [swap(): return lax.ppermute(block, ('lat', 'lon'), pairs)]
  transfers between devices with their start and end apart: 12 -> 12, of which waited for: 6 -> 5; matrix products, arithmetic and copies ran while one was open for 0% -> 0% of each run, Pallas kernels for 9% -> 9%
where the time goes in v15:
time: 24.3 us; the launch traced here: 24.1 us
  starting transfers between devices  15.2 us (63%)
  waiting for transfers between devices  4.56 us (19%)
  Pallas kernels  4.23 us (17%)
    ppermute x6, starting transfers between devices, over_columns(): return lax.ppermute(message, 'lon', pairs) if apart else message  10.2 us
    pallas_call x11, Pallas kernels, call(): pl.pallas_call(kernel, out_shape=out_shape, in_specs=[VMEM] * len(operand...  4.23 us
    ppermute x5, starting transfers between devices, swap(): return lax.ppermute(block, ('lat', 'lon'), pairs)  3.45 us
    ppermute x6, waiting for transfers between devices, over_columns(): return lax.ppermute(message, 'lon', pairs) if apart else message  3.45 us
    ppermute x1, starting transfers between devices, over_sides(): return lax.ppermute(block, 'lon', [(i, i ^ 1) for i in range(count)])  1.49 us
    ppermute x5, waiting for transfers between devices, swap(): return lax.ppermute(block, ('lat', 'lon'), pairs)  1.11 us
  transfers between devices with their start and end apart: 12, of which 5 were waited for; matrix products, arithmetic and copies ran while one was open for 0% of the time, Pallas kernels for 9%

profile of v15, /device:TPU:0, one launch (start us, length us, event | category | flops | bytes accessed | tf_op | source)
XLA Modules:
  0.0 24.1 jit_solution(6191975592213087895)
XLA Ops:
  0.0 0.0 copy-start.2
  0.0 4.0 %collective-permute-start = (bf16[12,2,640]{2,1,0:T(2,128)(2,1)}, bf16[12,2,640]{2,1,0:T(2,128)(2,1)S(1)}, u32[]{:S(2)}, u32[]{:S(2)}) collective-permute-start(bf16[12,2,640]{2,1,0:T(2,128)(2,1)} %bitcast.6), channel_id=1, source_target_pairs={{0,4},{1,5},{2,6},{3,7},{4,0},{5,1},{6,2},{7,3},{8,12},{9,13},{10,... | collective-permute-start | bytes 92168 | tf_op jit(solution)/shard_map/ppermute | solution.py:407
  4.1 0.0 copy-done.2
  4.1 0.0 copy-start.1
  4.1 0.0 copy-start.3
  4.1 0.0 copy-start.4
  4.1 0.2 pack.1
  4.3 1.7 %collective-permute-start.1 = (bf16[32,128]{1,0:T(8,128)(2,1)S(1)}, bf16[32,128]{1,0:T(8,128)(2,1)S(1)}, u32[]{:S(2)}, u32[]{:S(2)}) collective-permute-start(bf16[32,128]{1,0:T(8,128)(2,1)S(1)} %get-tuple-element.22), channel_id=1, source_target_pairs={{0,6},{1,7},{2,4},{3,5},{4,2},{5,3},{6,0},{7,1},{8,14},{9,15},{10,... | collective-permute-start | bytes 24584 | tf_op jit(solution)/shard_map/ppermute | solution.py:407
  6.0 0.0 collective-permute-start.2
  6.0 0.0 copy-done.1
  6.0 1.5 %collective-permute-start.8 = (bf16[9,20,80]{2,1,0:T(8,128)(2,1)S(1)}, bf16[9,20,80]{2,1,0:T(8,128)(2,1)S(1)}, u32[]{:S(2)}, u32[]{:S(2)}) collective-permute-start(bf16[9,20,80]{2,1,0:T(8,128)(2,1)S(1)} %bitcast.4), channel_id=1, source_target_pairs={{0,1},{1,0},{2,3},{3,2},{4,5},{5,4},{6,7},{7,6},{8,9},{9,8},{10,11... | collective-permute-start | bytes 86408 | tf_op jit(solution)/shard_map/ppermute | solution.py:411
  7.5 0.0 copy-done.3
  7.5 0.0 copy-done.4
  7.5 0.4 %tables.1.table_ref = bf16[2,432,384]{2,1,0:T(8,128)(2,1)S(1)} custom-call(bf16[9,96]{1,0:T(8,128)(2,1)S(1)} %copy-done.3, bf16[3,2,9]{2,1,0:T(2,128)(2,1)S(1)} %bitcast.9, s32[96,128]{1,0:T(8,128)S(1)} %apart.1.apart_ref), custom_call_target="tpu_custom_call" | custom-call | flops 1000000 | bytes 1000000 | tf_op jit(solution)/shard_map/tables/pallas_call | solution.py:393
  7.9 0.0 collective-permute-done.raw_ref
  7.9 0.2 cut.1.refs_0_
  8.1 1.7 %collective-permute-done.1.refs_1_ = bf16[32,128]{1,0:T(8,128)(2,1)S(1)} collective-permute-done((bf16[32,128]{1,0:T(8,128)(2,1)S(1)}, bf16[32,128]{1,0:T(8,128)(2,1)S(1)}, u32[]{:S(2)}, u32[]{:S(2)}) %collective-permute-start.1) | collective-permute-done | bytes 8224 | tf_op jit(solution)/shard_map/ppermute | solution.py:407
  9.8 0.0 collective-permute-done.2.refs_2_
  9.8 1.6 %collective-permute-start.5 = (bf16[4,32,128]{2,1,0:T(8,128)(2,1)S(1)}, bf16[4,32,128]{2,1,0:T(8,128)(2,1)S(1)}, u32[]{:S(2)}, u32[]{:S(2)}) collective-permute-start(bf16[4,32,128]{2,1,0:T(8,128)(2,1)S(1)} %join_columns.1.own_ref), channel_id=1, source_target_pairs={{0,1},{1,0},{2,3},{3,2},{4,5},{5,4},{6,7},{7,6},{8,9},{9,8},{10,11... | collective-permute-start | bytes 98312 | tf_op jit(solution)/shard_map/ppermute | solution.py:420
  11.4 0.0 collective-permute-start.7
  11.4 0.1 unpack.1.own
  11.5 0.5 %collective-permute-start.3 = (bf16[4,32,128]{2,1,0:T(8,128)(2,1)S(1)}, bf16[4,32,128]{2,1,0:T(8,128)(2,1)S(1)}, u32[]{:S(2)}, u32[]{:S(2)}) collective-permute-start(bf16[4,32,128]{2,1,0:T(8,128)(2,1)S(1)} %join_columns.1.own_ref), channel_id=1, source_target_pairs={{0,1},{1,0},{2,3},{3,2},{4,5},{5,4},{6,7},{7,6},{8,17},{9,16},{10,... | collective-permute-start | bytes 98312 | tf_op jit(solution)/shard_map/ppermute | solution.py:420
  12.0 1.4 %collective-permute-start.4 = (bf16[4,32,128]{2,1,0:T(8,128)(2,1)S(1)}, bf16[4,32,128]{2,1,0:T(8,128)(2,1)S(1)}, u32[]{:S(2)}, u32[]{:S(2)}) collective-permute-start(bf16[4,32,128]{2,1,0:T(8,128)(2,1)S(1)} %join_columns.1.own_ref), channel_id=1, source_target_pairs={{0,24},{1,25},{2,26},{3,27},{4,28},{5,29},{6,30},{7,31},{8,16},{9,... | collective-permute-start | bytes 98312 | tf_op jit(solution)/shard_map/ppermute | solution.py:420
  13.3 0.0 collective-permute-done.8.mate_ref
  13.3 0.4 %collective-permute-done.5.mate = bf16[4,32,128]{2,1,0:T(8,128)(2,1)S(1)} collective-permute-done((bf16[4,32,128]{2,1,0:T(8,128)(2,1)S(1)}, bf16[4,32,128]{2,1,0:T(8,128)(2,1)S(1)}, u32[]{:S(2)}, u32[]{:S(2)}) %collective-permute-start.5) | collective-permute-done | bytes 32800 | tf_op jit(solution)/shard_map/ppermute | solution.py:420
  13.8 0.0 collective-permute-start.6
  13.8 0.5 %squares.1.squares_ref = bf16[2304,256]{1,0:T(8,128)(2,1)S(1)} custom-call(bf16[9,20,80]{2,1,0:T(8,128)(2,1)S(1)} %bitcast.5, bf16[9,20,80]{2,1,0:T(8,128)(2,1)S(1)} %collective-permute-done.8.mate_ref), custom_call_target="tpu_custom_call" | custom-call | flops 300000000 | bytes 1000000 | tf_op jit(solution)/shard_map/squares/pallas_call | solution.py:393
  14.4 0.0 collective-permute-done.7.even
  14.4 0.3 %conv_own.1 = (f32[2,432,256]{2,1,0:T(8,128)S(1)}, bf16[2,4,16,256]{3,2,1,0:T(8,128)(2,1)S(1)}) custom-call(bf16[4,32,128]{2,1,0:T(8,128)(2,1)S(1)} %collective-permute-done.5.mate, bf16[2,4,16,256]{3,2,1,0:T(8,128)(2,1)S(1)} %unpack.1.own, bf16[4,32,128]{2,1,0:T(8,128)(2,1)S(1)} %collective-permute-done.7.even, bf16[2,432,384]{2,1,0:T(8,128)(2,1)S(1)} %tables.1.table_ref), custom_call_target="tpu_custom_call" | custom-call | flops 300000000 | bytes 1000000 | tf_op jit(solution)/shard_map/conv_own/pallas_call | solution.py:393
  14.7 0.7 %collective-permute-done.3.odd_mate = bf16[4,32,128]{2,1,0:T(8,128)(2,1)S(1)} collective-permute-done((bf16[4,32,128]{2,1,0:T(8,128)(2,1)S(1)}, bf16[4,32,128]{2,1,0:T(8,128)(2,1)S(1)}, u32[]{:S(2)}, u32[]{:S(2)}) %collective-permute-start.3) | collective-permute-done | bytes 32800 | tf_op jit(solution)/shard_map/ppermute | solution.py:420
  15.4 0.0 collective-permute-done.4.odd_own
  15.4 0.0 collective-permute-done.6.even_mate
  15.4 0.0 copy-start
  15.4 0.8 %conv.1 = (bf16[32,128]{1,0:T(8,128)(2,1)S(1)}, bf16[32,128]{1,0:T(8,128)(2,1)S(1)}, bf16[32,128]{1,0:T(8,128)(2,1)S(1)}, bf16[32,128]{1,0:T(8,128)(2,1)S(1)}) custom-call(bf16[4,32,128]{2,1,0:T(8,128)(2,1)S(1)} %collective-permute-done.3.odd_mate, bf16[4,32,128]{2,1,0:T(8,128)(2,1)S(1)} %collective-permute-done.4.odd_own, ...), custom_call_target="tpu_custom_call" | custom-call | flops 10000000000 | bytes 1000000 | tf_op jit(solution)/shard_map/conv/pallas_call | solution.py:393
  16.2 0.0 copy-start.5
  16.2 2.0 %collective-permute-start.11 = (bf16[32,128]{1,0:T(8,128)(2,1)S(1)}, bf16[32,128]{1,0:T(8,128)(2,1)S(1)}, u32[]{:S(2)}, u32[]{:S(2)}) collective-permute-start(bf16[32,128]{1,0:T(8,128)(2,1)S(1)} %get-tuple-element.32), channel_id=1, source_target_pairs={{0,6},{1,7},{2,4},{3,5},{4,2},{5,3},{6,0},{7,1},{8,14},{9,15},{10,... | collective-permute-start | bytes 24584 | tf_op jit(solution)/shard_map/ppermute | solution.py:407
  18.2 0.0 collective-permute-start.10
  18.2 2.4 %collective-permute-start.9 = (bf16[32,128]{1,0:T(8,128)(2,1)S(1)}, bf16[32,128]{1,0:T(8,128)(2,1)S(1)}, u32[]{:S(2)}, u32[]{:S(2)}) collective-permute-start(bf16[32,128]{1,0:T(8,128)(2,1)S(1)} %get-tuple-element.29), channel_id=1, source_target_pairs={{0,2},{1,3},{2,0},{3,1},{4,6},{5,7},{6,4},{7,5},{8,10},{9,11},{10,... | collective-permute-start | bytes 24584 | tf_op jit(solution)/shard_map/ppermute | solution.py:407
  20.6 1.1 %collective-permute-done.11.first_ref = bf16[32,128]{1,0:T(8,128)(2,1)S(1)} collective-permute-done((bf16[32,128]{1,0:T(8,128)(2,1)S(1)}, bf16[32,128]{1,0:T(8,128)(2,1)S(1)}, u32[]{:S(2)}, u32[]{:S(2)}) %collective-permute-start.11) | collective-permute-done | bytes 8224 | tf_op jit(solution)/shard_map/ppermute | solution.py:407
  21.7 0.0 copy-done
  21.7 0.4 %lift.1 = (f32[4,24,256]{2,1,0:T(8,128)S(1)}, f32[24,640]{1,0:T(8,128)S(1)}, f32[32,1280]{1,0:T(8,128)S(1)}, f32[2,24,128]{2,1,0:T(8,128)S(1)}) custom-call(bf16[32,128]{1,0:T(8,128)(2,1)S(1)} %get-tuple-element.31.own_ref, bf16[32,128]{1,0:T(8,128)(2,1)S(1)} %collective-permute-done.11.first_ref, bf16[12,2,640]{2,1,0:T(2,128)(2,1)S(1)} %bitcast.8, ...), custom_call_target="tpu_custom_call" | custom-call | flops 100000000 | bytes 1000000 | tf_op jit(solution)/shard_map/lift/pallas_call | solution.py:393
  22.1 0.7 %collective-permute-done.10.refs_1_ = bf16[32,128]{1,0:T(8,128)(2,1)S(1)} collective-permute-done((bf16[32,128]{1,0:T(8,128)(2,1)S(1)}, bf16[32,128]{1,0:T(8,128)(2,1)S(1)}, u32[]{:S(2)}, u32[]{:S(2)}) %collective-permute-start.10) | collective-permute-done | bytes 8224 | tf_op jit(solution)/shard_map/ppermute | solution.py:407
  22.8 0.0 collective-permute-done.9.refs_0_
  22.8 0.0 copy-done.5
  22.8 1.3 %tail.1 = bf16[12,2,640]{2,1,0:T(2,128)(2,1)} custom-call(bf16[32,128]{1,0:T(8,128)(2,1)S(1)} %collective-permute-done.9.refs_0_, bf16[32,128]{1,0:T(8,128)(2,1)S(1)} %collective-permute-done.10.refs_1_, f32[4,24,256]{2,1,0:T(8,128)S(1)} %get-tuple-element.33.refs_2_, f32[24,640]{1,0:T(8,128)S(1)} %get-tuple-element.34.refs_3_, ...), custom_call_target="tpu_custom_call" | custom-call | flops 1000000000 | bytes 1000000 | tf_op jit(solution)/shard_map/tail/pallas_call | solution.py:393
  (2 shorter events, 0.0 us)
Async XLA Ops:
  0.0 4.1 %copy-start.2 = (bf16[2,12,640]{2,0,1:T(2,128)(2,1)S(1)}, bf16[2,12,640]{2,0,1:T(2,128)(2,1)}, u32[]{:S(2)}) copy-start(bf16[2,12,640]{2,0,1:T(2,128)(2,1)} %param.7) | copy-start | bytes 92164
  0.0 7.9 %collective-permute-start = (bf16[12,2,640]{2,1,0:T(2,128)(2,1)}, bf16[12,2,640]{2,1,0:T(2,128)(2,1)S(1)}, u32[]{:S(2)}, u32[]{:S(2)}) collective-permute-start(bf16[12,2,640]{2,1,0:T(2,128)(2,1)} %bitcast.6), channel_id=1, source_target_pairs={{0,4},{1,5},{2,6},{3,7},{4,0},{5,1},{6,2},{7,3},{8,12},{9,13},{10,... | collective-permute-start | bytes 92168 | tf_op jit(solution)/shard_map/ppermute | solution.py:407
  4.1 2.0 %copy-start.1 = (bf16[9,80,20]{1,2,0:T(8,128)(2,1)S(1)}, bf16[9,80,20]{1,2,0:T(8,128)(2,1)}, u32[]{:S(2)}) copy-start(bf16[9,80,20]{1,2,0:T(8,128)(2,1)} %param.9) | copy-start | bytes 86404
  4.1 3.4 %copy-start.3 = (bf16[9,96]{1,0:T(8,128)(2,1)S(1)}, bf16[9,96]{1,0:T(8,128)(2,1)}, u32[]{:S(2)}) copy-start(bf16[9,96]{1,0:T(8,128)(2,1)} %filter_ref.1) | copy-start | bytes 5188
  4.1 3.4 %copy-start.4 = (bf16[9,2,3]{0,1,2:T(2,128)(2,1)S(1)}, bf16[9,2,3]{0,1,2:T(2,128)(2,1)}, u32[]{:S(2)}) copy-start(bf16[9,2,3]{0,1,2:T(2,128)(2,1)} %param.10) | copy-start | bytes 328
  4.3 5.5 %collective-permute-start.1 = (bf16[32,128]{1,0:T(8,128)(2,1)S(1)}, bf16[32,128]{1,0:T(8,128)(2,1)S(1)}, u32[]{:S(2)}, u32[]{:S(2)}) collective-permute-start(bf16[32,128]{1,0:T(8,128)(2,1)S(1)} %get-tuple-element.22), channel_id=1, source_target_pairs={{0,6},{1,7},{2,4},{3,5},{4,2},{5,3},{6,0},{7,1},{8,14},{9,15},{10,... | collective-permute-start | bytes 24584 | tf_op jit(solution)/shard_map/ppermute | solution.py:407
  6.0 3.8 %collective-permute-start.2 = (bf16[32,128]{1,0:T(8,128)(2,1)S(1)}, bf16[32,128]{1,0:T(8,128)(2,1)S(1)}, u32[]{:S(2)}, u32[]{:S(2)}) collective-permute-start(bf16[32,128]{1,0:T(8,128)(2,1)S(1)} %get-tuple-element.23), channel_id=1, source_target_pairs={{0,2},{1,3},{2,0},{3,1},{4,6},{5,7},{6,4},{7,5},{8,10},{9,11},{10,... | collective-permute-start | bytes 24584 | tf_op jit(solution)/shard_map/ppermute | solution.py:407
  6.0 7.3 %collective-permute-start.8 = (bf16[9,20,80]{2,1,0:T(8,128)(2,1)S(1)}, bf16[9,20,80]{2,1,0:T(8,128)(2,1)S(1)}, u32[]{:S(2)}, u32[]{:S(2)}) collective-permute-start(bf16[9,20,80]{2,1,0:T(8,128)(2,1)S(1)} %bitcast.4), channel_id=1, source_target_pairs={{0,1},{1,0},{2,3},{3,2},{4,5},{5,4},{6,7},{7,6},{8,9},{9,8},{10,11... | collective-permute-start | bytes 86408 | tf_op jit(solution)/shard_map/ppermute | solution.py:411
  9.8 4.0 %collective-permute-start.5 = (bf16[4,32,128]{2,1,0:T(8,128)(2,1)S(1)}, bf16[4,32,128]{2,1,0:T(8,128)(2,1)S(1)}, u32[]{:S(2)}, u32[]{:S(2)}) collective-permute-start(bf16[4,32,128]{2,1,0:T(8,128)(2,1)S(1)} %join_columns.1.own_ref), channel_id=1, source_target_pairs={{0,1},{1,0},{2,3},{3,2},{4,5},{5,4},{6,7},{7,6},{8,9},{9,8},{10,11... | collective-permute-start | bytes 98312 | tf_op jit(solution)/shard_map/ppermute | solution.py:420
  11.4 3.0 %collective-permute-start.7 = (bf16[4,32,128]{2,1,0:T(8,128)(2,1)S(1)}, bf16[4,32,128]{2,1,0:T(8,128)(2,1)S(1)}, u32[]{:S(2)}, u32[]{:S(2)}) collective-permute-start(bf16[4,32,128]{2,1,0:T(8,128)(2,1)S(1)} %join_columns.1.own_ref), channel_id=1, source_target_pairs={{0,8},{1,9},{2,10},{3,11},{4,12},{5,13},{6,14},{7,15},{8,0},{9,1},... | collective-permute-start | bytes 98312 | tf_op jit(solution)/shard_map/ppermute | solution.py:420
  11.5 3.9 %collective-permute-start.3 = (bf16[4,32,128]{2,1,0:T(8,128)(2,1)S(1)}, bf16[4,32,128]{2,1,0:T(8,128)(2,1)S(1)}, u32[]{:S(2)}, u32[]{:S(2)}) collective-permute-start(bf16[4,32,128]{2,1,0:T(8,128)(2,1)S(1)} %join_columns.1.own_ref), channel_id=1, source_target_pairs={{0,1},{1,0},{2,3},{3,2},{4,5},{5,4},{6,7},{7,6},{8,17},{9,16},{10,... | collective-permute-start | bytes 98312 | tf_op jit(solution)/shard_map/ppermute | solution.py:420
  12.0 3.4 %collective-permute-start.4 = (bf16[4,32,128]{2,1,0:T(8,128)(2,1)S(1)}, bf16[4,32,128]{2,1,0:T(8,128)(2,1)S(1)}, u32[]{:S(2)}, u32[]{:S(2)}) collective-permute-start(bf16[4,32,128]{2,1,0:T(8,128)(2,1)S(1)} %join_columns.1.own_ref), channel_id=1, source_target_pairs={{0,24},{1,25},{2,26},{3,27},{4,28},{5,29},{6,30},{7,31},{8,16},{9,... | collective-permute-start | bytes 98312 | tf_op jit(solution)/shard_map/ppermute | solution.py:420
  13.8 1.6 %collective-permute-start.6 = (bf16[4,32,128]{2,1,0:T(8,128)(2,1)S(1)}, bf16[4,32,128]{2,1,0:T(8,128)(2,1)S(1)}, u32[]{:S(2)}, u32[]{:S(2)}) collective-permute-start(bf16[4,32,128]{2,1,0:T(8,128)(2,1)S(1)} %collective-permute-done.5.mate), channel_id=1, source_target_pairs={{0,8},{1,9},{2,10},{3,11},{4,12},{5,13},{6,14},{7,15},{8,0},{9,1},... | collective-permute-start | bytes 98312 | tf_op jit(solution)/shard_map/ppermute | solution.py:420
  15.4 6.3 %copy-start = (bf16[640,1280]{1,0:T(8,128)(2,1)S(1)}, bf16[640,1280]{1,0:T(8,128)(2,1)}, u32[]{:S(2)}) copy-start(bf16[640,1280]{1,0:T(8,128)(2,1)} %refs_6_.1) | copy-start | bytes 4915204
  16.2 6.6 %copy-start.5 = (bf16[1280,640]{1,0:T(8,128)(2,1)S(1)}, bf16[1280,640]{1,0:T(8,128)(2,1)}, u32[]{:S(2)}) copy-start(bf16[1280,640]{1,0:T(8,128)(2,1)} %refs_7_.1) | copy-start | bytes 4915204
  16.2 5.5 %collective-permute-start.11 = (bf16[32,128]{1,0:T(8,128)(2,1)S(1)}, bf16[32,128]{1,0:T(8,128)(2,1)S(1)}, u32[]{:S(2)}, u32[]{:S(2)}) collective-permute-start(bf16[32,128]{1,0:T(8,128)(2,1)S(1)} %get-tuple-element.32), channel_id=1, source_target_pairs={{0,6},{1,7},{2,4},{3,5},{4,2},{5,3},{6,0},{7,1},{8,14},{9,15},{10,... | collective-permute-start | bytes 24584 | tf_op jit(solution)/shard_map/ppermute | solution.py:407
  18.2 4.6 %collective-permute-start.10 = (bf16[32,128]{1,0:T(8,128)(2,1)S(1)}, bf16[32,128]{1,0:T(8,128)(2,1)S(1)}, u32[]{:S(2)}, u32[]{:S(2)}) collective-permute-start(bf16[32,128]{1,0:T(8,128)(2,1)S(1)} %get-tuple-element.30), channel_id=1, source_target_pairs={{0,4},{1,5},{2,6},{3,7},{4,0},{5,1},{6,2},{7,3},{8,12},{9,13},{10,... | collective-permute-start | bytes 24584 | tf_op jit(solution)/shard_map/ppermute | solution.py:407
  18.2 4.6 %collective-permute-start.9 = (bf16[32,128]{1,0:T(8,128)(2,1)S(1)}, bf16[32,128]{1,0:T(8,128)(2,1)S(1)}, u32[]{:S(2)}, u32[]{:S(2)}) collective-permute-start(bf16[32,128]{1,0:T(8,128)(2,1)S(1)} %get-tuple-element.29), channel_id=1, source_target_pairs={{0,2},{1,3},{2,0},{3,1},{4,6},{5,7},{6,4},{7,5},{8,10},{9,11},{10,... | collective-permute-start | bytes 24584 | tf_op jit(solution)/shard_map/ppermute | solution.py:407

commit v16 on v15

--- a/solution.py
+++ b/solution.py
@@ -373,12 +373,18 @@
     variance = (early_squares + squares - away * away / chans) / chans
     scale = lax.rsqrt(variance + 1e-05)
     count = summed_ref.shape[0]
-    hidden = scale * (raised[:count] - mean * raised[count : count + 1])
-    hidden = (0.5 * hidden * (1.0 + lax.erf(hidden * 0.5**0.5))).astype(BF16)
+    product = None
+    units = raised.shape[1]
+    for start in range(0, units, 2 * LANES):
+        taken = slice(start, min(start + 2 * LANES, units))
+        hidden = scale * (raised[:count, taken] - mean * raised[count : count + 1, taken])
+        hidden = (0.5 * hidden * (1.0 + lax.erf(hidden * 0.5**0.5))).astype(BF16)
+        part = jnp.dot(hidden, down_ref[taken], preferred_element_type=F32)
+        product = part if product is None else product + part
     summed = summed_ref[...]
     for there, other in theirs:
         summed = summed + placed(there, other, chans, block)
-    result = summed + jnp.dot(hidden, down_ref[...], preferred_element_type=F32)
+    result = summed + product
     for row in range(rows):
         out_ref[:SUBLANES, row, :] = result[row * SUBLANES : (row + 1) * SUBLANES].astype(BF16)
         at = rows * SUBLANES + row * rest

time: 24.3 us -> 24.2 us (level)
  no operation moved by 1% of the time
where the time goes in v16:
time: 24.2 us; the launch traced here: 24.1 us
  starting transfers between devices  15.2 us (63%)
  waiting for transfers between devices  4.56 us (19%)
  Pallas kernels  4.18 us (17%)
    ppermute x6, starting transfers between devices, over_columns(): return lax.ppermute(message, 'lon', pairs) if apart else message  10.2 us
    pallas_call x11, Pallas kernels, call(): pl.pallas_call(kernel, out_shape=out_shape, in_specs=[VMEM] * len(operand...  4.18 us
    ppermute x5, starting transfers between devices, swap(): return lax.ppermute(block, ('lat', 'lon'), pairs)  3.45 us
    ppermute x6, waiting for transfers between devices, over_columns(): return lax.ppermute(message, 'lon', pairs) if apart else message  3.45 us
    ppermute x1, starting transfers between devices, over_sides(): return lax.ppermute(block, 'lon', [(i, i ^ 1) for i in range(count)])  1.49 us
    ppermute x5, waiting for transfers between devices, swap(): return lax.ppermute(block, ('lat', 'lon'), pairs)  1.11 us
  transfers between devices with their start and end apart: 12, of which 5 were waited for; matrix products, arithmetic and copies ran while one was open for 0% of the time, Pallas kernels for 9%

profile of v16, /device:TPU:0, one launch (start us, length us, event | category | flops | bytes accessed | tf_op | source)
XLA Modules:
  0.0 24.1 jit_solution(10147410993425369899)
XLA Ops:
  0.0 0.0 copy-start.2
  0.0 4.0 %collective-permute-start = (bf16[12,2,640]{2,1,0:T(2,128)(2,1)}, bf16[12,2,640]{2,1,0:T(2,128)(2,1)S(1)}, u32[]{:S(2)}, u32[]{:S(2)}) collective-permute-start(bf16[12,2,640]{2,1,0:T(2,128)(2,1)} %bitcast.6), channel_id=1, source_target_pairs={{0,4},{1,5},{2,6},{3,7},{4,0},{5,1},{6,2},{7,3},{8,12},{9,13},{10,... | collective-permute-start | bytes 92168 | tf_op jit(solution)/shard_map/ppermute | solution.py:413
  4.1 0.0 copy-done.2
  4.1 0.0 copy-start.1
  4.1 0.0 copy-start.3
  4.1 0.0 copy-start.4
  4.1 0.2 pack.1
  4.3 1.7 %collective-permute-start.1 = (bf16[32,128]{1,0:T(8,128)(2,1)S(1)}, bf16[32,128]{1,0:T(8,128)(2,1)S(1)}, u32[]{:S(2)}, u32[]{:S(2)}) collective-permute-start(bf16[32,128]{1,0:T(8,128)(2,1)S(1)} %get-tuple-element.22), channel_id=1, source_target_pairs={{0,6},{1,7},{2,4},{3,5},{4,2},{5,3},{6,0},{7,1},{8,14},{9,15},{10,... | collective-permute-start | bytes 24584 | tf_op jit(solution)/shard_map/ppermute | solution.py:413
  6.0 0.0 collective-permute-start.2
  6.0 0.0 copy-done.1
  6.0 1.5 %collective-permute-start.8 = (bf16[9,20,80]{2,1,0:T(8,128)(2,1)S(1)}, bf16[9,20,80]{2,1,0:T(8,128)(2,1)S(1)}, u32[]{:S(2)}, u32[]{:S(2)}) collective-permute-start(bf16[9,20,80]{2,1,0:T(8,128)(2,1)S(1)} %bitcast.4), channel_id=1, source_target_pairs={{0,1},{1,0},{2,3},{3,2},{4,5},{5,4},{6,7},{7,6},{8,9},{9,8},{10,11... | collective-permute-start | bytes 86408 | tf_op jit(solution)/shard_map/ppermute | solution.py:417
  7.5 0.0 copy-done.3
  7.5 0.0 copy-done.4
  7.5 0.4 %tables.1.table_ref = bf16[2,432,384]{2,1,0:T(8,128)(2,1)S(1)} custom-call(bf16[9,96]{1,0:T(8,128)(2,1)S(1)} %copy-done.3, bf16[3,2,9]{2,1,0:T(2,128)(2,1)S(1)} %bitcast.9, s32[96,128]{1,0:T(8,128)S(1)} %apart.1.apart_ref), custom_call_target="tpu_custom_call" | custom-call | flops 1000000 | bytes 1000000 | tf_op jit(solution)/shard_map/tables/pallas_call | solution.py:399
  7.9 0.0 collective-permute-done.raw_ref
  7.9 0.2 cut.1.refs_0_
  8.1 1.7 %collective-permute-done.1.refs_1_ = bf16[32,128]{1,0:T(8,128)(2,1)S(1)} collective-permute-done((bf16[32,128]{1,0:T(8,128)(2,1)S(1)}, bf16[32,128]{1,0:T(8,128)(2,1)S(1)}, u32[]{:S(2)}, u32[]{:S(2)}) %collective-permute-start.1) | collective-permute-done | bytes 8224 | tf_op jit(solution)/shard_map/ppermute | solution.py:413
  9.8 0.0 collective-permute-done.2.refs_2_
  9.8 1.6 %collective-permute-start.5 = (bf16[4,32,128]{2,1,0:T(8,128)(2,1)S(1)}, bf16[4,32,128]{2,1,0:T(8,128)(2,1)S(1)}, u32[]{:S(2)}, u32[]{:S(2)}) collective-permute-start(bf16[4,32,128]{2,1,0:T(8,128)(2,1)S(1)} %join_columns.1.own_ref), channel_id=1, source_target_pairs={{0,1},{1,0},{2,3},{3,2},{4,5},{5,4},{6,7},{7,6},{8,9},{9,8},{10,11... | collective-permute-start | bytes 98312 | tf_op jit(solution)/shard_map/ppermute | solution.py:426
  11.4 0.0 collective-permute-start.7
  11.4 0.1 unpack.1.own
  11.5 0.5 %collective-permute-start.3 = (bf16[4,32,128]{2,1,0:T(8,128)(2,1)S(1)}, bf16[4,32,128]{2,1,0:T(8,128)(2,1)S(1)}, u32[]{:S(2)}, u32[]{:S(2)}) collective-permute-start(bf16[4,32,128]{2,1,0:T(8,128)(2,1)S(1)} %join_columns.1.own_ref), channel_id=1, source_target_pairs={{0,1},{1,0},{2,3},{3,2},{4,5},{5,4},{6,7},{7,6},{8,17},{9,16},{10,... | collective-permute-start | bytes 98312 | tf_op jit(solution)/shard_map/ppermute | solution.py:426
  12.0 1.4 %collective-permute-start.4 = (bf16[4,32,128]{2,1,0:T(8,128)(2,1)S(1)}, bf16[4,32,128]{2,1,0:T(8,128)(2,1)S(1)}, u32[]{:S(2)}, u32[]{:S(2)}) collective-permute-start(bf16[4,32,128]{2,1,0:T(8,128)(2,1)S(1)} %join_columns.1.own_ref), channel_id=1, source_target_pairs={{0,24},{1,25},{2,26},{3,27},{4,28},{5,29},{6,30},{7,31},{8,16},{9,... | collective-permute-start | bytes 98312 | tf_op jit(solution)/shard_map/ppermute | solution.py:426
  13.3 0.0 collective-permute-done.8.mate_ref
  13.3 0.4 %collective-permute-done.5.mate = bf16[4,32,128]{2,1,0:T(8,128)(2,1)S(1)} collective-permute-done((bf16[4,32,128]{2,1,0:T(8,128)(2,1)S(1)}, bf16[4,32,128]{2,1,0:T(8,128)(2,1)S(1)}, u32[]{:S(2)}, u32[]{:S(2)}) %collective-permute-start.5) | collective-permute-done | bytes 32800 | tf_op jit(solution)/shard_map/ppermute | solution.py:426
  13.8 0.0 collective-permute-start.6
  13.8 0.5 %squares.1.squares_ref = bf16[2304,256]{1,0:T(8,128)(2,1)S(1)} custom-call(bf16[9,20,80]{2,1,0:T(8,128)(2,1)S(1)} %bitcast.5, bf16[9,20,80]{2,1,0:T(8,128)(2,1)S(1)} %collective-permute-done.8.mate_ref), custom_call_target="tpu_custom_call" | custom-call | flops 300000000 | bytes 1000000 | tf_op jit(solution)/shard_map/squares/pallas_call | solution.py:399
  14.4 0.0 collective-permute-done.7.even
  14.4 0.3 %conv_own.1 = (f32[2,432,256]{2,1,0:T(8,128)S(1)}, bf16[2,4,16,256]{3,2,1,0:T(8,128)(2,1)S(1)}) custom-call(bf16[4,32,128]{2,1,0:T(8,128)(2,1)S(1)} %collective-permute-done.5.mate, bf16[2,4,16,256]{3,2,1,0:T(8,128)(2,1)S(1)} %unpack.1.own, bf16[4,32,128]{2,1,0:T(8,128)(2,1)S(1)} %collective-permute-done.7.even, bf16[2,432,384]{2,1,0:T(8,128)(2,1)S(1)} %tables.1.table_ref), custom_call_target="tpu_custom_call" | custom-call | flops 300000000 | bytes 1000000 | tf_op jit(solution)/shard_map/conv_own/pallas_call | solution.py:399
  14.7 0.7 %collective-permute-done.3.odd_mate = bf16[4,32,128]{2,1,0:T(8,128)(2,1)S(1)} collective-permute-done((bf16[4,32,128]{2,1,0:T(8,128)(2,1)S(1)}, bf16[4,32,128]{2,1,0:T(8,128)(2,1)S(1)}, u32[]{:S(2)}, u32[]{:S(2)}) %collective-permute-start.3) | collective-permute-done | bytes 32800 | tf_op jit(solution)/shard_map/ppermute | solution.py:426
  15.4 0.0 collective-permute-done.4.odd_own
  15.4 0.0 collective-permute-done.6.even_mate
  15.4 0.0 copy-start
  15.4 0.8 %conv.1 = (bf16[32,128]{1,0:T(8,128)(2,1)S(1)}, bf16[32,128]{1,0:T(8,128)(2,1)S(1)}, bf16[32,128]{1,0:T(8,128)(2,1)S(1)}, bf16[32,128]{1,0:T(8,128)(2,1)S(1)}) custom-call(bf16[4,32,128]{2,1,0:T(8,128)(2,1)S(1)} %collective-permute-done.3.odd_mate, bf16[4,32,128]{2,1,0:T(8,128)(2,1)S(1)} %collective-permute-done.4.odd_own, ...), custom_call_target="tpu_custom_call" | custom-call | flops 10000000000 | bytes 1000000 | tf_op jit(solution)/shard_map/conv/pallas_call | solution.py:399
  16.2 0.0 copy-start.5
  16.2 2.0 %collective-permute-start.11 = (bf16[32,128]{1,0:T(8,128)(2,1)S(1)}, bf16[32,128]{1,0:T(8,128)(2,1)S(1)}, u32[]{:S(2)}, u32[]{:S(2)}) collective-permute-start(bf16[32,128]{1,0:T(8,128)(2,1)S(1)} %get-tuple-element.32), channel_id=1, source_target_pairs={{0,6},{1,7},{2,4},{3,5},{4,2},{5,3},{6,0},{7,1},{8,14},{9,15},{10,... | collective-permute-start | bytes 24584 | tf_op jit(solution)/shard_map/ppermute | solution.py:413
  18.2 0.0 collective-permute-start.10
  18.2 2.4 %collective-permute-start.9 = (bf16[32,128]{1,0:T(8,128)(2,1)S(1)}, bf16[32,128]{1,0:T(8,128)(2,1)S(1)}, u32[]{:S(2)}, u32[]{:S(2)}) collective-permute-start(bf16[32,128]{1,0:T(8,128)(2,1)S(1)} %get-tuple-element.29), channel_id=1, source_target_pairs={{0,2},{1,3},{2,0},{3,1},{4,6},{5,7},{6,4},{7,5},{8,10},{9,11},{10,... | collective-permute-start | bytes 24584 | tf_op jit(solution)/shard_map/ppermute | solution.py:413
  20.6 1.1 %collective-permute-done.11.first_ref = bf16[32,128]{1,0:T(8,128)(2,1)S(1)} collective-permute-done((bf16[32,128]{1,0:T(8,128)(2,1)S(1)}, bf16[32,128]{1,0:T(8,128)(2,1)S(1)}, u32[]{:S(2)}, u32[]{:S(2)}) %collective-permute-start.11) | collective-permute-done | bytes 8224 | tf_op jit(solution)/shard_map/ppermute | solution.py:413
  21.7 0.0 copy-done
  21.7 0.4 %lift.1 = (f32[4,24,256]{2,1,0:T(8,128)S(1)}, f32[24,640]{1,0:T(8,128)S(1)}, f32[32,1280]{1,0:T(8,128)S(1)}, f32[2,24,128]{2,1,0:T(8,128)S(1)}) custom-call(bf16[32,128]{1,0:T(8,128)(2,1)S(1)} %get-tuple-element.31.own_ref, bf16[32,128]{1,0:T(8,128)(2,1)S(1)} %collective-permute-done.11.first_ref, bf16[12,2,640]{2,1,0:T(2,128)(2,1)S(1)} %bitcast.8, ...), custom_call_target="tpu_custom_call" | custom-call | flops 100000000 | bytes 1000000 | tf_op jit(solution)/shard_map/lift/pallas_call | solution.py:399
  22.1 0.7 %collective-permute-done.10.refs_1_ = bf16[32,128]{1,0:T(8,128)(2,1)S(1)} collective-permute-done((bf16[32,128]{1,0:T(8,128)(2,1)S(1)}, bf16[32,128]{1,0:T(8,128)(2,1)S(1)}, u32[]{:S(2)}, u32[]{:S(2)}) %collective-permute-start.10) | collective-permute-done | bytes 8224 | tf_op jit(solution)/shard_map/ppermute | solution.py:413
  22.8 0.0 collective-permute-done.9.refs_0_
  22.8 0.0 copy-done.5
  22.8 1.3 %tail.1 = bf16[12,2,640]{2,1,0:T(2,128)(2,1)} custom-call(bf16[32,128]{1,0:T(8,128)(2,1)S(1)} %collective-permute-done.9.refs_0_, bf16[32,128]{1,0:T(8,128)(2,1)S(1)} %collective-permute-done.10.refs_1_, f32[4,24,256]{2,1,0:T(8,128)S(1)} %get-tuple-element.33.refs_2_, f32[24,640]{1,0:T(8,128)S(1)} %get-tuple-element.34.refs_3_, ...), custom_call_target="tpu_custom_call" | custom-call | flops 1000000000 | bytes 1000000 | tf_op jit(solution)/shard_map/tail/pallas_call | solution.py:399
  (2 shorter events, 0.0 us)
Async XLA Ops:
  0.0 4.1 %copy-start.2 = (bf16[2,12,640]{2,0,1:T(2,128)(2,1)S(1)}, bf16[2,12,640]{2,0,1:T(2,128)(2,1)}, u32[]{:S(2)}) copy-start(bf16[2,12,640]{2,0,1:T(2,128)(2,1)} %param.7) | copy-start | bytes 92164
  0.0 7.9 %collective-permute-start = (bf16[12,2,640]{2,1,0:T(2,128)(2,1)}, bf16[12,2,640]{2,1,0:T(2,128)(2,1)S(1)}, u32[]{:S(2)}, u32[]{:S(2)}) collective-permute-start(bf16[12,2,640]{2,1,0:T(2,128)(2,1)} %bitcast.6), channel_id=1, source_target_pairs={{0,4},{1,5},{2,6},{3,7},{4,0},{5,1},{6,2},{7,3},{8,12},{9,13},{10,... | collective-permute-start | bytes 92168 | tf_op jit(solution)/shard_map/ppermute | solution.py:413
  4.1 2.0 %copy-start.1 = (bf16[9,80,20]{1,2,0:T(8,128)(2,1)S(1)}, bf16[9,80,20]{1,2,0:T(8,128)(2,1)}, u32[]{:S(2)}) copy-start(bf16[9,80,20]{1,2,0:T(8,128)(2,1)} %param.9) | copy-start | bytes 86404
  4.1 3.4 %copy-start.3 = (bf16[9,96]{1,0:T(8,128)(2,1)S(1)}, bf16[9,96]{1,0:T(8,128)(2,1)}, u32[]{:S(2)}) copy-start(bf16[9,96]{1,0:T(8,128)(2,1)} %filter_ref.1) | copy-start | bytes 5188
  4.1 3.4 %copy-start.4 = (bf16[9,2,3]{0,1,2:T(2,128)(2,1)S(1)}, bf16[9,2,3]{0,1,2:T(2,128)(2,1)}, u32[]{:S(2)}) copy-start(bf16[9,2,3]{0,1,2:T(2,128)(2,1)} %param.10) | copy-start | bytes 328
  4.3 5.5 %collective-permute-start.1 = (bf16[32,128]{1,0:T(8,128)(2,1)S(1)}, bf16[32,128]{1,0:T(8,128)(2,1)S(1)}, u32[]{:S(2)}, u32[]{:S(2)}) collective-permute-start(bf16[32,128]{1,0:T(8,128)(2,1)S(1)} %get-tuple-element.22), channel_id=1, source_target_pairs={{0,6},{1,7},{2,4},{3,5},{4,2},{5,3},{6,0},{7,1},{8,14},{9,15},{10,... | collective-permute-start | bytes 24584 | tf_op jit(solution)/shard_map/ppermute | solution.py:413
  6.0 3.8 %collective-permute-start.2 = (bf16[32,128]{1,0:T(8,128)(2,1)S(1)}, bf16[32,128]{1,0:T(8,128)(2,1)S(1)}, u32[]{:S(2)}, u32[]{:S(2)}) collective-permute-start(bf16[32,128]{1,0:T(8,128)(2,1)S(1)} %get-tuple-element.23), channel_id=1, source_target_pairs={{0,2},{1,3},{2,0},{3,1},{4,6},{5,7},{6,4},{7,5},{8,10},{9,11},{10,... | collective-permute-start | bytes 24584 | tf_op jit(solution)/shard_map/ppermute | solution.py:413
  6.0 7.3 %collective-permute-start.8 = (bf16[9,20,80]{2,1,0:T(8,128)(2,1)S(1)}, bf16[9,20,80]{2,1,0:T(8,128)(2,1)S(1)}, u32[]{:S(2)}, u32[]{:S(2)}) collective-permute-start(bf16[9,20,80]{2,1,0:T(8,128)(2,1)S(1)} %bitcast.4), channel_id=1, source_target_pairs={{0,1},{1,0},{2,3},{3,2},{4,5},{5,4},{6,7},{7,6},{8,9},{9,8},{10,11... | collective-permute-start | bytes 86408 | tf_op jit(solution)/shard_map/ppermute | solution.py:417
  9.8 4.0 %collective-permute-start.5 = (bf16[4,32,128]{2,1,0:T(8,128)(2,1)S(1)}, bf16[4,32,128]{2,1,0:T(8,128)(2,1)S(1)}, u32[]{:S(2)}, u32[]{:S(2)}) collective-permute-start(bf16[4,32,128]{2,1,0:T(8,128)(2,1)S(1)} %join_columns.1.own_ref), channel_id=1, source_target_pairs={{0,1},{1,0},{2,3},{3,2},{4,5},{5,4},{6,7},{7,6},{8,9},{9,8},{10,11... | collective-permute-start | bytes 98312 | tf_op jit(solution)/shard_map/ppermute | solution.py:426
  11.4 3.0 %collective-permute-start.7 = (bf16[4,32,128]{2,1,0:T(8,128)(2,1)S(1)}, bf16[4,32,128]{2,1,0:T(8,128)(2,1)S(1)}, u32[]{:S(2)}, u32[]{:S(2)}) collective-permute-start(bf16[4,32,128]{2,1,0:T(8,128)(2,1)S(1)} %join_columns.1.own_ref), channel_id=1, source_target_pairs={{0,8},{1,9},{2,10},{3,11},{4,12},{5,13},{6,14},{7,15},{8,0},{9,1},... | collective-permute-start | bytes 98312 | tf_op jit(solution)/shard_map/ppermute | solution.py:426
  11.5 3.9 %collective-permute-start.3 = (bf16[4,32,128]{2,1,0:T(8,128)(2,1)S(1)}, bf16[4,32,128]{2,1,0:T(8,128)(2,1)S(1)}, u32[]{:S(2)}, u32[]{:S(2)}) collective-permute-start(bf16[4,32,128]{2,1,0:T(8,128)(2,1)S(1)} %join_columns.1.own_ref), channel_id=1, source_target_pairs={{0,1},{1,0},{2,3},{3,2},{4,5},{5,4},{6,7},{7,6},{8,17},{9,16},{10,... | collective-permute-start | bytes 98312 | tf_op jit(solution)/shard_map/ppermute | solution.py:426
  12.0 3.4 %collective-permute-start.4 = (bf16[4,32,128]{2,1,0:T(8,128)(2,1)S(1)}, bf16[4,32,128]{2,1,0:T(8,128)(2,1)S(1)}, u32[]{:S(2)}, u32[]{:S(2)}) collective-permute-start(bf16[4,32,128]{2,1,0:T(8,128)(2,1)S(1)} %join_columns.1.own_ref), channel_id=1, source_target_pairs={{0,24},{1,25},{2,26},{3,27},{4,28},{5,29},{6,30},{7,31},{8,16},{9,... | collective-permute-start | bytes 98312 | tf_op jit(solution)/shard_map/ppermute | solution.py:426
  13.8 1.6 %collective-permute-start.6 = (bf16[4,32,128]{2,1,0:T(8,128)(2,1)S(1)}, bf16[4,32,128]{2,1,0:T(8,128)(2,1)S(1)}, u32[]{:S(2)}, u32[]{:S(2)}) collective-permute-start(bf16[4,32,128]{2,1,0:T(8,128)(2,1)S(1)} %collective-permute-done.5.mate), channel_id=1, source_target_pairs={{0,8},{1,9},{2,10},{3,11},{4,12},{5,13},{6,14},{7,15},{8,0},{9,1},... | collective-permute-start | bytes 98312 | tf_op jit(solution)/shard_map/ppermute | solution.py:426
  15.4 6.3 %copy-start = (bf16[640,1280]{1,0:T(8,128)(2,1)S(1)}, bf16[640,1280]{1,0:T(8,128)(2,1)}, u32[]{:S(2)}) copy-start(bf16[640,1280]{1,0:T(8,128)(2,1)} %refs_6_.1) | copy-start | bytes 4915204
  16.2 6.6 %copy-start.5 = (bf16[1280,640]{1,0:T(8,128)(2,1)S(1)}, bf16[1280,640]{1,0:T(8,128)(2,1)}, u32[]{:S(2)}) copy-start(bf16[1280,640]{1,0:T(8,128)(2,1)} %refs_7_.1) | copy-start | bytes 4915204
  16.2 5.5 %collective-permute-start.11 = (bf16[32,128]{1,0:T(8,128)(2,1)S(1)}, bf16[32,128]{1,0:T(8,128)(2,1)S(1)}, u32[]{:S(2)}, u32[]{:S(2)}) collective-permute-start(bf16[32,128]{1,0:T(8,128)(2,1)S(1)} %get-tuple-element.32), channel_id=1, source_target_pairs={{0,6},{1,7},{2,4},{3,5},{4,2},{5,3},{6,0},{7,1},{8,14},{9,15},{10,... | collective-permute-start | bytes 24584 | tf_op jit(solution)/shard_map/ppermute | solution.py:413
  18.2 4.6 %collective-permute-start.10 = (bf16[32,128]{1,0:T(8,128)(2,1)S(1)}, bf16[32,128]{1,0:T(8,128)(2,1)S(1)}, u32[]{:S(2)}, u32[]{:S(2)}) collective-permute-start(bf16[32,128]{1,0:T(8,128)(2,1)S(1)} %get-tuple-element.30), channel_id=1, source_target_pairs={{0,4},{1,5},{2,6},{3,7},{4,0},{5,1},{6,2},{7,3},{8,12},{9,13},{10,... | collective-permute-start | bytes 24584 | tf_op jit(solution)/shard_map/ppermute | solution.py:413
  18.2 4.6 %collective-permute-start.9 = (bf16[32,128]{1,0:T(8,128)(2,1)S(1)}, bf16[32,128]{1,0:T(8,128)(2,1)S(1)}, u32[]{:S(2)}, u32[]{:S(2)}) collective-permute-start(bf16[32,128]{1,0:T(8,128)(2,1)S(1)} %get-tuple-element.29), channel_id=1, source_target_pairs={{0,2},{1,3},{2,0},{3,1},{4,6},{5,7},{6,4},{7,5},{8,10},{9,11},{10,... | collective-permute-start | bytes 24584 | tf_op jit(solution)/shard_map/ppermute | solution.py:413

commit v17 on v16

--- a/solution.py
+++ b/solution.py
@@ -287,13 +287,13 @@
     return jnp.where(kept, latent_block + convolved, 0.0).astype(BF16)
 
 
-def raised_block(summed, column, block, up_ref):
+def raised_block(summed, column, block, up_ref, taken=slice(None)):
     count = summed.shape[0]
     ones = jnp.ones((up_to(count, 2 * SUBLANES) - count, block), BF16)
     rows = pl.multiple_of(column * block, block)
     return jnp.dot(
         jnp.concatenate([summed[:, :block], ones], axis=0),
-        up_ref[pl.ds(rows, block), :],
+        up_ref[pl.ds(rows, block), taken],
         preferred_element_type=F32,
     )
 
@@ -356,7 +356,6 @@
     rest = width - SUBLANES
     block = chans // blocks_ref.shape[0]
     column, _ = column_and_side()
-    raised = raised_ref[...]
     early_mean, early_squares = stats_ref[0, :, :1], stats_ref[1, :, :1]
     theirs = []
     away = squares = None
@@ -364,7 +363,6 @@
         other = column ^ apart
         there = summed_block(blocks_ref[other], ref[...], block)
         theirs.append((there, other))
-        raised = raised + raised_block(there, other, block, up_ref)
         apart_from = deviations(there, early_mean, block)
         away = apart_from if away is None else away + apart_from
         squares = apart_from**2 if squares is None else squares + apart_from**2
@@ -374,10 +372,13 @@
     scale = lax.rsqrt(variance + 1e-05)
     count = summed_ref.shape[0]
     product = None
-    units = raised.shape[1]
+    units = raised_ref.shape[1]
     for start in range(0, units, 2 * LANES):
         taken = slice(start, min(start + 2 * LANES, units))
-        hidden = scale * (raised[:count, taken] - mean * raised[count : count + 1, taken])
+        raised = raised_ref[:, taken]
+        for there, other in theirs:
+            raised = raised + raised_block(there, other, block, up_ref, taken)
+        hidden = scale * (raised[:count] - mean * raised[count : count + 1])
         hidden = (0.5 * hidden * (1.0 + lax.erf(hidden * 0.5**0.5))).astype(BF16)
         part = jnp.dot(hidden, down_ref[taken], preferred_element_type=F32)
         product = part if product is None else product + part

time: 24.2 us -> 24.6 us (1.017)
  Pallas kernels: 4.18 us -> 4.57 us
    pallas_call x11, Pallas kernels: 4.18 us -> 4.57 us  [call(): pl.pallas_call(kernel, out_shape=out_shape, in_specs=[VMEM] * len(operand...]
where the time goes in v17:
time: 24.6 us; the launch traced here: 24.5 us
  starting transfers between devices  15.2 us (62%)
  Pallas kernels  4.57 us (19%)
  waiting for transfers between devices  4.56 us (19%)
    ppermute x6, starting transfers between devices, over_columns(): return lax.ppermute(message, 'lon', pairs) if apart else message  10.2 us
    pallas_call x11, Pallas kernels, call(): pl.pallas_call(kernel, out_shape=out_shape, in_specs=[VMEM] * len(operand...  4.57 us
    ppermute x5, starting transfers between devices, swap(): return lax.ppermute(block, ('lat', 'lon'), pairs)  3.45 us
    ppermute x6, waiting for transfers between devices, over_columns(): return lax.ppermute(message, 'lon', pairs) if apart else message  3.45 us
    ppermute x1, starting transfers between devices, over_sides(): return lax.ppermute(block, 'lon', [(i, i ^ 1) for i in range(count)])  1.49 us
    ppermute x5, waiting for transfers between devices, swap(): return lax.ppermute(block, ('lat', 'lon'), pairs)  1.11 us
  transfers between devices with their start and end apart: 12, of which 5 were waited for; matrix products, arithmetic and copies ran while one was open for 0% of the time, Pallas kernels for 9%

profile of v17, /device:TPU:0, one launch (start us, length us, event | category | flops | bytes accessed | tf_op | source)
XLA Modules:
  0.0 24.5 jit_solution(15819891189353500970)
XLA Ops:
  0.0 0.0 copy-start.2
  0.0 4.0 %collective-permute-start = (bf16[12,2,640]{2,1,0:T(2,128)(2,1)}, bf16[12,2,640]{2,1,0:T(2,128)(2,1)S(1)}, u32[]{:S(2)}, u32[]{:S(2)}) collective-permute-start(bf16[12,2,640]{2,1,0:T(2,128)(2,1)} %bitcast.6), channel_id=1, source_target_pairs={{0,4},{1,5},{2,6},{3,7},{4,0},{5,1},{6,2},{7,3},{8,12},{9,13},{10,... | collective-permute-start | bytes 92168 | tf_op jit(solution)/shard_map/ppermute | solution.py:414
  4.1 0.0 copy-done.2
  4.1 0.0 copy-start.1
  4.1 0.0 copy-start.3
  4.1 0.0 copy-start.4
  4.1 0.2 pack.1
  4.3 1.7 %collective-permute-start.1 = (bf16[32,128]{1,0:T(8,128)(2,1)S(1)}, bf16[32,128]{1,0:T(8,128)(2,1)S(1)}, u32[]{:S(2)}, u32[]{:S(2)}) collective-permute-start(bf16[32,128]{1,0:T(8,128)(2,1)S(1)} %get-tuple-element.22), channel_id=1, source_target_pairs={{0,6},{1,7},{2,4},{3,5},{4,2},{5,3},{6,0},{7,1},{8,14},{9,15},{10,... | collective-permute-start | bytes 24584 | tf_op jit(solution)/shard_map/ppermute | solution.py:414
  6.0 0.0 collective-permute-start.2
  6.0 0.0 copy-done.1
  6.0 1.5 %collective-permute-start.8 = (bf16[9,20,80]{2,1,0:T(8,128)(2,1)S(1)}, bf16[9,20,80]{2,1,0:T(8,128)(2,1)S(1)}, u32[]{:S(2)}, u32[]{:S(2)}) collective-permute-start(bf16[9,20,80]{2,1,0:T(8,128)(2,1)S(1)} %bitcast.4), channel_id=1, source_target_pairs={{0,1},{1,0},{2,3},{3,2},{4,5},{5,4},{6,7},{7,6},{8,9},{9,8},{10,11... | collective-permute-start | bytes 86408 | tf_op jit(solution)/shard_map/ppermute | solution.py:418
  7.5 0.0 copy-done.3
  7.5 0.0 copy-done.4
  7.5 0.4 %tables.1.table_ref = bf16[2,432,384]{2,1,0:T(8,128)(2,1)S(1)} custom-call(bf16[9,96]{1,0:T(8,128)(2,1)S(1)} %copy-done.3, bf16[3,2,9]{2,1,0:T(2,128)(2,1)S(1)} %bitcast.9, s32[96,128]{1,0:T(8,128)S(1)} %apart.1.apart_ref), custom_call_target="tpu_custom_call" | custom-call | flops 1000000 | bytes 1000000 | tf_op jit(solution)/shard_map/tables/pallas_call | solution.py:400
  7.9 0.0 collective-permute-done.raw_ref
  7.9 0.2 cut.1.refs_0_
  8.1 1.7 %collective-permute-done.1.refs_1_ = bf16[32,128]{1,0:T(8,128)(2,1)S(1)} collective-permute-done((bf16[32,128]{1,0:T(8,128)(2,1)S(1)}, bf16[32,128]{1,0:T(8,128)(2,1)S(1)}, u32[]{:S(2)}, u32[]{:S(2)}) %collective-permute-start.1) | collective-permute-done | bytes 8224 | tf_op jit(solution)/shard_map/ppermute | solution.py:414
  9.8 0.0 collective-permute-done.2.refs_2_
  9.8 1.6 %collective-permute-start.5 = (bf16[4,32,128]{2,1,0:T(8,128)(2,1)S(1)}, bf16[4,32,128]{2,1,0:T(8,128)(2,1)S(1)}, u32[]{:S(2)}, u32[]{:S(2)}) collective-permute-start(bf16[4,32,128]{2,1,0:T(8,128)(2,1)S(1)} %join_columns.1.own_ref), channel_id=1, source_target_pairs={{0,1},{1,0},{2,3},{3,2},{4,5},{5,4},{6,7},{7,6},{8,9},{9,8},{10,11... | collective-permute-start | bytes 98312 | tf_op jit(solution)/shard_map/ppermute | solution.py:427
  11.4 0.0 collective-permute-start.7
  11.4 0.1 unpack.1.own
  11.5 0.5 %collective-permute-start.3 = (bf16[4,32,128]{2,1,0:T(8,128)(2,1)S(1)}, bf16[4,32,128]{2,1,0:T(8,128)(2,1)S(1)}, u32[]{:S(2)}, u32[]{:S(2)}) collective-permute-start(bf16[4,32,128]{2,1,0:T(8,128)(2,1)S(1)} %join_columns.1.own_ref), channel_id=1, source_target_pairs={{0,1},{1,0},{2,3},{3,2},{4,5},{5,4},{6,7},{7,6},{8,17},{9,16},{10,... | collective-permute-start | bytes 98312 | tf_op jit(solution)/shard_map/ppermute | solution.py:427
  12.0 1.4 %collective-permute-start.4 = (bf16[4,32,128]{2,1,0:T(8,128)(2,1)S(1)}, bf16[4,32,128]{2,1,0:T(8,128)(2,1)S(1)}, u32[]{:S(2)}, u32[]{:S(2)}) collective-permute-start(bf16[4,32,128]{2,1,0:T(8,128)(2,1)S(1)} %join_columns.1.own_ref), channel_id=1, source_target_pairs={{0,24},{1,25},{2,26},{3,27},{4,28},{5,29},{6,30},{7,31},{8,16},{9,... | collective-permute-start | bytes 98312 | tf_op jit(solution)/shard_map/ppermute | solution.py:427
  13.3 0.0 collective-permute-done.8.mate_ref
  13.3 0.4 %collective-permute-done.5.mate = bf16[4,32,128]{2,1,0:T(8,128)(2,1)S(1)} collective-permute-done((bf16[4,32,128]{2,1,0:T(8,128)(2,1)S(1)}, bf16[4,32,128]{2,1,0:T(8,128)(2,1)S(1)}, u32[]{:S(2)}, u32[]{:S(2)}) %collective-permute-start.5) | collective-permute-done | bytes 32800 | tf_op jit(solution)/shard_map/ppermute | solution.py:427
  13.8 0.0 collective-permute-start.6
  13.8 0.5 %squares.1.squares_ref = bf16[2304,256]{1,0:T(8,128)(2,1)S(1)} custom-call(bf16[9,20,80]{2,1,0:T(8,128)(2,1)S(1)} %bitcast.5, bf16[9,20,80]{2,1,0:T(8,128)(2,1)S(1)} %collective-permute-done.8.mate_ref), custom_call_target="tpu_custom_call" | custom-call | flops 300000000 | bytes 1000000 | tf_op jit(solution)/shard_map/squares/pallas_call | solution.py:400
  14.4 0.0 collective-permute-done.7.even
  14.4 0.3 %conv_own.1 = (f32[2,432,256]{2,1,0:T(8,128)S(1)}, bf16[2,4,16,256]{3,2,1,0:T(8,128)(2,1)S(1)}) custom-call(bf16[4,32,128]{2,1,0:T(8,128)(2,1)S(1)} %collective-permute-done.5.mate, bf16[2,4,16,256]{3,2,1,0:T(8,128)(2,1)S(1)} %unpack.1.own, bf16[4,32,128]{2,1,0:T(8,128)(2,1)S(1)} %collective-permute-done.7.even, bf16[2,432,384]{2,1,0:T(8,128)(2,1)S(1)} %tables.1.table_ref), custom_call_target="tpu_custom_call" | custom-call | flops 300000000 | bytes 1000000 | tf_op jit(solution)/shard_map/conv_own/pallas_call | solution.py:400
  14.7 0.7 %collective-permute-done.3.odd_mate = bf16[4,32,128]{2,1,0:T(8,128)(2,1)S(1)} collective-permute-done((bf16[4,32,128]{2,1,0:T(8,128)(2,1)S(1)}, bf16[4,32,128]{2,1,0:T(8,128)(2,1)S(1)}, u32[]{:S(2)}, u32[]{:S(2)}) %collective-permute-start.3) | collective-permute-done | bytes 32800 | tf_op jit(solution)/shard_map/ppermute | solution.py:427
  15.4 0.0 collective-permute-done.4.odd_own
  15.4 0.0 collective-permute-done.6.even_mate
  15.4 0.0 copy-start
  15.4 0.8 %conv.1 = (bf16[32,128]{1,0:T(8,128)(2,1)S(1)}, bf16[32,128]{1,0:T(8,128)(2,1)S(1)}, bf16[32,128]{1,0:T(8,128)(2,1)S(1)}, bf16[32,128]{1,0:T(8,128)(2,1)S(1)}) custom-call(bf16[4,32,128]{2,1,0:T(8,128)(2,1)S(1)} %collective-permute-done.3.odd_mate, bf16[4,32,128]{2,1,0:T(8,128)(2,1)S(1)} %collective-permute-done.4.odd_own, ...), custom_call_target="tpu_custom_call" | custom-call | flops 10000000000 | bytes 1000000 | tf_op jit(solution)/shard_map/conv/pallas_call | solution.py:400
  16.2 0.0 copy-start.5
  16.2 2.0 %collective-permute-start.11 = (bf16[32,128]{1,0:T(8,128)(2,1)S(1)}, bf16[32,128]{1,0:T(8,128)(2,1)S(1)}, u32[]{:S(2)}, u32[]{:S(2)}) collective-permute-start(bf16[32,128]{1,0:T(8,128)(2,1)S(1)} %get-tuple-element.32), channel_id=1, source_target_pairs={{0,6},{1,7},{2,4},{3,5},{4,2},{5,3},{6,0},{7,1},{8,14},{9,15},{10,... | collective-permute-start | bytes 24584 | tf_op jit(solution)/shard_map/ppermute | solution.py:414
  18.2 0.0 collective-permute-start.10
  18.2 2.4 %collective-permute-start.9 = (bf16[32,128]{1,0:T(8,128)(2,1)S(1)}, bf16[32,128]{1,0:T(8,128)(2,1)S(1)}, u32[]{:S(2)}, u32[]{:S(2)}) collective-permute-start(bf16[32,128]{1,0:T(8,128)(2,1)S(1)} %get-tuple-element.29), channel_id=1, source_target_pairs={{0,2},{1,3},{2,0},{3,1},{4,6},{5,7},{6,4},{7,5},{8,10},{9,11},{10,... | collective-permute-start | bytes 24584 | tf_op jit(solution)/shard_map/ppermute | solution.py:414
  20.6 1.1 %collective-permute-done.11.first_ref = bf16[32,128]{1,0:T(8,128)(2,1)S(1)} collective-permute-done((bf16[32,128]{1,0:T(8,128)(2,1)S(1)}, bf16[32,128]{1,0:T(8,128)(2,1)S(1)}, u32[]{:S(2)}, u32[]{:S(2)}) %collective-permute-start.11) | collective-permute-done | bytes 8224 | tf_op jit(solution)/shard_map/ppermute | solution.py:414
  21.7 0.0 copy-done
  21.7 0.4 %lift.1 = (f32[4,24,256]{2,1,0:T(8,128)S(1)}, f32[24,640]{1,0:T(8,128)S(1)}, f32[32,1280]{1,0:T(8,128)S(1)}, f32[2,24,128]{2,1,0:T(8,128)S(1)}) custom-call(bf16[32,128]{1,0:T(8,128)(2,1)S(1)} %get-tuple-element.31.own_ref, bf16[32,128]{1,0:T(8,128)(2,1)S(1)} %collective-permute-done.11.first_ref, bf16[12,2,640]{2,1,0:T(2,128)(2,1)S(1)} %bitcast.8, ...), custom_call_target="tpu_custom_call" | custom-call | flops 100000000 | bytes 1000000 | tf_op jit(solution)/shard_map/lift/pallas_call | solution.py:400
  22.1 0.7 %collective-permute-done.10.refs_1_ = bf16[32,128]{1,0:T(8,128)(2,1)S(1)} collective-permute-done((bf16[32,128]{1,0:T(8,128)(2,1)S(1)}, bf16[32,128]{1,0:T(8,128)(2,1)S(1)}, u32[]{:S(2)}, u32[]{:S(2)}) %collective-permute-start.10) | collective-permute-done | bytes 8224 | tf_op jit(solution)/shard_map/ppermute | solution.py:414
  22.8 0.0 collective-permute-done.9.refs_0_
  22.8 0.0 copy-done.5
  22.8 1.7 %tail.1 = bf16[12,2,640]{2,1,0:T(2,128)(2,1)} custom-call(bf16[32,128]{1,0:T(8,128)(2,1)S(1)} %collective-permute-done.9.refs_0_, bf16[32,128]{1,0:T(8,128)(2,1)S(1)} %collective-permute-done.10.refs_1_, f32[4,24,256]{2,1,0:T(8,128)S(1)} %get-tuple-element.33.refs_2_, f32[24,640]{1,0:T(8,128)S(1)} %get-tuple-element.34.refs_3_, ...), custom_call_target="tpu_custom_call" | custom-call | flops 1000000000 | bytes 1000000 | tf_op jit(solution)/shard_map/tail/pallas_call | solution.py:400
  (2 shorter events, 0.0 us)
Async XLA Ops:
  0.0 4.1 %copy-start.2 = (bf16[2,12,640]{2,0,1:T(2,128)(2,1)S(1)}, bf16[2,12,640]{2,0,1:T(2,128)(2,1)}, u32[]{:S(2)}) copy-start(bf16[2,12,640]{2,0,1:T(2,128)(2,1)} %param.7) | copy-start | bytes 92164
  0.0 7.9 %collective-permute-start = (bf16[12,2,640]{2,1,0:T(2,128)(2,1)}, bf16[12,2,640]{2,1,0:T(2,128)(2,1)S(1)}, u32[]{:S(2)}, u32[]{:S(2)}) collective-permute-start(bf16[12,2,640]{2,1,0:T(2,128)(2,1)} %bitcast.6), channel_id=1, source_target_pairs={{0,4},{1,5},{2,6},{3,7},{4,0},{5,1},{6,2},{7,3},{8,12},{9,13},{10,... | collective-permute-start | bytes 92168 | tf_op jit(solution)/shard_map/ppermute | solution.py:414
  4.1 2.0 %copy-start.1 = (bf16[9,80,20]{1,2,0:T(8,128)(2,1)S(1)}, bf16[9,80,20]{1,2,0:T(8,128)(2,1)}, u32[]{:S(2)}) copy-start(bf16[9,80,20]{1,2,0:T(8,128)(2,1)} %param.9) | copy-start | bytes 86404
  4.1 3.4 %copy-start.3 = (bf16[9,96]{1,0:T(8,128)(2,1)S(1)}, bf16[9,96]{1,0:T(8,128)(2,1)}, u32[]{:S(2)}) copy-start(bf16[9,96]{1,0:T(8,128)(2,1)} %filter_ref.1) | copy-start | bytes 5188
  4.1 3.4 %copy-start.4 = (bf16[9,2,3]{0,1,2:T(2,128)(2,1)S(1)}, bf16[9,2,3]{0,1,2:T(2,128)(2,1)}, u32[]{:S(2)}) copy-start(bf16[9,2,3]{0,1,2:T(2,128)(2,1)} %param.10) | copy-start | bytes 328
  4.3 5.5 %collective-permute-start.1 = (bf16[32,128]{1,0:T(8,128)(2,1)S(1)}, bf16[32,128]{1,0:T(8,128)(2,1)S(1)}, u32[]{:S(2)}, u32[]{:S(2)}) collective-permute-start(bf16[32,128]{1,0:T(8,128)(2,1)S(1)} %get-tuple-element.22), channel_id=1, source_target_pairs={{0,6},{1,7},{2,4},{3,5},{4,2},{5,3},{6,0},{7,1},{8,14},{9,15},{10,... | collective-permute-start | bytes 24584 | tf_op jit(solution)/shard_map/ppermute | solution.py:414
  6.0 3.8 %collective-permute-start.2 = (bf16[32,128]{1,0:T(8,128)(2,1)S(1)}, bf16[32,128]{1,0:T(8,128)(2,1)S(1)}, u32[]{:S(2)}, u32[]{:S(2)}) collective-permute-start(bf16[32,128]{1,0:T(8,128)(2,1)S(1)} %get-tuple-element.23), channel_id=1, source_target_pairs={{0,2},{1,3},{2,0},{3,1},{4,6},{5,7},{6,4},{7,5},{8,10},{9,11},{10,... | collective-permute-start | bytes 24584 | tf_op jit(solution)/shard_map/ppermute | solution.py:414
  6.0 7.3 %collective-permute-start.8 = (bf16[9,20,80]{2,1,0:T(8,128)(2,1)S(1)}, bf16[9,20,80]{2,1,0:T(8,128)(2,1)S(1)}, u32[]{:S(2)}, u32[]{:S(2)}) collective-permute-start(bf16[9,20,80]{2,1,0:T(8,128)(2,1)S(1)} %bitcast.4), channel_id=1, source_target_pairs={{0,1},{1,0},{2,3},{3,2},{4,5},{5,4},{6,7},{7,6},{8,9},{9,8},{10,11... | collective-permute-start | bytes 86408 | tf_op jit(solution)/shard_map/ppermute | solution.py:418
  9.8 4.0 %collective-permute-start.5 = (bf16[4,32,128]{2,1,0:T(8,128)(2,1)S(1)}, bf16[4,32,128]{2,1,0:T(8,128)(2,1)S(1)}, u32[]{:S(2)}, u32[]{:S(2)}) collective-permute-start(bf16[4,32,128]{2,1,0:T(8,128)(2,1)S(1)} %join_columns.1.own_ref), channel_id=1, source_target_pairs={{0,1},{1,0},{2,3},{3,2},{4,5},{5,4},{6,7},{7,6},{8,9},{9,8},{10,11... | collective-permute-start | bytes 98312 | tf_op jit(solution)/shard_map/ppermute | solution.py:427
  11.4 3.0 %collective-permute-start.7 = (bf16[4,32,128]{2,1,0:T(8,128)(2,1)S(1)}, bf16[4,32,128]{2,1,0:T(8,128)(2,1)S(1)}, u32[]{:S(2)}, u32[]{:S(2)}) collective-permute-start(bf16[4,32,128]{2,1,0:T(8,128)(2,1)S(1)} %join_columns.1.own_ref), channel_id=1, source_target_pairs={{0,8},{1,9},{2,10},{3,11},{4,12},{5,13},{6,14},{7,15},{8,0},{9,1},... | collective-permute-start | bytes 98312 | tf_op jit(solution)/shard_map/ppermute | solution.py:427
  11.5 3.9 %collective-permute-start.3 = (bf16[4,32,128]{2,1,0:T(8,128)(2,1)S(1)}, bf16[4,32,128]{2,1,0:T(8,128)(2,1)S(1)}, u32[]{:S(2)}, u32[]{:S(2)}) collective-permute-start(bf16[4,32,128]{2,1,0:T(8,128)(2,1)S(1)} %join_columns.1.own_ref), channel_id=1, source_target_pairs={{0,1},{1,0},{2,3},{3,2},{4,5},{5,4},{6,7},{7,6},{8,17},{9,16},{10,... | collective-permute-start | bytes 98312 | tf_op jit(solution)/shard_map/ppermute | solution.py:427
  12.0 3.4 %collective-permute-start.4 = (bf16[4,32,128]{2,1,0:T(8,128)(2,1)S(1)}, bf16[4,32,128]{2,1,0:T(8,128)(2,1)S(1)}, u32[]{:S(2)}, u32[]{:S(2)}) collective-permute-start(bf16[4,32,128]{2,1,0:T(8,128)(2,1)S(1)} %join_columns.1.own_ref), channel_id=1, source_target_pairs={{0,24},{1,25},{2,26},{3,27},{4,28},{5,29},{6,30},{7,31},{8,16},{9,... | collective-permute-start | bytes 98312 | tf_op jit(solution)/shard_map/ppermute | solution.py:427
  13.8 1.6 %collective-permute-start.6 = (bf16[4,32,128]{2,1,0:T(8,128)(2,1)S(1)}, bf16[4,32,128]{2,1,0:T(8,128)(2,1)S(1)}, u32[]{:S(2)}, u32[]{:S(2)}) collective-permute-start(bf16[4,32,128]{2,1,0:T(8,128)(2,1)S(1)} %collective-permute-done.5.mate), channel_id=1, source_target_pairs={{0,8},{1,9},{2,10},{3,11},{4,12},{5,13},{6,14},{7,15},{8,0},{9,1},... | collective-permute-start | bytes 98312 | tf_op jit(solution)/shard_map/ppermute | solution.py:427
  15.4 6.3 %copy-start = (bf16[640,1280]{1,0:T(8,128)(2,1)S(1)}, bf16[640,1280]{1,0:T(8,128)(2,1)}, u32[]{:S(2)}) copy-start(bf16[640,1280]{1,0:T(8,128)(2,1)} %refs_6_.1) | copy-start | bytes 4915204
  16.2 6.6 %copy-start.5 = (bf16[1280,640]{1,0:T(8,128)(2,1)S(1)}, bf16[1280,640]{1,0:T(8,128)(2,1)}, u32[]{:S(2)}) copy-start(bf16[1280,640]{1,0:T(8,128)(2,1)} %refs_7_.1) | copy-start | bytes 4915204
  16.2 5.5 %collective-permute-start.11 = (bf16[32,128]{1,0:T(8,128)(2,1)S(1)}, bf16[32,128]{1,0:T(8,128)(2,1)S(1)}, u32[]{:S(2)}, u32[]{:S(2)}) collective-permute-start(bf16[32,128]{1,0:T(8,128)(2,1)S(1)} %get-tuple-element.32), channel_id=1, source_target_pairs={{0,6},{1,7},{2,4},{3,5},{4,2},{5,3},{6,0},{7,1},{8,14},{9,15},{10,... | collective-permute-start | bytes 24584 | tf_op jit(solution)/shard_map/ppermute | solution.py:414
  18.2 4.6 %collective-permute-start.10 = (bf16[32,128]{1,0:T(8,128)(2,1)S(1)}, bf16[32,128]{1,0:T(8,128)(2,1)S(1)}, u32[]{:S(2)}, u32[]{:S(2)}) collective-permute-start(bf16[32,128]{1,0:T(8,128)(2,1)S(1)} %get-tuple-element.30), channel_id=1, source_target_pairs={{0,4},{1,5},{2,6},{3,7},{4,0},{5,1},{6,2},{7,3},{8,12},{9,13},{10,... | collective-permute-start | bytes 24584 | tf_op jit(solution)/shard_map/ppermute | solution.py:414
  18.2 4.6 %collective-permute-start.9 = (bf16[32,128]{1,0:T(8,128)(2,1)S(1)}, bf16[32,128]{1,0:T(8,128)(2,1)S(1)}, u32[]{:S(2)}, u32[]{:S(2)}) collective-permute-start(bf16[32,128]{1,0:T(8,128)(2,1)S(1)} %get-tuple-element.29), channel_id=1, source_target_pairs={{0,2},{1,3},{2,0},{3,1},{4,6},{5,7},{6,4},{7,5},{8,10},{9,11},{10,... | collective-permute-start | bytes 24584 | tf_op jit(solution)/shard_map/ppermute | solution.py:414

commit v18 on v16

--- a/solution.py
+++ b/solution.py
@@ -375,8 +375,8 @@
     count = summed_ref.shape[0]
     product = None
     units = raised.shape[1]
-    for start in range(0, units, 2 * LANES):
-        taken = slice(start, min(start + 2 * LANES, units))
+    for start in range(0, units, 4 * LANES):
+        taken = slice(start, min(start + 4 * LANES, units))
         hidden = scale * (raised[:count, taken] - mean * raised[count : count + 1, taken])
         hidden = (0.5 * hidden * (1.0 + lax.erf(hidden * 0.5**0.5))).astype(BF16)
         part = jnp.dot(hidden, down_ref[taken], preferred_element_type=F32)

time: 24.2 us -> 24.2 us (level)
  no operation moved by 1% of the time
where the time goes in v18:
time: 24.2 us; the launch traced here: 24.1 us
  starting transfers between devices  15.2 us (63%)
  waiting for transfers between devices  4.56 us (19%)
  Pallas kernels  4.22 us (17%)
    ppermute x6, starting transfers between devices, over_columns(): return lax.ppermute(message, 'lon', pairs) if apart else message  10.2 us
    pallas_call x11, Pallas kernels, call(): pl.pallas_call(kernel, out_shape=out_shape, in_specs=[VMEM] * len(operand...  4.22 us
    ppermute x5, starting transfers between devices, swap(): return lax.ppermute(block, ('lat', 'lon'), pairs)  3.45 us
    ppermute x6, waiting for transfers between devices, over_columns(): return lax.ppermute(message, 'lon', pairs) if apart else message  3.45 us
    ppermute x1, starting transfers between devices, over_sides(): return lax.ppermute(block, 'lon', [(i, i ^ 1) for i in range(count)])  1.49 us
    ppermute x5, waiting for transfers between devices, swap(): return lax.ppermute(block, ('lat', 'lon'), pairs)  1.11 us
  transfers between devices with their start and end apart: 12, of which 5 were waited for; matrix products, arithmetic and copies ran while one was open for 0% of the time, Pallas kernels for 9%

profile of v18, /device:TPU:0, one launch (start us, length us, event | category | flops | bytes accessed | tf_op | source)
XLA Modules:
  0.0 24.1 jit_solution(6241302304783815959)
XLA Ops:
  0.0 0.0 copy-start.2
  0.0 4.0 %collective-permute-start = (bf16[12,2,640]{2,1,0:T(2,128)(2,1)}, bf16[12,2,640]{2,1,0:T(2,128)(2,1)S(1)}, u32[]{:S(2)}, u32[]{:S(2)}) collective-permute-start(bf16[12,2,640]{2,1,0:T(2,128)(2,1)} %bitcast.6), channel_id=1, source_target_pairs={{0,4},{1,5},{2,6},{3,7},{4,0},{5,1},{6,2},{7,3},{8,12},{9,13},{10,... | collective-permute-start | bytes 92168 | tf_op jit(solution)/shard_map/ppermute | solution.py:413
  4.1 0.0 copy-done.2
  4.1 0.0 copy-start.1
  4.1 0.0 copy-start.3
  4.1 0.0 copy-start.4
  4.1 0.2 pack.1
  4.3 1.7 %collective-permute-start.1 = (bf16[32,128]{1,0:T(8,128)(2,1)S(1)}, bf16[32,128]{1,0:T(8,128)(2,1)S(1)}, u32[]{:S(2)}, u32[]{:S(2)}) collective-permute-start(bf16[32,128]{1,0:T(8,128)(2,1)S(1)} %get-tuple-element.22), channel_id=1, source_target_pairs={{0,6},{1,7},{2,4},{3,5},{4,2},{5,3},{6,0},{7,1},{8,14},{9,15},{10,... | collective-permute-start | bytes 24584 | tf_op jit(solution)/shard_map/ppermute | solution.py:413
  6.0 0.0 collective-permute-start.2
  6.0 0.0 copy-done.1
  6.0 1.5 %collective-permute-start.8 = (bf16[9,20,80]{2,1,0:T(8,128)(2,1)S(1)}, bf16[9,20,80]{2,1,0:T(8,128)(2,1)S(1)}, u32[]{:S(2)}, u32[]{:S(2)}) collective-permute-start(bf16[9,20,80]{2,1,0:T(8,128)(2,1)S(1)} %bitcast.4), channel_id=1, source_target_pairs={{0,1},{1,0},{2,3},{3,2},{4,5},{5,4},{6,7},{7,6},{8,9},{9,8},{10,11... | collective-permute-start | bytes 86408 | tf_op jit(solution)/shard_map/ppermute | solution.py:417
  7.5 0.0 copy-done.3
  7.5 0.0 copy-done.4
  7.5 0.4 %tables.1.table_ref = bf16[2,432,384]{2,1,0:T(8,128)(2,1)S(1)} custom-call(bf16[9,96]{1,0:T(8,128)(2,1)S(1)} %copy-done.3, bf16[3,2,9]{2,1,0:T(2,128)(2,1)S(1)} %bitcast.9, s32[96,128]{1,0:T(8,128)S(1)} %apart.1.apart_ref), custom_call_target="tpu_custom_call" | custom-call | flops 1000000 | bytes 1000000 | tf_op jit(solution)/shard_map/tables/pallas_call | solution.py:399
  7.9 0.0 collective-permute-done.raw_ref
  7.9 0.2 cut.1.refs_0_
  8.1 1.7 %collective-permute-done.1.refs_1_ = bf16[32,128]{1,0:T(8,128)(2,1)S(1)} collective-permute-done((bf16[32,128]{1,0:T(8,128)(2,1)S(1)}, bf16[32,128]{1,0:T(8,128)(2,1)S(1)}, u32[]{:S(2)}, u32[]{:S(2)}) %collective-permute-start.1) | collective-permute-done | bytes 8224 | tf_op jit(solution)/shard_map/ppermute | solution.py:413
  9.8 0.0 collective-permute-done.2.refs_2_
  9.8 1.6 %collective-permute-start.5 = (bf16[4,32,128]{2,1,0:T(8,128)(2,1)S(1)}, bf16[4,32,128]{2,1,0:T(8,128)(2,1)S(1)}, u32[]{:S(2)}, u32[]{:S(2)}) collective-permute-start(bf16[4,32,128]{2,1,0:T(8,128)(2,1)S(1)} %join_columns.1.own_ref), channel_id=1, source_target_pairs={{0,1},{1,0},{2,3},{3,2},{4,5},{5,4},{6,7},{7,6},{8,9},{9,8},{10,11... | collective-permute-start | bytes 98312 | tf_op jit(solution)/shard_map/ppermute | solution.py:426
  11.4 0.0 collective-permute-start.7
  11.4 0.1 unpack.1.own
  11.5 0.5 %collective-permute-start.3 = (bf16[4,32,128]{2,1,0:T(8,128)(2,1)S(1)}, bf16[4,32,128]{2,1,0:T(8,128)(2,1)S(1)}, u32[]{:S(2)}, u32[]{:S(2)}) collective-permute-start(bf16[4,32,128]{2,1,0:T(8,128)(2,1)S(1)} %join_columns.1.own_ref), channel_id=1, source_target_pairs={{0,1},{1,0},{2,3},{3,2},{4,5},{5,4},{6,7},{7,6},{8,17},{9,16},{10,... | collective-permute-start | bytes 98312 | tf_op jit(solution)/shard_map/ppermute | solution.py:426
  12.0 1.4 %collective-permute-start.4 = (bf16[4,32,128]{2,1,0:T(8,128)(2,1)S(1)}, bf16[4,32,128]{2,1,0:T(8,128)(2,1)S(1)}, u32[]{:S(2)}, u32[]{:S(2)}) collective-permute-start(bf16[4,32,128]{2,1,0:T(8,128)(2,1)S(1)} %join_columns.1.own_ref), channel_id=1, source_target_pairs={{0,24},{1,25},{2,26},{3,27},{4,28},{5,29},{6,30},{7,31},{8,16},{9,... | collective-permute-start | bytes 98312 | tf_op jit(solution)/shard_map/ppermute | solution.py:426
  13.3 0.0 collective-permute-done.8.mate_ref
  13.3 0.4 %collective-permute-done.5.mate = bf16[4,32,128]{2,1,0:T(8,128)(2,1)S(1)} collective-permute-done((bf16[4,32,128]{2,1,0:T(8,128)(2,1)S(1)}, bf16[4,32,128]{2,1,0:T(8,128)(2,1)S(1)}, u32[]{:S(2)}, u32[]{:S(2)}) %collective-permute-start.5) | collective-permute-done | bytes 32800 | tf_op jit(solution)/shard_map/ppermute | solution.py:426
  13.8 0.0 collective-permute-start.6
  13.8 0.5 %squares.1.squares_ref = bf16[2304,256]{1,0:T(8,128)(2,1)S(1)} custom-call(bf16[9,20,80]{2,1,0:T(8,128)(2,1)S(1)} %bitcast.5, bf16[9,20,80]{2,1,0:T(8,128)(2,1)S(1)} %collective-permute-done.8.mate_ref), custom_call_target="tpu_custom_call" | custom-call | flops 300000000 | bytes 1000000 | tf_op jit(solution)/shard_map/squares/pallas_call | solution.py:399
  14.4 0.0 collective-permute-done.7.even
  14.4 0.3 %conv_own.1 = (f32[2,432,256]{2,1,0:T(8,128)S(1)}, bf16[2,4,16,256]{3,2,1,0:T(8,128)(2,1)S(1)}) custom-call(bf16[4,32,128]{2,1,0:T(8,128)(2,1)S(1)} %collective-permute-done.5.mate, bf16[2,4,16,256]{3,2,1,0:T(8,128)(2,1)S(1)} %unpack.1.own, bf16[4,32,128]{2,1,0:T(8,128)(2,1)S(1)} %collective-permute-done.7.even, bf16[2,432,384]{2,1,0:T(8,128)(2,1)S(1)} %tables.1.table_ref), custom_call_target="tpu_custom_call" | custom-call | flops 300000000 | bytes 1000000 | tf_op jit(solution)/shard_map/conv_own/pallas_call | solution.py:399
  14.7 0.7 %collective-permute-done.3.odd_mate = bf16[4,32,128]{2,1,0:T(8,128)(2,1)S(1)} collective-permute-done((bf16[4,32,128]{2,1,0:T(8,128)(2,1)S(1)}, bf16[4,32,128]{2,1,0:T(8,128)(2,1)S(1)}, u32[]{:S(2)}, u32[]{:S(2)}) %collective-permute-start.3) | collective-permute-done | bytes 32800 | tf_op jit(solution)/shard_map/ppermute | solution.py:426
  15.4 0.0 collective-permute-done.4.odd_own
  15.4 0.0 collective-permute-done.6.even_mate
  15.4 0.0 copy-start
  15.4 0.8 %conv.1 = (bf16[32,128]{1,0:T(8,128)(2,1)S(1)}, bf16[32,128]{1,0:T(8,128)(2,1)S(1)}, bf16[32,128]{1,0:T(8,128)(2,1)S(1)}, bf16[32,128]{1,0:T(8,128)(2,1)S(1)}) custom-call(bf16[4,32,128]{2,1,0:T(8,128)(2,1)S(1)} %collective-permute-done.3.odd_mate, bf16[4,32,128]{2,1,0:T(8,128)(2,1)S(1)} %collective-permute-done.4.odd_own, ...), custom_call_target="tpu_custom_call" | custom-call | flops 10000000000 | bytes 1000000 | tf_op jit(solution)/shard_map/conv/pallas_call | solution.py:399
  16.2 0.0 copy-start.5
  16.2 2.0 %collective-permute-start.11 = (bf16[32,128]{1,0:T(8,128)(2,1)S(1)}, bf16[32,128]{1,0:T(8,128)(2,1)S(1)}, u32[]{:S(2)}, u32[]{:S(2)}) collective-permute-start(bf16[32,128]{1,0:T(8,128)(2,1)S(1)} %get-tuple-element.32), channel_id=1, source_target_pairs={{0,6},{1,7},{2,4},{3,5},{4,2},{5,3},{6,0},{7,1},{8,14},{9,15},{10,... | collective-permute-start | bytes 24584 | tf_op jit(solution)/shard_map/ppermute | solution.py:413
  18.2 0.0 collective-permute-start.10
  18.2 2.4 %collective-permute-start.9 = (bf16[32,128]{1,0:T(8,128)(2,1)S(1)}, bf16[32,128]{1,0:T(8,128)(2,1)S(1)}, u32[]{:S(2)}, u32[]{:S(2)}) collective-permute-start(bf16[32,128]{1,0:T(8,128)(2,1)S(1)} %get-tuple-element.29), channel_id=1, source_target_pairs={{0,2},{1,3},{2,0},{3,1},{4,6},{5,7},{6,4},{7,5},{8,10},{9,11},{10,... | collective-permute-start | bytes 24584 | tf_op jit(solution)/shard_map/ppermute | solution.py:413
  20.6 1.1 %collective-permute-done.11.first_ref = bf16[32,128]{1,0:T(8,128)(2,1)S(1)} collective-permute-done((bf16[32,128]{1,0:T(8,128)(2,1)S(1)}, bf16[32,128]{1,0:T(8,128)(2,1)S(1)}, u32[]{:S(2)}, u32[]{:S(2)}) %collective-permute-start.11) | collective-permute-done | bytes 8224 | tf_op jit(solution)/shard_map/ppermute | solution.py:413
  21.7 0.0 copy-done
  21.7 0.4 %lift.1 = (f32[4,24,256]{2,1,0:T(8,128)S(1)}, f32[24,640]{1,0:T(8,128)S(1)}, f32[32,1280]{1,0:T(8,128)S(1)}, f32[2,24,128]{2,1,0:T(8,128)S(1)}) custom-call(bf16[32,128]{1,0:T(8,128)(2,1)S(1)} %get-tuple-element.31.own_ref, bf16[32,128]{1,0:T(8,128)(2,1)S(1)} %collective-permute-done.11.first_ref, bf16[12,2,640]{2,1,0:T(2,128)(2,1)S(1)} %bitcast.8, ...), custom_call_target="tpu_custom_call" | custom-call | flops 100000000 | bytes 1000000 | tf_op jit(solution)/shard_map/lift/pallas_call | solution.py:399
  22.1 0.7 %collective-permute-done.10.refs_1_ = bf16[32,128]{1,0:T(8,128)(2,1)S(1)} collective-permute-done((bf16[32,128]{1,0:T(8,128)(2,1)S(1)}, bf16[32,128]{1,0:T(8,128)(2,1)S(1)}, u32[]{:S(2)}, u32[]{:S(2)}) %collective-permute-start.10) | collective-permute-done | bytes 8224 | tf_op jit(solution)/shard_map/ppermute | solution.py:413
  22.8 0.0 collective-permute-done.9.refs_0_
  22.8 0.0 copy-done.5
  22.8 1.3 %tail.1 = bf16[12,2,640]{2,1,0:T(2,128)(2,1)} custom-call(bf16[32,128]{1,0:T(8,128)(2,1)S(1)} %collective-permute-done.9.refs_0_, bf16[32,128]{1,0:T(8,128)(2,1)S(1)} %collective-permute-done.10.refs_1_, f32[4,24,256]{2,1,0:T(8,128)S(1)} %get-tuple-element.33.refs_2_, f32[24,640]{1,0:T(8,128)S(1)} %get-tuple-element.34.refs_3_, ...), custom_call_target="tpu_custom_call" | custom-call | flops 1000000000 | bytes 1000000 | tf_op jit(solution)/shard_map/tail/pallas_call | solution.py:399
  (2 shorter events, 0.0 us)
Async XLA Ops:
  0.0 4.1 %copy-start.2 = (bf16[2,12,640]{2,0,1:T(2,128)(2,1)S(1)}, bf16[2,12,640]{2,0,1:T(2,128)(2,1)}, u32[]{:S(2)}) copy-start(bf16[2,12,640]{2,0,1:T(2,128)(2,1)} %param.7) | copy-start | bytes 92164
  0.0 7.9 %collective-permute-start = (bf16[12,2,640]{2,1,0:T(2,128)(2,1)}, bf16[12,2,640]{2,1,0:T(2,128)(2,1)S(1)}, u32[]{:S(2)}, u32[]{:S(2)}) collective-permute-start(bf16[12,2,640]{2,1,0:T(2,128)(2,1)} %bitcast.6), channel_id=1, source_target_pairs={{0,4},{1,5},{2,6},{3,7},{4,0},{5,1},{6,2},{7,3},{8,12},{9,13},{10,... | collective-permute-start | bytes 92168 | tf_op jit(solution)/shard_map/ppermute | solution.py:413
  4.1 2.0 %copy-start.1 = (bf16[9,80,20]{1,2,0:T(8,128)(2,1)S(1)}, bf16[9,80,20]{1,2,0:T(8,128)(2,1)}, u32[]{:S(2)}) copy-start(bf16[9,80,20]{1,2,0:T(8,128)(2,1)} %param.9) | copy-start | bytes 86404
  4.1 3.4 %copy-start.3 = (bf16[9,96]{1,0:T(8,128)(2,1)S(1)}, bf16[9,96]{1,0:T(8,128)(2,1)}, u32[]{:S(2)}) copy-start(bf16[9,96]{1,0:T(8,128)(2,1)} %filter_ref.1) | copy-start | bytes 5188
  4.1 3.4 %copy-start.4 = (bf16[9,2,3]{0,1,2:T(2,128)(2,1)S(1)}, bf16[9,2,3]{0,1,2:T(2,128)(2,1)}, u32[]{:S(2)}) copy-start(bf16[9,2,3]{0,1,2:T(2,128)(2,1)} %param.10) | copy-start | bytes 328
  4.3 5.5 %collective-permute-start.1 = (bf16[32,128]{1,0:T(8,128)(2,1)S(1)}, bf16[32,128]{1,0:T(8,128)(2,1)S(1)}, u32[]{:S(2)}, u32[]{:S(2)}) collective-permute-start(bf16[32,128]{1,0:T(8,128)(2,1)S(1)} %get-tuple-element.22), channel_id=1, source_target_pairs={{0,6},{1,7},{2,4},{3,5},{4,2},{5,3},{6,0},{7,1},{8,14},{9,15},{10,... | collective-permute-start | bytes 24584 | tf_op jit(solution)/shard_map/ppermute | solution.py:413
  6.0 3.8 %collective-permute-start.2 = (bf16[32,128]{1,0:T(8,128)(2,1)S(1)}, bf16[32,128]{1,0:T(8,128)(2,1)S(1)}, u32[]{:S(2)}, u32[]{:S(2)}) collective-permute-start(bf16[32,128]{1,0:T(8,128)(2,1)S(1)} %get-tuple-element.23), channel_id=1, source_target_pairs={{0,2},{1,3},{2,0},{3,1},{4,6},{5,7},{6,4},{7,5},{8,10},{9,11},{10,... | collective-permute-start | bytes 24584 | tf_op jit(solution)/shard_map/ppermute | solution.py:413
  6.0 7.3 %collective-permute-start.8 = (bf16[9,20,80]{2,1,0:T(8,128)(2,1)S(1)}, bf16[9,20,80]{2,1,0:T(8,128)(2,1)S(1)}, u32[]{:S(2)}, u32[]{:S(2)}) collective-permute-start(bf16[9,20,80]{2,1,0:T(8,128)(2,1)S(1)} %bitcast.4), channel_id=1, source_target_pairs={{0,1},{1,0},{2,3},{3,2},{4,5},{5,4},{6,7},{7,6},{8,9},{9,8},{10,11... | collective-permute-start | bytes 86408 | tf_op jit(solution)/shard_map/ppermute | solution.py:417
  9.8 4.0 %collective-permute-start.5 = (bf16[4,32,128]{2,1,0:T(8,128)(2,1)S(1)}, bf16[4,32,128]{2,1,0:T(8,128)(2,1)S(1)}, u32[]{:S(2)}, u32[]{:S(2)}) collective-permute-start(bf16[4,32,128]{2,1,0:T(8,128)(2,1)S(1)} %join_columns.1.own_ref), channel_id=1, source_target_pairs={{0,1},{1,0},{2,3},{3,2},{4,5},{5,4},{6,7},{7,6},{8,9},{9,8},{10,11... | collective-permute-start | bytes 98312 | tf_op jit(solution)/shard_map/ppermute | solution.py:426
  11.4 3.0 %collective-permute-start.7 = (bf16[4,32,128]{2,1,0:T(8,128)(2,1)S(1)}, bf16[4,32,128]{2,1,0:T(8,128)(2,1)S(1)}, u32[]{:S(2)}, u32[]{:S(2)}) collective-permute-start(bf16[4,32,128]{2,1,0:T(8,128)(2,1)S(1)} %join_columns.1.own_ref), channel_id=1, source_target_pairs={{0,8},{1,9},{2,10},{3,11},{4,12},{5,13},{6,14},{7,15},{8,0},{9,1},... | collective-permute-start | bytes 98312 | tf_op jit(solution)/shard_map/ppermute | solution.py:426
  11.5 3.9 %collective-permute-start.3 = (bf16[4,32,128]{2,1,0:T(8,128)(2,1)S(1)}, bf16[4,32,128]{2,1,0:T(8,128)(2,1)S(1)}, u32[]{:S(2)}, u32[]{:S(2)}) collective-permute-start(bf16[4,32,128]{2,1,0:T(8,128)(2,1)S(1)} %join_columns.1.own_ref), channel_id=1, source_target_pairs={{0,1},{1,0},{2,3},{3,2},{4,5},{5,4},{6,7},{7,6},{8,17},{9,16},{10,... | collective-permute-start | bytes 98312 | tf_op jit(solution)/shard_map/ppermute | solution.py:426
  12.0 3.4 %collective-permute-start.4 = (bf16[4,32,128]{2,1,0:T(8,128)(2,1)S(1)}, bf16[4,32,128]{2,1,0:T(8,128)(2,1)S(1)}, u32[]{:S(2)}, u32[]{:S(2)}) collective-permute-start(bf16[4,32,128]{2,1,0:T(8,128)(2,1)S(1)} %join_columns.1.own_ref), channel_id=1, source_target_pairs={{0,24},{1,25},{2,26},{3,27},{4,28},{5,29},{6,30},{7,31},{8,16},{9,... | collective-permute-start | bytes 98312 | tf_op jit(solution)/shard_map/ppermute | solution.py:426
  13.8 1.6 %collective-permute-start.6 = (bf16[4,32,128]{2,1,0:T(8,128)(2,1)S(1)}, bf16[4,32,128]{2,1,0:T(8,128)(2,1)S(1)}, u32[]{:S(2)}, u32[]{:S(2)}) collective-permute-start(bf16[4,32,128]{2,1,0:T(8,128)(2,1)S(1)} %collective-permute-done.5.mate), channel_id=1, source_target_pairs={{0,8},{1,9},{2,10},{3,11},{4,12},{5,13},{6,14},{7,15},{8,0},{9,1},... | collective-permute-start | bytes 98312 | tf_op jit(solution)/shard_map/ppermute | solution.py:426
  15.4 6.3 %copy-start = (bf16[640,1280]{1,0:T(8,128)(2,1)S(1)}, bf16[640,1280]{1,0:T(8,128)(2,1)}, u32[]{:S(2)}) copy-start(bf16[640,1280]{1,0:T(8,128)(2,1)} %refs_6_.1) | copy-start | bytes 4915204
  16.2 6.6 %copy-start.5 = (bf16[1280,640]{1,0:T(8,128)(2,1)S(1)}, bf16[1280,640]{1,0:T(8,128)(2,1)}, u32[]{:S(2)}) copy-start(bf16[1280,640]{1,0:T(8,128)(2,1)} %refs_7_.1) | copy-start | bytes 4915204
  16.2 5.5 %collective-permute-start.11 = (bf16[32,128]{1,0:T(8,128)(2,1)S(1)}, bf16[32,128]{1,0:T(8,128)(2,1)S(1)}, u32[]{:S(2)}, u32[]{:S(2)}) collective-permute-start(bf16[32,128]{1,0:T(8,128)(2,1)S(1)} %get-tuple-element.32), channel_id=1, source_target_pairs={{0,6},{1,7},{2,4},{3,5},{4,2},{5,3},{6,0},{7,1},{8,14},{9,15},{10,... | collective-permute-start | bytes 24584 | tf_op jit(solution)/shard_map/ppermute | solution.py:413
  18.2 4.6 %collective-permute-start.10 = (bf16[32,128]{1,0:T(8,128)(2,1)S(1)}, bf16[32,128]{1,0:T(8,128)(2,1)S(1)}, u32[]{:S(2)}, u32[]{:S(2)}) collective-permute-start(bf16[32,128]{1,0:T(8,128)(2,1)S(1)} %get-tuple-element.30), channel_id=1, source_target_pairs={{0,4},{1,5},{2,6},{3,7},{4,0},{5,1},{6,2},{7,3},{8,12},{9,13},{10,... | collective-permute-start | bytes 24584 | tf_op jit(solution)/shard_map/ppermute | solution.py:413
  18.2 4.6 %collective-permute-start.9 = (bf16[32,128]{1,0:T(8,128)(2,1)S(1)}, bf16[32,128]{1,0:T(8,128)(2,1)S(1)}, u32[]{:S(2)}, u32[]{:S(2)}) collective-permute-start(bf16[32,128]{1,0:T(8,128)(2,1)S(1)} %get-tuple-element.29), channel_id=1, source_target_pairs={{0,2},{1,3},{2,0},{3,1},{4,6},{5,7},{6,4},{7,5},{8,10},{9,11},{10,... | collective-permute-start | bytes 24584 | tf_op jit(solution)/shard_map/ppermute | solution.py:413

commit v19 on v18

--- a/solution.py
+++ b/solution.py
@@ -375,8 +375,8 @@
     count = summed_ref.shape[0]
     product = None
     units = raised.shape[1]
-    for start in range(0, units, 4 * LANES):
-        taken = slice(start, min(start + 4 * LANES, units))
+    for start in range(0, units, LANES):
+        taken = slice(start, min(start + LANES, units))
         hidden = scale * (raised[:count, taken] - mean * raised[count : count + 1, taken])
         hidden = (0.5 * hidden * (1.0 + lax.erf(hidden * 0.5**0.5))).astype(BF16)
         part = jnp.dot(hidden, down_ref[taken], preferred_element_type=F32)

time: 24.2 us -> 24.3 us (level)
  no operation moved by 1% of the time
where the time goes in v19:
time: 24.3 us; the launch traced here: 24.2 us
  starting transfers between devices  15.2 us (63%)
  waiting for transfers between devices  4.56 us (19%)
  Pallas kernels  4.3 us (18%)
    ppermute x6, starting transfers between devices, over_columns(): return lax.ppermute(message, 'lon', pairs) if apart else message  10.2 us
    pallas_call x11, Pallas kernels, call(): pl.pallas_call(kernel, out_shape=out_shape, in_specs=[VMEM] * len(operand...  4.3 us
    ppermute x5, starting transfers between devices, swap(): return lax.ppermute(block, ('lat', 'lon'), pairs)  3.45 us
    ppermute x6, waiting for transfers between devices, over_columns(): return lax.ppermute(message, 'lon', pairs) if apart else message  3.45 us
    ppermute x1, starting transfers between devices, over_sides(): return lax.ppermute(block, 'lon', [(i, i ^ 1) for i in range(count)])  1.49 us
    ppermute x5, waiting for transfers between devices, swap(): return lax.ppermute(block, ('lat', 'lon'), pairs)  1.11 us
  transfers between devices with their start and end apart: 12, of which 5 were waited for; matrix products, arithmetic and copies ran while one was open for 0% of the time, Pallas kernels for 9%

profile of v19, /device:TPU:0, one launch (start us, length us, event | category | flops | bytes accessed | tf_op | source)
XLA Modules:
  0.0 24.2 jit_solution(16381275737479558396)
XLA Ops:
  0.0 0.0 copy-start.2
  0.0 4.0 %collective-permute-start = (bf16[12,2,640]{2,1,0:T(2,128)(2,1)}, bf16[12,2,640]{2,1,0:T(2,128)(2,1)S(1)}, u32[]{:S(2)}, u32[]{:S(2)}) collective-permute-start(bf16[12,2,640]{2,1,0:T(2,128)(2,1)} %bitcast.6), channel_id=1, source_target_pairs={{0,4},{1,5},{2,6},{3,7},{4,0},{5,1},{6,2},{7,3},{8,12},{9,13},{10,... | collective-permute-start | bytes 92168 | tf_op jit(solution)/shard_map/ppermute | solution.py:413
  4.1 0.0 copy-done.2
  4.1 0.0 copy-start.1
  4.1 0.0 copy-start.3
  4.1 0.0 copy-start.4
  4.1 0.2 pack.1
  4.3 1.7 %collective-permute-start.1 = (bf16[32,128]{1,0:T(8,128)(2,1)S(1)}, bf16[32,128]{1,0:T(8,128)(2,1)S(1)}, u32[]{:S(2)}, u32[]{:S(2)}) collective-permute-start(bf16[32,128]{1,0:T(8,128)(2,1)S(1)} %get-tuple-element.22), channel_id=1, source_target_pairs={{0,6},{1,7},{2,4},{3,5},{4,2},{5,3},{6,0},{7,1},{8,14},{9,15},{10,... | collective-permute-start | bytes 24584 | tf_op jit(solution)/shard_map/ppermute | solution.py:413
  6.0 0.0 collective-permute-start.2
  6.0 0.0 copy-done.1
  6.0 1.5 %collective-permute-start.8 = (bf16[9,20,80]{2,1,0:T(8,128)(2,1)S(1)}, bf16[9,20,80]{2,1,0:T(8,128)(2,1)S(1)}, u32[]{:S(2)}, u32[]{:S(2)}) collective-permute-start(bf16[9,20,80]{2,1,0:T(8,128)(2,1)S(1)} %bitcast.4), channel_id=1, source_target_pairs={{0,1},{1,0},{2,3},{3,2},{4,5},{5,4},{6,7},{7,6},{8,9},{9,8},{10,11... | collective-permute-start | bytes 86408 | tf_op jit(solution)/shard_map/ppermute | solution.py:417
  7.5 0.0 copy-done.3
  7.5 0.0 copy-done.4
  7.5 0.4 %tables.1.table_ref = bf16[2,432,384]{2,1,0:T(8,128)(2,1)S(1)} custom-call(bf16[9,96]{1,0:T(8,128)(2,1)S(1)} %copy-done.3, bf16[3,2,9]{2,1,0:T(2,128)(2,1)S(1)} %bitcast.9, s32[96,128]{1,0:T(8,128)S(1)} %apart.1.apart_ref), custom_call_target="tpu_custom_call" | custom-call | flops 1000000 | bytes 1000000 | tf_op jit(solution)/shard_map/tables/pallas_call | solution.py:399
  7.9 0.0 collective-permute-done.raw_ref
  7.9 0.2 cut.1.refs_0_
  8.1 1.7 %collective-permute-done.1.refs_1_ = bf16[32,128]{1,0:T(8,128)(2,1)S(1)} collective-permute-done((bf16[32,128]{1,0:T(8,128)(2,1)S(1)}, bf16[32,128]{1,0:T(8,128)(2,1)S(1)}, u32[]{:S(2)}, u32[]{:S(2)}) %collective-permute-start.1) | collective-permute-done | bytes 8224 | tf_op jit(solution)/shard_map/ppermute | solution.py:413
  9.8 0.0 collective-permute-done.2.refs_2_
  9.8 1.6 %collective-permute-start.5 = (bf16[4,32,128]{2,1,0:T(8,128)(2,1)S(1)}, bf16[4,32,128]{2,1,0:T(8,128)(2,1)S(1)}, u32[]{:S(2)}, u32[]{:S(2)}) collective-permute-start(bf16[4,32,128]{2,1,0:T(8,128)(2,1)S(1)} %join_columns.1.own_ref), channel_id=1, source_target_pairs={{0,1},{1,0},{2,3},{3,2},{4,5},{5,4},{6,7},{7,6},{8,9},{9,8},{10,11... | collective-permute-start | bytes 98312 | tf_op jit(solution)/shard_map/ppermute | solution.py:426
  11.4 0.0 collective-permute-start.7
  11.4 0.1 unpack.1.own
  11.5 0.5 %collective-permute-start.3 = (bf16[4,32,128]{2,1,0:T(8,128)(2,1)S(1)}, bf16[4,32,128]{2,1,0:T(8,128)(2,1)S(1)}, u32[]{:S(2)}, u32[]{:S(2)}) collective-permute-start(bf16[4,32,128]{2,1,0:T(8,128)(2,1)S(1)} %join_columns.1.own_ref), channel_id=1, source_target_pairs={{0,1},{1,0},{2,3},{3,2},{4,5},{5,4},{6,7},{7,6},{8,17},{9,16},{10,... | collective-permute-start | bytes 98312 | tf_op jit(solution)/shard_map/ppermute | solution.py:426
  12.0 1.4 %collective-permute-start.4 = (bf16[4,32,128]{2,1,0:T(8,128)(2,1)S(1)}, bf16[4,32,128]{2,1,0:T(8,128)(2,1)S(1)}, u32[]{:S(2)}, u32[]{:S(2)}) collective-permute-start(bf16[4,32,128]{2,1,0:T(8,128)(2,1)S(1)} %join_columns.1.own_ref), channel_id=1, source_target_pairs={{0,24},{1,25},{2,26},{3,27},{4,28},{5,29},{6,30},{7,31},{8,16},{9,... | collective-permute-start | bytes 98312 | tf_op jit(solution)/shard_map/ppermute | solution.py:426
  13.3 0.0 collective-permute-done.8.mate_ref
  13.3 0.4 %collective-permute-done.5.mate = bf16[4,32,128]{2,1,0:T(8,128)(2,1)S(1)} collective-permute-done((bf16[4,32,128]{2,1,0:T(8,128)(2,1)S(1)}, bf16[4,32,128]{2,1,0:T(8,128)(2,1)S(1)}, u32[]{:S(2)}, u32[]{:S(2)}) %collective-permute-start.5) | collective-permute-done | bytes 32800 | tf_op jit(solution)/shard_map/ppermute | solution.py:426
  13.8 0.0 collective-permute-start.6
  13.8 0.5 %squares.1.squares_ref = bf16[2304,256]{1,0:T(8,128)(2,1)S(1)} custom-call(bf16[9,20,80]{2,1,0:T(8,128)(2,1)S(1)} %bitcast.5, bf16[9,20,80]{2,1,0:T(8,128)(2,1)S(1)} %collective-permute-done.8.mate_ref), custom_call_target="tpu_custom_call" | custom-call | flops 300000000 | bytes 1000000 | tf_op jit(solution)/shard_map/squares/pallas_call | solution.py:399
  14.4 0.0 collective-permute-done.7.even
  14.4 0.3 %conv_own.1 = (f32[2,432,256]{2,1,0:T(8,128)S(1)}, bf16[2,4,16,256]{3,2,1,0:T(8,128)(2,1)S(1)}) custom-call(bf16[4,32,128]{2,1,0:T(8,128)(2,1)S(1)} %collective-permute-done.5.mate, bf16[2,4,16,256]{3,2,1,0:T(8,128)(2,1)S(1)} %unpack.1.own, bf16[4,32,128]{2,1,0:T(8,128)(2,1)S(1)} %collective-permute-done.7.even, bf16[2,432,384]{2,1,0:T(8,128)(2,1)S(1)} %tables.1.table_ref), custom_call_target="tpu_custom_call" | custom-call | flops 300000000 | bytes 1000000 | tf_op jit(solution)/shard_map/conv_own/pallas_call | solution.py:399
  14.7 0.7 %collective-permute-done.3.odd_mate = bf16[4,32,128]{2,1,0:T(8,128)(2,1)S(1)} collective-permute-done((bf16[4,32,128]{2,1,0:T(8,128)(2,1)S(1)}, bf16[4,32,128]{2,1,0:T(8,128)(2,1)S(1)}, u32[]{:S(2)}, u32[]{:S(2)}) %collective-permute-start.3) | collective-permute-done | bytes 32800 | tf_op jit(solution)/shard_map/ppermute | solution.py:426
  15.4 0.0 collective-permute-done.4.odd_own
  15.4 0.0 collective-permute-done.6.even_mate
  15.4 0.0 copy-start
  15.4 0.8 %conv.1 = (bf16[32,128]{1,0:T(8,128)(2,1)S(1)}, bf16[32,128]{1,0:T(8,128)(2,1)S(1)}, bf16[32,128]{1,0:T(8,128)(2,1)S(1)}, bf16[32,128]{1,0:T(8,128)(2,1)S(1)}) custom-call(bf16[4,32,128]{2,1,0:T(8,128)(2,1)S(1)} %collective-permute-done.3.odd_mate, bf16[4,32,128]{2,1,0:T(8,128)(2,1)S(1)} %collective-permute-done.4.odd_own, ...), custom_call_target="tpu_custom_call" | custom-call | flops 10000000000 | bytes 1000000 | tf_op jit(solution)/shard_map/conv/pallas_call | solution.py:399
  16.2 0.0 copy-start.5
  16.2 2.0 %collective-permute-start.11 = (bf16[32,128]{1,0:T(8,128)(2,1)S(1)}, bf16[32,128]{1,0:T(8,128)(2,1)S(1)}, u32[]{:S(2)}, u32[]{:S(2)}) collective-permute-start(bf16[32,128]{1,0:T(8,128)(2,1)S(1)} %get-tuple-element.32), channel_id=1, source_target_pairs={{0,6},{1,7},{2,4},{3,5},{4,2},{5,3},{6,0},{7,1},{8,14},{9,15},{10,... | collective-permute-start | bytes 24584 | tf_op jit(solution)/shard_map/ppermute | solution.py:413
  18.2 0.0 collective-permute-start.10
  18.2 2.4 %collective-permute-start.9 = (bf16[32,128]{1,0:T(8,128)(2,1)S(1)}, bf16[32,128]{1,0:T(8,128)(2,1)S(1)}, u32[]{:S(2)}, u32[]{:S(2)}) collective-permute-start(bf16[32,128]{1,0:T(8,128)(2,1)S(1)} %get-tuple-element.29), channel_id=1, source_target_pairs={{0,2},{1,3},{2,0},{3,1},{4,6},{5,7},{6,4},{7,5},{8,10},{9,11},{10,... | collective-permute-start | bytes 24584 | tf_op jit(solution)/shard_map/ppermute | solution.py:413
  20.6 1.1 %collective-permute-done.11.first_ref = bf16[32,128]{1,0:T(8,128)(2,1)S(1)} collective-permute-done((bf16[32,128]{1,0:T(8,128)(2,1)S(1)}, bf16[32,128]{1,0:T(8,128)(2,1)S(1)}, u32[]{:S(2)}, u32[]{:S(2)}) %collective-permute-start.11) | collective-permute-done | bytes 8224 | tf_op jit(solution)/shard_map/ppermute | solution.py:413
  21.7 0.0 copy-done
  21.7 0.4 %lift.1 = (f32[4,24,256]{2,1,0:T(8,128)S(1)}, f32[24,640]{1,0:T(8,128)S(1)}, f32[32,1280]{1,0:T(8,128)S(1)}, f32[2,24,128]{2,1,0:T(8,128)S(1)}) custom-call(bf16[32,128]{1,0:T(8,128)(2,1)S(1)} %get-tuple-element.31.own_ref, bf16[32,128]{1,0:T(8,128)(2,1)S(1)} %collective-permute-done.11.first_ref, bf16[12,2,640]{2,1,0:T(2,128)(2,1)S(1)} %bitcast.8, ...), custom_call_target="tpu_custom_call" | custom-call | flops 100000000 | bytes 1000000 | tf_op jit(solution)/shard_map/lift/pallas_call | solution.py:399
  22.1 0.7 %collective-permute-done.10.refs_1_ = bf16[32,128]{1,0:T(8,128)(2,1)S(1)} collective-permute-done((bf16[32,128]{1,0:T(8,128)(2,1)S(1)}, bf16[32,128]{1,0:T(8,128)(2,1)S(1)}, u32[]{:S(2)}, u32[]{:S(2)}) %collective-permute-start.10) | collective-permute-done | bytes 8224 | tf_op jit(solution)/shard_map/ppermute | solution.py:413
  22.8 0.0 collective-permute-done.9.refs_0_
  22.8 0.0 copy-done.5
  22.8 1.4 %tail.1 = bf16[12,2,640]{2,1,0:T(2,128)(2,1)} custom-call(bf16[32,128]{1,0:T(8,128)(2,1)S(1)} %collective-permute-done.9.refs_0_, bf16[32,128]{1,0:T(8,128)(2,1)S(1)} %collective-permute-done.10.refs_1_, f32[4,24,256]{2,1,0:T(8,128)S(1)} %get-tuple-element.33.refs_2_, f32[24,640]{1,0:T(8,128)S(1)} %get-tuple-element.34.refs_3_, ...), custom_call_target="tpu_custom_call" | custom-call | flops 1000000000 | bytes 1000000 | tf_op jit(solution)/shard_map/tail/pallas_call | solution.py:399
  (2 shorter events, 0.0 us)
Async XLA Ops:
  0.0 4.1 %copy-start.2 = (bf16[2,12,640]{2,0,1:T(2,128)(2,1)S(1)}, bf16[2,12,640]{2,0,1:T(2,128)(2,1)}, u32[]{:S(2)}) copy-start(bf16[2,12,640]{2,0,1:T(2,128)(2,1)} %param.7) | copy-start | bytes 92164
  0.0 7.9 %collective-permute-start = (bf16[12,2,640]{2,1,0:T(2,128)(2,1)}, bf16[12,2,640]{2,1,0:T(2,128)(2,1)S(1)}, u32[]{:S(2)}, u32[]{:S(2)}) collective-permute-start(bf16[12,2,640]{2,1,0:T(2,128)(2,1)} %bitcast.6), channel_id=1, source_target_pairs={{0,4},{1,5},{2,6},{3,7},{4,0},{5,1},{6,2},{7,3},{8,12},{9,13},{10,... | collective-permute-start | bytes 92168 | tf_op jit(solution)/shard_map/ppermute | solution.py:413
  4.1 2.0 %copy-start.1 = (bf16[9,80,20]{1,2,0:T(8,128)(2,1)S(1)}, bf16[9,80,20]{1,2,0:T(8,128)(2,1)}, u32[]{:S(2)}) copy-start(bf16[9,80,20]{1,2,0:T(8,128)(2,1)} %param.9) | copy-start | bytes 86404
  4.1 3.4 %copy-start.3 = (bf16[9,96]{1,0:T(8,128)(2,1)S(1)}, bf16[9,96]{1,0:T(8,128)(2,1)}, u32[]{:S(2)}) copy-start(bf16[9,96]{1,0:T(8,128)(2,1)} %filter_ref.1) | copy-start | bytes 5188
  4.1 3.4 %copy-start.4 = (bf16[9,2,3]{0,1,2:T(2,128)(2,1)S(1)}, bf16[9,2,3]{0,1,2:T(2,128)(2,1)}, u32[]{:S(2)}) copy-start(bf16[9,2,3]{0,1,2:T(2,128)(2,1)} %param.10) | copy-start | bytes 328
  4.3 5.5 %collective-permute-start.1 = (bf16[32,128]{1,0:T(8,128)(2,1)S(1)}, bf16[32,128]{1,0:T(8,128)(2,1)S(1)}, u32[]{:S(2)}, u32[]{:S(2)}) collective-permute-start(bf16[32,128]{1,0:T(8,128)(2,1)S(1)} %get-tuple-element.22), channel_id=1, source_target_pairs={{0,6},{1,7},{2,4},{3,5},{4,2},{5,3},{6,0},{7,1},{8,14},{9,15},{10,... | collective-permute-start | bytes 24584 | tf_op jit(solution)/shard_map/ppermute | solution.py:413
  6.0 3.8 %collective-permute-start.2 = (bf16[32,128]{1,0:T(8,128)(2,1)S(1)}, bf16[32,128]{1,0:T(8,128)(2,1)S(1)}, u32[]{:S(2)}, u32[]{:S(2)}) collective-permute-start(bf16[32,128]{1,0:T(8,128)(2,1)S(1)} %get-tuple-element.23), channel_id=1, source_target_pairs={{0,2},{1,3},{2,0},{3,1},{4,6},{5,7},{6,4},{7,5},{8,10},{9,11},{10,... | collective-permute-start | bytes 24584 | tf_op jit(solution)/shard_map/ppermute | solution.py:413
  6.0 7.3 %collective-permute-start.8 = (bf16[9,20,80]{2,1,0:T(8,128)(2,1)S(1)}, bf16[9,20,80]{2,1,0:T(8,128)(2,1)S(1)}, u32[]{:S(2)}, u32[]{:S(2)}) collective-permute-start(bf16[9,20,80]{2,1,0:T(8,128)(2,1)S(1)} %bitcast.4), channel_id=1, source_target_pairs={{0,1},{1,0},{2,3},{3,2},{4,5},{5,4},{6,7},{7,6},{8,9},{9,8},{10,11... | collective-permute-start | bytes 86408 | tf_op jit(solution)/shard_map/ppermute | solution.py:417
  9.8 4.0 %collective-permute-start.5 = (bf16[4,32,128]{2,1,0:T(8,128)(2,1)S(1)}, bf16[4,32,128]{2,1,0:T(8,128)(2,1)S(1)}, u32[]{:S(2)}, u32[]{:S(2)}) collective-permute-start(bf16[4,32,128]{2,1,0:T(8,128)(2,1)S(1)} %join_columns.1.own_ref), channel_id=1, source_target_pairs={{0,1},{1,0},{2,3},{3,2},{4,5},{5,4},{6,7},{7,6},{8,9},{9,8},{10,11... | collective-permute-start | bytes 98312 | tf_op jit(solution)/shard_map/ppermute | solution.py:426
  11.4 3.0 %collective-permute-start.7 = (bf16[4,32,128]{2,1,0:T(8,128)(2,1)S(1)}, bf16[4,32,128]{2,1,0:T(8,128)(2,1)S(1)}, u32[]{:S(2)}, u32[]{:S(2)}) collective-permute-start(bf16[4,32,128]{2,1,0:T(8,128)(2,1)S(1)} %join_columns.1.own_ref), channel_id=1, source_target_pairs={{0,8},{1,9},{2,10},{3,11},{4,12},{5,13},{6,14},{7,15},{8,0},{9,1},... | collective-permute-start | bytes 98312 | tf_op jit(solution)/shard_map/ppermute | solution.py:426
  11.5 3.9 %collective-permute-start.3 = (bf16[4,32,128]{2,1,0:T(8,128)(2,1)S(1)}, bf16[4,32,128]{2,1,0:T(8,128)(2,1)S(1)}, u32[]{:S(2)}, u32[]{:S(2)}) collective-permute-start(bf16[4,32,128]{2,1,0:T(8,128)(2,1)S(1)} %join_columns.1.own_ref), channel_id=1, source_target_pairs={{0,1},{1,0},{2,3},{3,2},{4,5},{5,4},{6,7},{7,6},{8,17},{9,16},{10,... | collective-permute-start | bytes 98312 | tf_op jit(solution)/shard_map/ppermute | solution.py:426
  12.0 3.4 %collective-permute-start.4 = (bf16[4,32,128]{2,1,0:T(8,128)(2,1)S(1)}, bf16[4,32,128]{2,1,0:T(8,128)(2,1)S(1)}, u32[]{:S(2)}, u32[]{:S(2)}) collective-permute-start(bf16[4,32,128]{2,1,0:T(8,128)(2,1)S(1)} %join_columns.1.own_ref), channel_id=1, source_target_pairs={{0,24},{1,25},{2,26},{3,27},{4,28},{5,29},{6,30},{7,31},{8,16},{9,... | collective-permute-start | bytes 98312 | tf_op jit(solution)/shard_map/ppermute | solution.py:426
  13.8 1.6 %collective-permute-start.6 = (bf16[4,32,128]{2,1,0:T(8,128)(2,1)S(1)}, bf16[4,32,128]{2,1,0:T(8,128)(2,1)S(1)}, u32[]{:S(2)}, u32[]{:S(2)}) collective-permute-start(bf16[4,32,128]{2,1,0:T(8,128)(2,1)S(1)} %collective-permute-done.5.mate), channel_id=1, source_target_pairs={{0,8},{1,9},{2,10},{3,11},{4,12},{5,13},{6,14},{7,15},{8,0},{9,1},... | collective-permute-start | bytes 98312 | tf_op jit(solution)/shard_map/ppermute | solution.py:426
  15.4 6.3 %copy-start = (bf16[640,1280]{1,0:T(8,128)(2,1)S(1)}, bf16[640,1280]{1,0:T(8,128)(2,1)}, u32[]{:S(2)}) copy-start(bf16[640,1280]{1,0:T(8,128)(2,1)} %refs_6_.1) | copy-start | bytes 4915204
  16.2 6.6 %copy-start.5 = (bf16[1280,640]{1,0:T(8,128)(2,1)S(1)}, bf16[1280,640]{1,0:T(8,128)(2,1)}, u32[]{:S(2)}) copy-start(bf16[1280,640]{1,0:T(8,128)(2,1)} %refs_7_.1) | copy-start | bytes 4915204
  16.2 5.5 %collective-permute-start.11 = (bf16[32,128]{1,0:T(8,128)(2,1)S(1)}, bf16[32,128]{1,0:T(8,128)(2,1)S(1)}, u32[]{:S(2)}, u32[]{:S(2)}) collective-permute-start(bf16[32,128]{1,0:T(8,128)(2,1)S(1)} %get-tuple-element.32), channel_id=1, source_target_pairs={{0,6},{1,7},{2,4},{3,5},{4,2},{5,3},{6,0},{7,1},{8,14},{9,15},{10,... | collective-permute-start | bytes 24584 | tf_op jit(solution)/shard_map/ppermute | solution.py:413
  18.2 4.6 %collective-permute-start.10 = (bf16[32,128]{1,0:T(8,128)(2,1)S(1)}, bf16[32,128]{1,0:T(8,128)(2,1)S(1)}, u32[]{:S(2)}, u32[]{:S(2)}) collective-permute-start(bf16[32,128]{1,0:T(8,128)(2,1)S(1)} %get-tuple-element.30), channel_id=1, source_target_pairs={{0,4},{1,5},{2,6},{3,7},{4,0},{5,1},{6,2},{7,3},{8,12},{9,13},{10,... | collective-permute-start | bytes 24584 | tf_op jit(solution)/shard_map/ppermute | solution.py:413
  18.2 4.6 %collective-permute-start.9 = (bf16[32,128]{1,0:T(8,128)(2,1)S(1)}, bf16[32,128]{1,0:T(8,128)(2,1)S(1)}, u32[]{:S(2)}, u32[]{:S(2)}) collective-permute-start(bf16[32,128]{1,0:T(8,128)(2,1)S(1)} %get-tuple-element.29), channel_id=1, source_target_pairs={{0,2},{1,3},{2,0},{3,1},{4,6},{5,7},{6,4},{7,5},{8,10},{9,11},{10,... | collective-permute-start | bytes 24584 | tf_op jit(solution)/shard_map/ppermute | solution.py:413
